TPU v7x, 256 devices: a whole 4x4x8 slice. The times are simulated.
256 devices in a mesh: dom: 64 (over z, y, core), ray: 4 (over x).
Axes of the slice: x: 4, y: 4, z: 8, core: 2. Of those that a mesh axis runs over, the one named last changes fastest.
Arguments:
- projections: bfloat16 [64, 64, 8192], P('dom', None, 'ray'), may hold values from -6 to 6
- phase_kernel: bfloat16 [129], replicated, may hold values from -0.5 to 0.5
- image: bfloat16 [131072, 64], P('dom'), may hold values from -6 to 6
- tile_library: bfloat16 [64, 4, 16, 128, 128], P('dom', 'ray'), may hold values from -0.25 to 0.25
- tile_entry: int32 [64, 4, 256], P('dom', 'ray'), may hold values from 0 to 15
- tile_image: int32 [64, 4, 256], P('dom', 'ray'), may hold values from 0 to 15
- tile_slot: int32 [64, 4, 256], P('dom', 'ray'), may hold values from 0 to 63
- tile_count: int32 [64, 4], P('dom', 'ray'), may hold values from 64 to 256, as said below
- slot_block: int32 [64, 4, 64], P('dom', 'ray'), may hold values from 0 to 15
Outputs:
- residual: bfloat16 [64, 64, 8192], P('dom', None, 'ray')
- image_next: float32 [131072, 64], P(('dom', 'ray'))
Inputs may be any that keep to these rules, and one draw needn't show every extreme that they name: `tile_count`: each device has at most 256 live tiles; some device holds exactly 256. Entries beyond a device's count are not used.
All inputs are finite; a program needn't handle non-finite values.
Results may differ from a plain program's by a relative error of at most 0.0075.
Values may be sent and summed in bfloat16 or wider, within the bound.
No kernel may reach another device: no remote copies, remote signals or barrier semaphores. Data moves between devices by JAX's collectives and lax.ppermute only.
A program may use at most 64 MiB of HBM per device.

v0:
```python
import jax
import jax.numpy as jnp
from jax import lax
from jax.sharding import Mesh
from jax.sharding import PartitionSpec as P

SMOOTH = 8
DOM = ("dom_0", "dom_1", "dom_2")
DOM_RAY = ("dom_0", "dom_1", "dom_2", "ray")


relax_factor = 0.25


def with_halo(cells, sides, width):
    for axis, dim in sides:
        count = lax.axis_size(axis)
        ends = count - 1
        head = lax.slice_in_dim(cells, 0, width, axis=dim)
        tail = lax.slice_in_dim(cells, cells.shape[dim] - width, cells.shape[dim], axis=dim)
        cells = jnp.concatenate(
            [
                lax.ppermute(tail, axis, [(i, (i + 1) % count) for i in range(ends)]),
                cells,
                lax.ppermute(head, axis, [((i + 1) % count, i) for i in range(ends)]),
            ],
            axis=dim,
        )
    return cells


def whole_of(array, axes, dim):
    for axis in reversed(axes):
        array = lax.all_gather(array, axis, axis=dim, tiled=True)
    return array


def split_up(array, dim, length):
    dims = array.shape
    parts = array.reshape(*dims[:dim], length, dims[dim] // length, *dims[dim + 1 :])
    return jnp.moveaxis(parts, dim, 0)


def sent_and_summed(array, axis, dim):
    parts = split_up(array, dim, lax.axis_size(axis))
    arrived = lax.all_to_all(parts, axis, split_axis=0, concat_axis=0, tiled=True)
    return arrived.sum(axis=0)


def toeplitz(kernel, tile_size):
    taps = kernel.shape[0]
    padded = jnp.concatenate([kernel, jnp.zeros((2 * tile_size + 1 - taps,), kernel.dtype)])
    tiled = jnp.tile(padded, tile_size)[: 2 * tile_size * tile_size]
    return tiled.reshape(tile_size, 2 * tile_size).T


def phase_filter(projections, phase_kernel, tile_size):
    half_width = (phase_kernel.shape[0] - 1) // 2
    angles, slices, columns = projections.shape
    block_count = columns // tile_size
    rimmed = with_halo(projections, (("ray", 2),), half_width)
    padded = jnp.pad(rimmed, ((0, 0), (0, 0), (0, 2 * tile_size - 2 * half_width)))
    blocks = padded.reshape(angles, slices, block_count + 2, tile_size)
    windows = jnp.concatenate(
        [blocks[:, :, :block_count], blocks[:, :, 1 : block_count + 1]], axis=-1
    )
    filtered = jnp.einsum(
        "asbi,ij->asbj",
        windows,
        toeplitz(phase_kernel, tile_size),
        preferred_element_type=jnp.float32,
    )
    return filtered.reshape(angles, slices, columns).astype(jnp.bfloat16)


def stripe_profile(gathered):
    profile = jnp.median(gathered.astype(jnp.float32), axis=0)
    columns = profile.shape[1]
    rimmed = with_halo(profile, (("ray", 1),), SMOOTH)
    window_sum = jnp.zeros_like(profile)
    for offset in range(2 * SMOOTH + 1):
        window_sum = window_sum + rimmed[:, offset : offset + columns]
    position = lax.axis_index("ray") * columns + jnp.arange(columns)
    detector = lax.axis_size("ray") * columns
    in_range = (
        jnp.minimum(position + SMOOTH, detector - 1) - jnp.maximum(position - SMOOTH, 0) + 1
    ).astype(jnp.float32)
    return (profile - window_sum / in_range).astype(jnp.bfloat16)


def shards(
    projections,
    phase_kernel,
    image,
    tile_library,
    tile_entry,
    tile_image,
    tile_slot,
    tile_count,
    slot_block,
):
    tile_size = tile_library.shape[-1]
    angles, slices, columns = projections.shape
    phase = phase_filter(projections, phase_kernel, tile_size)
    gathered = lax.all_to_all(phase, DOM, split_axis=1, concat_axis=0, tiled=True)
    stripe = stripe_profile(gathered)
    stripe_all = whole_of(stripe, DOM, 0)
    corrected = (phase.astype(jnp.float32) - stripe_all.astype(jnp.float32)[None]).astype(
        jnp.bfloat16
    )
    owners = lax.axis_size(DOM)
    library = tile_library[0, 0]
    entries = tile_entry[0, 0]
    images = tile_image[0, 0]
    slots = tile_slot[0, 0]
    capacity = entries.shape[0]
    block_size = 64
    turn_count = capacity // block_size
    image_blocks = image.reshape(-1, tile_size, slices)
    block_total = image_blocks.shape[0]
    live_mask = jnp.arange(capacity) < tile_count[0, 0]
    slot_target = jnp.where(live_mask, slots, owners)
    image_target = jnp.where(live_mask, images, block_total)

    def forward_turn(turn_index, partial_value):
        first_tile = turn_index * block_size
        chosen = lax.dynamic_slice_in_dim(entries, first_tile, block_size)
        placed = lax.dynamic_slice_in_dim(images, first_tile, block_size)
        destined = lax.dynamic_slice_in_dim(slot_target, first_tile, block_size)
        product = jnp.einsum(
            "krp,kps->ksr",
            library[chosen],
            image_blocks[placed],
            preferred_element_type=jnp.float32,
        )
        return partial_value.at[destined].add(product, mode="drop")

    partial_value = lax.fori_loop(
        0, turn_count, forward_turn, jnp.zeros((owners, slices, tile_size), jnp.float32)
    )
    received = lax.all_to_all(
        partial_value.astype(jnp.bfloat16), DOM, split_axis=0, concat_axis=0, tiled=True
    )
    per_owner = columns // tile_size
    carried = slot_block[0, 0]
    block_ids = jnp.arange(angles * per_owner).reshape(angles, per_owner)
    selector = (block_ids[:, :, None] == carried[None, None, :]).astype(jnp.bfloat16)
    forward = jnp.einsum("abd,dst->asbt", selector, received, preferred_element_type=jnp.float32)
    residual = (corrected.astype(jnp.float32) - forward.reshape(angles, slices, columns)).astype(
        jnp.bfloat16
    )
    back = jnp.einsum(
        "abd,asbt->dst",
        selector,
        residual.reshape(angles, slices, per_owner, tile_size),
        preferred_element_type=jnp.float32,
    ).astype(jnp.bfloat16)
    returned = lax.all_to_all(back, DOM, split_axis=0, concat_axis=0, tiled=True)

    def adjoint_turn(turn_index, gradient):
        first_tile = turn_index * block_size
        chosen = lax.dynamic_slice_in_dim(entries, first_tile, block_size)
        sourced = lax.dynamic_slice_in_dim(slots, first_tile, block_size)
        destined = lax.dynamic_slice_in_dim(image_target, first_tile, block_size)
        product = jnp.einsum(
            "krp,ksr->kps", library[chosen], returned[sourced], preferred_element_type=jnp.float32
        )
        return gradient.at[destined].add(product, mode="drop")

    gradient = lax.fori_loop(
        0, turn_count, adjoint_turn, jnp.zeros((block_total, tile_size, slices), jnp.float32)
    )
    gradient = gradient.reshape(-1, slices)
    rows_own = gradient.shape[0] // lax.axis_size("ray")
    update = sent_and_summed(gradient, "ray", 0)
    own_image = lax.dynamic_slice_in_dim(image, lax.axis_index("ray") * rows_own, rows_own)
    image_next = own_image.astype(jnp.float32) + relax_factor * update
    return (residual, image_next)


def solution(mesh):
    finer = Mesh(
        mesh.devices.reshape(8, 4, 2, mesh.shape["ray"]), ("dom_0", "dom_1", "dom_2", "ray")
    )
    return jax.shard_map(
        shards,
        mesh=finer,
        in_specs=(
            P(DOM, None, "ray"),
            P(),
            P(DOM, None),
            P(DOM, "ray", None, None, None),
            P(DOM, "ray", None),
            P(DOM, "ray", None),
            P(DOM, "ray", None),
            P(DOM, "ray"),
            P(DOM, "ray", None),
        ),
        out_specs=(P(DOM, None, "ray"), P(DOM_RAY, None)),
        check_vma=False,
    )
```

profile of v0, /device:TPU:8, one launch (start us, length us, event | category | flops | bytes accessed | tf_op | source)
XLA Modules:
  0.0 279.8 jit_solution(15336875585059590275)
XLA Ops:
  1.4 3.4 %collective-permute-start = (bf16[1,64,64]{2,1,0:T(8,128)(2,1)S(1)}, bf16[1,64,64]{2,1,0:T(8,128)(2,1)S(1)}, u32[]{:S(2)}, u32[]{:S(2)}) collective-permute-start(bf16[1,64,64]{2,1,0:T(8,128)(2,1)S(1)} %get-tuple-element.326), channel_id=1, source_target_pairs={{0,1},{1,2},{2,3},{4,5},{5,6},{6,7},{8,9},{9,10},{10,11},{12,13},{... | collective-permute-start | bytes 24584 | tf_op jit(solution)/shard_map/ppermute | solution.py:23
  16.0 12.3 %all-to-all-start = ((bf16[64,2,1024]{2,1,0:T(2,128)(2,1)}), bf16[64,2,1024]{2,1,0:T(2,128)(2,1)}, u32[]{:S(2)}, u32[]{:S(2)}) async-start(bf16[64,2,1024]{2,1,0:T(2,128)(2,1)} %reshape.340), calls=%async_computation | async-start | bytes 524288 | tf_op jit(solution)/shard_map/all_to_all | solution.py:105
  29.9 70.2 %while.28 = (s32[]{:T(128)}, f32[64,64,128]{2,1,0:T(8,128)}, s32[256]{0:T(256)S(1)}, s32[256]{0:T(256)S(1)}, bf16[16,128,64]{2,1,0:T(8,128)(2,1)S(1)}, /*index=5...) while((s32[]{:T(128)}, f32[64,64,128]{2,1,0:T(8,128)}, ...), condition=%wide.region_4.5_spmd, body=%wide.region_2.4_spmd.sunk | while | flops 134744640 | bytes 17836972 | solution.py:138
  34.4 3.7 %fusion.69 = f32[64,64,128]{2,1,0:T(8,128)S(1)} fusion(bf16[64,128,64]{2,1,0:T(8,128)(2,1)} %gather_fusion, bf16[64,128,128]{2,1,0:T(8,128)(2,1)} %gather_fusion.1), kind=kOutput, calls=%fused_computation.101.clone.1 | convolution fusion | flops 134217728 | bytes 5242880 | tf_op jit(solution)/shard_map/while/body/eval_jaxpr/krp,kps->ksr/dot_general | solution.py:130
  38.1 9.0 %scatter_fusion = f32[64,64,128]{2,1,0:T(8,128)} fusion(f32[64,64,128]{2,1,0:T(8,128)} %get-tuple-element.435, s32[64]{0:T(128)S(1)} %compare_select_fusion.10, f32[64,64,128]{2,1,0:T(8,128)S(1)} %fusion.69), kind=kCustom, calls=%fused_computation.4.clone.1 | custom fusion | flops 524288 | bytes 6291712 | tf_op jit(solution)/shard_map/while/body/eval_jaxpr/scatter-add | solution.py:136
  51.6 3.7 %fusion.69 = f32[64,64,128]{2,1,0:T(8,128)S(1)} fusion(bf16[64,128,64]{2,1,0:T(8,128)(2,1)} %gather_fusion, bf16[64,128,128]{2,1,0:T(8,128)(2,1)} %gather_fusion.1), kind=kOutput, calls=%fused_computation.101.clone.1 | convolution fusion | flops 134217728 | bytes 5242880 | tf_op jit(solution)/shard_map/while/body/eval_jaxpr/krp,kps->ksr/dot_general | solution.py:130
  55.3 9.5 %scatter_fusion = f32[64,64,128]{2,1,0:T(8,128)} fusion(f32[64,64,128]{2,1,0:T(8,128)} %get-tuple-element.435, s32[64]{0:T(128)S(1)} %compare_select_fusion.10, f32[64,64,128]{2,1,0:T(8,128)S(1)} %fusion.69), kind=kCustom, calls=%fused_computation.4.clone.1 | custom fusion | flops 524288 | bytes 6291712 | tf_op jit(solution)/shard_map/while/body/eval_jaxpr/scatter-add | solution.py:136
  69.3 3.7 %fusion.69 = f32[64,64,128]{2,1,0:T(8,128)S(1)} fusion(bf16[64,128,64]{2,1,0:T(8,128)(2,1)} %gather_fusion, bf16[64,128,128]{2,1,0:T(8,128)(2,1)} %gather_fusion.1), kind=kOutput, calls=%fused_computation.101.clone.1 | convolution fusion | flops 134217728 | bytes 5242880 | tf_op jit(solution)/shard_map/while/body/eval_jaxpr/krp,kps->ksr/dot_general | solution.py:130
  73.0 9.4 %scatter_fusion = f32[64,64,128]{2,1,0:T(8,128)} fusion(f32[64,64,128]{2,1,0:T(8,128)} %get-tuple-element.435, s32[64]{0:T(128)S(1)} %compare_select_fusion.10, f32[64,64,128]{2,1,0:T(8,128)S(1)} %fusion.69), kind=kCustom, calls=%fused_computation.4.clone.1 | custom fusion | flops 524288 | bytes 6291712 | tf_op jit(solution)/shard_map/while/body/eval_jaxpr/scatter-add | solution.py:136
  86.9 3.7 %fusion.69 = f32[64,64,128]{2,1,0:T(8,128)S(1)} fusion(bf16[64,128,64]{2,1,0:T(8,128)(2,1)} %gather_fusion, bf16[64,128,128]{2,1,0:T(8,128)(2,1)} %gather_fusion.1), kind=kOutput, calls=%fused_computation.101.clone.1 | convolution fusion | flops 134217728 | bytes 5242880 | tf_op jit(solution)/shard_map/while/body/eval_jaxpr/krp,kps->ksr/dot_general | solution.py:130
  90.7 9.4 %scatter_fusion = f32[64,64,128]{2,1,0:T(8,128)} fusion(f32[64,64,128]{2,1,0:T(8,128)} %get-tuple-element.435, s32[64]{0:T(128)S(1)} %compare_select_fusion.10, f32[64,64,128]{2,1,0:T(8,128)S(1)} %fusion.69), kind=kCustom, calls=%fused_computation.4.clone.1 | custom fusion | flops 524288 | bytes 6291712 | tf_op jit(solution)/shard_map/while/body/eval_jaxpr/scatter-add | solution.py:136
  100.1 2.8 convert_element_type.99
  102.9 10.3 %all-to-all-start.1 = ((bf16[64,64,128]{2,1,0:T(8,128)(2,1)}), bf16[64,64,128]{2,1,0:T(8,128)(2,1)S(1)}, u32[]{:S(2)}, u32[]{:S(2)}) async-start(bf16[64,64,128]{2,1,0:T(8,128)(2,1)} %convert_element_type.99), calls=%async_computation.1 | async-start | bytes 2097152 | tf_op jit(solution)/shard_map/all_to_all | solution.py:141
  116.0 10.9 %sort.16 = (f32[64,1,2048]{2,0,1:T(8,128)}, s32[64,1,2048]{2,0,1:T(8,128)}) sort(f32[64,1,2048]{2,0,1:T(8,128)S(1)} %convert_select_fusion, s32[64,1,2048]{2,0,1:T(8,128)S(1)} %iota.18), dimensions={0}, to_apply=%region_1.2 | sort | flops 2228224 | bytes 2097152 | tf_op jit(solution)/shard_map/jit(median)/jit(quantile)/sort | solution.py:77
  129.1 4.5 %collective-permute-start.2 = (f32[1,8]{1,0:T(1,128)S(1)}, f32[1,8]{1,0:T(1,128)S(1)}, u32[]{:S(2)}, u32[]{:S(2)}) collective-permute-start(f32[1,8]{1,0:T(1,128)S(1)} %get-tuple-element.327), channel_id=1, source_target_pairs={{0,1},{1,2},{2,3},{4,5},{5,6},{6,7},{8,9},{9,10},{10,11},{12,13},{... | collective-permute-start | bytes 104 | tf_op jit(solution)/shard_map/ppermute | solution.py:23
  137.2 11.9 %all-gather.1 = bf16[4,2,2048]{2,1,0:T(2,128)(2,1)S(1)} all-gather(bf16[1,2,2048]{2,1,0:T(2,128)(2,1)S(1)} %bitcast.88), channel_id=1, replica_groups=mesh['dom_0'=8,'dom_1'=4,'dom_2'=2,'ray'=4] {'dom_1'}, dimensions={0}, use_global_device_ids=true | all-gather | bytes 40960 | tf_op jit(solution)/shard_map/all_gather | solution.py:34
  149.1 26.0 %all_gather.11 = bf16[64,2048]{1,0:T(8,128)(2,1)S(1)} all-gather(bf16[8,2048]{1,0:T(8,128)(2,1)S(1)} %reshape.334), channel_id=1, replica_groups=mesh['dom_0'=8,'dom_1'=4,'dom_2'=2,'ray'=4] {'dom_0'}, dimensions={0}, use_global_device_ids=true | all-gather | bytes 294912 | tf_op jit(solution)/shard_map/all_gather | solution.py:34
  178.8 9.1 %all-to-all-start.2 = ((bf16[64,64,128]{2,1,0:T(8,128)(2,1)}), bf16[64,64,128]{2,1,0:T(8,128)(2,1)}, u32[]{:S(2)}, u32[]{:S(2)}) async-start(bf16[64,64,128]{2,1,0:T(8,128)(2,1)} %copy.33), calls=%async_computation.2 | async-start | bytes 2097152 | tf_op jit(solution)/shard_map/all_to_all | solution.py:158
  188.0 28.7 %all-to-all-done.2 = bf16[64,64,128]{2,1,0:T(8,128)(2,1)} async-done(((bf16[64,64,128]{2,1,0:T(8,128)(2,1)}), bf16[64,64,128]{2,1,0:T(8,128)(2,1)}, u32[]{:S(2)}, u32[]{:S(2)}) %all-to-all-start.2) | async-done | bytes 1048608 | tf_op jit(solution)/shard_map/all_to_all | solution.py:158
  216.7 46.4 %while.29 = (s32[]{:T(128)}, f32[16,128,64]{1,2,0:T(8,128)S(1)}, s32[256]{0:T(256)S(1)}, s32[256]{0:T(256)S(1)}, bf16[16,128,128]{2,1,0:T(8,128)(2,1)S(1)}, /*in...) while((s32[]{:T(128)}, f32[16,128,64]{1,2,0:T(8,128)S(1)}, ...), condition=%wide.region_7.8_spmd, body=%wide.region_5.7_spmd.sunk | while | flops 134744640 | bytes 17836972 | solution.py:170
  216.9 2.9 %gather_fusion.2 = bf16[64,64,128]{2,1,0:T(8,128)(2,1)} fusion(bf16[64,64,128]{2,1,0:T(8,128)(2,1)} %get-tuple-element.484, s32[1024]{0:T(1024)S(1)} %pad_clamp_fusion.10), kind=kCustom, calls=%fused_computation.3.clone.1 | custom fusion | bytes 2097408 | tf_op jit(solution)/shard_map/while/body/eval_jaxpr/gather | solution.py:166
  221.9 2.6 fusion.72
  224.5 3.7 %scatter_fusion.1 = f32[16,128,64]{1,2,0:T(8,128)S(1)} fusion(f32[16,128,64]{1,2,0:T(8,128)S(1)} %get-tuple-element.468, s32[64]{0:T(128)S(1)} %compare_select_fusion.12, f32[64,128,64]{1,2,0:T(8,128)S(1)} %fusion.72), kind=kCustom, calls=%fused_computation.5.clone.1 | custom fusion | flops 524288 | bytes 6291712 | tf_op jit(solution)/shard_map/while/body/eval_jaxpr/scatter-add | solution.py:168
  228.5 2.9 %gather_fusion.2 = bf16[64,64,128]{2,1,0:T(8,128)(2,1)} fusion(bf16[64,64,128]{2,1,0:T(8,128)(2,1)} %get-tuple-element.484, s32[1024]{0:T(1024)S(1)} %pad_clamp_fusion.10), kind=kCustom, calls=%fused_computation.3.clone.1 | custom fusion | bytes 2097408 | tf_op jit(solution)/shard_map/while/body/eval_jaxpr/gather | solution.py:166
  233.5 2.6 fusion.72
  236.1 3.7 %scatter_fusion.1 = f32[16,128,64]{1,2,0:T(8,128)S(1)} fusion(f32[16,128,64]{1,2,0:T(8,128)S(1)} %get-tuple-element.468, s32[64]{0:T(128)S(1)} %compare_select_fusion.12, f32[64,128,64]{1,2,0:T(8,128)S(1)} %fusion.72), kind=kCustom, calls=%fused_computation.5.clone.1 | custom fusion | flops 524288 | bytes 6291712 | tf_op jit(solution)/shard_map/while/body/eval_jaxpr/scatter-add | solution.py:168
  240.1 2.9 %gather_fusion.2 = bf16[64,64,128]{2,1,0:T(8,128)(2,1)} fusion(bf16[64,64,128]{2,1,0:T(8,128)(2,1)} %get-tuple-element.484, s32[1024]{0:T(1024)S(1)} %pad_clamp_fusion.10), kind=kCustom, calls=%fused_computation.3.clone.1 | custom fusion | bytes 2097408 | tf_op jit(solution)/shard_map/while/body/eval_jaxpr/gather | solution.py:166
  247.7 3.8 %scatter_fusion.1 = f32[16,128,64]{1,2,0:T(8,128)S(1)} fusion(f32[16,128,64]{1,2,0:T(8,128)S(1)} %get-tuple-element.468, s32[64]{0:T(128)S(1)} %compare_select_fusion.12, f32[64,128,64]{1,2,0:T(8,128)S(1)} %fusion.72), kind=kCustom, calls=%fused_computation.5.clone.1 | custom fusion | flops 524288 | bytes 6291712 | tf_op jit(solution)/shard_map/while/body/eval_jaxpr/scatter-add | solution.py:168
  251.7 2.9 %gather_fusion.2 = bf16[64,64,128]{2,1,0:T(8,128)(2,1)} fusion(bf16[64,64,128]{2,1,0:T(8,128)(2,1)} %get-tuple-element.484, s32[1024]{0:T(1024)S(1)} %pad_clamp_fusion.10), kind=kCustom, calls=%fused_computation.3.clone.1 | custom fusion | bytes 2097408 | tf_op jit(solution)/shard_map/while/body/eval_jaxpr/gather | solution.py:166
  259.3 3.8 %scatter_fusion.1 = f32[16,128,64]{1,2,0:T(8,128)S(1)} fusion(f32[16,128,64]{1,2,0:T(8,128)S(1)} %get-tuple-element.468, s32[64]{0:T(128)S(1)} %compare_select_fusion.12, f32[64,128,64]{1,2,0:T(8,128)S(1)} %fusion.72), kind=kCustom, calls=%fused_computation.5.clone.1 | custom fusion | flops 524288 | bytes 6291712 | tf_op jit(solution)/shard_map/while/body/eval_jaxpr/scatter-add | solution.py:168
  264.6 5.3 %all-to-all-start.3 = ((f32[4,512,64]{1,2,0:T(8,128)}), f32[4,512,64]{1,2,0:T(8,128)S(1)}, u32[]{:S(2)}, u32[]{:S(2)}) async-start(f32[4,512,64]{1,2,0:T(8,128)} %copy.35), calls=%async_computation.3 | async-start | bytes 1048576 | tf_op jit(solution)/shard_map/all_to_all | solution.py:46
  270.9 7.4 %all-to-all-done.3 = f32[4,512,64]{1,2,0:T(8,128)S(1)} async-done(((f32[4,512,64]{1,2,0:T(8,128)}), f32[4,512,64]{1,2,0:T(8,128)S(1)}, u32[]{:S(2)}, u32[]{:S(2)}) %all-to-all-start.3) | async-done | bytes 524320 | tf_op jit(solution)/shard_map/all_to_all | solution.py:46
  (114 shorter events, 61.3 us)
Async XLA Ops:
  1.4 8.3 %collective-permute-start = (bf16[1,64,64]{2,1,0:T(8,128)(2,1)S(1)}, bf16[1,64,64]{2,1,0:T(8,128)(2,1)S(1)}, u32[]{:S(2)}, u32[]{:S(2)}) collective-permute-start(bf16[1,64,64]{2,1,0:T(8,128)(2,1)S(1)} %get-tuple-element.326), channel_id=1, source_target_pairs={{0,1},{1,2},{2,3},{4,5},{5,6},{6,7},{8,9},{9,10},{10,11},{12,13},{... | collective-permute-start | bytes 24584 | tf_op jit(solution)/shard_map/ppermute | solution.py:23
  4.8 5.6 %collective-permute-start.1 = (bf16[1,64,64]{2,1,0:T(8,128)(2,1)S(1)}, bf16[1,64,64]{2,1,0:T(8,128)(2,1)S(1)}, u32[]{:S(2)}, u32[]{:S(2)}) collective-permute-start(bf16[1,64,64]{2,1,0:T(8,128)(2,1)S(1)} %get-tuple-element.325), channel_id=1, source_target_pairs={{1,0},{2,1},{3,2},{5,4},{6,5},{7,6},{9,8},{10,9},{11,10},{13,12},{... | collective-permute-start | bytes 24584 | tf_op jit(solution)/shard_map/ppermute | solution.py:25
  12.4 17.5 %copy-start = (bf16[1,1,16,128,128]{4,3,2,1,0:T(8,128)(2,1)S(1)}, bf16[1,1,16,128,128]{4,3,2,1,0:T(8,128)(2,1)}, u32[]{:S(2)}) copy-start(bf16[1,1,16,128,128]{4,3,2,1,0:T(8,128)(2,1)} %param.16) | copy-start | bytes 1572868
  12.5 17.5 %copy-start.5 = (s32[1,1,256]{2,1,0:T(1,128)S(1)}, s32[1,1,256]{2,1,0:T(1,128)}, u32[]{:S(2)}) copy-start(s32[1,1,256]{2,1,0:T(1,128)} %param.17) | copy-start | bytes 3076
  12.5 17.5 %copy-start.6 = (s32[1,1,256]{2,1,0:T(1,128)S(1)}, s32[1,1,256]{2,1,0:T(1,128)}, u32[]{:S(2)}) copy-start(s32[1,1,256]{2,1,0:T(1,128)} %param.18) | copy-start | bytes 3076
  16.0 86.9 %all-to-all-start = ((bf16[64,2,1024]{2,1,0:T(2,128)(2,1)}), bf16[64,2,1024]{2,1,0:T(2,128)(2,1)}, u32[]{:S(2)}, u32[]{:S(2)}) async-start(bf16[64,2,1024]{2,1,0:T(2,128)(2,1)} %reshape.340), calls=%async_computation | async-start | bytes 524288 | tf_op jit(solution)/shard_map/all_to_all | solution.py:105
  102.9 72.2 %all-to-all-start.1 = ((bf16[64,64,128]{2,1,0:T(8,128)(2,1)}), bf16[64,64,128]{2,1,0:T(8,128)(2,1)S(1)}, u32[]{:S(2)}, u32[]{:S(2)}) async-start(bf16[64,64,128]{2,1,0:T(8,128)(2,1)} %convert_element_type.99), calls=%async_computation.1 | async-start | bytes 2097152 | tf_op jit(solution)/shard_map/all_to_all | solution.py:141
  113.2 62.5 %copy-start.1 = (f32[8,8,16,128]{3,2,1,0:T(8,128)}, f32[8,8,16,128]{3,2,1,0:T(8,128)S(1)}, u32[]{:S(2)}) copy-start(f32[8,8,16,128]{3,2,1,0:T(8,128)S(1)} %convert.11) | copy-start | bytes 1572868
  113.3 61.8 %copy-start.8 = (s32[1,1,64]{2,1,0:T(1,128)S(1)}, s32[1,1,64]{2,1,0:T(1,128)}, u32[]{:S(2)}) copy-start(s32[1,1,64]{2,1,0:T(1,128)} %param.21) | copy-start | bytes 772
  127.9 5.8 %collective-permute-start.3 = (f32[1,8]{1,0:T(1,128)S(1)}, f32[1,8]{1,0:T(1,128)S(1)}, u32[]{:S(2)}, u32[]{:S(2)}) collective-permute-start(f32[1,8]{1,0:T(1,128)S(1)} %get-tuple-element.328), channel_id=1, source_target_pairs={{1,0},{2,1},{3,2},{5,4},{6,5},{7,6},{9,8},{10,9},{11,10},{13,12},{... | collective-permute-start | bytes 104 | tf_op jit(solution)/shard_map/ppermute | solution.py:25
  129.1 5.8 %collective-permute-start.2 = (f32[1,8]{1,0:T(1,128)S(1)}, f32[1,8]{1,0:T(1,128)S(1)}, u32[]{:S(2)}, u32[]{:S(2)}) collective-permute-start(f32[1,8]{1,0:T(1,128)S(1)} %get-tuple-element.327), channel_id=1, source_target_pairs={{0,1},{1,2},{2,3},{4,5},{5,6},{6,7},{8,9},{9,10},{10,11},{12,13},{... | collective-permute-start | bytes 104 | tf_op jit(solution)/shard_map/ppermute | solution.py:23
  175.8 0.8 copy-start.3
  177.1 39.6 %copy-start.7 = (s32[1,1,256]{2,1,0:T(1,128)S(1)}, s32[1,1,256]{2,1,0:T(1,128)}, u32[]{:S(2)}) copy-start(s32[1,1,256]{2,1,0:T(1,128)} %param.19) | copy-start | bytes 3076
  178.8 37.8 %all-to-all-start.2 = ((bf16[64,64,128]{2,1,0:T(8,128)(2,1)}), bf16[64,64,128]{2,1,0:T(8,128)(2,1)}, u32[]{:S(2)}, u32[]{:S(2)}) async-start(bf16[64,64,128]{2,1,0:T(8,128)(2,1)} %copy.33), calls=%async_computation.2 | async-start | bytes 2097152 | tf_op jit(solution)/shard_map/all_to_all | solution.py:158
  263.1 6.8 %copy-start.2 = (f32[8,8,16,128]{3,2,1,0:T(8,128)S(1)}, f32[8,8,16,128]{3,2,1,0:T(8,128)}, u32[]{:S(2)}) copy-start(f32[8,8,16,128]{3,2,1,0:T(8,128)} %copy-done.1) | copy-start | bytes 1572868
  263.1 6.8 %copy-start.4 = (f32[64,128,16]{1,2,0:T(8,128)S(1)}, f32[64,128,16]{1,2,0:T(8,128)}, u32[]{:S(2)}) copy-start(f32[64,128,16]{1,2,0:T(8,128)} %copy-done.3) | copy-start | bytes 1572868
  264.6 13.7 %all-to-all-start.3 = ((f32[4,512,64]{1,2,0:T(8,128)}), f32[4,512,64]{1,2,0:T(8,128)S(1)}, u32[]{:S(2)}, u32[]{:S(2)}) async-start(f32[4,512,64]{1,2,0:T(8,128)} %copy.35), calls=%async_computation.3 | async-start | bytes 1048576 | tf_op jit(solution)/shard_map/all_to_all | solution.py:46
where the time goes:
time: 283 us; the launch traced here: 280 us
  other arithmetic  74.8 us (26%)
  local copies, waits for them, and re-layouts  51.1 us (18%)
  starting transfers between devices  47.5 us (17%)
  blocking collectives  39.7 us (14%)
  waiting for transfers between devices  38.1 us (13%)
  matrix products  26.8 us (9%)
    all_gather x3, blocking collectives, whole_of(): array = lax.all_gather(array, axis, axis=dim, tiled=True)  39.7 us
    scatter-add x4, other arithmetic, forward_turn(): return partial_value.at[destined].add(product, mode='drop')  37.4 us
    all_to_all x1, waiting for transfers between devices, shards(): lax.all_to_all(back, DOM, split_axis=0, concat_axis=0, tiled=True)  28.7 us
    scatter-add x4, other arithmetic, adjoint_turn(): return gradient.at[destined].add(product, mode='drop')  15 us
    dot_general x4, matrix products, forward_turn(): jnp.einsum('krp,kps->ksr', library[chosen], image_blocks[placed], preferr...  15 us
    all_to_all x1, starting transfers between devices, shards(): lax.all_to_all(phase, DOM, split_axis=1, concat_axis=0, tiled=True)  12.3 us
    gather x4, local copies, waits for them, and re-layouts, adjoint_turn(): returned[sourced]  11.5 us
    sort x1, other arithmetic, stripe_profile(): profile = jnp.median(gathered.astype(jnp.float32), axis=0)  10.9 us
  transfers between devices with their start and end apart: 8, of which 4 were waited for; matrix products, arithmetic and copies ran while one was open for 33% of the time, Pallas kernels for 0%

commit v1 on v0

v1 whole, which is shorter than its diff:
```python
import jax
import jax.numpy as jnp
from jax import lax
from jax.experimental import pallas as pl
from jax.experimental.pallas import tpu as pltpu
from jax.sharding import PartitionSpec as P

T = 128
SMOOTH = 8
RELAX = 0.25
CHUNKS = 1
SECTION = 32
LIMIT = 48 * 2**20
F32, BF16 = jnp.float32, jnp.bfloat16
NT = (((1,), (1,)), ((), ()))
VMEM = pl.BlockSpec(memory_space=pltpu.VMEM)
SMEM = pl.BlockSpec(memory_space=pltpu.SMEM)
ANY = pl.BlockSpec(memory_space=pl.ANY)


def params(**more):
    return pltpu.CompilerParams(vmem_limit_bytes=LIMIT, **more)


def middle_network(n):
    pairs = []
    p = 1
    while p < n:
        k = p
        while k >= 1:
            for j in range(k % p, n - k, 2 * k):
                for i in range(min(k, n - j - k)):
                    if (i + j) // (2 * p) == (i + j + k) // (2 * p):
                        pairs.append((i + j, i + j + k))
            k //= 2
        p *= 2
    needed = {n // 2 - 1, n // 2}
    kept = []
    for a, b in reversed(pairs):
        if a in needed or b in needed:
            kept.append((a, b, a in needed, b in needed))
            needed |= {a, b}
    return kept[::-1]


def band(kernel):
    taps = kernel.shape[0]
    padded = jnp.concatenate([kernel, jnp.zeros((2 * T + 1 - taps,), kernel.dtype)])
    tiled = jnp.tile(padded, T)[: 2 * T * T].reshape(T, 2 * T)
    return jnp.pad(tiled, ((0, 0), (T // 2, T // 2)))


def lanes(block):
    return pl.ds(pl.multiple_of(block * T, T), T)


def forward_call(lists, image, library, first, size, rows, blocks, owners):
    entries = library.shape[0]
    capacity = lists.shape[1]

    def kernel(lists_ref, image_ref, library_ref, send_ref, turned, product, total, packed, sem):
        for i in range(blocks):
            block = image_ref[i * T : (i + 1) * T, :].astype(F32)
            turned[i * size : (i + 1) * size, :] = block.T[first : first + size, :].astype(BF16)
        for e in range(entries):
            product[:, e * T : (e + 1) * T] = lax.dot_general(
                turned[...], library_ref[e], NT, preferred_element_type=F32
            )
        total[...] = jnp.zeros_like(total)

        def add(k):
            e, i, s = lists_ref[0, k], lists_ref[1, k], lists_ref[2, k]
            total[s] += product[pl.ds(pl.multiple_of(i * size, size), size), lanes(e)]

        def group(g, carry):
            for u in range(8):
                add(g * 8 + u)
            return carry

        lax.fori_loop(0, lists_ref[3, 0], group, 0)
        packed[...] = total[:owners].astype(BF16)
        copy = pltpu.make_async_copy(packed, send_ref.at[:, pl.ds(0, size), :], sem)
        copy.start()
        copy.wait()

    return pl.pallas_call(
        kernel,
        out_shape=jax.ShapeDtypeStruct((owners, rows, T), BF16),
        in_specs=[SMEM, VMEM, VMEM],
        out_specs=ANY,
        scratch_shapes=[
            pltpu.VMEM((blocks * size, T), BF16),
            pltpu.VMEM((blocks * size, entries * T), F32),
            pltpu.VMEM((owners + 1, size, T), F32),
            pltpu.VMEM((owners, size, T), BF16),
            pltpu.SemaphoreType.DMA,
        ],
        compiler_params=params(),
        cost_estimate=pl.CostEstimate(
            flops=2 * capacity * size * T * T, bytes_accessed=8 * 2**20, transcendentals=0
        ),
        name="forward_tiles",
    )(lists, image, library)


def phase_call(projections, left, right, taps, numbers, send, offset):
    slices, columns = projections.shape
    per = columns // T

    def kernel(x_ref, l_ref, r_ref, taps_ref, n_ref, _, phase_ref, send_ref, wide, spread, packed, sem):
        wide[:, :T] = l_ref[...]
        wide[:, T : T + columns] = x_ref[...]
        wide[:, T + columns :] = r_ref[...]
        spread[...] = jnp.zeros_like(spread)

        def put(row, value):
            spread[pl.ds(row, slices, stride=SECTION), :] = value

        def product(start, stop, low):
            return lax.dot_general(
                wide[:, start * T : stop * T],
                taps_ref[:, low * T : (low + stop - start) * T],
                NT,
                preferred_element_type=F32,
            ).astype(BF16)

        for b in range(per):
            value = product(b, b + 3, 0)
            phase_ref[:, b * T : (b + 1) * T] = value
            put(b, value.astype(F32))
        put(per, product(0, 2, 1).astype(F32))
        put(per + 1, product(per, per + 2, 0).astype(F32))
        put(per + 2, n_ref[...])
        packed[...] = spread[...].astype(BF16).reshape(slices, SECTION, T)
        copy = pltpu.make_async_copy(packed, send_ref.at[:, pl.ds(offset, SECTION), :], sem)
        copy.start()
        copy.wait()

    return pl.pallas_call(
        kernel,
        out_shape=[
            jax.ShapeDtypeStruct((slices, columns), BF16),
            jax.ShapeDtypeStruct(send.shape, BF16),
        ],
        in_specs=[VMEM, VMEM, VMEM, VMEM, VMEM, ANY],
        out_specs=[VMEM, ANY],
        scratch_shapes=[
            pltpu.VMEM((slices, columns + 2 * T), BF16),
            pltpu.VMEM((slices * SECTION, T), F32),
            pltpu.VMEM((slices, SECTION, T), BF16),
            pltpu.SemaphoreType.DMA,
        ],
        input_output_aliases={5: 1},
        compiler_params=params(),
        cost_estimate=pl.CostEstimate(flops=2**26, bytes_accessed=2**20, transcendentals=0),
        name="phase_filter",
    )(projections, left, right, taps, numbers, send)


def stripe_of(quarter, quarters, arrived_ref, offset, values, rimmed):
    angles = arrived_ref.shape[0]
    for a in range(angles):
        values[a] = arrived_ref[a, offset : offset + SECTION, :].astype(F32)[:24]
    network = middle_network(angles)

    def middle(g, carry):
        rows = pl.ds(pl.multiple_of(g * 8, 8), 8)
        v = [values[a, rows, :] for a in range(angles)]
        for a, b, low, high in network:
            x, y = v[a], v[b]
            if low:
                v[a] = jnp.minimum(x, y)
            if high:
                v[b] = jnp.maximum(x, y)
        rimmed[pl.ds(g * 8 + 1, 8), :] = (v[angles // 2 - 1] + v[angles // 2]) * 0.5
        return carry

    lax.fori_loop(0, 3, middle, 0)
    before, after = rimmed[17:18, :], rimmed[18:19, :]
    rimmed[0:1, :] = jnp.where(quarter == 0, jnp.zeros_like(before), before)
    rimmed[17:18, :] = jnp.where(quarter == quarters - 1, jnp.zeros_like(after), after)
    prev, cur, nxt = rimmed[0:16, :], rimmed[1:17, :], rimmed[2:18, :]
    lane = lax.broadcasted_iota(jnp.int32, (16, T), 1)
    total = cur
    for o in range(1, SMOOTH + 1):
        total += pltpu.roll(jnp.where(lane < o, nxt, cur), T - o, 1)
        total += pltpu.roll(jnp.where(lane >= T - o, prev, cur), o, 1)
    place = quarter * (16 * T) + lax.broadcasted_iota(jnp.int32, (16, T), 0) * T + lane
    last = quarters * 16 * T - 1
    count = jnp.minimum(place + SMOOTH, last) - jnp.maximum(place - SMOOTH, 0) + 1
    return cur - total / count.astype(F32)


def residual_call(carried, quarter, arrived, phase, first, size, rows, section, quarters):
    owners = arrived.shape[0]
    columns = phase.shape[1]

    def kernel(c_ref, q_ref, arrived_ref, phase_ref, forward_ref, back_ref, values, rimmed, less):
        forward_ref[...] = jnp.zeros_like(forward_ref)
        for d in range(owners):
            forward_ref[:, lanes(c_ref[0, d])] += arrived_ref[d, :size, :].astype(F32)
        less[...] = (phase_ref[first : first + size, :].astype(F32) - forward_ref[...]).astype(BF16)
        for d in range(owners):
            back_ref[d, :size, :] = less[:, lanes(c_ref[0, d])]
        if section:
            stripe = stripe_of(q_ref[0], quarters, arrived_ref, size, values, rimmed).astype(BF16)
            for d in range(owners):
                back_ref[d, size:, :] = stripe

    return pl.pallas_call(
        kernel,
        out_shape=[
            jax.ShapeDtypeStruct((size, columns), F32),
            jax.ShapeDtypeStruct((owners, rows, T), BF16),
        ],
        in_specs=[SMEM, SMEM, VMEM, VMEM],
        out_specs=[VMEM, VMEM],
        scratch_shapes=[
            pltpu.VMEM((owners, 24, T), F32),
            pltpu.VMEM((32, T), F32),
            pltpu.VMEM((size, columns), BF16),
        ],
        compiler_params=params(),
        cost_estimate=pl.CostEstimate(flops=2**24, bytes_accessed=8 * 2**20, transcendentals=0),
        name="slot_residual",
    )(carried, quarter, arrived, phase)


def adjoint_call(lists, carried, returned, striped, offset, library, first, size, blocks, own):
    entries = library.shape[0]
    owners = returned.shape[0]
    per = 16
    same = striped is returned

    def kernel(*refs):
        refs = list(refs)
        lists_ref, c_ref, returned_ref = refs[:3]
        refs = refs[3:]
        striped_ref = returned_ref if same else refs.pop(0)
        library_ref = refs.pop(0)
        if own:
            phase_ref = refs.pop(0)
            forward_refs = [refs.pop(0) for _ in own[1]]
        update_ref = refs.pop(0)
        if own:
            residual_ref = refs.pop(0)
        stripes, terms, bins = refs
        stripes[...] = striped_ref[:, offset : offset + per, :].astype(F32).reshape(owners * per, T)
        for e in range(owners):
            stripe = stripes[pl.ds(first * per + c_ref[e], size, stride=per), :]
            terms[e] = returned_ref[e, :size, :].astype(F32) - stripe
        bins[...] = jnp.zeros_like(bins)

        def add(k):
            e, i, s = lists_ref[0, k], lists_ref[1, k], lists_ref[2, k]
            bins[pl.ds(pl.multiple_of(i * size, size), size), lanes(e)] += terms[s]

        def group(g, carry):
            for u in range(8):
                add(g * 8 + u)
            return carry

        terms[owners] = jnp.zeros((size, T), F32)
        lax.fori_loop(0, lists_ref[3, 0], group, 0)
        update_ref[...] = (
            jnp.dot(
                bins[...].astype(BF16),
                library_ref[...].reshape(entries * T, T),
                preferred_element_type=F32,
            )
            .astype(BF16)
            .reshape(blocks, size, T)
        )
        if own:
            for n, forward_ref in enumerate(forward_refs):
                depth = forward_ref.shape[0]
                for b in range(per):
                    where = slice(b * T, (b + 1) * T)
                    stripe = stripes[pl.ds(n * depth * per + b, depth, stride=per), :]
                    value = phase_ref[n * depth : (n + 1) * depth, where].astype(F32) - stripe
                    value = value.astype(BF16).astype(F32) - forward_ref[:, where]
                    residual_ref[n * depth : (n + 1) * depth, where] = value.astype(BF16)

    args = [lists, carried, returned] + ([] if same else [striped]) + [library]
    out_shape = [jax.ShapeDtypeStruct((blocks, size, T), BF16)]
    if own:
        args += [own[0], *own[1]]
        out_shape.append(jax.ShapeDtypeStruct(own[0].shape, BF16))
    return pl.pallas_call(
        kernel,
        out_shape=out_shape,
        in_specs=[SMEM, SMEM] + [VMEM] * (len(args) - 2),
        out_specs=[VMEM] * len(out_shape),
        scratch_shapes=[
            pltpu.VMEM((owners * per, T), F32),
            pltpu.VMEM((owners + 1, size, T), F32),
            pltpu.VMEM((blocks * size, entries * T), F32),
        ],
        compiler_params=params(),
        cost_estimate=pl.CostEstimate(
            flops=2 * 256 * size * T * T, bytes_accessed=8 * 2**20, transcendentals=0
        ),
        name="adjoint_tiles",
    )(*args)


def image_call(quarter, image, parts, quarters):
    pixels, slices = image.shape
    held = pixels // quarters
    mine = held // T

    def kernel(q_ref, image_ref, *refs):
        parts_refs, out_ref = refs[:-1], refs[-1]
        start = q_ref[0] * held
        for i in range(mine):
            pieces = []
            for ref in parts_refs:
                total = ref[i].astype(F32)
                for q in range(1, quarters):
                    total += ref[q * mine + i].astype(F32)
                pieces.append(total)
            update = jnp.concatenate(pieces, axis=0) if len(pieces) > 1 else pieces[0]
            rows = pl.ds(pl.multiple_of(start + i * T, T), T)
            out_ref[i * T : (i + 1) * T, :] = image_ref[rows, :].astype(F32) + RELAX * update.T

    return pl.pallas_call(
        kernel,
        out_shape=jax.ShapeDtypeStruct((held, slices), F32),
        in_specs=[SMEM, VMEM] + [VMEM] * len(parts),
        out_specs=VMEM,
        compiler_params=params(),
        cost_estimate=pl.CostEstimate(flops=2**18, bytes_accessed=2**20, transcendentals=0),
        name="image_step",
    )(quarter, image, *parts)


def exchanged(array, axis):
    return lax.all_to_all(array, axis, split_axis=0, concat_axis=0, tiled=True)


def shards(projections, phase_kernel, image, tile_library, tile_entry, tile_image, tile_slot, tile_count, slot_block):
    projections = projections[0]
    library = tile_library[0, 0]
    slices = projections.shape[0]
    owners, quarters = lax.axis_size("dom"), lax.axis_size("ray")
    blocks = image.shape[0] // T
    quarter = lax.axis_index("ray").astype(jnp.int32).reshape(1)
    capacity = tile_entry.shape[-1]
    count = tile_count[0, 0]
    live = jnp.arange(capacity) < count
    lists = jnp.stack(
        [
            jnp.where(live, tile_entry[0, 0], 0),
            jnp.where(live, tile_image[0, 0], 0),
            jnp.where(live, tile_slot[0, 0], owners),
            jnp.full((capacity,), (count + 7) // 8, jnp.int32),
        ]
    )
    carried = slot_block[0]
    size = slices // CHUNKS

    left = lax.ppermute(projections[:, -T:], "ray", [(i, i + 1) for i in range(quarters - 1)])
    right = lax.ppermute(projections[:, :T], "ray", [(i + 1, i) for i in range(quarters - 1)])
    taps = band(phase_kernel)
    numbers = jnp.broadcast_to(carried[0].astype(F32)[:, None], (owners, T))

    arrived, forwards, returned, updates = [], [], [], []
    for n in range(CHUNKS):
        rows = size + (SECTION if n == 0 else 0)
        send = forward_call(lists, image, library, n * size, size, rows, blocks, owners)
        if n == 0:
            phase, send = phase_call(projections, left, right, taps, numbers, send, size)
        arrived.append(exchanged(send, "dom"))
    theirs = arrived[0][:, size + 18, 0].astype(jnp.int32)
    for n in range(CHUNKS):
        rows = size + (16 if n == 0 else 0)
        forward, back = residual_call(
            carried, quarter, arrived[n], phase, n * size, size, rows, n == 0, quarters
        )
        forwards.append(forward)
        returned.append(exchanged(back, "dom"))
    for n in range(CHUNKS):
        own = (phase, forwards) if n == 0 else None
        made = adjoint_call(
            lists, theirs, returned[n], returned[0], size, library, n * size, size, blocks, own
        )
        if own:
            residual = made[1]
        updates.append(exchanged(made[0], "ray"))
    image_next = image_call(quarter, image, updates, quarters)
    return residual[None], image_next


def solution(mesh):
    return jax.shard_map(
        shards,
        mesh=mesh,
        in_specs=(
            P("dom", None, "ray"),
            P(),
            P("dom", None),
            P("dom", "ray", None, None, None),
            P("dom", "ray", None),
            P("dom", "ray", None),
            P("dom", "ray", None),
            P("dom", "ray"),
            P("dom", "ray", None),
        ),
        out_specs=(P("dom", None, "ray"), P(("dom", "ray"), None)),
        check_vma=False,
    )
```

time: 283 us -> 137 us (0.48)
  other arithmetic: 74.8 us -> 3.35 us
  local copies, waits for them, and re-layouts: 51.1 us -> 9.36 us
  waiting for transfers between devices: 38.1 us -> 73.2 us
  blocking collectives: 39.7 us -> 11.3 us
  matrix products: 26.8 us -> 0 us
  starting transfers between devices: 47.5 us -> 24.6 us
  Pallas kernels: 0 us -> 13.1 us
    scatter-add x8 -> x0, other arithmetic: 52.4 us -> none  [the longest x4 37.4 us: forward_turn(): return partial_value.at[destined].add(product, mode='drop')]
    all_gather x3 -> x0, blocking collectives: 39.7 us -> none  [whole_of(): array = lax.all_gather(array, axis, axis=dim, tiled=True)]
    gather x16 -> x0, local copies, waits for them, and re-layouts: 37.3 us -> none  [the longest x4 11.5 us: adjoint_turn(): returned[sourced]]
    all_to_all x4 -> x2, waiting for transfers between devices: 36.1 us -> 73.2 us  [exchanged(): return lax.all_to_all(array, axis, split_axis=0, concat_axis=0, tiled=True)]
    dot_general x11 -> x0, matrix products: 26.8 us -> none  [the longest x4 15 us: forward_turn(): jnp.einsum('krp,kps->ksr', library[chosen], image_blocks[placed], preferr...]
    all_to_all x4 -> x2, starting transfers between devices: 37 us -> 18.7 us  [exchanged(): return lax.all_to_all(array, axis, split_axis=0, concat_axis=0, tiled=True)]
    pallas_call x0 -> x5, Pallas kernels: none -> 13.1 us  [the longest x1 5.15 us: adjoint_call(): pl.pallas_call(kernel, out_shape=out_shape, in_specs=[SMEM, SMEM] + [VMEM...]
    all_to_all x0 -> x1, blocking collectives: none -> 11.3 us  [exchanged(): return lax.all_to_all(array, axis, split_axis=0, concat_axis=0, tiled=True)]
  transfers between devices with their start and end apart: 8 -> 4, of which waited for: 4 -> 2; matrix products, arithmetic and copies ran while one was open for 33% -> 4% of each run, Pallas kernels for 0% -> 3%
where the time goes in v1:
time: 137 us; the launch traced here: 136 us
  waiting for transfers between devices  73.2 us (53%)
  starting transfers between devices  24.6 us (18%)
  Pallas kernels  13.1 us (10%)
  blocking collectives  11.3 us (8%)
  local copies, waits for them, and re-layouts  9.36 us (7%)
  other arithmetic  3.35 us (2%)
  between operations  1.47 us (1%)
    all_to_all x2, waiting for transfers between devices, exchanged(): return lax.all_to_all(array, axis, split_axis=0, concat_axis=0, tiled=True)  73.2 us
    all_to_all x2, starting transfers between devices, exchanged(): return lax.all_to_all(array, axis, split_axis=0, concat_axis=0, tiled=True)  18.7 us
    all_to_all x1, blocking collectives, exchanged(): return lax.all_to_all(array, axis, split_axis=0, concat_axis=0, tiled=True)  11.3 us
    unnamed x22, local copies, waits for them, and re-layouts  7.98 us
    pallas_call x1, Pallas kernels, adjoint_call(): pl.pallas_call(kernel, out_shape=out_shape, in_specs=[SMEM, SMEM] + [VMEM...  5.15 us
    ppermute x1, starting transfers between devices, shards(): lax.ppermute(projections[:, -T:], 'ray', [(i, i + 1) for i in range(quart...  4.55 us
    pallas_call x1, Pallas kernels, forward_call(): pl.pallas_call(kernel, out_shape=jax.ShapeDtypeStruct((owners, rows, T),...  3.8 us
  transfers between devices with their start and end apart: 4, of which 2 were waited for; matrix products, arithmetic and copies ran while one was open for 4% of the time, Pallas kernels for 3%

profile of v1, /device:TPU:8, one launch (start us, length us, event | category | flops | bytes accessed | tf_op | source)
XLA Modules:
  0.0 136.3 jit_solution(12142325470830608615)
XLA Ops:
  0.6 0.7 fusion.1
  1.4 1.3 collective-permute-start.1
  2.7 4.5 %collective-permute-start = (bf16[64,128]{1,0:T(8,128)(2,1)S(1)}, bf16[64,128]{1,0:T(8,128)(2,1)S(1)}, u32[]{:S(2)}, u32[]{:S(2)}) collective-permute-start(bf16[64,128]{1,0:T(8,128)(2,1)S(1)} %get-tuple-element.19), channel_id=1, source_target_pairs={{0,1},{1,2},{2,3},{4,5},{5,6},{6,7},{8,9},{9,10},{10,11},{12,13},{... | collective-permute-start | bytes 49160 | tf_op jit(solution)/shard_map/ppermute | solution.py:362
  7.9 0.1 pad.9.clone
  8.0 0.7 convert_bitcast_fusion
  8.6 1.2 copy.15.image_ref
  9.9 0.7 bitcast_select_fusion.2
  10.6 0.7 bitcast_select_fusion
  11.3 0.1 add_add_fusion.lists_ref.refs_0_
  11.3 1.0 copy-done
  12.4 3.8 %forward_tiles.1._ = bf16[64,96,128]{2,1,0:T(8,128)(2,1)} custom-call(s32[4,256]{1,0:T(4,128)S(1)} %add_add_fusion.lists_ref.refs_0_, bf16[2048,64]{1,0:T(8,128)(2,1)S(1)} %copy.15.image_ref, bf16[16,128,128]{2,1,0:T(8,128)(2,1)S(1)} %bitcast.18), custom_call_target="tpu_custom_call" | custom-call | flops 536870912 | bytes 8388608 | tf_op jit(solution)/shard_map/forward_tiles/pallas_call | solution.py:86
  16.2 0.3 tile.10
  16.6 0.1 pad.5.taps_ref
  16.7 0.1 broadcast_in_dim.20.n_ref
  16.8 2.0 %phase_filter.1 = (bf16[64,2048]{1,0:T(8,128)(2,1)S(1)}, bf16[64,96,128]{2,1,0:T(8,128)(2,1)}) custom-call(bf16[64,2048]{1,0:T(8,128)(2,1)S(1)} %bitcast.21, bf16[64,128]{1,0:T(8,128)(2,1)S(1)} %collective-permute-done.l_ref, bf16[64,128]{1,0:T(8,128)(2,1)S(1)} %collective-permute-done.1.r_ref, ...), custom_call_target="tpu_custom_call", output_to_operand_aliasing={{1}: (5, {})} | custom-call | flops 67108864 | bytes 1048576 | tf_op jit(solution)/shard_map/phase_filter/pallas_call | solution.py:139
  18.8 0.0 copy-start.3
  18.8 0.0 copy-start.8
  18.8 13.3 %all-to-all-start = ((bf16[64,96,128]{2,1,0:T(8,128)(2,1)}), bf16[64,96,128]{2,1,0:T(8,128)(2,1)S(1)}, u32[]{:S(2)}, u32[]{:S(2)}) async-start(bf16[64,96,128]{2,1,0:T(8,128)(2,1)} %get-tuple-element.8), calls=%async_computation | async-start | bytes 3145728 | tf_op jit(solution)/shard_map/all_to_all | solution.py:338
  32.2 40.0 %all-to-all-done.arrived_ref = bf16[64,96,128]{2,1,0:T(8,128)(2,1)S(1)} async-done(((bf16[64,96,128]{2,1,0:T(8,128)(2,1)}), bf16[64,96,128]{2,1,0:T(8,128)(2,1)S(1)}, u32[]{:S(2)}, u32[]{:S(2)}) %all-to-all-start) | async-done | bytes 1572896 | tf_op jit(solution)/shard_map/all_to_all | solution.py:338
  72.2 2.0 %slot_residual.1 = (f32[64,2048]{1,0:T(8,128)S(1)}, bf16[64,80,128]{2,1,0:T(8,128)(2,1)S(1)}) custom-call(s32[1,64]{1,0:T(1,128)S(1)} %bitcast.22, s32[1]{0:T(128)} %bitcast.8.q_ref, bf16[64,96,128]{2,1,0:T(8,128)(2,1)S(1)} %all-to-all-done.arrived_ref, bf16[64,2048]{1,0:T(8,128)(2,1)S(1)} %get-tuple-element.9.phase_ref.refs_4_), custom_call_target="tpu_custom_call" | custom-call | flops 16777216 | bytes 8388608 | tf_op jit(solution)/shard_map/slot_residual/pallas_call | solution.py:210
  74.2 1.1 copy-done.2
  75.3 0.8 copy-done.5
  76.1 5.4 %all-to-all-start.1 = ((bf16[64,80,128]{2,1,0:T(8,128)(2,1)}), bf16[64,80,128]{2,1,0:T(8,128)(2,1)S(1)}, u32[]{:S(2)}, u32[]{:S(2)}) async-start(bf16[64,80,128]{2,1,0:T(8,128)(2,1)} %copy-done.2), calls=%async_computation.1 | async-start | bytes 2621440 | tf_op jit(solution)/shard_map/all_to_all | solution.py:338
  81.5 1.2 fusion.refs_1_
  82.7 33.2 %all-to-all-done.1.refs_2_ = bf16[64,80,128]{2,1,0:T(8,128)(2,1)S(1)} async-done(((bf16[64,80,128]{2,1,0:T(8,128)(2,1)}), bf16[64,80,128]{2,1,0:T(8,128)(2,1)S(1)}, u32[]{:S(2)}, u32[]{:S(2)}) %all-to-all-start.1) | async-done | bytes 1310752 | tf_op jit(solution)/shard_map/all_to_all | solution.py:338
  115.9 1.0 copy-done.1
  117.0 0.9 copy-done.4
  117.9 1.0 copy-done.6
  119.0 5.1 %adjoint_tiles.1 = (bf16[16,64,128]{2,1,0:T(8,128)(2,1)S(1)}, bf16[64,2048]{1,0:T(8,128)(2,1)}) custom-call(s32[4,256]{1,0:T(4,128)S(1)} %add_add_fusion.lists_ref.refs_0_, s32[64]{0:T(128)S(1)} %fusion.refs_1_, bf16[64,80,128]{2,1,0:T(8,128)(2,1)S(1)} %all-to-all-done.1.refs_2_, bf16[16,128,128]{2,1,0:T(8,128)(2,1)S(1)} %bitcast.19, ...), custom_call_target="tpu_custom_call" | custom-call | flops 536870912 | bytes 8388608 | tf_op jit(solution)/shard_map/adjoint_tiles/pallas_call | solution.py:289
  124.1 11.3 %all_to_all.15.refs_0_ = bf16[16,64,128]{2,1,0:T(8,128)(2,1)S(1)} all-to-all(bf16[16,64,128]{2,1,0:T(8,128)(2,1)S(1)} %get-tuple-element.13), channel_id=1, replica_groups=mesh['dom'=64,'ray'=4] {'ray'}, dimensions={0} | all-to-all | bytes 524288 | tf_op jit(solution)/shard_map/all_to_all | solution.py:338
  135.4 0.1 image_step.1
  135.5 0.8 copy.17
  (18 shorter events, 0.1 us)
Async XLA Ops:
  1.4 15.3 %collective-permute-start.1 = (bf16[64,128]{1,0:T(8,128)(2,1)S(1)}, bf16[64,128]{1,0:T(8,128)(2,1)S(1)}, u32[]{:S(2)}, u32[]{:S(2)}) collective-permute-start(bf16[64,128]{1,0:T(8,128)(2,1)S(1)} %get-tuple-element.18), channel_id=1, source_target_pairs={{1,0},{2,1},{3,2},{5,4},{6,5},{7,6},{9,8},{10,9},{11,10},{13,12},{... | collective-permute-start | bytes 49160 | tf_op jit(solution)/shard_map/ppermute | solution.py:363
  2.7 14.1 %collective-permute-start = (bf16[64,128]{1,0:T(8,128)(2,1)S(1)}, bf16[64,128]{1,0:T(8,128)(2,1)S(1)}, u32[]{:S(2)}, u32[]{:S(2)}) collective-permute-start(bf16[64,128]{1,0:T(8,128)(2,1)S(1)} %get-tuple-element.19), channel_id=1, source_target_pairs={{0,1},{1,2},{2,3},{4,5},{5,6},{6,7},{8,9},{9,10},{10,11},{12,13},{... | collective-permute-start | bytes 49160 | tf_op jit(solution)/shard_map/ppermute | solution.py:362
  8.6 7.6 %copy-start.9 = (bf16[129]{0:T(256)(128)(2,1)S(1)}, bf16[129]{0:T(256)(128)(2,1)}, u32[]{:S(2)}) copy-start(bf16[129]{0:T(256)(128)(2,1)} %param.10) | copy-start | bytes 778
  11.3 1.0 copy-start
  12.4 4.4 %copy-start.7 = (bf16[1,64,2048]{2,1,0:T(8,128)(2,1)S(1)}, bf16[1,64,2048]{2,1,0:T(8,128)(2,1)}, u32[]{:S(2)}) copy-start(bf16[1,64,2048]{2,1,0:T(8,128)(2,1)} %param.9) | copy-start | bytes 786436
  18.8 53.4 %copy-start.3 = (bf16[64,2048]{1,0:T(8,128)(2,1)}, bf16[64,2048]{1,0:T(8,128)(2,1)S(1)}, u32[]{:S(2)}) copy-start(bf16[64,2048]{1,0:T(8,128)(2,1)S(1)} %get-tuple-element.9.phase_ref.refs_4_) | copy-start | bytes 786436
  18.8 53.4 %copy-start.8 = (s32[1,1,64]{2,1,0:T(1,128)S(1)}, s32[1,1,64]{2,1,0:T(1,128)}, u32[]{:S(2)}) copy-start(s32[1,1,64]{2,1,0:T(1,128)} %param.17) | copy-start | bytes 772
  18.8 53.3 %all-to-all-start = ((bf16[64,96,128]{2,1,0:T(8,128)(2,1)}), bf16[64,96,128]{2,1,0:T(8,128)(2,1)S(1)}, u32[]{:S(2)}, u32[]{:S(2)}) async-start(bf16[64,96,128]{2,1,0:T(8,128)(2,1)} %get-tuple-element.8), calls=%async_computation | async-start | bytes 3145728 | tf_op jit(solution)/shard_map/all_to_all | solution.py:338
  74.2 1.1 copy-start.2
  75.3 0.8 copy-start.5
  76.1 39.8 %all-to-all-start.1 = ((bf16[64,80,128]{2,1,0:T(8,128)(2,1)}), bf16[64,80,128]{2,1,0:T(8,128)(2,1)S(1)}, u32[]{:S(2)}, u32[]{:S(2)}) async-start(bf16[64,80,128]{2,1,0:T(8,128)(2,1)} %copy-done.2), calls=%async_computation.1 | async-start | bytes 2621440 | tf_op jit(solution)/shard_map/all_to_all | solution.py:338
  115.9 1.0 copy-start.1
  117.0 0.9 copy-start.4
  117.9 1.0 copy-start.6

commit v2 on v1

v2 whole, which is shorter than its diff:
```python
import jax
import jax.numpy as jnp
from jax import lax
from jax.experimental import pallas as pl
from jax.experimental.pallas import tpu as pltpu
from jax.sharding import PartitionSpec as P

T = 128
SMOOTH = 8
RELAX = 0.25
SECTION = 32
MIB = 2**20
F32, BF16 = jnp.float32, jnp.bfloat16
NT = (((1,), (1,)), ((), ()))
VMEM = pl.BlockSpec(memory_space=pltpu.VMEM)
SMEM = pl.BlockSpec(memory_space=pltpu.SMEM)
HBM = pl.BlockSpec(memory_space=pltpu.HBM)


def params(limit=63):
    return pltpu.CompilerParams(vmem_limit_bytes=limit * MIB)


def middle_network(n):
    pairs = []
    p = 1
    while p < n:
        k = p
        while k >= 1:
            for j in range(k % p, n - k, 2 * k):
                for i in range(min(k, n - j - k)):
                    if (i + j) // (2 * p) == (i + j + k) // (2 * p):
                        pairs.append((i + j, i + j + k))
            k //= 2
        p *= 2
    needed = {n // 2 - 1, n // 2}
    kept = []
    for a, b in reversed(pairs):
        if a in needed or b in needed:
            kept.append((a, b, a in needed, b in needed))
            needed |= {a, b}
    return kept[::-1]


def band(kernel):
    taps = kernel.shape[0]
    padded = jnp.concatenate([kernel, jnp.zeros((2 * T + 1 - taps,), kernel.dtype)])
    tiled = jnp.tile(padded, T)[: 2 * T * T].reshape(T, 2 * T)
    return jnp.pad(tiled, ((0, 0), (T // 2, T // 2)))


def lanes(block):
    return pl.ds(pl.multiple_of(block * T, T), T)


def first_call(entry, place, slot, count, numbers, projections, left, right, taps, image, library):
    slices, columns = projections.shape
    entries, capacity = library.shape[0], entry.shape[1]
    blocks = image.shape[1] // T
    owners = slices
    per = columns // T
    rows = slices + SECTION
    parts = 4

    def kernel(
        entry_hbm, place_hbm, slot_hbm, count_ref, n_hbm, x_hbm, l_ref, r_ref, taps_ref, image_hbm, library_hbm,
        phase_ref, send_ref, entry_ref, place_ref, slot_ref, n_ref, library_ref, wide, spread, row, stacked,
        product, total, packed, sems, loads,
    ):
        pairs = [(x_hbm, wide.at[:, pl.ds(T, columns)]), (n_hbm, n_ref), (library_hbm, library_ref)]
        pairs += [
            (image_hbm.at[:, pl.ds(i * T, T)], stacked.at[pl.ds(i * slices, slices)]) for i in range(blocks)
        ]
        pairs += [(entry_hbm, entry_ref), (place_hbm, place_ref), (slot_hbm, slot_ref)]
        fetches = [pltpu.make_async_copy(a, b, loads.at[n]) for n, (a, b) in enumerate(pairs)]
        for fetch in fetches:
            fetch.start()
        wide[:, :T] = l_ref[...]
        wide[:, T + columns :] = r_ref[...]
        spread[...] = jnp.zeros_like(spread)

        def put(at, value):
            spread[pl.ds(at, slices, stride=SECTION), :] = value

        def filtered(start, stop, low):
            return lax.dot_general(
                wide[:, start * T : stop * T],
                taps_ref[:, low * T : (low + stop - start) * T],
                NT,
                preferred_element_type=F32,
            ).astype(BF16)

        fetches[0].wait()
        for b in range(per):
            value = filtered(b, b + 3, 0)
            phase_ref[:, b * T : (b + 1) * T] = value
            put(b, value.astype(F32))
        put(per, filtered(0, 2, 1).astype(F32))
        put(per + 1, filtered(per, per + 2, 0).astype(F32))
        row[...] = jnp.zeros_like(row)
        fetches[1].wait()
        row[0:1, :owners] = n_ref[...].astype(F32)
        put(per + 2, jnp.broadcast_to(row[0:1, :], (slices, T)))
        packed[:, slices:, :] = spread[...].astype(BF16).reshape(slices, SECTION, T)

        total[...] = jnp.zeros_like(total)
        for fetch in fetches[2:]:
            fetch.wait()
        for e in range(0, entries, 2):
            product[:, e * T : (e + 2) * T] = lax.dot_general(
                stacked[...], library_ref[e : e + 2].reshape(2 * T, T), NT, preferred_element_type=F32
            )

        def add(k):
            live = k < count_ref[0, 0]
            e = jnp.where(live, entry_ref[0, k], 0)
            i = jnp.where(live, place_ref[0, k], 0)
            s = jnp.where(live, slot_ref[0, k], owners)
            total[s] += product[pl.ds(pl.multiple_of(i * slices, slices), slices), lanes(e)]

        def group(g, carry):
            for u in range(8):
                add(g * 8 + u)
            return carry

        lax.fori_loop(0, (count_ref[0, 0] + 7) // 8, group, 0)
        step = owners // parts
        copies = []
        for n in range(parts):
            packed[n * step : (n + 1) * step, :slices, :] = total[n * step : (n + 1) * step].astype(BF16)
            here = pl.ds(n * step, step)
            copies.append(pltpu.make_async_copy(packed.at[here], send_ref.at[here], sems.at[n]))
            copies[-1].start()
        for copy in copies:
            copy.wait()

    return pl.pallas_call(
        kernel,
        out_shape=[
            jax.ShapeDtypeStruct((slices, columns), BF16),
            jax.ShapeDtypeStruct((owners, rows, T), BF16),
        ],
        in_specs=[HBM] * 3 + [SMEM, HBM, HBM] + [VMEM] * 3 + [HBM, HBM],
        out_specs=[VMEM, HBM],
        scratch_shapes=[
            pltpu.SMEM(entry.shape, jnp.int32),
            pltpu.SMEM(place.shape, jnp.int32),
            pltpu.SMEM(slot.shape, jnp.int32),
            pltpu.VMEM(numbers.shape, jnp.int32),
            pltpu.VMEM(library.shape, BF16),
            pltpu.VMEM((slices, columns + 2 * T), BF16),
            pltpu.VMEM((slices * SECTION, T), F32),
            pltpu.VMEM((8, T), F32),
            pltpu.VMEM((blocks * slices, T), BF16),
            pltpu.VMEM((blocks * slices, entries * T), F32),
            pltpu.VMEM((owners + 1, slices, T), F32),
            pltpu.VMEM((owners, rows, T), BF16),
            pltpu.SemaphoreType.DMA((parts,)),
            pltpu.SemaphoreType.DMA((blocks + 6,)),
        ],
        compiler_params=params(),
        cost_estimate=pl.CostEstimate(
            flops=2 * capacity * slices * T * T, bytes_accessed=8 * 2**20, transcendentals=0
        ),
        name="filter_and_forward",
    )(entry, place, slot, count, numbers, projections, left, right, taps, image, library)


def stripe_of(quarter, quarters, arrived_ref, offset, values, rimmed):
    angles = arrived_ref.shape[0]
    for a in range(angles):
        values[a] = arrived_ref[a, offset : offset + SECTION, :].astype(F32)[:24]
    network = middle_network(angles)

    def middle(g, carry):
        rows = pl.ds(pl.multiple_of(g * 8, 8), 8)
        v = [values[a, rows, :] for a in range(angles)]
        for a, b, low, high in network:
            x, y = v[a], v[b]
            if low:
                v[a] = jnp.minimum(x, y)
            if high:
                v[b] = jnp.maximum(x, y)
        rimmed[pl.ds(g * 8 + 1, 8), :] = (v[angles // 2 - 1] + v[angles // 2]) * 0.5
        return carry

    lax.fori_loop(0, 3, middle, 0)
    before, after = rimmed[17:18, :], rimmed[18:19, :]
    rimmed[0:1, :] = jnp.where(quarter == 0, jnp.zeros_like(before), before)
    rimmed[17:18, :] = jnp.where(quarter == quarters - 1, jnp.zeros_like(after), after)
    prev, cur, nxt = rimmed[0:16, :], rimmed[1:17, :], rimmed[2:18, :]
    lane = lax.broadcasted_iota(jnp.int32, (16, T), 1)
    total = cur
    for o in range(1, SMOOTH + 1):
        total += pltpu.roll(jnp.where(lane < o, nxt, cur), T - o, 1)
        total += pltpu.roll(jnp.where(lane >= T - o, prev, cur), o, 1)
    place = quarter * (16 * T) + lax.broadcasted_iota(jnp.int32, (16, T), 0) * T + lane
    last = quarters * 16 * T - 1
    count = jnp.minimum(place + SMOOTH, last) - jnp.maximum(place - SMOOTH, 0) + 1
    return cur - total / count.astype(F32)


def back_call(carried, quarter, arrived, phase, quarters):
    owners = arrived.shape[0]
    size, columns = phase.shape
    rows = size + 16
    parts = 4

    def kernel(c_ref, q_ref, arrived_ref, phase_ref, forward_ref, send_ref, values, rimmed, less, packed, sems):
        stripe = stripe_of(q_ref[0], quarters, arrived_ref, size, values, rimmed).astype(BF16)
        forward_ref[...] = jnp.zeros_like(forward_ref)
        for d in range(owners):
            forward_ref[:, lanes(c_ref[0, d])] += arrived_ref[d, :size, :].astype(F32)
        less[...] = (phase_ref[...].astype(F32) - forward_ref[...]).astype(BF16)
        step = owners // parts
        copies = []
        for n in range(parts):
            for d in range(n * step, (n + 1) * step):
                packed[d, :size, :] = less[:, lanes(c_ref[0, d])]
                packed[d, size:, :] = stripe
            here = pl.ds(n * step, step)
            copies.append(pltpu.make_async_copy(packed.at[here], send_ref.at[here], sems.at[n]))
            copies[-1].start()
        for copy in copies:
            copy.wait()

    return pl.pallas_call(
        kernel,
        out_shape=[
            jax.ShapeDtypeStruct((size, columns), F32),
            jax.ShapeDtypeStruct((owners, rows, T), BF16),
        ],
        in_specs=[SMEM, SMEM, VMEM, VMEM],
        out_specs=[VMEM, HBM],
        scratch_shapes=[
            pltpu.VMEM((owners, 24, T), F32),
            pltpu.VMEM((32, T), F32),
            pltpu.VMEM((size, columns), BF16),
            pltpu.VMEM((owners, rows, T), BF16),
            pltpu.SemaphoreType.DMA((parts,)),
        ],
        compiler_params=params(),
        cost_estimate=pl.CostEstimate(flops=2**24, bytes_accessed=8 * 2**20, transcendentals=0),
        name="sum_and_stripe",
    )(carried, quarter, arrived, phase)


def adjoint_call(entry, place, slot, count, theirs, returned, library, blocks):
    entries = library.shape[0]
    owners = returned.shape[0]
    per = 16
    size = returned.shape[1] - per

    def kernel(
        entry_hbm, place_hbm, slot_hbm, count_ref, c_ref, returned_ref, library_hbm,
        update_ref, stripe_ref, entry_ref, place_ref, slot_ref, library_ref, stripes, terms, bins, loads,
    ):
        pairs = [(entry_hbm, entry_ref), (place_hbm, place_ref), (slot_hbm, slot_ref), (library_hbm, library_ref)]
        fetches = [pltpu.make_async_copy(a, b, loads.at[n]) for n, (a, b) in enumerate(pairs)]
        for fetch in fetches:
            fetch.start()
        stripes[...] = returned_ref[:, size:, :].astype(F32).reshape(owners * per, T)
        for b in range(per):
            stripe_ref[b] = stripes[pl.ds(b, size, stride=per), :]
        for e in range(owners):
            terms[e] = returned_ref[e, :size, :].astype(F32) - stripe_ref[c_ref[e]]
        terms[owners] = jnp.zeros((size, T), F32)
        bins[...] = jnp.zeros_like(bins)
        for fetch in fetches:
            fetch.wait()

        def add(k):
            live = k < count_ref[0, 0]
            e = jnp.where(live, entry_ref[0, k], 0)
            i = jnp.where(live, place_ref[0, k], 0)
            s = jnp.where(live, slot_ref[0, k], owners)
            bins[pl.ds(pl.multiple_of(i * size, size), size), lanes(e)] += terms[s]

        def group(g, carry):
            for u in range(8):
                add(g * 8 + u)
            return carry

        lax.fori_loop(0, (count_ref[0, 0] + 7) // 8, group, 0)
        half = blocks // 2
        for h in range(2):
            update_ref[h * half : (h + 1) * half] = (
                jnp.dot(
                    bins[h * half * size : (h + 1) * half * size, :].astype(BF16),
                    library_ref[...].reshape(entries * T, T),
                    preferred_element_type=F32,
                )
                .astype(BF16)
                .reshape(half, size, T)
            )

    return pl.pallas_call(
        kernel,
        out_shape=[
            jax.ShapeDtypeStruct((blocks, size, T), BF16),
            jax.ShapeDtypeStruct((per, size, T), F32),
        ],
        in_specs=[HBM] * 3 + [SMEM, SMEM, VMEM, HBM],
        out_specs=[VMEM, VMEM],
        scratch_shapes=[
            pltpu.SMEM(entry.shape, jnp.int32),
            pltpu.SMEM(place.shape, jnp.int32),
            pltpu.SMEM(slot.shape, jnp.int32),
            pltpu.VMEM(library.shape, BF16),
            pltpu.VMEM((owners * per, T), F32),
            pltpu.VMEM((owners + 1, size, T), F32),
            pltpu.VMEM((blocks * size, entries * T), F32),
            pltpu.SemaphoreType.DMA((4,)),
        ],
        compiler_params=params(),
        cost_estimate=pl.CostEstimate(
            flops=2 * 256 * size * T * T, bytes_accessed=8 * 2**20, transcendentals=0
        ),
        name="adjoint_tiles",
    )(entry, place, slot, count, theirs, returned, library)


def residual_call(phase, stripe, forward):
    per = stripe.shape[0]

    def kernel(phase_ref, stripe_ref, forward_ref, residual_ref):
        for b in range(per):
            where = slice(b * T, (b + 1) * T)
            corrected = (phase_ref[:, where].astype(F32) - stripe_ref[b]).astype(BF16)
            residual_ref[:, where] = (corrected.astype(F32) - forward_ref[:, where]).astype(BF16)

    return pl.pallas_call(
        kernel,
        out_shape=jax.ShapeDtypeStruct(phase.shape, BF16),
        in_specs=[VMEM] * 3,
        out_specs=VMEM,
        compiler_params=params(12),
        cost_estimate=pl.CostEstimate(flops=2**19, bytes_accessed=2**21, transcendentals=0),
        name="residual",
    )(phase, stripe, forward)


def image_call(quarter, image, parts, quarters):
    slices, pixels = image.shape
    held = pixels // quarters
    mine = held // T

    def kernel(q_ref, image_ref, parts_ref, out_ref):
        for i in range(mine):
            total = parts_ref[i].astype(F32)
            for q in range(1, quarters):
                total += parts_ref[q * mine + i].astype(F32)
            own = image_ref[:, lanes(q_ref[0] * mine + i)].astype(F32)
            out_ref[:, i * T : (i + 1) * T] = own + RELAX * total

    return pl.pallas_call(
        kernel,
        out_shape=jax.ShapeDtypeStruct((slices, held), F32),
        in_specs=[SMEM, VMEM, VMEM],
        out_specs=VMEM,
        compiler_params=params(12),
        cost_estimate=pl.CostEstimate(flops=2**18, bytes_accessed=2**20, transcendentals=0),
        name="image_step",
    )(quarter, image, parts)


def exchanged(array, axis):
    return lax.all_to_all(array, axis, split_axis=0, concat_axis=0, tiled=True)


def shards(projections, phase_kernel, image, tile_library, tile_entry, tile_image, tile_slot, tile_count, slot_block):
    projections = projections[0]
    library = tile_library[0, 0]
    image = image.T
    slices = projections.shape[0]
    quarters = lax.axis_size("ray")
    quarter = lax.axis_index("ray").astype(jnp.int32).reshape(1)
    tiles = (tile_entry[0], tile_image[0], tile_slot[0], tile_count)
    carried = slot_block[0]

    left = lax.ppermute(projections[:, -T:], "ray", [(i, i + 1) for i in range(quarters - 1)])
    right = lax.ppermute(projections[:, :T], "ray", [(i + 1, i) for i in range(quarters - 1)])
    phase, send = first_call(*tiles, carried, projections, left, right, band(phase_kernel), image, library)
    arrived = exchanged(send, "dom")
    numbers = lax.dynamic_slice_in_dim(arrived[:, slices + 18, :], lax.axis_index("dom"), 1, axis=1)
    theirs = numbers[:, 0].astype(jnp.int32)
    forward, back = back_call(carried, quarter, arrived, phase, quarters)
    returned = exchanged(back, "dom")
    update, stripe = adjoint_call(*tiles, theirs, returned, library, image.shape[1] // T)
    parts = exchanged(update, "ray")
    residual = residual_call(phase, stripe, forward)
    image_next = image_call(quarter, image, parts, quarters)
    return residual[None], image_next.T


def solution(mesh):
    return jax.shard_map(
        shards,
        mesh=mesh,
        in_specs=(
            P("dom", None, "ray"),
            P(),
            P("dom", None),
            P("dom", "ray", None, None, None),
            P("dom", "ray", None),
            P("dom", "ray", None),
            P("dom", "ray", None),
            P("dom", "ray"),
            P("dom", "ray", None),
        ),
        out_specs=(P("dom", None, "ray"), P(("dom", "ray"), None)),
        check_vma=False,
    )
```

time: 137 us -> 134 us (0.978)
  blocking collectives: 11.3 us -> 0 us
  Pallas kernels: 13.1 us -> 18.8 us
  starting transfers between devices: 24.6 us -> 29.7 us
  local copies, waits for them, and re-layouts: 9.36 us -> 5.19 us
  waiting for transfers between devices: 73.2 us -> 76.3 us
  other arithmetic: 3.35 us -> 1.83 us
    all_to_all x1 -> x0, blocking collectives: 11.3 us -> none  [exchanged(): return lax.all_to_all(array, axis, split_axis=0, concat_axis=0, tiled=True)]
    unnamed x22 -> x12, local copies, waits for them, and re-layouts: 7.98 us -> 1.65 us
    pallas_call x5, Pallas kernels: 13.1 us -> 18.8 us  [the longest x1 7.46 us: first_call(): pl.pallas_call(kernel, out_shape=[jax.ShapeDtypeStruct((slices, columns),...]
    all_to_all x2 -> x3, starting transfers between devices: 18.7 us -> 23.9 us  [exchanged(): return lax.all_to_all(array, axis, split_axis=0, concat_axis=0, tiled=True)]
    all_to_all x2 -> x3, waiting for transfers between devices: 73.2 us -> 76.3 us  [exchanged(): return lax.all_to_all(array, axis, split_axis=0, concat_axis=0, tiled=True)]
    select_n x2 -> x0, other arithmetic: 1.39 us -> none  [the longest x1 0.7 us: shards(): jnp.where(live, tile_slot[0, 0], owners)]
  transfers between devices with their start and end apart: 4 -> 5, of which waited for: 2 -> 3; matrix products, arithmetic and copies ran while one was open for 4% -> 3% of each run, Pallas kernels for 3% -> 1%
where the time goes in v2:
time: 134 us; the launch traced here: 133 us
  waiting for transfers between devices  76.3 us (57%)
  starting transfers between devices  29.7 us (22%)
  Pallas kernels  18.8 us (14%)
  local copies, waits for them, and re-layouts  5.19 us (4%)
  other arithmetic  1.83 us (1%)
  between operations  1.41 us (1%)
    all_to_all x3, waiting for transfers between devices, exchanged(): return lax.all_to_all(array, axis, split_axis=0, concat_axis=0, tiled=True)  76.3 us
    all_to_all x3, starting transfers between devices, exchanged(): return lax.all_to_all(array, axis, split_axis=0, concat_axis=0, tiled=True)  23.9 us
    pallas_call x1, Pallas kernels, first_call(): pl.pallas_call(kernel, out_shape=[jax.ShapeDtypeStruct((slices, columns),...  7.46 us
    pallas_call x1, Pallas kernels, adjoint_call(): pl.pallas_call(kernel, out_shape=[jax.ShapeDtypeStruct((blocks, size, T),...  5.43 us
    ppermute x1, starting transfers between devices, shards(): lax.ppermute(projections[:, -T:], 'ray', [(i, i + 1) for i in range(quart...  4.55 us
    pallas_call x1, Pallas kernels, back_call(): pl.pallas_call(kernel, out_shape=[jax.ShapeDtypeStruct((size, columns), F...  4.38 us
  transfers between devices with their start and end apart: 5, of which 3 were waited for; matrix products, arithmetic and copies ran while one was open for 3% of the time, Pallas kernels for 1%

profile of v2, /device:TPU:8, one launch (start us, length us, event | category | flops | bytes accessed | tf_op | source)
XLA Modules:
  0.0 133.2 jit_solution(13229880823485283615)
XLA Ops:
  0.6 0.7 fusion
  1.4 1.3 collective-permute-start.1
  2.7 4.5 %collective-permute-start = (bf16[64,128]{1,0:T(8,128)(2,1)S(1)}, bf16[64,128]{1,0:T(8,128)(2,1)S(1)}, u32[]{:S(2)}, u32[]{:S(2)}) collective-permute-start(bf16[64,128]{1,0:T(8,128)(2,1)S(1)} %get-tuple-element.15), channel_id=1, source_target_pairs={{0,1},{1,2},{2,3},{4,5},{5,6},{6,7},{8,9},{9,10},{10,11},{12,13},{... | collective-permute-start | bytes 49160 | tf_op jit(solution)/shard_map/ppermute | solution.py:381
  7.9 0.7 concatenate.3
  8.5 0.3 tile.10
  8.9 0.7 pad.5.taps_ref
  9.7 0.0 collective-permute-done.1.r_ref
  9.7 0.0 copy-start.4
  9.7 0.0 collective-permute-done.l_ref
  9.7 0.0 copy-start.5
  9.7 0.6 copy-done.4
  10.3 0.0 copy-done.5
  10.3 7.5 %filter_and_forward.1 = (bf16[64,2048]{1,0:T(8,128)(2,1)}, bf16[64,96,128]{2,1,0:T(8,128)(2,1)}) custom-call(s32[1,256]{1,0:T(1,128)} %bitcast.20, s32[1,256]{1,0:T(1,128)} %bitcast.22, s32[1,256]{1,0:T(1,128)} %bitcast.24, s32[1,1]{1,0:T(1,128)S(6)} %copy.11.count_ref, s32[1,64]{1,0:T(1,128)} %bitcast.16, bf16[64,2048]{1,0:T(8,128)(2,1)} %bitcast.15, ...), custom_call_target="tpu_custom_call" | custom-call | flops 536870912 | bytes 8388608 | tf_op jit(solution)/shard_map/filter_and_forward/pallas_call | solution.py:137
  17.7 12.3 %all-to-all-start = ((bf16[64,96,128]{2,1,0:T(8,128)(2,1)}), bf16[64,96,128]{2,1,0:T(8,128)(2,1)}, u32[]{:S(2)}, u32[]{:S(2)}) async-start(bf16[64,96,128]{2,1,0:T(8,128)(2,1)} %get-tuple-element.9), calls=%async_computation | async-start | bytes 3145728 | tf_op jit(solution)/shard_map/all_to_all | solution.py:368
  30.0 40.0 %all-to-all-done.arrived_ref = bf16[64,96,128]{2,1,0:T(8,128)(2,1)} async-done(((bf16[64,96,128]{2,1,0:T(8,128)(2,1)}), bf16[64,96,128]{2,1,0:T(8,128)(2,1)}, u32[]{:S(2)}, u32[]{:S(2)}) %all-to-all-start) | async-done | bytes 1572896 | tf_op jit(solution)/shard_map/all_to_all | solution.py:368
  70.0 4.4 %sum_and_stripe.1 = (f32[64,2048]{1,0:T(8,128)}, bf16[64,80,128]{2,1,0:T(8,128)(2,1)}) custom-call(s32[1,64]{1,0:T(1,128)} %bitcast.17, s32[1]{0:T(128)} %bitcast.7.q_ref, bf16[64,96,128]{2,1,0:T(8,128)(2,1)} %all-to-all-done.arrived_ref, bf16[64,2048]{1,0:T(8,128)(2,1)} %get-tuple-element.8.phase_ref), custom_call_target="tpu_custom_call" | custom-call | flops 16777216 | bytes 8388608 | tf_op jit(solution)/shard_map/sum_and_stripe/pallas_call | solution.py:227
  74.4 5.6 %all-to-all-start.1 = ((bf16[64,80,128]{2,1,0:T(8,128)(2,1)}), bf16[64,80,128]{2,1,0:T(8,128)(2,1)}, u32[]{:S(2)}, u32[]{:S(2)}) async-start(bf16[64,80,128]{2,1,0:T(8,128)(2,1)} %get-tuple-element.10), calls=%async_computation.1 | async-start | bytes 2621440 | tf_op jit(solution)/shard_map/all_to_all | solution.py:368
  80.0 0.0 copy-start
  80.0 0.0 copy-start.1
  80.0 1.0 slice.19
  81.1 1.8 %convert_reduce_fusion.c_ref = s32[64]{0:T(128)} fusion(bf16[64,1,128]{2,1,0:T(2,128)(2,1)S(1)} %slice.19, s32[]{:T(128)S(6)} %select_n.3), kind=kLoop, calls=%fused_computation | loop fusion | flops 64 | bytes 388 | tf_op jit(solution)/shard_map/convert_element_type | solution.py:386
  82.9 31.5 %all-to-all-done.1.returned_ref = bf16[64,80,128]{2,1,0:T(8,128)(2,1)} async-done(((bf16[64,80,128]{2,1,0:T(8,128)(2,1)}), bf16[64,80,128]{2,1,0:T(8,128)(2,1)}, u32[]{:S(2)}, u32[]{:S(2)}) %all-to-all-start.1) | async-done | bytes 1310752 | tf_op jit(solution)/shard_map/all_to_all | solution.py:368
  114.4 5.4 %adjoint_tiles.1 = (bf16[16,64,128]{2,1,0:T(8,128)(2,1)}, f32[16,64,128]{2,1,0:T(8,128)}) custom-call(s32[1,256]{1,0:T(1,128)} %bitcast.21, s32[1,256]{1,0:T(1,128)} %bitcast.23, s32[1,256]{1,0:T(1,128)} %bitcast.25, s32[1,1]{1,0:T(1,128)S(6)} %copy.11.count_ref, s32[64]{0:T(128)} %convert_reduce_fusion.c_ref, ...), custom_call_target="tpu_custom_call" | custom-call | flops 536870912 | bytes 8388608 | tf_op jit(solution)/shard_map/adjoint_tiles/pallas_call | solution.py:297
  119.8 0.0 copy-start.3
  119.8 6.0 %all-to-all-start.2 = ((bf16[16,64,128]{2,1,0:T(8,128)(2,1)}), bf16[16,64,128]{2,1,0:T(8,128)(2,1)S(1)}, u32[]{:S(2)}, u32[]{:S(2)}) async-start(bf16[16,64,128]{2,1,0:T(8,128)(2,1)} %get-tuple-element.13), calls=%async_computation.2 | async-start | bytes 524288 | tf_op jit(solution)/shard_map/all_to_all | solution.py:368
  125.8 0.0 copy-done
  125.8 0.0 copy-done.1
  125.9 1.0 copy-done.2
  126.9 0.8 residual.1
  127.7 4.8 %all-to-all-done.2.parts_ref = bf16[16,64,128]{2,1,0:T(8,128)(2,1)S(1)} async-done(((bf16[16,64,128]{2,1,0:T(8,128)(2,1)}), bf16[16,64,128]{2,1,0:T(8,128)(2,1)S(1)}, u32[]{:S(2)}, u32[]{:S(2)}) %all-to-all-start.2) | async-done | bytes 262176 | tf_op jit(solution)/shard_map/all_to_all | solution.py:368
  132.5 0.0 copy-done.3
  132.5 0.7 image_step.1
  (4 shorter events, 0.0 us)
Async XLA Ops:
  1.4 8.3 %collective-permute-start.1 = (bf16[64,128]{1,0:T(8,128)(2,1)S(1)}, bf16[64,128]{1,0:T(8,128)(2,1)S(1)}, u32[]{:S(2)}, u32[]{:S(2)}) collective-permute-start(bf16[64,128]{1,0:T(8,128)(2,1)S(1)} %get-tuple-element.14), channel_id=1, source_target_pairs={{1,0},{2,1},{3,2},{5,4},{6,5},{7,6},{9,8},{10,9},{11,10},{13,12},{... | collective-permute-start | bytes 49160 | tf_op jit(solution)/shard_map/ppermute | solution.py:382
  2.7 7.0 %collective-permute-start = (bf16[64,128]{1,0:T(8,128)(2,1)S(1)}, bf16[64,128]{1,0:T(8,128)(2,1)S(1)}, u32[]{:S(2)}, u32[]{:S(2)}) collective-permute-start(bf16[64,128]{1,0:T(8,128)(2,1)S(1)} %get-tuple-element.15), channel_id=1, source_target_pairs={{0,1},{1,2},{2,3},{4,5},{5,6},{6,7},{8,9},{9,10},{10,11},{12,13},{... | collective-permute-start | bytes 49160 | tf_op jit(solution)/shard_map/ppermute | solution.py:381
  9.7 0.6 copy-start.4
  9.7 0.6 copy-start.5
  17.7 52.3 %all-to-all-start = ((bf16[64,96,128]{2,1,0:T(8,128)(2,1)}), bf16[64,96,128]{2,1,0:T(8,128)(2,1)}, u32[]{:S(2)}, u32[]{:S(2)}) async-start(bf16[64,96,128]{2,1,0:T(8,128)(2,1)} %get-tuple-element.9), calls=%async_computation | async-start | bytes 3145728 | tf_op jit(solution)/shard_map/all_to_all | solution.py:368
  74.4 40.0 %all-to-all-start.1 = ((bf16[64,80,128]{2,1,0:T(8,128)(2,1)}), bf16[64,80,128]{2,1,0:T(8,128)(2,1)}, u32[]{:S(2)}, u32[]{:S(2)}) async-start(bf16[64,80,128]{2,1,0:T(8,128)(2,1)} %get-tuple-element.10), calls=%async_computation.1 | async-start | bytes 2621440 | tf_op jit(solution)/shard_map/all_to_all | solution.py:368
  80.0 45.8 %copy-start = (bf16[64,2048]{1,0:T(8,128)(2,1)S(1)}, bf16[64,2048]{1,0:T(8,128)(2,1)}, u32[]{:S(2)}) copy-start(bf16[64,2048]{1,0:T(8,128)(2,1)} %get-tuple-element.8.phase_ref) | copy-start | bytes 786436
  80.0 45.8 %copy-start.1 = (f32[64,2048]{1,0:T(8,128)S(1)}, f32[64,2048]{1,0:T(8,128)}, u32[]{:S(2)}) copy-start(f32[64,2048]{1,0:T(8,128)} %get-tuple-element.12.forward_ref) | copy-start | bytes 1572868
  119.8 12.7 %copy-start.3 = (bf16[2048,64]{0,1:T(8,128)(2,1)S(1)}, bf16[2048,64]{0,1:T(8,128)(2,1)}, u32[]{:S(2)}) copy-start(bf16[2048,64]{0,1:T(8,128)(2,1)} %param.11) | copy-start | bytes 786436
  119.8 12.7 %all-to-all-start.2 = ((bf16[16,64,128]{2,1,0:T(8,128)(2,1)}), bf16[16,64,128]{2,1,0:T(8,128)(2,1)S(1)}, u32[]{:S(2)}, u32[]{:S(2)}) async-start(bf16[16,64,128]{2,1,0:T(8,128)(2,1)} %get-tuple-element.13), calls=%async_computation.2 | async-start | bytes 524288 | tf_op jit(solution)/shard_map/all_to_all | solution.py:368
  125.8 1.0 copy-start.2

commit v3 on v2

--- a/solution.py
+++ b/solution.py
@@ -42,13 +42,6 @@
     return kept[::-1]
 
 
-def band(kernel):
-    taps = kernel.shape[0]
-    padded = jnp.concatenate([kernel, jnp.zeros((2 * T + 1 - taps,), kernel.dtype)])
-    tiled = jnp.tile(padded, T)[: 2 * T * T].reshape(T, 2 * T)
-    return jnp.pad(tiled, ((0, 0), (T // 2, T // 2)))
-
-
 def lanes(block):
     return pl.ds(pl.multiple_of(block * T, T), T)
 
@@ -61,55 +54,67 @@
     per = columns // T
     rows = slices + SECTION
     parts = 4
+    loads = per + blocks + 8
 
     def kernel(
-        entry_hbm, place_hbm, slot_hbm, count_ref, n_hbm, x_hbm, l_ref, r_ref, taps_ref, image_hbm, library_hbm,
-        phase_ref, send_ref, entry_ref, place_ref, slot_ref, n_ref, library_ref, wide, spread, row, stacked,
-        product, total, packed, sems, loads,
+        entry_hbm, place_hbm, slot_hbm, count_hbm, n_hbm, x_hbm, l_hbm, r_hbm, taps_ref, image_hbm, library_hbm,
+        phase_ref, send_ref, entry_ref, place_ref, slot_ref, count_ref, n_ref, library_ref, wide, band, spread, row,
+        stacked, product, total, packed, sems, load_sems,
     ):
-        pairs = [(x_hbm, wide.at[:, pl.ds(T, columns)]), (n_hbm, n_ref), (library_hbm, library_ref)]
-        pairs += [
-            (image_hbm.at[:, pl.ds(i * T, T)], stacked.at[pl.ds(i * slices, slices)]) for i in range(blocks)
-        ]
-        pairs += [(entry_hbm, entry_ref), (place_hbm, place_ref), (slot_hbm, slot_ref)]
-        fetches = [pltpu.make_async_copy(a, b, loads.at[n]) for n, (a, b) in enumerate(pairs)]
+        def block(n):
+            return pl.ds(n * slices, slices)
+
+        pairs = [(x_hbm.at[:, pl.ds(b * T, T)], wide.at[block(b + 2)]) for b in range(per)]
+        pairs += [(l_hbm, wide.at[block(1)]), (r_hbm, wide.at[block(per + 2)]), (n_hbm, n_ref)]
+        early = len(pairs)
+        pairs += [(library_hbm, library_ref)]
+        pairs += [(image_hbm.at[:, pl.ds(i * T, T)], stacked.at[block(i)]) for i in range(blocks)]
+        late = len(pairs)
+        pairs += [(entry_hbm, entry_ref), (place_hbm, place_ref), (slot_hbm, slot_ref), (count_hbm, count_ref)]
+        fetches = [pltpu.make_async_copy(a, b, load_sems.at[n]) for n, (a, b) in enumerate(pairs)]
         for fetch in fetches:
             fetch.start()
-        wide[:, :T] = l_ref[...]
-        wide[:, T + columns :] = r_ref[...]
+
         spread[...] = jnp.zeros_like(spread)
-
-        def put(at, value):
-            spread[pl.ds(at, slices, stride=SECTION), :] = value
-
-        def filtered(start, stop, low):
-            return lax.dot_general(
-                wide[:, start * T : stop * T],
-                taps_ref[:, low * T : (low + stop - start) * T],
+        row[...] = jnp.zeros_like(row)
+        wide[block(0), :] = jnp.zeros((slices, T), BF16)
+        wide[block(per + 3), :] = jnp.zeros((slices, T), BF16)
+        spun = pltpu.roll(jnp.broadcast_to(taps_ref[0:1, :], (T, 3 * T)), T // 2, 1, stride=1, stride_axis=0)
+        band[...] = spun.astype(BF16)
+        for fetch in fetches[:early]:
+            fetch.wait()
+        filtered = sum(
+            lax.dot_general(
+                wide[n * slices : (n + per + 2) * slices, :],
+                band[:, n * T : (n + 1) * T],
                 NT,
                 preferred_element_type=F32,
-            ).astype(BF16)
-
-        fetches[0].wait()
+            )
+            for n in range(3)
+        ).astype(BF16)
+
+        def put(at, value):
+            spread[pl.ds(at, slices, stride=SECTION), :] = value.astype(F32)
+
         for b in range(per):
-            value = filtered(b, b + 3, 0)
+            value = filtered[(b + 1) * slices : (b + 2) * slices]
             phase_ref[:, b * T : (b + 1) * T] = value
-            put(b, value.astype(F32))
-        put(per, filtered(0, 2, 1).astype(F32))
-        put(per + 1, filtered(per, per + 2, 0).astype(F32))
-        row[...] = jnp.zeros_like(row)
-        fetches[1].wait()
+            put(b, value)
+        put(per, filtered[:slices])
+        put(per + 1, filtered[(per + 1) * slices :])
         row[0:1, :owners] = n_ref[...].astype(F32)
         put(per + 2, jnp.broadcast_to(row[0:1, :], (slices, T)))
         packed[:, slices:, :] = spread[...].astype(BF16).reshape(slices, SECTION, T)
 
         total[...] = jnp.zeros_like(total)
-        for fetch in fetches[2:]:
+        for fetch in fetches[early:late]:
             fetch.wait()
         for e in range(0, entries, 2):
             product[:, e * T : (e + 2) * T] = lax.dot_general(
                 stacked[...], library_ref[e : e + 2].reshape(2 * T, T), NT, preferred_element_type=F32
             )
+        for fetch in fetches[late:]:
+            fetch.wait()
 
         def add(k):
             live = k < count_ref[0, 0]
@@ -140,15 +145,17 @@
             jax.ShapeDtypeStruct((slices, columns), BF16),
             jax.ShapeDtypeStruct((owners, rows, T), BF16),
         ],
-        in_specs=[HBM] * 3 + [SMEM, HBM, HBM] + [VMEM] * 3 + [HBM, HBM],
+        in_specs=[HBM] * 8 + [VMEM] + [HBM] * 2,
         out_specs=[VMEM, HBM],
         scratch_shapes=[
             pltpu.SMEM(entry.shape, jnp.int32),
             pltpu.SMEM(place.shape, jnp.int32),
             pltpu.SMEM(slot.shape, jnp.int32),
+            pltpu.SMEM(count.shape, jnp.int32),
             pltpu.VMEM(numbers.shape, jnp.int32),
             pltpu.VMEM(library.shape, BF16),
-            pltpu.VMEM((slices, columns + 2 * T), BF16),
+            pltpu.VMEM(((per + 4) * slices, T), BF16),
+            pltpu.VMEM((T, 3 * T), BF16),
             pltpu.VMEM((slices * SECTION, T), F32),
             pltpu.VMEM((8, T), F32),
             pltpu.VMEM((blocks * slices, T), BF16),
@@ -156,7 +163,7 @@
             pltpu.VMEM((owners + 1, slices, T), F32),
             pltpu.VMEM((owners, rows, T), BF16),
             pltpu.SemaphoreType.DMA((parts,)),
-            pltpu.SemaphoreType.DMA((blocks + 6,)),
+            pltpu.SemaphoreType.DMA((loads,)),
         ],
         compiler_params=params(),
         cost_estimate=pl.CostEstimate(
@@ -166,10 +173,9 @@
     )(entry, place, slot, count, numbers, projections, left, right, taps, image, library)
 
 
-def stripe_of(quarter, quarters, arrived_ref, offset, values, rimmed):
-    angles = arrived_ref.shape[0]
-    for a in range(angles):
-        values[a] = arrived_ref[a, offset : offset + SECTION, :].astype(F32)[:24]
+def stripe_of(quarter, quarters, section, values, rimmed):
+    angles = section.shape[0]
+    values[...] = section[...].astype(F32)
     network = middle_network(angles)
 
     def middle(g, carry):
@@ -206,13 +212,26 @@
     rows = size + 16
     parts = 4
 
-    def kernel(c_ref, q_ref, arrived_ref, phase_ref, forward_ref, send_ref, values, rimmed, less, packed, sems):
-        stripe = stripe_of(q_ref[0], quarters, arrived_ref, size, values, rimmed).astype(BF16)
+    def kernel(
+        c_ref, q_ref, arrived_hbm, phase_ref, forward_ref, send_ref, values, rimmed, less, packed, section, partial,
+        sems, load_sems,
+    ):
+        step = owners // parts
+        pairs = [(arrived_hbm.at[:, pl.ds(size, SECTION), :], section)]
+        for n in range(parts):
+            here = pl.ds(n * step, step)
+            pairs.append((arrived_hbm.at[here, pl.ds(0, size), :], partial.at[here]))
+        fetches = [pltpu.make_async_copy(a, b, load_sems.at[n]) for n, (a, b) in enumerate(pairs)]
+        for fetch in fetches:
+            fetch.start()
         forward_ref[...] = jnp.zeros_like(forward_ref)
-        for d in range(owners):
-            forward_ref[:, lanes(c_ref[0, d])] += arrived_ref[d, :size, :].astype(F32)
+        fetches[0].wait()
+        stripe = stripe_of(q_ref[0], quarters, section, values, rimmed).astype(BF16)
+        for n in range(parts):
+            fetches[n + 1].wait()
+            for d in range(n * step, (n + 1) * step):
+                forward_ref[:, lanes(c_ref[0, d])] += partial[d].astype(F32)
         less[...] = (phase_ref[...].astype(F32) - forward_ref[...]).astype(BF16)
-        step = owners // parts
         copies = []
         for n in range(parts):
             for d in range(n * step, (n + 1) * step):
@@ -230,14 +249,17 @@
             jax.ShapeDtypeStruct((size, columns), F32),
             jax.ShapeDtypeStruct((owners, rows, T), BF16),
         ],
-        in_specs=[SMEM, SMEM, VMEM, VMEM],
+        in_specs=[SMEM, SMEM, HBM, VMEM],
         out_specs=[VMEM, HBM],
         scratch_shapes=[
-            pltpu.VMEM((owners, 24, T), F32),
+            pltpu.VMEM((owners, SECTION, T), F32),
             pltpu.VMEM((32, T), F32),
             pltpu.VMEM((size, columns), BF16),
             pltpu.VMEM((owners, rows, T), BF16),
+            pltpu.VMEM((owners, SECTION, T), BF16),
+            pltpu.VMEM((owners, size, T), BF16),
             pltpu.SemaphoreType.DMA((parts,)),
+            pltpu.SemaphoreType.DMA((parts + 1,)),
         ],
         compiler_params=params(),
         cost_estimate=pl.CostEstimate(flops=2**24, bytes_accessed=8 * 2**20, transcendentals=0),
@@ -252,21 +274,24 @@
     size = returned.shape[1] - per
 
     def kernel(
-        entry_hbm, place_hbm, slot_hbm, count_ref, c_ref, returned_ref, library_hbm,
-        update_ref, stripe_ref, entry_ref, place_ref, slot_ref, library_ref, stripes, terms, bins, loads,
+        entry_hbm, place_hbm, slot_hbm, count_hbm, c_ref, returned_hbm, library_hbm,
+        update_ref, stripe_ref, entry_ref, place_ref, slot_ref, count_ref, returned_ref, library_ref, stripes, terms,
+        bins, loads,
     ):
-        pairs = [(entry_hbm, entry_ref), (place_hbm, place_ref), (slot_hbm, slot_ref), (library_hbm, library_ref)]
+        pairs = [(returned_hbm, returned_ref), (entry_hbm, entry_ref), (place_hbm, place_ref), (slot_hbm, slot_ref)]
+        pairs += [(count_hbm, count_ref), (library_hbm, library_ref)]
         fetches = [pltpu.make_async_copy(a, b, loads.at[n]) for n, (a, b) in enumerate(pairs)]
         for fetch in fetches:
             fetch.start()
+        bins[...] = jnp.zeros_like(bins)
+        fetches[0].wait()
         stripes[...] = returned_ref[:, size:, :].astype(F32).reshape(owners * per, T)
         for b in range(per):
             stripe_ref[b] = stripes[pl.ds(b, size, stride=per), :]
         for e in range(owners):
             terms[e] = returned_ref[e, :size, :].astype(F32) - stripe_ref[c_ref[e]]
         terms[owners] = jnp.zeros((size, T), F32)
-        bins[...] = jnp.zeros_like(bins)
-        for fetch in fetches:
+        for fetch in fetches[1:]:
             fetch.wait()
 
         def add(k):
@@ -300,17 +325,19 @@
             jax.ShapeDtypeStruct((blocks, size, T), BF16),
             jax.ShapeDtypeStruct((per, size, T), F32),
         ],
-        in_specs=[HBM] * 3 + [SMEM, SMEM, VMEM, HBM],
+        in_specs=[HBM] * 4 + [SMEM, HBM, HBM],
         out_specs=[VMEM, VMEM],
         scratch_shapes=[
             pltpu.SMEM(entry.shape, jnp.int32),
             pltpu.SMEM(place.shape, jnp.int32),
             pltpu.SMEM(slot.shape, jnp.int32),
+            pltpu.SMEM(count.shape, jnp.int32),
+            pltpu.VMEM(returned.shape, BF16),
             pltpu.VMEM(library.shape, BF16),
             pltpu.VMEM((owners * per, T), F32),
             pltpu.VMEM((owners + 1, size, T), F32),
             pltpu.VMEM((blocks * size, entries * T), F32),
-            pltpu.SemaphoreType.DMA((4,)),
+            pltpu.SemaphoreType.DMA((6,)),
         ],
         compiler_params=params(),
         cost_estimate=pl.CostEstimate(
@@ -380,7 +407,8 @@
 
     left = lax.ppermute(projections[:, -T:], "ray", [(i, i + 1) for i in range(quarters - 1)])
     right = lax.ppermute(projections[:, :T], "ray", [(i + 1, i) for i in range(quarters - 1)])
-    phase, send = first_call(*tiles, carried, projections, left, right, band(phase_kernel), image, library)
+    taps = jnp.pad(phase_kernel.astype(F32), (0, 3 * T - phase_kernel.shape[0])).reshape(1, 3 * T)
+    phase, send = first_call(*tiles, carried, projections, left, right, taps, image, library)
     arrived = exchanged(send, "dom")
     numbers = lax.dynamic_slice_in_dim(arrived[:, slices + 18, :], lax.axis_index("dom"), 1, axis=1)
     theirs = numbers[:, 0].astype(jnp.int32)

time: 134 us -> 134 us (level)
  Pallas kernels: 18.8 us -> 21.7 us
  starting transfers between devices: 29.7 us -> 28.3 us
    all_to_all x3, starting transfers between devices: 23.9 us -> 22.5 us  [exchanged(): return lax.all_to_all(array, axis, split_axis=0, concat_axis=0, tiled=True)]
where the time goes in v3:
time: 134 us
  waiting for transfers between devices  76.3 us (57%)
  starting transfers between devices  28.3 us (21%)
  Pallas kernels  21.7 us (16%)
  local copies, waits for them, and re-layouts  3.99 us (3%)
  other arithmetic  2.49 us (2%)
  between operations  1.39 us (1%)
    all_to_all x3, waiting for transfers between devices, exchanged(): return lax.all_to_all(array, axis, split_axis=0, concat_axis=0, tiled=True)  76.3 us
    all_to_all x3, starting transfers between devices, exchanged(): return lax.all_to_all(array, axis, split_axis=0, concat_axis=0, tiled=True)  22.5 us
    pallas_call x1, Pallas kernels, first_call(): pl.pallas_call(kernel, out_shape=[jax.ShapeDtypeStruct((slices, columns),...  8.46 us
    pallas_call x1, Pallas kernels, adjoint_call(): pl.pallas_call(kernel, out_shape=[jax.ShapeDtypeStruct((blocks, size, T),...  6.59 us
    pallas_call x1, Pallas kernels, back_call(): pl.pallas_call(kernel, out_shape=[jax.ShapeDtypeStruct((size, columns), F...  5.13 us
    ppermute x1, starting transfers between devices, shards(): lax.ppermute(projections[:, -T:], 'ray', [(i, i + 1) for i in range(quart...  4.55 us
  transfers between devices with their start and end apart: 5, of which 3 were waited for; matrix products, arithmetic and copies ran while one was open for 3% of the time, Pallas kernels for 1%

profile of v3, /device:TPU:8, one launch (start us, length us, event | category | flops | bytes accessed | tf_op | source)
XLA Modules:
  0.0 134.2 jit_solution(11145822153574736931)
XLA Ops:
  0.6 0.7 fusion
  1.4 1.3 collective-permute-start.1
  2.7 4.5 %collective-permute-start = (bf16[64,128]{1,0:T(8,128)(2,1)S(1)}, bf16[64,128]{1,0:T(8,128)(2,1)S(1)}, u32[]{:S(2)}, u32[]{:S(2)}) collective-permute-start(bf16[64,128]{1,0:T(8,128)(2,1)S(1)} %get-tuple-element.15), channel_id=1, source_target_pairs={{0,1},{1,2},{2,3},{4,5},{5,6},{6,7},{8,9},{9,10},{10,11},{12,13},{... | collective-permute-start | bytes 49160 | tf_op jit(solution)/shard_map/ppermute | solution.py:408
  7.2 0.7 pad_convert_fusion
  8.5 0.6 reshape.20.taps_ref
  9.1 0.0 collective-permute-done.1.r_hbm
  9.1 0.0 copy-start.4
  9.1 0.0 collective-permute-done.l_hbm
  9.1 0.0 copy-start.5
  9.1 0.6 copy-done.4
  9.7 0.0 copy-done.5
  9.7 8.5 %filter_and_forward.1 = (bf16[64,2048]{1,0:T(8,128)(2,1)}, bf16[64,96,128]{2,1,0:T(8,128)(2,1)}) custom-call(s32[1,256]{1,0:T(1,128)} %bitcast.20, s32[1,256]{1,0:T(1,128)} %bitcast.22, s32[1,256]{1,0:T(1,128)} %bitcast.24, s32[1,1]{1,0:T(1,128)S(6)} %copy.11.count_hbm, s32[1,64]{1,0:T(1,128)} %bitcast.16, bf16[64,2048]{1,0:T(8,128)(2,1)} %bitcast.15, ...), custom_call_target="tpu_custom_call" | custom-call | flops 536870912 | bytes 8388608 | tf_op jit(solution)/shard_map/filter_and_forward/pallas_call | solution.py:142
  18.2 12.3 %all-to-all-start = ((bf16[64,96,128]{2,1,0:T(8,128)(2,1)}), bf16[64,96,128]{2,1,0:T(8,128)(2,1)}, u32[]{:S(2)}, u32[]{:S(2)}) async-start(bf16[64,96,128]{2,1,0:T(8,128)(2,1)} %get-tuple-element.9), calls=%async_computation | async-start | bytes 3145728 | tf_op jit(solution)/shard_map/all_to_all | solution.py:395
  30.5 40.0 %all-to-all-done.arrived_hbm = bf16[64,96,128]{2,1,0:T(8,128)(2,1)} async-done(((bf16[64,96,128]{2,1,0:T(8,128)(2,1)}), bf16[64,96,128]{2,1,0:T(8,128)(2,1)}, u32[]{:S(2)}, u32[]{:S(2)}) %all-to-all-start) | async-done | bytes 1572896 | tf_op jit(solution)/shard_map/all_to_all | solution.py:395
  70.4 5.1 %sum_and_stripe.1 = (f32[64,2048]{1,0:T(8,128)}, bf16[64,80,128]{2,1,0:T(8,128)(2,1)}) custom-call(s32[1,64]{1,0:T(1,128)} %bitcast.17, s32[1]{0:T(128)} %bitcast.7.q_ref, bf16[64,96,128]{2,1,0:T(8,128)(2,1)} %all-to-all-done.arrived_hbm, bf16[64,2048]{1,0:T(8,128)(2,1)} %get-tuple-element.8.phase_ref), custom_call_target="tpu_custom_call" | custom-call | flops 16777216 | bytes 8388608 | tf_op jit(solution)/shard_map/sum_and_stripe/pallas_call | solution.py:246
  75.6 5.6 %all-to-all-start.1 = ((bf16[64,80,128]{2,1,0:T(8,128)(2,1)}), bf16[64,80,128]{2,1,0:T(8,128)(2,1)}, u32[]{:S(2)}, u32[]{:S(2)}) async-start(bf16[64,80,128]{2,1,0:T(8,128)(2,1)} %get-tuple-element.10), calls=%async_computation.1 | async-start | bytes 2621440 | tf_op jit(solution)/shard_map/all_to_all | solution.py:395
  81.2 0.0 copy-start
  81.2 0.0 copy-start.1
  81.2 1.0 slice.14
  82.2 1.8 %convert_reduce_fusion.c_ref = s32[64]{0:T(128)} fusion(bf16[64,1,128]{2,1,0:T(2,128)(2,1)S(1)} %slice.14, s32[]{:T(128)S(6)} %select_n.3), kind=kLoop, calls=%fused_computation | loop fusion | flops 64 | bytes 388 | tf_op jit(solution)/shard_map/convert_element_type | solution.py:414
  84.1 31.5 %all-to-all-done.1.returned_hbm = bf16[64,80,128]{2,1,0:T(8,128)(2,1)} async-done(((bf16[64,80,128]{2,1,0:T(8,128)(2,1)}), bf16[64,80,128]{2,1,0:T(8,128)(2,1)}, u32[]{:S(2)}, u32[]{:S(2)}) %all-to-all-start.1) | async-done | bytes 1310752 | tf_op jit(solution)/shard_map/all_to_all | solution.py:395
  115.6 6.6 %adjoint_tiles.1 = (bf16[16,64,128]{2,1,0:T(8,128)(2,1)}, f32[16,64,128]{2,1,0:T(8,128)}) custom-call(s32[1,256]{1,0:T(1,128)} %bitcast.21, s32[1,256]{1,0:T(1,128)} %bitcast.23, s32[1,256]{1,0:T(1,128)} %bitcast.25, s32[1,1]{1,0:T(1,128)S(6)} %copy.11.count_hbm, s32[64]{0:T(128)} %convert_reduce_fusion.c_ref, ...), custom_call_target="tpu_custom_call" | custom-call | flops 536870912 | bytes 8388608 | tf_op jit(solution)/shard_map/adjoint_tiles/pallas_call | solution.py:322
  122.1 0.0 copy-start.3
  122.2 4.6 %all-to-all-start.2 = ((bf16[16,64,128]{2,1,0:T(8,128)(2,1)}), bf16[16,64,128]{2,1,0:T(8,128)(2,1)S(1)}, u32[]{:S(2)}, u32[]{:S(2)}) async-start(bf16[16,64,128]{2,1,0:T(8,128)(2,1)} %get-tuple-element.13), calls=%async_computation.2 | async-start | bytes 524288 | tf_op jit(solution)/shard_map/all_to_all | solution.py:395
  126.8 0.0 copy-done
  126.8 0.0 copy-done.1
  126.8 0.0 copy-start.2
  126.8 1.0 copy-done.2
  127.8 0.8 residual.1
  128.6 4.8 %all-to-all-done.2.parts_ref = bf16[16,64,128]{2,1,0:T(8,128)(2,1)S(1)} async-done(((bf16[16,64,128]{2,1,0:T(8,128)(2,1)}), bf16[16,64,128]{2,1,0:T(8,128)(2,1)S(1)}, u32[]{:S(2)}, u32[]{:S(2)}) %all-to-all-start.2) | async-done | bytes 262176 | tf_op jit(solution)/shard_map/all_to_all | solution.py:395
  133.4 0.0 copy-done.3
  133.4 0.7 image_step.1
Async XLA Ops:
  1.4 7.7 %collective-permute-start.1 = (bf16[64,128]{1,0:T(8,128)(2,1)S(1)}, bf16[64,128]{1,0:T(8,128)(2,1)S(1)}, u32[]{:S(2)}, u32[]{:S(2)}) collective-permute-start(bf16[64,128]{1,0:T(8,128)(2,1)S(1)} %get-tuple-element.14), channel_id=1, source_target_pairs={{1,0},{2,1},{3,2},{5,4},{6,5},{7,6},{9,8},{10,9},{11,10},{13,12},{... | collective-permute-start | bytes 49160 | tf_op jit(solution)/shard_map/ppermute | solution.py:409
  2.7 6.5 %collective-permute-start = (bf16[64,128]{1,0:T(8,128)(2,1)S(1)}, bf16[64,128]{1,0:T(8,128)(2,1)S(1)}, u32[]{:S(2)}, u32[]{:S(2)}) collective-permute-start(bf16[64,128]{1,0:T(8,128)(2,1)S(1)} %get-tuple-element.15), channel_id=1, source_target_pairs={{0,1},{1,2},{2,3},{4,5},{5,6},{6,7},{8,9},{9,10},{10,11},{12,13},{... | collective-permute-start | bytes 49160 | tf_op jit(solution)/shard_map/ppermute | solution.py:408
  9.1 0.6 copy-start.4
  9.1 0.6 copy-start.5
  18.2 52.3 %all-to-all-start = ((bf16[64,96,128]{2,1,0:T(8,128)(2,1)}), bf16[64,96,128]{2,1,0:T(8,128)(2,1)}, u32[]{:S(2)}, u32[]{:S(2)}) async-start(bf16[64,96,128]{2,1,0:T(8,128)(2,1)} %get-tuple-element.9), calls=%async_computation | async-start | bytes 3145728 | tf_op jit(solution)/shard_map/all_to_all | solution.py:395
  75.6 40.0 %all-to-all-start.1 = ((bf16[64,80,128]{2,1,0:T(8,128)(2,1)}), bf16[64,80,128]{2,1,0:T(8,128)(2,1)}, u32[]{:S(2)}, u32[]{:S(2)}) async-start(bf16[64,80,128]{2,1,0:T(8,128)(2,1)} %get-tuple-element.10), calls=%async_computation.1 | async-start | bytes 2621440 | tf_op jit(solution)/shard_map/all_to_all | solution.py:395
  81.2 45.6 %copy-start = (bf16[64,2048]{1,0:T(8,128)(2,1)S(1)}, bf16[64,2048]{1,0:T(8,128)(2,1)}, u32[]{:S(2)}) copy-start(bf16[64,2048]{1,0:T(8,128)(2,1)} %get-tuple-element.8.phase_ref) | copy-start | bytes 786436
  81.2 45.6 %copy-start.1 = (f32[64,2048]{1,0:T(8,128)S(1)}, f32[64,2048]{1,0:T(8,128)}, u32[]{:S(2)}) copy-start(f32[64,2048]{1,0:T(8,128)} %get-tuple-element.12.forward_ref) | copy-start | bytes 1572868
  122.1 11.3 %copy-start.3 = (bf16[2048,64]{0,1:T(8,128)(2,1)S(1)}, bf16[2048,64]{0,1:T(8,128)(2,1)}, u32[]{:S(2)}) copy-start(bf16[2048,64]{0,1:T(8,128)(2,1)} %param.11) | copy-start | bytes 786436
  122.2 11.3 %all-to-all-start.2 = ((bf16[16,64,128]{2,1,0:T(8,128)(2,1)}), bf16[16,64,128]{2,1,0:T(8,128)(2,1)S(1)}, u32[]{:S(2)}, u32[]{:S(2)}) async-start(bf16[16,64,128]{2,1,0:T(8,128)(2,1)} %get-tuple-element.13), calls=%async_computation.2 | async-start | bytes 524288 | tf_op jit(solution)/shard_map/all_to_all | solution.py:395
  126.8 1.0 copy-start.2

commit v4 on v3

--- a/solution.py
+++ b/solution.py
@@ -17,7 +17,7 @@
 HBM = pl.BlockSpec(memory_space=pltpu.HBM)
 
 
-def params(limit=63):
+def params(limit=32):
     return pltpu.CompilerParams(vmem_limit_bytes=limit * MIB)
 
 
@@ -54,23 +54,23 @@
     per = columns // T
     rows = slices + SECTION
     parts = 4
-    loads = per + blocks + 8
+    loads = per + blocks + 5
 
     def kernel(
-        entry_hbm, place_hbm, slot_hbm, count_hbm, n_hbm, x_hbm, l_hbm, r_hbm, taps_ref, image_hbm, library_hbm,
-        phase_ref, send_ref, entry_ref, place_ref, slot_ref, count_ref, n_ref, library_ref, wide, band, spread, row,
-        stacked, product, total, packed, sems, load_sems,
+        entry_hbm, place_hbm, slot_hbm, count_ref, n_hbm, x_hbm, l_ref, r_ref, taps_ref, image_hbm, library_hbm,
+        phase_ref, send_ref, entry_ref, place_ref, slot_ref, n_ref, library_ref, wide, band, spread, row,
+        stacked, product, total, packed, section, sems, load_sems,
     ):
         def block(n):
             return pl.ds(n * slices, slices)
 
         pairs = [(x_hbm.at[:, pl.ds(b * T, T)], wide.at[block(b + 2)]) for b in range(per)]
-        pairs += [(l_hbm, wide.at[block(1)]), (r_hbm, wide.at[block(per + 2)]), (n_hbm, n_ref)]
+        pairs += [(n_hbm, n_ref)]
         early = len(pairs)
         pairs += [(library_hbm, library_ref)]
         pairs += [(image_hbm.at[:, pl.ds(i * T, T)], stacked.at[block(i)]) for i in range(blocks)]
         late = len(pairs)
-        pairs += [(entry_hbm, entry_ref), (place_hbm, place_ref), (slot_hbm, slot_ref), (count_hbm, count_ref)]
+        pairs += [(entry_hbm, entry_ref), (place_hbm, place_ref), (slot_hbm, slot_ref)]
         fetches = [pltpu.make_async_copy(a, b, load_sems.at[n]) for n, (a, b) in enumerate(pairs)]
         for fetch in fetches:
             fetch.start()
@@ -78,6 +78,8 @@
         spread[...] = jnp.zeros_like(spread)
         row[...] = jnp.zeros_like(row)
         wide[block(0), :] = jnp.zeros((slices, T), BF16)
+        wide[block(1), :] = l_ref[...]
+        wide[block(per + 2), :] = r_ref[...]
         wide[block(per + 3), :] = jnp.zeros((slices, T), BF16)
         spun = pltpu.roll(jnp.broadcast_to(taps_ref[0:1, :], (T, 3 * T)), T // 2, 1, stride=1, stride_axis=0)
         band[...] = spun.astype(BF16)
@@ -104,7 +106,9 @@
         put(per + 1, filtered[(per + 1) * slices :])
         row[0:1, :owners] = n_ref[...].astype(F32)
         put(per + 2, jnp.broadcast_to(row[0:1, :], (slices, T)))
-        packed[:, slices:, :] = spread[...].astype(BF16).reshape(slices, SECTION, T)
+        section[...] = spread[...].astype(BF16).reshape(slices, SECTION, T)
+        copies = [pltpu.make_async_copy(section, send_ref.at[:, pl.ds(slices, SECTION), :], sems.at[parts])]
+        copies[0].start()
 
         total[...] = jnp.zeros_like(total)
         for fetch in fetches[early:late]:
@@ -130,11 +134,12 @@
 
         lax.fori_loop(0, (count_ref[0, 0] + 7) // 8, group, 0)
         step = owners // parts
-        copies = []
         for n in range(parts):
-            packed[n * step : (n + 1) * step, :slices, :] = total[n * step : (n + 1) * step].astype(BF16)
+            packed[n * step : (n + 1) * step] = total[n * step : (n + 1) * step].astype(BF16)
             here = pl.ds(n * step, step)
-            copies.append(pltpu.make_async_copy(packed.at[here], send_ref.at[here], sems.at[n]))
+            copies.append(
+                pltpu.make_async_copy(packed.at[here], send_ref.at[here, pl.ds(0, slices), :], sems.at[n])
+            )
             copies[-1].start()
         for copy in copies:
             copy.wait()
@@ -143,15 +148,14 @@
         kernel,
         out_shape=[
             jax.ShapeDtypeStruct((slices, columns), BF16),
-            jax.ShapeDtypeStruct((owners, rows, T), BF16),
-        ],
-        in_specs=[HBM] * 8 + [VMEM] + [HBM] * 2,
+            pltpu.HBM((owners, rows, T), BF16),
+        ],
+        in_specs=[HBM] * 3 + [SMEM] + [HBM] * 2 + [VMEM] * 3 + [HBM] * 2,
         out_specs=[VMEM, HBM],
         scratch_shapes=[
             pltpu.SMEM(entry.shape, jnp.int32),
             pltpu.SMEM(place.shape, jnp.int32),
             pltpu.SMEM(slot.shape, jnp.int32),
-            pltpu.SMEM(count.shape, jnp.int32),
             pltpu.VMEM(numbers.shape, jnp.int32),
             pltpu.VMEM(library.shape, BF16),
             pltpu.VMEM(((per + 4) * slices, T), BF16),
@@ -161,8 +165,9 @@
             pltpu.VMEM((blocks * slices, T), BF16),
             pltpu.VMEM((blocks * slices, entries * T), F32),
             pltpu.VMEM((owners + 1, slices, T), F32),
-            pltpu.VMEM((owners, rows, T), BF16),
-            pltpu.SemaphoreType.DMA((parts,)),
+            pltpu.VMEM((owners, slices, T), BF16),
+            pltpu.VMEM((slices, SECTION, T), BF16),
+            pltpu.SemaphoreType.DMA((parts + 1,)),
             pltpu.SemaphoreType.DMA((loads,)),
         ],
         compiler_params=params(),
@@ -170,12 +175,13 @@
             flops=2 * capacity * slices * T * T, bytes_accessed=8 * 2**20, transcendentals=0
         ),
         name="filter_and_forward",
-    )(entry, place, slot, count, numbers, projections, left, right, taps, image, library)
-
-
-def stripe_of(quarter, quarters, section, values, rimmed):
-    angles = section.shape[0]
-    values[...] = section[...].astype(F32)
+    )(*map(in_hbm, (entry, place, slot)), count, *map(in_hbm, (numbers, projections)), left, right, taps,
+      *map(in_hbm, (image, library)))
+
+
+def stripe_of(quarter, quarters, arrived_ref, offset, values, rimmed):
+    angles = arrived_ref.shape[0]
+    values[...] = arrived_ref[:, offset:, :].astype(F32)
     network = middle_network(angles)
 
     def middle(g, carry):
@@ -213,26 +219,16 @@
     parts = 4
 
     def kernel(
-        c_ref, q_ref, arrived_hbm, phase_ref, forward_ref, send_ref, values, rimmed, less, packed, section, partial,
-        sems, load_sems,
+        c_ref, q_ref, arrived_ref, phase_ref, forward_hbm, send_ref, values, rimmed, forward, less, packed, sems
     ):
+        forward[...] = jnp.zeros_like(forward)
+        for d in range(owners):
+            forward[:, lanes(c_ref[0, d])] += arrived_ref[d, :size, :].astype(F32)
+        copies = [pltpu.make_async_copy(forward, forward_hbm, sems.at[parts])]
+        copies[0].start()
+        stripe = stripe_of(q_ref[0], quarters, arrived_ref, size, values, rimmed).astype(BF16)
+        less[...] = (phase_ref[...].astype(F32) - forward[...]).astype(BF16)
         step = owners // parts
-        pairs = [(arrived_hbm.at[:, pl.ds(size, SECTION), :], section)]
-        for n in range(parts):
-            here = pl.ds(n * step, step)
-            pairs.append((arrived_hbm.at[here, pl.ds(0, size), :], partial.at[here]))
-        fetches = [pltpu.make_async_copy(a, b, load_sems.at[n]) for n, (a, b) in enumerate(pairs)]
-        for fetch in fetches:
-            fetch.start()
-        forward_ref[...] = jnp.zeros_like(forward_ref)
-        fetches[0].wait()
-        stripe = stripe_of(q_ref[0], quarters, section, values, rimmed).astype(BF16)
-        for n in range(parts):
-            fetches[n + 1].wait()
-            for d in range(n * step, (n + 1) * step):
-                forward_ref[:, lanes(c_ref[0, d])] += partial[d].astype(F32)
-        less[...] = (phase_ref[...].astype(F32) - forward_ref[...]).astype(BF16)
-        copies = []
         for n in range(parts):
             for d in range(n * step, (n + 1) * step):
                 packed[d, :size, :] = less[:, lanes(c_ref[0, d])]
@@ -246,19 +242,17 @@
     return pl.pallas_call(
         kernel,
         out_shape=[
-            jax.ShapeDtypeStruct((size, columns), F32),
-            jax.ShapeDtypeStruct((owners, rows, T), BF16),
-        ],
-        in_specs=[SMEM, SMEM, HBM, VMEM],
-        out_specs=[VMEM, HBM],
+            pltpu.HBM((size, columns), F32),
+            pltpu.HBM((owners, rows, T), BF16),
+        ],
+        in_specs=[SMEM, SMEM, VMEM, VMEM],
+        out_specs=[HBM, HBM],
         scratch_shapes=[
             pltpu.VMEM((owners, SECTION, T), F32),
             pltpu.VMEM((32, T), F32),
+            pltpu.VMEM((size, columns), F32),
             pltpu.VMEM((size, columns), BF16),
             pltpu.VMEM((owners, rows, T), BF16),
-            pltpu.VMEM((owners, SECTION, T), BF16),
-            pltpu.VMEM((owners, size, T), BF16),
-            pltpu.SemaphoreType.DMA((parts,)),
             pltpu.SemaphoreType.DMA((parts + 1,)),
         ],
         compiler_params=params(),
@@ -274,24 +268,22 @@
     size = returned.shape[1] - per
 
     def kernel(
-        entry_hbm, place_hbm, slot_hbm, count_hbm, c_ref, returned_hbm, library_hbm,
-        update_ref, stripe_ref, entry_ref, place_ref, slot_ref, count_ref, returned_ref, library_ref, stripes, terms,
-        bins, loads,
+        entry_hbm, place_hbm, slot_hbm, count_ref, c_ref, returned_ref, library_hbm,
+        update_hbm, stripe_ref, entry_ref, place_ref, slot_ref, library_ref, stripes, terms, bins, update, loads,
+        sems,
     ):
-        pairs = [(returned_hbm, returned_ref), (entry_hbm, entry_ref), (place_hbm, place_ref), (slot_hbm, slot_ref)]
-        pairs += [(count_hbm, count_ref), (library_hbm, library_ref)]
+        pairs = [(entry_hbm, entry_ref), (place_hbm, place_ref), (slot_hbm, slot_ref), (library_hbm, library_ref)]
         fetches = [pltpu.make_async_copy(a, b, loads.at[n]) for n, (a, b) in enumerate(pairs)]
         for fetch in fetches:
             fetch.start()
         bins[...] = jnp.zeros_like(bins)
-        fetches[0].wait()
         stripes[...] = returned_ref[:, size:, :].astype(F32).reshape(owners * per, T)
         for b in range(per):
             stripe_ref[b] = stripes[pl.ds(b, size, stride=per), :]
         for e in range(owners):
             terms[e] = returned_ref[e, :size, :].astype(F32) - stripe_ref[c_ref[e]]
         terms[owners] = jnp.zeros((size, T), F32)
-        for fetch in fetches[1:]:
+        for fetch in fetches:
             fetch.wait()
 
         def add(k):
@@ -308,8 +300,10 @@
 
         lax.fori_loop(0, (count_ref[0, 0] + 7) // 8, group, 0)
         half = blocks // 2
+        copies = []
         for h in range(2):
-            update_ref[h * half : (h + 1) * half] = (
+            here = pl.ds(h * half, half)
+            update[here] = (
                 jnp.dot(
                     bins[h * half * size : (h + 1) * half * size, :].astype(BF16),
                     library_ref[...].reshape(entries * T, T),
@@ -318,33 +312,37 @@
                 .astype(BF16)
                 .reshape(half, size, T)
             )
+            copies.append(pltpu.make_async_copy(update.at[here], update_hbm.at[here], sems.at[h]))
+            copies[-1].start()
+        for copy in copies:
+            copy.wait()
 
     return pl.pallas_call(
         kernel,
         out_shape=[
-            jax.ShapeDtypeStruct((blocks, size, T), BF16),
+            pltpu.HBM((blocks, size, T), BF16),
             jax.ShapeDtypeStruct((per, size, T), F32),
         ],
-        in_specs=[HBM] * 4 + [SMEM, HBM, HBM],
-        out_specs=[VMEM, VMEM],
+        in_specs=[HBM] * 3 + [SMEM, SMEM, VMEM, HBM],
+        out_specs=[HBM, VMEM],
         scratch_shapes=[
             pltpu.SMEM(entry.shape, jnp.int32),
             pltpu.SMEM(place.shape, jnp.int32),
             pltpu.SMEM(slot.shape, jnp.int32),
-            pltpu.SMEM(count.shape, jnp.int32),
-            pltpu.VMEM(returned.shape, BF16),
             pltpu.VMEM(library.shape, BF16),
             pltpu.VMEM((owners * per, T), F32),
             pltpu.VMEM((owners + 1, size, T), F32),
             pltpu.VMEM((blocks * size, entries * T), F32),
-            pltpu.SemaphoreType.DMA((6,)),
+            pltpu.VMEM((blocks, size, T), BF16),
+            pltpu.SemaphoreType.DMA((4,)),
+            pltpu.SemaphoreType.DMA((2,)),
         ],
         compiler_params=params(),
         cost_estimate=pl.CostEstimate(
             flops=2 * 256 * size * T * T, bytes_accessed=8 * 2**20, transcendentals=0
         ),
         name="adjoint_tiles",
-    )(entry, place, slot, count, theirs, returned, library)
+    )(*map(in_hbm, (entry, place, slot)), count, theirs, returned, in_hbm(library))
 
 
 def residual_call(phase, stripe, forward):
@@ -361,7 +359,7 @@
         out_shape=jax.ShapeDtypeStruct(phase.shape, BF16),
         in_specs=[VMEM] * 3,
         out_specs=VMEM,
-        compiler_params=params(12),
+        compiler_params=params(),
         cost_estimate=pl.CostEstimate(flops=2**19, bytes_accessed=2**21, transcendentals=0),
         name="residual",
     )(phase, stripe, forward)
@@ -385,10 +383,14 @@
         out_shape=jax.ShapeDtypeStruct((slices, held), F32),
         in_specs=[SMEM, VMEM, VMEM],
         out_specs=VMEM,
-        compiler_params=params(12),
+        compiler_params=params(),
         cost_estimate=pl.CostEstimate(flops=2**18, bytes_accessed=2**20, transcendentals=0),
         name="image_step",
     )(quarter, image, parts)
+
+
+def in_hbm(array):
+    return pltpu.with_memory_space_constraint(array, pltpu.HBM)
 
 
 def exchanged(array, axis):
@@ -407,7 +409,7 @@
 
     left = lax.ppermute(projections[:, -T:], "ray", [(i, i + 1) for i in range(quarters - 1)])
     right = lax.ppermute(projections[:, :T], "ray", [(i + 1, i) for i in range(quarters - 1)])
-    taps = jnp.pad(phase_kernel.astype(F32), (0, 3 * T - phase_kernel.shape[0])).reshape(1, 3 * T)
+    taps = jnp.pad(phase_kernel[None].astype(F32), ((0, 0), (0, 3 * T - phase_kernel.shape[0])))
     phase, send = first_call(*tiles, carried, projections, left, right, taps, image, library)
     arrived = exchanged(send, "dom")
     numbers = lax.dynamic_slice_in_dim(arrived[:, slices + 18, :], lax.axis_index("dom"), 1, axis=1)

time: 134 us -> 128 us (0.955)
  Pallas kernels: 21.7 us -> 14.9 us
  waiting for transfers between devices: 76.3 us -> 79 us
  local copies, waits for them, and re-layouts: 3.99 us -> 1.46 us
    pallas_call x2, Pallas kernels: 11.7 us -> 7.41 us  [the longest x1 4.63 us: adjoint_call(): pl.pallas_call(kernel, out_shape=[pltpu.HBM((blocks, size, T), BF16), jax...]
    all_to_all x3, waiting for transfers between devices: 76.3 us -> 78.9 us  [exchanged(): return lax.all_to_all(array, axis, split_axis=0, concat_axis=0, tiled=True)]
    pallas_call x1, Pallas kernels: 8.46 us -> 6.02 us  [first_call(): pl.pallas_call(kernel, out_shape=[jax.ShapeDtypeStruct((slices, columns),...]
    unnamed x12 -> x6, local copies, waits for them, and re-layouts: 1.66 us -> 0.02 us
  transfers between devices with their start and end apart: 5 -> 5, of which waited for: 3 -> 4; matrix products, arithmetic and copies ran while one was open for 3% -> 2% of each run, Pallas kernels for 1% -> 1%
where the time goes in v4:
time: 128 us; the launch traced here: 127 us
  waiting for transfers between devices  79 us (62%)
  starting transfers between devices  29.1 us (23%)
  Pallas kernels  14.9 us (12%)
  local copies, waits for them, and re-layouts  1.46 us (1%)
  between operations  1.39 us (1%)
  other arithmetic  1.32 us (1%)
    all_to_all x3, waiting for transfers between devices, exchanged(): return lax.all_to_all(array, axis, split_axis=0, concat_axis=0, tiled=True)  78.9 us
    all_to_all x3, starting transfers between devices, exchanged(): return lax.all_to_all(array, axis, split_axis=0, concat_axis=0, tiled=True)  23.3 us
    pallas_call x1, Pallas kernels, first_call(): pl.pallas_call(kernel, out_shape=[jax.ShapeDtypeStruct((slices, columns),...  6.02 us
    pallas_call x1, Pallas kernels, adjoint_call(): pl.pallas_call(kernel, out_shape=[pltpu.HBM((blocks, size, T), BF16), jax...  4.63 us
    ppermute x1, starting transfers between devices, shards(): lax.ppermute(projections[:, -T:], 'ray', [(i, i + 1) for i in range(quart...  4.55 us
    pallas_call x1, Pallas kernels, back_call(): pl.pallas_call(kernel, out_shape=[pltpu.HBM((size, columns), F32), pltpu....  2.78 us
  transfers between devices with their start and end apart: 5, of which 4 were waited for; matrix products, arithmetic and copies ran while one was open for 2% of the time, Pallas kernels for 1%

profile of v4, /device:TPU:8, one launch (start us, length us, event | category | flops | bytes accessed | tf_op | source)
XLA Modules:
  0.0 127.2 jit_solution(6174733624312090365)
XLA Ops:
  0.6 0.7 fusion
  1.4 1.3 %collective-permute-start.1 = (bf16[64,128]{1,0:T(8,128)(2,1)S(1)}, bf16[64,128]{1,0:T(8,128)(2,1)S(1)}, u32[]{:S(2)}, u32[]{:S(2)}) collective-permute-start(bf16[64,128]{1,0:T(8,128)(2,1)S(1)} %get-tuple-element.14), channel_id=1, source_target_pairs={{1,0},{2,1},{3,2},{5,4},{6,5},{7,6},{9,8},{10,9},{11,10},{13,12},{... | collective-permute-start | bytes 49160 | tf_op jit(solution)/shard_map/ppermute | solution.py:411
  2.7 4.5 %collective-permute-start = (bf16[64,128]{1,0:T(8,128)(2,1)S(1)}, bf16[64,128]{1,0:T(8,128)(2,1)S(1)}, u32[]{:S(2)}, u32[]{:S(2)}) collective-permute-start(bf16[64,128]{1,0:T(8,128)(2,1)S(1)} %get-tuple-element.15), channel_id=1, source_target_pairs={{0,1},{1,2},{2,3},{4,5},{5,6},{6,7},{8,9},{9,10},{10,11},{12,13},{... | collective-permute-start | bytes 49160 | tf_op jit(solution)/shard_map/ppermute | solution.py:410
  7.2 0.7 convert_element_type.11
  8.5 0.0 collective-permute-done.1.r_ref
  8.5 0.1 collective-permute-done.l_ref
  8.6 6.0 %filter_and_forward.1 = (bf16[64,2048]{1,0:T(8,128)(2,1)S(1)}, bf16[64,96,128]{2,1,0:T(8,128)(2,1)}) custom-call(s32[1,256]{1,0:T(1,128)} %bitcast.20, s32[1,256]{1,0:T(1,128)} %bitcast.22, s32[1,256]{1,0:T(1,128)} %bitcast.24, s32[1,1]{1,0:T(1,128)S(6)} %copy.11.count_ref, s32[1,64]{1,0:T(1,128)} %bitcast.12, bf16[64,2048]{1,0:T(8,128)(2,1)} %bitcast.17, ...), custom_call_target="tpu_custom_call" | custom-call | flops 536870912 | bytes 8388608 | tf_op jit(solution)/shard_map/filter_and_forward/pallas_call | solution.py:147
  14.7 0.0 copy-start.2
  14.7 12.1 %all-to-all-start = ((bf16[64,96,128]{2,1,0:T(8,128)(2,1)}), bf16[64,96,128]{2,1,0:T(8,128)(2,1)S(1)}, u32[]{:S(2)}, u32[]{:S(2)}) async-start(bf16[64,96,128]{2,1,0:T(8,128)(2,1)} %get-tuple-element.9), calls=%async_computation | async-start | bytes 3145728 | tf_op jit(solution)/shard_map/all_to_all | solution.py:397
  26.8 40.0 %all-to-all-done.arrived_ref = bf16[64,96,128]{2,1,0:T(8,128)(2,1)S(1)} async-done(((bf16[64,96,128]{2,1,0:T(8,128)(2,1)}), bf16[64,96,128]{2,1,0:T(8,128)(2,1)S(1)}, u32[]{:S(2)}, u32[]{:S(2)}) %all-to-all-start) | async-done | bytes 1572896 | tf_op jit(solution)/shard_map/all_to_all | solution.py:397
  66.8 0.0 copy-done.2
  66.8 2.8 %sum_and_stripe.1 = (f32[64,2048]{1,0:T(8,128)}, bf16[64,80,128]{2,1,0:T(8,128)(2,1)}) custom-call(s32[1,64]{1,0:T(1,128)S(1)} %bitcast.13, s32[1]{0:T(128)} %bitcast.7.q_ref, bf16[64,96,128]{2,1,0:T(8,128)(2,1)S(1)} %all-to-all-done.arrived_ref, bf16[64,2048]{1,0:T(8,128)(2,1)S(1)} %get-tuple-element.8.phase_ref), custom_call_target="tpu_custom_call" | custom-call | flops 16777216 | bytes 8388608 | tf_op jit(solution)/shard_map/sum_and_stripe/pallas_call | solution.py:242
  69.6 5.4 %all-to-all-start.1 = ((bf16[64,80,128]{2,1,0:T(8,128)(2,1)}), bf16[64,80,128]{2,1,0:T(8,128)(2,1)S(1)}, u32[]{:S(2)}, u32[]{:S(2)}) async-start(bf16[64,80,128]{2,1,0:T(8,128)(2,1)} %get-tuple-element.10), calls=%async_computation.1 | async-start | bytes 2621440 | tf_op jit(solution)/shard_map/all_to_all | solution.py:397
  75.1 0.0 copy-start
  75.1 1.3 %convert_reduce_fusion.c_ref = s32[64]{0:T(128)S(1)} fusion(bf16[64,1,128]{2,1,0:T(2,128)(2,1)S(1)} %slice.14, s32[]{:T(128)S(6)} %select_n.3), kind=kLoop, calls=%fused_computation | loop fusion | flops 64 | bytes 388 | tf_op jit(solution)/shard_map/convert_element_type | solution.py:416
  76.4 0.0 copy-start.1
  76.5 33.0 %all-to-all-done.1.returned_ref = bf16[64,80,128]{2,1,0:T(8,128)(2,1)S(1)} async-done(((bf16[64,80,128]{2,1,0:T(8,128)(2,1)}), bf16[64,80,128]{2,1,0:T(8,128)(2,1)S(1)}, u32[]{:S(2)}, u32[]{:S(2)}) %all-to-all-start.1) | async-done | bytes 1310752 | tf_op jit(solution)/shard_map/all_to_all | solution.py:397
  109.5 4.6 %adjoint_tiles.1 = (bf16[16,64,128]{2,1,0:T(8,128)(2,1)}, f32[16,64,128]{2,1,0:T(8,128)S(1)}) custom-call(s32[1,256]{1,0:T(1,128)} %bitcast.21, s32[1,256]{1,0:T(1,128)} %bitcast.23, s32[1,256]{1,0:T(1,128)} %bitcast.25, s32[1,1]{1,0:T(1,128)S(6)} %copy.11.count_ref, s32[64]{0:T(128)S(1)} %convert_reduce_fusion.c_ref, ...), custom_call_target="tpu_custom_call" | custom-call | flops 536870912 | bytes 8388608 | tf_op jit(solution)/shard_map/adjoint_tiles/pallas_call | solution.py:320
  114.1 5.7 %all-to-all-start.2 = ((bf16[16,64,128]{2,1,0:T(8,128)(2,1)}), bf16[16,64,128]{2,1,0:T(8,128)(2,1)S(1)}, u32[]{:S(2)}, u32[]{:S(2)}) async-start(bf16[16,64,128]{2,1,0:T(8,128)(2,1)} %get-tuple-element.13), calls=%async_computation.2 | async-start | bytes 524288 | tf_op jit(solution)/shard_map/all_to_all | solution.py:397
  119.8 0.0 copy-done
  119.8 0.8 residual.1
  120.6 5.9 %all-to-all-done.2.parts_ref = bf16[16,64,128]{2,1,0:T(8,128)(2,1)S(1)} async-done(((bf16[16,64,128]{2,1,0:T(8,128)(2,1)}), bf16[16,64,128]{2,1,0:T(8,128)(2,1)S(1)}, u32[]{:S(2)}, u32[]{:S(2)}) %all-to-all-start.2) | async-done | bytes 262176 | tf_op jit(solution)/shard_map/all_to_all | solution.py:397
  126.5 0.0 copy-done.1
  126.5 0.7 image_step.1
  (2 shorter events, 0.0 us)
Async XLA Ops:
  1.4 7.2 %collective-permute-start.1 = (bf16[64,128]{1,0:T(8,128)(2,1)S(1)}, bf16[64,128]{1,0:T(8,128)(2,1)S(1)}, u32[]{:S(2)}, u32[]{:S(2)}) collective-permute-start(bf16[64,128]{1,0:T(8,128)(2,1)S(1)} %get-tuple-element.14), channel_id=1, source_target_pairs={{1,0},{2,1},{3,2},{5,4},{6,5},{7,6},{9,8},{10,9},{11,10},{13,12},{... | collective-permute-start | bytes 49160 | tf_op jit(solution)/shard_map/ppermute | solution.py:411
  2.7 6.0 %collective-permute-start = (bf16[64,128]{1,0:T(8,128)(2,1)S(1)}, bf16[64,128]{1,0:T(8,128)(2,1)S(1)}, u32[]{:S(2)}, u32[]{:S(2)}) collective-permute-start(bf16[64,128]{1,0:T(8,128)(2,1)S(1)} %get-tuple-element.15), channel_id=1, source_target_pairs={{0,1},{1,2},{2,3},{4,5},{5,6},{6,7},{8,9},{9,10},{10,11},{12,13},{... | collective-permute-start | bytes 49160 | tf_op jit(solution)/shard_map/ppermute | solution.py:410
  14.7 52.2 %copy-start.2 = (s32[1,1,64]{2,1,0:T(1,128)S(1)}, s32[1,1,64]{2,1,0:T(1,128)}, u32[]{:S(2)}) copy-start(s32[1,1,64]{2,1,0:T(1,128)} %param.17) | copy-start | bytes 772
  14.7 52.2 %all-to-all-start = ((bf16[64,96,128]{2,1,0:T(8,128)(2,1)}), bf16[64,96,128]{2,1,0:T(8,128)(2,1)S(1)}, u32[]{:S(2)}, u32[]{:S(2)}) async-start(bf16[64,96,128]{2,1,0:T(8,128)(2,1)} %get-tuple-element.9), calls=%async_computation | async-start | bytes 3145728 | tf_op jit(solution)/shard_map/all_to_all | solution.py:397
  69.6 39.9 %all-to-all-start.1 = ((bf16[64,80,128]{2,1,0:T(8,128)(2,1)}), bf16[64,80,128]{2,1,0:T(8,128)(2,1)S(1)}, u32[]{:S(2)}, u32[]{:S(2)}) async-start(bf16[64,80,128]{2,1,0:T(8,128)(2,1)} %get-tuple-element.10), calls=%async_computation.1 | async-start | bytes 2621440 | tf_op jit(solution)/shard_map/all_to_all | solution.py:397
  75.1 44.7 %copy-start = (f32[64,2048]{1,0:T(8,128)S(1)}, f32[64,2048]{1,0:T(8,128)}, u32[]{:S(2)}) copy-start(f32[64,2048]{1,0:T(8,128)} %get-tuple-element.12.forward_ref) | copy-start | bytes 1572868
  76.4 50.1 %copy-start.1 = (bf16[2048,64]{0,1:T(8,128)(2,1)S(1)}, bf16[2048,64]{0,1:T(8,128)(2,1)}, u32[]{:S(2)}) copy-start(bf16[2048,64]{0,1:T(8,128)(2,1)} %param.11) | copy-start | bytes 786436
  114.1 12.4 %all-to-all-start.2 = ((bf16[16,64,128]{2,1,0:T(8,128)(2,1)}), bf16[16,64,128]{2,1,0:T(8,128)(2,1)S(1)}, u32[]{:S(2)}, u32[]{:S(2)}) async-start(bf16[16,64,128]{2,1,0:T(8,128)(2,1)} %get-tuple-element.13), calls=%async_computation.2 | async-start | bytes 524288 | tf_op jit(solution)/shard_map/all_to_all | solution.py:397

commit v5 on v4

--- a/solution.py
+++ b/solution.py
@@ -58,7 +58,7 @@
 
     def kernel(
         entry_hbm, place_hbm, slot_hbm, count_ref, n_hbm, x_hbm, l_ref, r_ref, taps_ref, image_hbm, library_hbm,
-        phase_ref, send_ref, entry_ref, place_ref, slot_ref, n_ref, library_ref, wide, band, spread, row,
+        phase_ref, send_ref, entry_ref, place_ref, slot_ref, n_ref, library_ref, wide, band, spread, row, line,
         stacked, product, total, packed, section, sems, load_sems,
     ):
         def block(n):
@@ -81,7 +81,9 @@
         wide[block(1), :] = l_ref[...]
         wide[block(per + 2), :] = r_ref[...]
         wide[block(per + 3), :] = jnp.zeros((slices, T), BF16)
-        spun = pltpu.roll(jnp.broadcast_to(taps_ref[0:1, :], (T, 3 * T)), T // 2, 1, stride=1, stride_axis=0)
+        line[...] = jnp.zeros_like(line)
+        line[0:1, : taps_ref.shape[1]] = taps_ref[...].astype(F32)
+        spun = pltpu.roll(jnp.broadcast_to(line[0:1, :], (T, 3 * T)), T // 2, 1, stride=1, stride_axis=0)
         band[...] = spun.astype(BF16)
         for fetch in fetches[:early]:
             fetch.wait()
@@ -162,6 +164,7 @@
             pltpu.VMEM((T, 3 * T), BF16),
             pltpu.VMEM((slices * SECTION, T), F32),
             pltpu.VMEM((8, T), F32),
+            pltpu.VMEM((8, 3 * T), F32),
             pltpu.VMEM((blocks * slices, T), BF16),
             pltpu.VMEM((blocks * slices, entries * T), F32),
             pltpu.VMEM((owners + 1, slices, T), F32),
@@ -261,59 +264,102 @@
     )(carried, quarter, arrived, phase)
 
 
-def adjoint_call(entry, place, slot, count, theirs, returned, library, blocks):
+def counts_call(entry, place, slot, count, owner, arrived, entries, blocks):
+    capacity = entry.shape[1]
+    owners = arrived.shape[0]
+    size = arrived.shape[1] - SECTION
+
+    def kernel(
+        entry_hbm, place_hbm, slot_hbm, count_ref, owner_ref, arrived_ref,
+        weights_ref, entry_ref, place_ref, slot_ref, loads,
+    ):
+        pairs = [(entry_hbm, entry_ref), (place_hbm, place_ref), (slot_hbm, slot_ref)]
+        fetches = [pltpu.make_async_copy(a, b, loads.at[n]) for n, (a, b) in enumerate(pairs)]
+        for fetch in fetches:
+            fetch.start()
+        lane = lax.broadcasted_iota(jnp.int32, (owners, T), 1)
+        numbers = arrived_ref[:, size + 16 :, :].astype(F32)[:, 2, :]
+        theirs = jnp.sum(jnp.where(lane == owner_ref[0], numbers, 0.0), axis=1, keepdims=True)
+        carries = (theirs.astype(jnp.int32) + owners == lane).astype(F32).astype(BF16)
+
+        def ones(rows, match):
+            return (lax.broadcasted_iota(jnp.int32, (rows, match.shape[1]), 0) == match).astype(F32).astype(BF16)
+
+        for fetch in fetches:
+            fetch.wait()
+        live = lax.broadcasted_iota(jnp.int32, (1, capacity), 1) < count_ref[0, 0]
+        of_bin = ones(entries * blocks, jnp.where(live, entry_ref[...] * blocks + place_ref[...], -1))
+        of_slot = ones(T, slot_ref[...])
+        met = lax.dot_general(of_bin, of_slot, NT, preferred_element_type=F32)
+        stripe_met = jnp.dot(met[:, :owners].astype(BF16), carries, preferred_element_type=F32)
+        weights_ref[...] = (met - stripe_met).astype(BF16)
+
+    return pl.pallas_call(
+        kernel,
+        out_shape=jax.ShapeDtypeStruct((entries * blocks, T), BF16),
+        in_specs=[HBM] * 3 + [SMEM, SMEM, VMEM],
+        out_specs=VMEM,
+        scratch_shapes=[
+            pltpu.VMEM(entry.shape, jnp.int32),
+            pltpu.VMEM(place.shape, jnp.int32),
+            pltpu.VMEM(slot.shape, jnp.int32),
+            pltpu.SemaphoreType.DMA((3,)),
+        ],
+        compiler_params=params(),
+        cost_estimate=pl.CostEstimate(flops=2**24, bytes_accessed=2**20, transcendentals=0),
+        name="tile_counts",
+    )(*map(in_hbm, (entry, place, slot)), count, owner, arrived)
+
+
+def adjoint_call(weights, returned, library, blocks):
     entries = library.shape[0]
     owners = returned.shape[0]
     per = 16
     size = returned.shape[1] - per
+    parts = 4
 
     def kernel(
-        entry_hbm, place_hbm, slot_hbm, count_ref, c_ref, returned_ref, library_hbm,
-        update_hbm, stripe_ref, entry_ref, place_ref, slot_ref, library_ref, stripes, terms, bins, update, loads,
-        sems,
+        weights_ref, returned_ref, library_hbm, update_hbm, stripe_ref, library_ref, stripes, terms, bins, whole,
+        update, load, sems,
     ):
-        pairs = [(entry_hbm, entry_ref), (place_hbm, place_ref), (slot_hbm, slot_ref), (library_hbm, library_ref)]
-        fetches = [pltpu.make_async_copy(a, b, loads.at[n]) for n, (a, b) in enumerate(pairs)]
-        for fetch in fetches:
-            fetch.start()
-        bins[...] = jnp.zeros_like(bins)
+        fetch = pltpu.make_async_copy(library_hbm, library_ref, load)
+        fetch.start()
         stripes[...] = returned_ref[:, size:, :].astype(F32).reshape(owners * per, T)
+        terms[...] = returned_ref[:, :size, :].astype(F32).reshape(owners * size, T)
+        weights = weights_ref[:, : owners + per]
+
+        def both(n):
+            here = terms[pl.ds(n, owners, stride=size), :].astype(BF16)
+            return jnp.concatenate([here, returned_ref[n, size:, :]], axis=0)
+
+        for n in range(0, size, 2):
+            made = jnp.dot(
+                weights, jnp.concatenate([both(n), both(n + 1)], axis=1), preferred_element_type=F32
+            ).astype(BF16)
+            for u in range(2):
+                for e in range(entries):
+                    bins[(n + u) * blocks : (n + u + 1) * blocks, e * T : (e + 1) * T] = made[
+                        e * blocks : (e + 1) * blocks, u * T : (u + 1) * T
+                    ]
+        fetch.wait()
+        held = size // parts
+        copies = []
+        for h in range(parts):
+            rows = slice(h * held * blocks, (h + 1) * held * blocks)
+            whole[rows, :] = jnp.dot(
+                bins[rows, :], library_ref[...].reshape(entries * T, T), preferred_element_type=F32
+            )
+            for i in range(blocks):
+                update[i, h * held : (h + 1) * held, :] = whole[
+                    pl.ds(h * held * blocks + i, held, stride=blocks), :
+                ].astype(BF16)
+            here = pl.ds(h * held, held)
+            copies.append(
+                pltpu.make_async_copy(update.at[:, here, :], update_hbm.at[:, here, :], sems.at[h])
+            )
+            copies[-1].start()
         for b in range(per):
             stripe_ref[b] = stripes[pl.ds(b, size, stride=per), :]
-        for e in range(owners):
-            terms[e] = returned_ref[e, :size, :].astype(F32) - stripe_ref[c_ref[e]]
-        terms[owners] = jnp.zeros((size, T), F32)
-        for fetch in fetches:
-            fetch.wait()
-
-        def add(k):
-            live = k < count_ref[0, 0]
-            e = jnp.where(live, entry_ref[0, k], 0)
-            i = jnp.where(live, place_ref[0, k], 0)
-            s = jnp.where(live, slot_ref[0, k], owners)
-            bins[pl.ds(pl.multiple_of(i * size, size), size), lanes(e)] += terms[s]
-
-        def group(g, carry):
-            for u in range(8):
-                add(g * 8 + u)
-            return carry
-
-        lax.fori_loop(0, (count_ref[0, 0] + 7) // 8, group, 0)
-        half = blocks // 2
-        copies = []
-        for h in range(2):
-            here = pl.ds(h * half, half)
-            update[here] = (
-                jnp.dot(
-                    bins[h * half * size : (h + 1) * half * size, :].astype(BF16),
-                    library_ref[...].reshape(entries * T, T),
-                    preferred_element_type=F32,
-                )
-                .astype(BF16)
-                .reshape(half, size, T)
-            )
-            copies.append(pltpu.make_async_copy(update.at[here], update_hbm.at[here], sems.at[h]))
-            copies[-1].start()
         for copy in copies:
             copy.wait()
 
@@ -323,26 +369,24 @@
             pltpu.HBM((blocks, size, T), BF16),
             jax.ShapeDtypeStruct((per, size, T), F32),
         ],
-        in_specs=[HBM] * 3 + [SMEM, SMEM, VMEM, HBM],
+        in_specs=[VMEM, VMEM, HBM],
         out_specs=[HBM, VMEM],
         scratch_shapes=[
-            pltpu.SMEM(entry.shape, jnp.int32),
-            pltpu.SMEM(place.shape, jnp.int32),
-            pltpu.SMEM(slot.shape, jnp.int32),
             pltpu.VMEM(library.shape, BF16),
             pltpu.VMEM((owners * per, T), F32),
-            pltpu.VMEM((owners + 1, size, T), F32),
-            pltpu.VMEM((blocks * size, entries * T), F32),
+            pltpu.VMEM((owners * size, T), F32),
+            pltpu.VMEM((size * blocks, entries * T), BF16),
+            pltpu.VMEM((size * blocks, T), F32),
             pltpu.VMEM((blocks, size, T), BF16),
-            pltpu.SemaphoreType.DMA((4,)),
-            pltpu.SemaphoreType.DMA((2,)),
+            pltpu.SemaphoreType.DMA,
+            pltpu.SemaphoreType.DMA((parts,)),
         ],
         compiler_params=params(),
         cost_estimate=pl.CostEstimate(
             flops=2 * 256 * size * T * T, bytes_accessed=8 * 2**20, transcendentals=0
         ),
         name="adjoint_tiles",
-    )(*map(in_hbm, (entry, place, slot)), count, theirs, returned, in_hbm(library))
+    )(weights, returned, in_hbm(library))
 
 
 def residual_call(phase, stripe, forward):
@@ -409,14 +453,15 @@
 
     left = lax.ppermute(projections[:, -T:], "ray", [(i, i + 1) for i in range(quarters - 1)])
     right = lax.ppermute(projections[:, :T], "ray", [(i + 1, i) for i in range(quarters - 1)])
-    taps = jnp.pad(phase_kernel[None].astype(F32), ((0, 0), (0, 3 * T - phase_kernel.shape[0])))
+    taps = phase_kernel.reshape(1, -1)
     phase, send = first_call(*tiles, carried, projections, left, right, taps, image, library)
     arrived = exchanged(send, "dom")
-    numbers = lax.dynamic_slice_in_dim(arrived[:, slices + 18, :], lax.axis_index("dom"), 1, axis=1)
-    theirs = numbers[:, 0].astype(jnp.int32)
     forward, back = back_call(carried, quarter, arrived, phase, quarters)
+    owner = lax.axis_index("dom").astype(jnp.int32).reshape(1)
+    blocks = image.shape[1] // T
+    weights = counts_call(*tiles, owner, arrived, library.shape[0], blocks)
     returned = exchanged(back, "dom")
-    update, stripe = adjoint_call(*tiles, theirs, returned, library, image.shape[1] // T)
+    update, stripe = adjoint_call(weights, returned, library, blocks)
     parts = exchanged(update, "ray")
     residual = residual_call(phase, stripe, forward)
     image_next = image_call(quarter, image, parts, quarters)

time: 128 us -> 129 us (level)
  Pallas kernels: 14.9 us -> 17.6 us
  other arithmetic: 1.32 us -> 0 us
    convert_element_type x1 -> x0, other arithmetic: 1.31 us -> none  [shards(): theirs = numbers[:, 0].astype(jnp.int32)]
  transfers between devices with their start and end apart: 5 -> 5, of which waited for: 4 -> 4; matrix products, arithmetic and copies ran while one was open for 2% -> 1% of each run, Pallas kernels for 1% -> 1%
where the time goes in v5:
time: 129 us; the launch traced here: 128 us
  waiting for transfers between devices  79.3 us (61%)
  starting transfers between devices  28.3 us (22%)
  Pallas kernels  17.6 us (14%)
  local copies, waits for them, and re-layouts  1.42 us (1%)
  between operations  1.38 us (1%)
    all_to_all x3, waiting for transfers between devices, exchanged(): return lax.all_to_all(array, axis, split_axis=0, concat_axis=0, tiled=True)  79.2 us
    all_to_all x3, starting transfers between devices, exchanged(): return lax.all_to_all(array, axis, split_axis=0, concat_axis=0, tiled=True)  22.5 us
    pallas_call x1, Pallas kernels, first_call(): pl.pallas_call(kernel, out_shape=[jax.ShapeDtypeStruct((slices, columns),...  7.06 us
    pallas_call x1, Pallas kernels, adjoint_call(): pl.pallas_call(kernel, out_shape=[pltpu.HBM((blocks, size, T), BF16), jax...  5.17 us
    ppermute x1, starting transfers between devices, shards(): lax.ppermute(projections[:, -T:], 'ray', [(i, i + 1) for i in range(quart...  4.55 us
    pallas_call x1, Pallas kernels, back_call(): pl.pallas_call(kernel, out_shape=[pltpu.HBM((size, columns), F32), pltpu....  2.77 us
  transfers between devices with their start and end apart: 5, of which 4 were waited for; matrix products, arithmetic and copies ran while one was open for 1% of the time, Pallas kernels for 1%

profile of v5, /device:TPU:8, one launch (start us, length us, event | category | flops | bytes accessed | tf_op | source)
XLA Modules:
  0.0 128.0 jit_solution(14035933140842842778)
XLA Ops:
  0.6 0.7 fusion
  1.4 1.3 collective-permute-start.1
  2.7 4.5 %collective-permute-start = (bf16[64,128]{1,0:T(8,128)(2,1)S(1)}, bf16[64,128]{1,0:T(8,128)(2,1)S(1)}, u32[]{:S(2)}, u32[]{:S(2)}) collective-permute-start(bf16[64,128]{1,0:T(8,128)(2,1)S(1)} %get-tuple-element.15), channel_id=1, source_target_pairs={{0,1},{1,2},{2,3},{4,5},{5,6},{6,7},{8,9},{9,10},{10,11},{12,13},{... | collective-permute-start | bytes 49160 | tf_op jit(solution)/shard_map/ppermute | solution.py:454
  7.9 0.7 reshape.13.taps_ref
  8.5 0.0 collective-permute-done.1.r_ref
  8.5 0.1 collective-permute-done.l_ref
  8.6 7.1 %filter_and_forward.1 = (bf16[64,2048]{1,0:T(8,128)(2,1)S(1)}, bf16[64,96,128]{2,1,0:T(8,128)(2,1)}) custom-call(s32[1,256]{1,0:T(1,128)} %bitcast.19, s32[1,256]{1,0:T(1,128)} %bitcast.21, s32[1,256]{1,0:T(1,128)} %bitcast.23, s32[1,1]{1,0:T(1,128)S(6)} %copy.11.count_ref, s32[1,64]{1,0:T(1,128)} %bitcast.13, bf16[64,2048]{1,0:T(8,128)(2,1)} %bitcast.18, ...), custom_call_target="tpu_custom_call" | custom-call | flops 536870912 | bytes 8388608 | tf_op jit(solution)/shard_map/filter_and_forward/pallas_call | solution.py:149
  15.7 0.0 copy-start.2
  15.7 11.9 %all-to-all-start = ((bf16[64,96,128]{2,1,0:T(8,128)(2,1)}), bf16[64,96,128]{2,1,0:T(8,128)(2,1)S(1)}, u32[]{:S(2)}, u32[]{:S(2)}) async-start(bf16[64,96,128]{2,1,0:T(8,128)(2,1)} %get-tuple-element.9), calls=%async_computation | async-start | bytes 3145728 | tf_op jit(solution)/shard_map/all_to_all | solution.py:441
  27.7 40.0 %all-to-all-done.arrived_ref = bf16[64,96,128]{2,1,0:T(8,128)(2,1)S(1)} async-done(((bf16[64,96,128]{2,1,0:T(8,128)(2,1)}), bf16[64,96,128]{2,1,0:T(8,128)(2,1)S(1)}, u32[]{:S(2)}, u32[]{:S(2)}) %all-to-all-start) | async-done | bytes 1572896 | tf_op jit(solution)/shard_map/all_to_all | solution.py:441
  67.7 0.0 copy-done.2
  67.7 2.8 %sum_and_stripe.1 = (f32[64,2048]{1,0:T(8,128)}, bf16[64,80,128]{2,1,0:T(8,128)(2,1)}) custom-call(s32[1,64]{1,0:T(1,128)S(1)} %bitcast.14, s32[1]{0:T(128)} %bitcast.8.q_ref, bf16[64,96,128]{2,1,0:T(8,128)(2,1)S(1)} %all-to-all-done.arrived_ref, bf16[64,2048]{1,0:T(8,128)(2,1)S(1)} %get-tuple-element.8.phase_ref), custom_call_target="tpu_custom_call" | custom-call | flops 16777216 | bytes 8388608 | tf_op jit(solution)/shard_map/sum_and_stripe/pallas_call | solution.py:245
  70.5 5.4 %all-to-all-start.1 = ((bf16[64,80,128]{2,1,0:T(8,128)(2,1)}), bf16[64,80,128]{2,1,0:T(8,128)(2,1)S(1)}, u32[]{:S(2)}, u32[]{:S(2)}) async-start(bf16[64,80,128]{2,1,0:T(8,128)(2,1)} %get-tuple-element.10), calls=%async_computation.1 | async-start | bytes 2621440 | tf_op jit(solution)/shard_map/all_to_all | solution.py:441
  75.9 1.1 tile_counts.1.weights_ref
  77.0 0.0 copy-start
  77.0 0.0 copy-start.1
  77.1 33.3 %all-to-all-done.1.returned_ref = bf16[64,80,128]{2,1,0:T(8,128)(2,1)S(1)} async-done(((bf16[64,80,128]{2,1,0:T(8,128)(2,1)}), bf16[64,80,128]{2,1,0:T(8,128)(2,1)S(1)}, u32[]{:S(2)}, u32[]{:S(2)}) %all-to-all-start.1) | async-done | bytes 1310752 | tf_op jit(solution)/shard_map/all_to_all | solution.py:441
  110.3 5.2 %adjoint_tiles.1 = (bf16[16,64,128]{2,1,0:T(8,128)(2,1)}, f32[16,64,128]{2,1,0:T(8,128)S(1)}) custom-call(bf16[256,128]{1,0:T(8,128)(2,1)S(1)} %tile_counts.1.weights_ref, bf16[64,80,128]{2,1,0:T(8,128)(2,1)S(1)} %all-to-all-done.1.returned_ref, bf16[16,128,128]{2,1,0:T(8,128)(2,1)} %bitcast.26), custom_call_target="tpu_custom_call" | custom-call | flops 536870912 | bytes 8388608 | tf_op jit(solution)/shard_map/adjoint_tiles/pallas_call | solution.py:366
  115.5 5.1 %all-to-all-start.2 = ((bf16[16,64,128]{2,1,0:T(8,128)(2,1)}), bf16[16,64,128]{2,1,0:T(8,128)(2,1)S(1)}, u32[]{:S(2)}, u32[]{:S(2)}) async-start(bf16[16,64,128]{2,1,0:T(8,128)(2,1)} %get-tuple-element.13), calls=%async_computation.2 | async-start | bytes 524288 | tf_op jit(solution)/shard_map/all_to_all | solution.py:441
  120.7 0.0 copy-done
  120.7 0.8 residual.1
  121.5 5.9 %all-to-all-done.2.parts_ref = bf16[16,64,128]{2,1,0:T(8,128)(2,1)S(1)} async-done(((bf16[16,64,128]{2,1,0:T(8,128)(2,1)}), bf16[16,64,128]{2,1,0:T(8,128)(2,1)S(1)}, u32[]{:S(2)}, u32[]{:S(2)}) %all-to-all-start.2) | async-done | bytes 262176 | tf_op jit(solution)/shard_map/all_to_all | solution.py:441
  127.3 0.0 copy-done.1
  127.3 0.7 image_step.1
Async XLA Ops:
  1.4 7.2 %collective-permute-start.1 = (bf16[64,128]{1,0:T(8,128)(2,1)S(1)}, bf16[64,128]{1,0:T(8,128)(2,1)S(1)}, u32[]{:S(2)}, u32[]{:S(2)}) collective-permute-start(bf16[64,128]{1,0:T(8,128)(2,1)S(1)} %get-tuple-element.14), channel_id=1, source_target_pairs={{1,0},{2,1},{3,2},{5,4},{6,5},{7,6},{9,8},{10,9},{11,10},{13,12},{... | collective-permute-start | bytes 49160 | tf_op jit(solution)/shard_map/ppermute | solution.py:455
  2.7 6.0 %collective-permute-start = (bf16[64,128]{1,0:T(8,128)(2,1)S(1)}, bf16[64,128]{1,0:T(8,128)(2,1)S(1)}, u32[]{:S(2)}, u32[]{:S(2)}) collective-permute-start(bf16[64,128]{1,0:T(8,128)(2,1)S(1)} %get-tuple-element.15), channel_id=1, source_target_pairs={{0,1},{1,2},{2,3},{4,5},{5,6},{6,7},{8,9},{9,10},{10,11},{12,13},{... | collective-permute-start | bytes 49160 | tf_op jit(solution)/shard_map/ppermute | solution.py:454
  15.7 52.0 %copy-start.2 = (s32[1,1,64]{2,1,0:T(1,128)S(1)}, s32[1,1,64]{2,1,0:T(1,128)}, u32[]{:S(2)}) copy-start(s32[1,1,64]{2,1,0:T(1,128)} %param.17) | copy-start | bytes 772
  15.7 52.0 %all-to-all-start = ((bf16[64,96,128]{2,1,0:T(8,128)(2,1)}), bf16[64,96,128]{2,1,0:T(8,128)(2,1)S(1)}, u32[]{:S(2)}, u32[]{:S(2)}) async-start(bf16[64,96,128]{2,1,0:T(8,128)(2,1)} %get-tuple-element.9), calls=%async_computation | async-start | bytes 3145728 | tf_op jit(solution)/shard_map/all_to_all | solution.py:441
  70.5 39.9 %all-to-all-start.1 = ((bf16[64,80,128]{2,1,0:T(8,128)(2,1)}), bf16[64,80,128]{2,1,0:T(8,128)(2,1)S(1)}, u32[]{:S(2)}, u32[]{:S(2)}) async-start(bf16[64,80,128]{2,1,0:T(8,128)(2,1)} %get-tuple-element.10), calls=%async_computation.1 | async-start | bytes 2621440 | tf_op jit(solution)/shard_map/all_to_all | solution.py:441
  77.0 43.6 %copy-start = (f32[64,2048]{1,0:T(8,128)S(1)}, f32[64,2048]{1,0:T(8,128)}, u32[]{:S(2)}) copy-start(f32[64,2048]{1,0:T(8,128)} %get-tuple-element.12.forward_ref) | copy-start | bytes 1572868
  77.0 50.3 %copy-start.1 = (bf16[2048,64]{0,1:T(8,128)(2,1)S(1)}, bf16[2048,64]{0,1:T(8,128)(2,1)}, u32[]{:S(2)}) copy-start(bf16[2048,64]{0,1:T(8,128)(2,1)} %param.11) | copy-start | bytes 786436
  115.5 11.8 %all-to-all-start.2 = ((bf16[16,64,128]{2,1,0:T(8,128)(2,1)}), bf16[16,64,128]{2,1,0:T(8,128)(2,1)S(1)}, u32[]{:S(2)}, u32[]{:S(2)}) async-start(bf16[16,64,128]{2,1,0:T(8,128)(2,1)} %get-tuple-element.13), calls=%async_computation.2 | async-start | bytes 524288 | tf_op jit(solution)/shard_map/all_to_all | solution.py:441

commit v6 on v5

--- a/solution.py
+++ b/solution.py
@@ -311,17 +311,15 @@
     )(*map(in_hbm, (entry, place, slot)), count, owner, arrived)
 
 
-def adjoint_call(weights, returned, library, blocks):
+def adjoint_call(quarter, weights, returned, library, blocks, quarters):
     entries = library.shape[0]
     owners = returned.shape[0]
     per = 16
     size = returned.shape[1] - per
-    parts = 4
-
-    def kernel(
-        weights_ref, returned_ref, library_hbm, update_hbm, stripe_ref, library_ref, stripes, terms, bins, whole,
-        update, load, sems,
-    ):
+    held = blocks // quarters
+
+    def kernel(q_ref, weights_ref, returned_ref, library_hbm, *refs):
+        outs, (stripe_ref, library_ref, stripes, terms, bins, whole, load) = refs[:quarters], refs[quarters:]
         fetch = pltpu.make_async_copy(library_hbm, library_ref, load)
         fetch.start()
         stripes[...] = returned_ref[:, size:, :].astype(F32).reshape(owners * per, T)
@@ -342,51 +340,36 @@
                         e * blocks : (e + 1) * blocks, u * T : (u + 1) * T
                     ]
         fetch.wait()
-        held = size // parts
-        copies = []
-        for h in range(parts):
-            rows = slice(h * held * blocks, (h + 1) * held * blocks)
-            whole[rows, :] = jnp.dot(
-                bins[rows, :], library_ref[...].reshape(entries * T, T), preferred_element_type=F32
-            )
-            for i in range(blocks):
-                update[i, h * held : (h + 1) * held, :] = whole[
-                    pl.ds(h * held * blocks + i, held, stride=blocks), :
-                ].astype(BF16)
-            here = pl.ds(h * held, held)
-            copies.append(
-                pltpu.make_async_copy(update.at[:, here, :], update_hbm.at[:, here, :], sems.at[h])
-            )
-            copies[-1].start()
+        whole[...] = jnp.dot(bins[...], library_ref[...].reshape(entries * T, T), preferred_element_type=F32)
+        for m, out_ref in enumerate(outs):
+            start = lax.rem(q_ref[0] + m, quarters) * held
+            for t in range(held):
+                out_ref[t] = whole[pl.ds(start + t, size, stride=blocks), :].astype(out_ref.dtype)
         for b in range(per):
             stripe_ref[b] = stripes[pl.ds(b, size, stride=per), :]
-        for copy in copies:
-            copy.wait()
 
     return pl.pallas_call(
         kernel,
         out_shape=[
-            pltpu.HBM((blocks, size, T), BF16),
+            *(jax.ShapeDtypeStruct((held, size, T), BF16 if m else F32) for m in range(quarters)),
             jax.ShapeDtypeStruct((per, size, T), F32),
         ],
-        in_specs=[VMEM, VMEM, HBM],
-        out_specs=[HBM, VMEM],
+        in_specs=[SMEM, VMEM, VMEM, HBM],
+        out_specs=[VMEM] * (quarters + 1),
         scratch_shapes=[
             pltpu.VMEM(library.shape, BF16),
             pltpu.VMEM((owners * per, T), F32),
             pltpu.VMEM((owners * size, T), F32),
             pltpu.VMEM((size * blocks, entries * T), BF16),
             pltpu.VMEM((size * blocks, T), F32),
-            pltpu.VMEM((blocks, size, T), BF16),
             pltpu.SemaphoreType.DMA,
-            pltpu.SemaphoreType.DMA((parts,)),
         ],
         compiler_params=params(),
         cost_estimate=pl.CostEstimate(
             flops=2 * 256 * size * T * T, bytes_accessed=8 * 2**20, transcendentals=0
         ),
         name="adjoint_tiles",
-    )(weights, returned, in_hbm(library))
+    )(quarter, weights, returned, in_hbm(library))
 
 
 def residual_call(phase, stripe, forward):
@@ -409,28 +392,28 @@
     )(phase, stripe, forward)
 
 
-def image_call(quarter, image, parts, quarters):
-    slices, pixels = image.shape
-    held = pixels // quarters
-    mine = held // T
-
-    def kernel(q_ref, image_ref, parts_ref, out_ref):
+def image_call(quarter, image, own, others):
+    slices = image.shape[0]
+    mine = own.shape[0]
+
+    def kernel(q_ref, image_ref, own_ref, *refs):
+        others_refs, out_ref = refs[:-1], refs[-1]
         for i in range(mine):
-            total = parts_ref[i].astype(F32)
-            for q in range(1, quarters):
-                total += parts_ref[q * mine + i].astype(F32)
-            own = image_ref[:, lanes(q_ref[0] * mine + i)].astype(F32)
-            out_ref[:, i * T : (i + 1) * T] = own + RELAX * total
-
-    return pl.pallas_call(
-        kernel,
-        out_shape=jax.ShapeDtypeStruct((slices, held), F32),
-        in_specs=[SMEM, VMEM, VMEM],
+            total = own_ref[i]
+            for ref in others_refs:
+                total += ref[i].astype(F32)
+            pixels = image_ref[:, lanes(q_ref[0] * mine + i)].astype(F32)
+            out_ref[:, i * T : (i + 1) * T] = pixels + RELAX * total
+
+    return pl.pallas_call(
+        kernel,
+        out_shape=jax.ShapeDtypeStruct((slices, mine * T), F32),
+        in_specs=[SMEM, VMEM, VMEM] + [VMEM] * len(others),
         out_specs=VMEM,
         compiler_params=params(),
         cost_estimate=pl.CostEstimate(flops=2**18, bytes_accessed=2**20, transcendentals=0),
         name="image_step",
-    )(quarter, image, parts)
+    )(quarter, image, own, *others)
 
 
 def in_hbm(array):
@@ -461,10 +444,13 @@
     blocks = image.shape[1] // T
     weights = counts_call(*tiles, owner, arrived, library.shape[0], blocks)
     returned = exchanged(back, "dom")
-    update, stripe = adjoint_call(weights, returned, library, blocks)
-    parts = exchanged(update, "ray")
+    own, *sent, stripe = adjoint_call(quarter, weights, returned, library, blocks, quarters)
+    others = [
+        lax.ppermute(part, "ray", [(i, (i + m) % quarters) for i in range(quarters)])
+        for m, part in enumerate(sent, 1)
+    ]
     residual = residual_call(phase, stripe, forward)
-    image_next = image_call(quarter, image, parts, quarters)
+    image_next = image_call(quarter, image, own, others)
     return residual[None], image_next.T
 
 

time: 129 us -> 126 us (0.977)
  waiting for transfers between devices: 79.3 us -> 75.7 us
  starting transfers between devices: 28.3 us -> 31.1 us
  Pallas kernels: 17.6 us -> 15.7 us
    ppermute x0 -> x3, starting transfers between devices: none -> 6.53 us  [shards(): lax.ppermute(part, 'ray', [(i, (i + m) % quarters) for i in range(quarter...]
    all_to_all x3 -> x2, waiting for transfers between devices: 79.2 us -> 73.3 us  [exchanged(): return lax.all_to_all(array, axis, split_axis=0, concat_axis=0, tiled=True)]
    all_to_all x3 -> x2, starting transfers between devices: 22.5 us -> 18.7 us  [exchanged(): return lax.all_to_all(array, axis, split_axis=0, concat_axis=0, tiled=True)]
    ppermute x0 -> x3, waiting for transfers between devices: none -> 2.33 us  [shards(): lax.ppermute(part, 'ray', [(i, (i + m) % quarters) for i in range(quarter...]
  transfers between devices with their start and end apart: 5 -> 7, of which waited for: 4 -> 5; matrix products, arithmetic and copies ran while one was open for 1% -> 1% of each run, Pallas kernels for 1% -> 2%
where the time goes in v6:
time: 126 us; the launch traced here: 125 us
  waiting for transfers between devices  75.7 us (60%)
  starting transfers between devices  31.1 us (25%)
  Pallas kernels  15.7 us (12%)
  local copies, waits for them, and re-layouts  1.42 us (1%)
  between operations  1.38 us (1%)
    all_to_all x2, waiting for transfers between devices, exchanged(): return lax.all_to_all(array, axis, split_axis=0, concat_axis=0, tiled=True)  73.3 us
    all_to_all x2, starting transfers between devices, exchanged(): return lax.all_to_all(array, axis, split_axis=0, concat_axis=0, tiled=True)  18.7 us
    ppermute x3, starting transfers between devices, shards(): lax.ppermute(part, 'ray', [(i, (i + m) % quarters) for i in range(quarter...  6.53 us
    pallas_call x1, Pallas kernels, first_call(): pl.pallas_call(kernel, out_shape=[jax.ShapeDtypeStruct((slices, columns),...  5.82 us
    ppermute x1, starting transfers between devices, shards(): lax.ppermute(projections[:, -T:], 'ray', [(i, i + 1) for i in range(quart...  4.55 us
    pallas_call x1, Pallas kernels, adjoint_call(): pl.pallas_call(kernel, out_shape=[*(jax.ShapeDtypeStruct((held, size, T),...  4.53 us
    pallas_call x1, Pallas kernels, back_call(): pl.pallas_call(kernel, out_shape=[pltpu.HBM((size, columns), F32), pltpu....  2.76 us
  transfers between devices with their start and end apart: 7, of which 5 were waited for; matrix products, arithmetic and copies ran while one was open for 1% of the time, Pallas kernels for 2%

profile of v6, /device:TPU:8, one launch (start us, length us, event | category | flops | bytes accessed | tf_op | source)
XLA Modules:
  0.0 125.3 jit_solution(2490529590768788338)
XLA Ops:
  0.6 0.7 fusion
  1.4 1.3 %collective-permute-start.1 = (bf16[64,128]{1,0:T(8,128)(2,1)S(1)}, bf16[64,128]{1,0:T(8,128)(2,1)S(1)}, u32[]{:S(2)}, u32[]{:S(2)}) collective-permute-start(bf16[64,128]{1,0:T(8,128)(2,1)S(1)} %get-tuple-element.20), channel_id=1, source_target_pairs={{1,0},{2,1},{3,2},{5,4},{6,5},{7,6},{9,8},{10,9},{11,10},{13,12},{... | collective-permute-start | bytes 49160 | tf_op jit(solution)/shard_map/ppermute | solution.py:438
  2.7 4.5 %collective-permute-start = (bf16[64,128]{1,0:T(8,128)(2,1)S(1)}, bf16[64,128]{1,0:T(8,128)(2,1)S(1)}, u32[]{:S(2)}, u32[]{:S(2)}) collective-permute-start(bf16[64,128]{1,0:T(8,128)(2,1)S(1)} %get-tuple-element.21), channel_id=1, source_target_pairs={{0,1},{1,2},{2,3},{4,5},{5,6},{6,7},{8,9},{9,10},{10,11},{12,13},{... | collective-permute-start | bytes 49160 | tf_op jit(solution)/shard_map/ppermute | solution.py:437
  7.9 0.7 reshape.13.taps_ref
  8.5 0.0 collective-permute-done.1.r_ref
  8.5 0.1 collective-permute-done.l_ref
  8.6 5.8 %filter_and_forward.1 = (bf16[64,2048]{1,0:T(8,128)(2,1)S(1)}, bf16[64,96,128]{2,1,0:T(8,128)(2,1)}) custom-call(s32[1,256]{1,0:T(1,128)} %bitcast.19, s32[1,256]{1,0:T(1,128)} %bitcast.21, s32[1,256]{1,0:T(1,128)} %bitcast.23, s32[1,1]{1,0:T(1,128)S(6)} %copy.11.count_ref, s32[1,64]{1,0:T(1,128)} %bitcast.13, bf16[64,2048]{1,0:T(8,128)(2,1)} %bitcast.18, ...), custom_call_target="tpu_custom_call" | custom-call | flops 536870912 | bytes 8388608 | tf_op jit(solution)/shard_map/filter_and_forward/pallas_call | solution.py:149
  14.5 0.0 copy-start.2
  14.5 13.3 %all-to-all-start = ((bf16[64,96,128]{2,1,0:T(8,128)(2,1)}), bf16[64,96,128]{2,1,0:T(8,128)(2,1)S(1)}, u32[]{:S(2)}, u32[]{:S(2)}) async-start(bf16[64,96,128]{2,1,0:T(8,128)(2,1)} %get-tuple-element.12), calls=%async_computation | async-start | bytes 3145728 | tf_op jit(solution)/shard_map/all_to_all | solution.py:424
  27.8 40.0 %all-to-all-done.arrived_ref = bf16[64,96,128]{2,1,0:T(8,128)(2,1)S(1)} async-done(((bf16[64,96,128]{2,1,0:T(8,128)(2,1)}), bf16[64,96,128]{2,1,0:T(8,128)(2,1)S(1)}, u32[]{:S(2)}, u32[]{:S(2)}) %all-to-all-start) | async-done | bytes 1572896 | tf_op jit(solution)/shard_map/all_to_all | solution.py:424
  67.8 0.0 copy-done.2
  67.8 2.8 %sum_and_stripe.1 = (f32[64,2048]{1,0:T(8,128)}, bf16[64,80,128]{2,1,0:T(8,128)(2,1)}) custom-call(s32[1,64]{1,0:T(1,128)S(1)} %bitcast.14, s32[1]{0:T(128)} %bitcast.7.q_ref, bf16[64,96,128]{2,1,0:T(8,128)(2,1)S(1)} %all-to-all-done.arrived_ref, bf16[64,2048]{1,0:T(8,128)(2,1)S(1)} %get-tuple-element.11.phase_ref), custom_call_target="tpu_custom_call" | custom-call | flops 16777216 | bytes 8388608 | tf_op jit(solution)/shard_map/sum_and_stripe/pallas_call | solution.py:245
  70.6 5.4 %all-to-all-start.1 = ((bf16[64,80,128]{2,1,0:T(8,128)(2,1)}), bf16[64,80,128]{2,1,0:T(8,128)(2,1)S(1)}, u32[]{:S(2)}, u32[]{:S(2)}) async-start(bf16[64,80,128]{2,1,0:T(8,128)(2,1)} %get-tuple-element.13), calls=%async_computation.1 | async-start | bytes 2621440 | tf_op jit(solution)/shard_map/all_to_all | solution.py:424
  76.0 1.1 tile_counts.1.weights_ref
  77.1 0.0 copy-start
  77.1 0.0 copy-start.1
  77.2 33.3 %all-to-all-done.1.returned_ref = bf16[64,80,128]{2,1,0:T(8,128)(2,1)S(1)} async-done(((bf16[64,80,128]{2,1,0:T(8,128)(2,1)}), bf16[64,80,128]{2,1,0:T(8,128)(2,1)S(1)}, u32[]{:S(2)}, u32[]{:S(2)}) %all-to-all-start.1) | async-done | bytes 1310752 | tf_op jit(solution)/shard_map/all_to_all | solution.py:424
  110.4 4.5 %adjoint_tiles.1 = (f32[4,64,128]{2,1,0:T(8,128)S(1)}, bf16[4,64,128]{2,1,0:T(8,128)(2,1)S(1)}, bf16[4,64,128]{2,1,0:T(8,128)(2,1)S(1)}, bf16[4,64,128]{2,1,0:T(8,128)(2,1)S(1)}, f32[16,64,128]{2,1,0:T(8,128)S(1)}) custom-call(s32[1]{0:T(128)} %bitcast.7.q_ref, bf16[256,128]{1,0:T(8,128)(2,1)S(1)} %tile_counts.1.weights_ref, ...), custom_call_target="tpu_custom_call" | custom-call | flops 536870912 | bytes 8388608 | tf_op jit(solution)/shard_map/adjoint_tiles/pallas_call | solution.py:351
  115.0 2.2 %collective-permute-start.2 = (bf16[4,64,128]{2,1,0:T(8,128)(2,1)S(1)}, bf16[4,64,128]{2,1,0:T(8,128)(2,1)S(1)}, u32[]{:S(2)}, u32[]{:S(2)}) collective-permute-start(bf16[4,64,128]{2,1,0:T(8,128)(2,1)S(1)} %get-tuple-element.17), channel_id=1, source_target_pairs={{0,1},{1,2},{2,3},{3,0},{4,5},{5,6},{6,7},{7,4},{8,9},{9,10},{10,1... | collective-permute-start | bytes 196616 | tf_op jit(solution)/shard_map/ppermute | solution.py:449
  117.2 3.2 %collective-permute-start.3 = (bf16[4,64,128]{2,1,0:T(8,128)(2,1)S(1)}, bf16[4,64,128]{2,1,0:T(8,128)(2,1)S(1)}, u32[]{:S(2)}, u32[]{:S(2)}) collective-permute-start(bf16[4,64,128]{2,1,0:T(8,128)(2,1)S(1)} %get-tuple-element.18), channel_id=1, source_target_pairs={{0,2},{1,3},{2,0},{3,1},{4,6},{5,7},{6,4},{7,5},{8,10},{9,11},{10,... | collective-permute-start | bytes 196616 | tf_op jit(solution)/shard_map/ppermute | solution.py:449
  120.4 1.1 collective-permute-start.4
  121.5 0.0 copy-done
  121.5 0.8 residual.1
  122.3 0.0 collective-permute-done.2.refs_0_
  122.3 1.0 collective-permute-done.3.refs_1_
  123.3 1.3 %collective-permute-done.4.refs_2_ = bf16[4,64,128]{2,1,0:T(8,128)(2,1)S(1)} collective-permute-done((bf16[4,64,128]{2,1,0:T(8,128)(2,1)S(1)}, bf16[4,64,128]{2,1,0:T(8,128)(2,1)S(1)}, u32[]{:S(2)}, u32[]{:S(2)}) %collective-permute-start.4) | collective-permute-done | bytes 65568 | tf_op jit(solution)/shard_map/ppermute | solution.py:449
  124.6 0.0 copy-done.1
  124.6 0.7 image_step.1
Async XLA Ops:
  1.4 7.2 %collective-permute-start.1 = (bf16[64,128]{1,0:T(8,128)(2,1)S(1)}, bf16[64,128]{1,0:T(8,128)(2,1)S(1)}, u32[]{:S(2)}, u32[]{:S(2)}) collective-permute-start(bf16[64,128]{1,0:T(8,128)(2,1)S(1)} %get-tuple-element.20), channel_id=1, source_target_pairs={{1,0},{2,1},{3,2},{5,4},{6,5},{7,6},{9,8},{10,9},{11,10},{13,12},{... | collective-permute-start | bytes 49160 | tf_op jit(solution)/shard_map/ppermute | solution.py:438
  2.7 6.0 %collective-permute-start = (bf16[64,128]{1,0:T(8,128)(2,1)S(1)}, bf16[64,128]{1,0:T(8,128)(2,1)S(1)}, u32[]{:S(2)}, u32[]{:S(2)}) collective-permute-start(bf16[64,128]{1,0:T(8,128)(2,1)S(1)} %get-tuple-element.21), channel_id=1, source_target_pairs={{0,1},{1,2},{2,3},{4,5},{5,6},{6,7},{8,9},{9,10},{10,11},{12,13},{... | collective-permute-start | bytes 49160 | tf_op jit(solution)/shard_map/ppermute | solution.py:437
  14.5 53.3 %copy-start.2 = (s32[1,1,64]{2,1,0:T(1,128)S(1)}, s32[1,1,64]{2,1,0:T(1,128)}, u32[]{:S(2)}) copy-start(s32[1,1,64]{2,1,0:T(1,128)} %param.17) | copy-start | bytes 772
  14.5 53.3 %all-to-all-start = ((bf16[64,96,128]{2,1,0:T(8,128)(2,1)}), bf16[64,96,128]{2,1,0:T(8,128)(2,1)S(1)}, u32[]{:S(2)}, u32[]{:S(2)}) async-start(bf16[64,96,128]{2,1,0:T(8,128)(2,1)} %get-tuple-element.12), calls=%async_computation | async-start | bytes 3145728 | tf_op jit(solution)/shard_map/all_to_all | solution.py:424
  70.6 39.9 %all-to-all-start.1 = ((bf16[64,80,128]{2,1,0:T(8,128)(2,1)}), bf16[64,80,128]{2,1,0:T(8,128)(2,1)S(1)}, u32[]{:S(2)}, u32[]{:S(2)}) async-start(bf16[64,80,128]{2,1,0:T(8,128)(2,1)} %get-tuple-element.13), calls=%async_computation.1 | async-start | bytes 2621440 | tf_op jit(solution)/shard_map/all_to_all | solution.py:424
  77.1 44.4 %copy-start = (f32[64,2048]{1,0:T(8,128)S(1)}, f32[64,2048]{1,0:T(8,128)}, u32[]{:S(2)}) copy-start(f32[64,2048]{1,0:T(8,128)} %get-tuple-element.15.forward_ref) | copy-start | bytes 1572868
  77.1 47.5 %copy-start.1 = (bf16[2048,64]{0,1:T(8,128)(2,1)S(1)}, bf16[2048,64]{0,1:T(8,128)(2,1)}, u32[]{:S(2)}) copy-start(bf16[2048,64]{0,1:T(8,128)(2,1)} %param.11) | copy-start | bytes 786436
  115.0 7.3 %collective-permute-start.2 = (bf16[4,64,128]{2,1,0:T(8,128)(2,1)S(1)}, bf16[4,64,128]{2,1,0:T(8,128)(2,1)S(1)}, u32[]{:S(2)}, u32[]{:S(2)}) collective-permute-start(bf16[4,64,128]{2,1,0:T(8,128)(2,1)S(1)} %get-tuple-element.17), channel_id=1, source_target_pairs={{0,1},{1,2},{2,3},{3,0},{4,5},{5,6},{6,7},{7,4},{8,9},{9,10},{10,1... | collective-permute-start | bytes 196616 | tf_op jit(solution)/shard_map/ppermute | solution.py:449
  117.2 6.1 %collective-permute-start.3 = (bf16[4,64,128]{2,1,0:T(8,128)(2,1)S(1)}, bf16[4,64,128]{2,1,0:T(8,128)(2,1)S(1)}, u32[]{:S(2)}, u32[]{:S(2)}) collective-permute-start(bf16[4,64,128]{2,1,0:T(8,128)(2,1)S(1)} %get-tuple-element.18), channel_id=1, source_target_pairs={{0,2},{1,3},{2,0},{3,1},{4,6},{5,7},{6,4},{7,5},{8,10},{9,11},{10,... | collective-permute-start | bytes 196616 | tf_op jit(solution)/shard_map/ppermute | solution.py:449
  120.4 4.3 %collective-permute-start.4 = (bf16[4,64,128]{2,1,0:T(8,128)(2,1)S(1)}, bf16[4,64,128]{2,1,0:T(8,128)(2,1)S(1)}, u32[]{:S(2)}, u32[]{:S(2)}) collective-permute-start(bf16[4,64,128]{2,1,0:T(8,128)(2,1)S(1)} %get-tuple-element.19), channel_id=1, source_target_pairs={{0,3},{1,0},{2,1},{3,2},{4,7},{5,4},{6,5},{7,6},{8,11},{9,8},{10,9... | collective-permute-start | bytes 196616 | tf_op jit(solution)/shard_map/ppermute | solution.py:449

commit v7 on v6

--- a/solution.py
+++ b/solution.py
@@ -54,18 +54,18 @@
     per = columns // T
     rows = slices + SECTION
     parts = 4
-    loads = per + blocks + 5
+    loads = per + blocks + 6
 
     def kernel(
-        entry_hbm, place_hbm, slot_hbm, count_ref, n_hbm, x_hbm, l_ref, r_ref, taps_ref, image_hbm, library_hbm,
-        phase_ref, send_ref, entry_ref, place_ref, slot_ref, n_ref, library_ref, wide, band, spread, row, line,
+        entry_hbm, place_hbm, slot_hbm, count_ref, n_hbm, x_hbm, l_ref, r_ref, taps_hbm, image_hbm, library_hbm,
+        phase_ref, send_ref, entry_ref, place_ref, slot_ref, n_ref, taps_ref, library_ref, wide, band, spread, row, line,
         stacked, product, total, packed, section, sems, load_sems,
     ):
         def block(n):
             return pl.ds(n * slices, slices)
 
         pairs = [(x_hbm.at[:, pl.ds(b * T, T)], wide.at[block(b + 2)]) for b in range(per)]
-        pairs += [(n_hbm, n_ref)]
+        pairs += [(n_hbm, n_ref), (taps_hbm, taps_ref)]
         early = len(pairs)
         pairs += [(library_hbm, library_ref)]
         pairs += [(image_hbm.at[:, pl.ds(i * T, T)], stacked.at[block(i)]) for i in range(blocks)]
@@ -81,12 +81,12 @@
         wide[block(1), :] = l_ref[...]
         wide[block(per + 2), :] = r_ref[...]
         wide[block(per + 3), :] = jnp.zeros((slices, T), BF16)
+        for fetch in fetches[:early]:
+            fetch.wait()
         line[...] = jnp.zeros_like(line)
-        line[0:1, : taps_ref.shape[1]] = taps_ref[...].astype(F32)
+        line[0:1, : taps_ref.shape[0]] = taps_ref[...].astype(F32).reshape(1, -1)
         spun = pltpu.roll(jnp.broadcast_to(line[0:1, :], (T, 3 * T)), T // 2, 1, stride=1, stride_axis=0)
         band[...] = spun.astype(BF16)
-        for fetch in fetches[:early]:
-            fetch.wait()
         filtered = sum(
             lax.dot_general(
                 wide[n * slices : (n + per + 2) * slices, :],
@@ -152,13 +152,14 @@
             jax.ShapeDtypeStruct((slices, columns), BF16),
             pltpu.HBM((owners, rows, T), BF16),
         ],
-        in_specs=[HBM] * 3 + [SMEM] + [HBM] * 2 + [VMEM] * 3 + [HBM] * 2,
+        in_specs=[HBM] * 3 + [SMEM] + [HBM] * 2 + [VMEM] * 2 + [HBM] * 3,
         out_specs=[VMEM, HBM],
         scratch_shapes=[
             pltpu.SMEM(entry.shape, jnp.int32),
             pltpu.SMEM(place.shape, jnp.int32),
             pltpu.SMEM(slot.shape, jnp.int32),
             pltpu.VMEM(numbers.shape, jnp.int32),
+            pltpu.VMEM(taps.shape, BF16),
             pltpu.VMEM(library.shape, BF16),
             pltpu.VMEM(((per + 4) * slices, T), BF16),
             pltpu.VMEM((T, 3 * T), BF16),
@@ -178,8 +179,8 @@
             flops=2 * capacity * slices * T * T, bytes_accessed=8 * 2**20, transcendentals=0
         ),
         name="filter_and_forward",
-    )(*map(in_hbm, (entry, place, slot)), count, *map(in_hbm, (numbers, projections)), left, right, taps,
-      *map(in_hbm, (image, library)))
+    )(*map(in_hbm, (entry, place, slot)), count, *map(in_hbm, (numbers, projections)), left, right,
+      *map(in_hbm, (taps, image, library)))
 
 
 def stripe_of(quarter, quarters, arrived_ref, offset, values, rimmed):
@@ -222,23 +223,26 @@
     parts = 4
 
     def kernel(
-        c_ref, q_ref, arrived_ref, phase_ref, forward_hbm, send_ref, values, rimmed, forward, less, packed, sems
+        c_ref, q_ref, arrived_ref, phase_ref, forward_hbm, send_ref, values, rimmed, forward, less, packed, repeated,
+        sems,
     ):
         forward[...] = jnp.zeros_like(forward)
         for d in range(owners):
             forward[:, lanes(c_ref[0, d])] += arrived_ref[d, :size, :].astype(F32)
         copies = [pltpu.make_async_copy(forward, forward_hbm, sems.at[parts])]
         copies[0].start()
-        stripe = stripe_of(q_ref[0], quarters, arrived_ref, size, values, rimmed).astype(BF16)
         less[...] = (phase_ref[...].astype(F32) - forward[...]).astype(BF16)
         step = owners // parts
         for n in range(parts):
             for d in range(n * step, (n + 1) * step):
-                packed[d, :size, :] = less[:, lanes(c_ref[0, d])]
-                packed[d, size:, :] = stripe
+                packed[d] = less[:, lanes(c_ref[0, d])]
             here = pl.ds(n * step, step)
-            copies.append(pltpu.make_async_copy(packed.at[here], send_ref.at[here], sems.at[n]))
+            copies.append(pltpu.make_async_copy(packed.at[here], send_ref.at[here, pl.ds(0, size), :], sems.at[n]))
             copies[-1].start()
+        stripe = stripe_of(q_ref[0], quarters, arrived_ref, size, values, rimmed).astype(BF16)
+        repeated[...] = jnp.broadcast_to(stripe[None], repeated.shape)
+        copies.append(pltpu.make_async_copy(repeated, send_ref.at[:, pl.ds(size, 16), :], sems.at[parts + 1]))
+        copies[-1].start()
         for copy in copies:
             copy.wait()
 
@@ -255,8 +259,9 @@
             pltpu.VMEM((32, T), F32),
             pltpu.VMEM((size, columns), F32),
             pltpu.VMEM((size, columns), BF16),
-            pltpu.VMEM((owners, rows, T), BF16),
-            pltpu.SemaphoreType.DMA((parts + 1,)),
+            pltpu.VMEM((owners, size, T), BF16),
+            pltpu.VMEM((owners, 16, T), BF16),
+            pltpu.SemaphoreType.DMA((parts + 2,)),
         ],
         compiler_params=params(),
         cost_estimate=pl.CostEstimate(flops=2**24, bytes_accessed=8 * 2**20, transcendentals=0),
@@ -436,7 +441,7 @@
 
     left = lax.ppermute(projections[:, -T:], "ray", [(i, i + 1) for i in range(quarters - 1)])
     right = lax.ppermute(projections[:, :T], "ray", [(i + 1, i) for i in range(quarters - 1)])
-    taps = phase_kernel.reshape(1, -1)
+    taps = phase_kernel
     phase, send = first_call(*tiles, carried, projections, left, right, taps, image, library)
     arrived = exchanged(send, "dom")
     forward, back = back_call(carried, quarter, arrived, phase, quarters)

time: 126 us -> 126 us (level)
  waiting for transfers between devices: 75.7 us -> 77.4 us
  transfers between devices with their start and end apart: 7 -> 7, of which waited for: 5 -> 6; matrix products, arithmetic and copies ran while one was open for 1% -> 0% of each run, Pallas kernels for 2% -> 2%
where the time goes in v7:
time: 126 us; the launch traced here: 125 us
  waiting for transfers between devices  77.4 us (61%)
  starting transfers between devices  30.1 us (24%)
  Pallas kernels  15.5 us (12%)
  between operations  1.39 us (1%)
    all_to_all x2, waiting for transfers between devices, exchanged(): return lax.all_to_all(array, axis, split_axis=0, concat_axis=0, tiled=True)  73.3 us
    all_to_all x2, starting transfers between devices, exchanged(): return lax.all_to_all(array, axis, split_axis=0, concat_axis=0, tiled=True)  18.3 us
    ppermute x3, starting transfers between devices, shards(): lax.ppermute(part, 'ray', [(i, (i + m) % quarters) for i in range(quarter...  5.98 us
    pallas_call x1, Pallas kernels, first_call(): pl.pallas_call(kernel, out_shape=[jax.ShapeDtypeStruct((slices, columns),...  5.68 us
    ppermute x1, starting transfers between devices, shards(): lax.ppermute(projections[:, -T:], 'ray', [(i, i + 1) for i in range(quart...  4.55 us
    pallas_call x1, Pallas kernels, adjoint_call(): pl.pallas_call(kernel, out_shape=[*(jax.ShapeDtypeStruct((held, size, T),...  4.53 us
    ppermute x3, waiting for transfers between devices, shards(): lax.ppermute(part, 'ray', [(i, (i + m) % quarters) for i in range(quarter...  3.32 us
    pallas_call x1, Pallas kernels, back_call(): pl.pallas_call(kernel, out_shape=[pltpu.HBM((size, columns), F32), pltpu....  2.71 us
  transfers between devices with their start and end apart: 7, of which 6 were waited for; matrix products, arithmetic and copies ran while one was open for 0% of the time, Pallas kernels for 2%

profile of v7, /device:TPU:8, one launch (start us, length us, event | category | flops | bytes accessed | tf_op | source)
XLA Modules:
  0.0 125.1 jit_solution(5777241117880183679)
XLA Ops:
  0.6 0.7 fusion
  1.4 1.3 %collective-permute-start.1 = (bf16[64,128]{1,0:T(8,128)(2,1)S(1)}, bf16[64,128]{1,0:T(8,128)(2,1)S(1)}, u32[]{:S(2)}, u32[]{:S(2)}) collective-permute-start(bf16[64,128]{1,0:T(8,128)(2,1)S(1)} %get-tuple-element.20), channel_id=1, source_target_pairs={{1,0},{2,1},{3,2},{5,4},{6,5},{7,6},{9,8},{10,9},{11,10},{13,12},{... | collective-permute-start | bytes 49160 | tf_op jit(solution)/shard_map/ppermute | solution.py:443
  2.7 4.5 %collective-permute-start = (bf16[64,128]{1,0:T(8,128)(2,1)S(1)}, bf16[64,128]{1,0:T(8,128)(2,1)S(1)}, u32[]{:S(2)}, u32[]{:S(2)}) collective-permute-start(bf16[64,128]{1,0:T(8,128)(2,1)S(1)} %get-tuple-element.21), channel_id=1, source_target_pairs={{0,1},{1,2},{2,3},{4,5},{5,6},{6,7},{8,9},{9,10},{10,11},{12,13},{... | collective-permute-start | bytes 49160 | tf_op jit(solution)/shard_map/ppermute | solution.py:442
  7.9 0.0 collective-permute-done.1.r_ref
  7.9 0.8 collective-permute-done.l_ref
  8.6 5.7 %filter_and_forward.1 = (bf16[64,2048]{1,0:T(8,128)(2,1)S(1)}, bf16[64,96,128]{2,1,0:T(8,128)(2,1)}) custom-call(s32[1,256]{1,0:T(1,128)} %bitcast.19, s32[1,256]{1,0:T(1,128)} %bitcast.21, s32[1,256]{1,0:T(1,128)} %bitcast.23, s32[1,1]{1,0:T(1,128)S(6)} %copy.11.count_ref, s32[1,64]{1,0:T(1,128)} %bitcast.13, bf16[64,2048]{1,0:T(8,128)(2,1)} %bitcast.18, ...), custom_call_target="tpu_custom_call" | custom-call | flops 536870912 | bytes 8388608 | tf_op jit(solution)/shard_map/filter_and_forward/pallas_call | solution.py:149
  14.3 0.0 copy-start.2
  14.3 12.8 %all-to-all-start = ((bf16[64,96,128]{2,1,0:T(8,128)(2,1)}), bf16[64,96,128]{2,1,0:T(8,128)(2,1)S(1)}, u32[]{:S(2)}, u32[]{:S(2)}) async-start(bf16[64,96,128]{2,1,0:T(8,128)(2,1)} %get-tuple-element.12), calls=%async_computation | async-start | bytes 3145728 | tf_op jit(solution)/shard_map/all_to_all | solution.py:429
  27.2 40.0 %all-to-all-done.arrived_ref = bf16[64,96,128]{2,1,0:T(8,128)(2,1)S(1)} async-done(((bf16[64,96,128]{2,1,0:T(8,128)(2,1)}), bf16[64,96,128]{2,1,0:T(8,128)(2,1)S(1)}, u32[]{:S(2)}, u32[]{:S(2)}) %all-to-all-start) | async-done | bytes 1572896 | tf_op jit(solution)/shard_map/all_to_all | solution.py:429
  67.2 0.0 copy-done.2
  67.2 2.7 %sum_and_stripe.1 = (f32[64,2048]{1,0:T(8,128)}, bf16[64,80,128]{2,1,0:T(8,128)(2,1)}) custom-call(s32[1,64]{1,0:T(1,128)S(1)} %bitcast.14, s32[1]{0:T(128)} %bitcast.7.q_ref, bf16[64,96,128]{2,1,0:T(8,128)(2,1)S(1)} %all-to-all-done.arrived_ref, bf16[64,2048]{1,0:T(8,128)(2,1)S(1)} %get-tuple-element.11.phase_ref), custom_call_target="tpu_custom_call" | custom-call | flops 16777216 | bytes 8388608 | tf_op jit(solution)/shard_map/sum_and_stripe/pallas_call | solution.py:249
  69.9 5.4 %all-to-all-start.1 = ((bf16[64,80,128]{2,1,0:T(8,128)(2,1)}), bf16[64,80,128]{2,1,0:T(8,128)(2,1)S(1)}, u32[]{:S(2)}, u32[]{:S(2)}) async-start(bf16[64,80,128]{2,1,0:T(8,128)(2,1)} %get-tuple-element.13), calls=%async_computation.1 | async-start | bytes 2621440 | tf_op jit(solution)/shard_map/all_to_all | solution.py:429
  75.4 1.1 tile_counts.1.weights_ref
  76.5 0.0 copy-start
  76.5 0.0 copy-start.1
  76.5 33.3 %all-to-all-done.1.returned_ref = bf16[64,80,128]{2,1,0:T(8,128)(2,1)S(1)} async-done(((bf16[64,80,128]{2,1,0:T(8,128)(2,1)}), bf16[64,80,128]{2,1,0:T(8,128)(2,1)S(1)}, u32[]{:S(2)}, u32[]{:S(2)}) %all-to-all-start.1) | async-done | bytes 1310752 | tf_op jit(solution)/shard_map/all_to_all | solution.py:429
  109.8 4.5 %adjoint_tiles.1 = (f32[4,64,128]{2,1,0:T(8,128)S(1)}, bf16[4,64,128]{2,1,0:T(8,128)(2,1)S(1)}, bf16[4,64,128]{2,1,0:T(8,128)(2,1)S(1)}, bf16[4,64,128]{2,1,0:T(8,128)(2,1)S(1)}, f32[16,64,128]{2,1,0:T(8,128)S(1)}) custom-call(s32[1]{0:T(128)} %bitcast.7.q_ref, bf16[256,128]{1,0:T(8,128)(2,1)S(1)} %tile_counts.1.weights_ref, ...), custom_call_target="tpu_custom_call" | custom-call | flops 536870912 | bytes 8388608 | tf_op jit(solution)/shard_map/adjoint_tiles/pallas_call | solution.py:356
  114.3 3.0 %collective-permute-start.2 = (bf16[4,64,128]{2,1,0:T(8,128)(2,1)S(1)}, bf16[4,64,128]{2,1,0:T(8,128)(2,1)S(1)}, u32[]{:S(2)}, u32[]{:S(2)}) collective-permute-start(bf16[4,64,128]{2,1,0:T(8,128)(2,1)S(1)} %get-tuple-element.17), channel_id=1, source_target_pairs={{0,1},{1,2},{2,3},{3,0},{4,5},{5,6},{6,7},{7,4},{8,9},{9,10},{10,1... | collective-permute-start | bytes 196616 | tf_op jit(solution)/shard_map/ppermute | solution.py:454
  117.3 2.8 %collective-permute-start.3 = (bf16[4,64,128]{2,1,0:T(8,128)(2,1)S(1)}, bf16[4,64,128]{2,1,0:T(8,128)(2,1)S(1)}, u32[]{:S(2)}, u32[]{:S(2)}) collective-permute-start(bf16[4,64,128]{2,1,0:T(8,128)(2,1)S(1)} %get-tuple-element.18), channel_id=1, source_target_pairs={{0,2},{1,3},{2,0},{3,1},{4,6},{5,7},{6,4},{7,5},{8,10},{9,11},{10,... | collective-permute-start | bytes 196616 | tf_op jit(solution)/shard_map/ppermute | solution.py:454
  120.2 0.1 collective-permute-start.4
  120.3 0.0 copy-done
  120.3 0.8 residual.1
  121.1 0.4 collective-permute-done.2.refs_0_
  121.5 1.6 %collective-permute-done.3.refs_1_ = bf16[4,64,128]{2,1,0:T(8,128)(2,1)S(1)} collective-permute-done((bf16[4,64,128]{2,1,0:T(8,128)(2,1)S(1)}, bf16[4,64,128]{2,1,0:T(8,128)(2,1)S(1)}, u32[]{:S(2)}, u32[]{:S(2)}) %collective-permute-start.3) | collective-permute-done | bytes 65568 | tf_op jit(solution)/shard_map/ppermute | solution.py:454
  123.1 1.3 %collective-permute-done.4.refs_2_ = bf16[4,64,128]{2,1,0:T(8,128)(2,1)S(1)} collective-permute-done((bf16[4,64,128]{2,1,0:T(8,128)(2,1)S(1)}, bf16[4,64,128]{2,1,0:T(8,128)(2,1)S(1)}, u32[]{:S(2)}, u32[]{:S(2)}) %collective-permute-start.4) | collective-permute-done | bytes 65568 | tf_op jit(solution)/shard_map/ppermute | solution.py:454
  124.4 0.0 copy-done.1
  124.4 0.7 image_step.1
Async XLA Ops:
  1.4 6.5 %collective-permute-start.1 = (bf16[64,128]{1,0:T(8,128)(2,1)S(1)}, bf16[64,128]{1,0:T(8,128)(2,1)S(1)}, u32[]{:S(2)}, u32[]{:S(2)}) collective-permute-start(bf16[64,128]{1,0:T(8,128)(2,1)S(1)} %get-tuple-element.20), channel_id=1, source_target_pairs={{1,0},{2,1},{3,2},{5,4},{6,5},{7,6},{9,8},{10,9},{11,10},{13,12},{... | collective-permute-start | bytes 49160 | tf_op jit(solution)/shard_map/ppermute | solution.py:443
  2.7 6.0 %collective-permute-start = (bf16[64,128]{1,0:T(8,128)(2,1)S(1)}, bf16[64,128]{1,0:T(8,128)(2,1)S(1)}, u32[]{:S(2)}, u32[]{:S(2)}) collective-permute-start(bf16[64,128]{1,0:T(8,128)(2,1)S(1)} %get-tuple-element.21), channel_id=1, source_target_pairs={{0,1},{1,2},{2,3},{4,5},{5,6},{6,7},{8,9},{9,10},{10,11},{12,13},{... | collective-permute-start | bytes 49160 | tf_op jit(solution)/shard_map/ppermute | solution.py:442
  14.3 52.9 %copy-start.2 = (s32[1,1,64]{2,1,0:T(1,128)S(1)}, s32[1,1,64]{2,1,0:T(1,128)}, u32[]{:S(2)}) copy-start(s32[1,1,64]{2,1,0:T(1,128)} %param.17) | copy-start | bytes 772
  14.3 52.9 %all-to-all-start = ((bf16[64,96,128]{2,1,0:T(8,128)(2,1)}), bf16[64,96,128]{2,1,0:T(8,128)(2,1)S(1)}, u32[]{:S(2)}, u32[]{:S(2)}) async-start(bf16[64,96,128]{2,1,0:T(8,128)(2,1)} %get-tuple-element.12), calls=%async_computation | async-start | bytes 3145728 | tf_op jit(solution)/shard_map/all_to_all | solution.py:429
  69.9 39.9 %all-to-all-start.1 = ((bf16[64,80,128]{2,1,0:T(8,128)(2,1)}), bf16[64,80,128]{2,1,0:T(8,128)(2,1)S(1)}, u32[]{:S(2)}, u32[]{:S(2)}) async-start(bf16[64,80,128]{2,1,0:T(8,128)(2,1)} %get-tuple-element.13), calls=%async_computation.1 | async-start | bytes 2621440 | tf_op jit(solution)/shard_map/all_to_all | solution.py:429
  76.5 43.8 %copy-start = (f32[64,2048]{1,0:T(8,128)S(1)}, f32[64,2048]{1,0:T(8,128)}, u32[]{:S(2)}) copy-start(f32[64,2048]{1,0:T(8,128)} %get-tuple-element.15.forward_ref) | copy-start | bytes 1572868
  76.5 47.9 %copy-start.1 = (bf16[2048,64]{0,1:T(8,128)(2,1)S(1)}, bf16[2048,64]{0,1:T(8,128)(2,1)}, u32[]{:S(2)}) copy-start(bf16[2048,64]{0,1:T(8,128)(2,1)} %param.11) | copy-start | bytes 786436
  114.3 7.2 %collective-permute-start.2 = (bf16[4,64,128]{2,1,0:T(8,128)(2,1)S(1)}, bf16[4,64,128]{2,1,0:T(8,128)(2,1)S(1)}, u32[]{:S(2)}, u32[]{:S(2)}) collective-permute-start(bf16[4,64,128]{2,1,0:T(8,128)(2,1)S(1)} %get-tuple-element.17), channel_id=1, source_target_pairs={{0,1},{1,2},{2,3},{3,0},{4,5},{5,6},{6,7},{7,4},{8,9},{9,10},{10,1... | collective-permute-start | bytes 196616 | tf_op jit(solution)/shard_map/ppermute | solution.py:454
  117.3 5.8 %collective-permute-start.3 = (bf16[4,64,128]{2,1,0:T(8,128)(2,1)S(1)}, bf16[4,64,128]{2,1,0:T(8,128)(2,1)S(1)}, u32[]{:S(2)}, u32[]{:S(2)}) collective-permute-start(bf16[4,64,128]{2,1,0:T(8,128)(2,1)S(1)} %get-tuple-element.18), channel_id=1, source_target_pairs={{0,2},{1,3},{2,0},{3,1},{4,6},{5,7},{6,4},{7,5},{8,10},{9,11},{10,... | collective-permute-start | bytes 196616 | tf_op jit(solution)/shard_map/ppermute | solution.py:454
  120.2 4.3 %collective-permute-start.4 = (bf16[4,64,128]{2,1,0:T(8,128)(2,1)S(1)}, bf16[4,64,128]{2,1,0:T(8,128)(2,1)S(1)}, u32[]{:S(2)}, u32[]{:S(2)}) collective-permute-start(bf16[4,64,128]{2,1,0:T(8,128)(2,1)S(1)} %get-tuple-element.19), channel_id=1, source_target_pairs={{0,3},{1,0},{2,1},{3,2},{4,7},{5,4},{6,5},{7,6},{8,11},{9,8},{10,9... | collective-permute-start | bytes 196616 | tf_op jit(solution)/shard_map/ppermute | solution.py:454

commit v8 on v6

--- a/solution.py
+++ b/solution.py
@@ -8,7 +8,8 @@
 T = 128
 SMOOTH = 8
 RELAX = 0.25
-SECTION = 32
+PER = 16
+ROOM = 32
 MIB = 2**20
 F32, BF16 = jnp.float32, jnp.bfloat16
 NT = (((1,), (1,)), ((), ()))
@@ -46,81 +47,46 @@
     return pl.ds(pl.multiple_of(block * T, T), T)
 
 
-def first_call(entry, place, slot, count, numbers, projections, left, right, taps, image, library):
+def first_call(entry, place, slot, count, numbers, projections, image, library):
     slices, columns = projections.shape
     entries, capacity = library.shape[0], entry.shape[1]
     blocks = image.shape[1] // T
     owners = slices
-    per = columns // T
-    rows = slices + SECTION
+    rows = slices + PER
     parts = 4
-    loads = per + blocks + 5
+    loads = blocks + 6
 
     def kernel(
-        entry_hbm, place_hbm, slot_hbm, count_ref, n_hbm, x_hbm, l_ref, r_ref, taps_ref, image_hbm, library_hbm,
-        phase_ref, send_ref, entry_ref, place_ref, slot_ref, n_ref, library_ref, wide, band, spread, row, line,
+        entry_hbm, place_hbm, slot_hbm, count_ref, n_hbm, x_hbm, image_hbm, library_hbm,
+        send_ref, head_ref, tail_ref, row_ref, entry_ref, place_ref, slot_ref, n_ref, library_ref, x_ref, spread,
         stacked, product, total, packed, section, sems, load_sems,
     ):
-        def block(n):
-            return pl.ds(n * slices, slices)
-
-        pairs = [(x_hbm.at[:, pl.ds(b * T, T)], wide.at[block(b + 2)]) for b in range(per)]
-        pairs += [(n_hbm, n_ref)]
-        early = len(pairs)
-        pairs += [(library_hbm, library_ref)]
-        pairs += [(image_hbm.at[:, pl.ds(i * T, T)], stacked.at[block(i)]) for i in range(blocks)]
-        late = len(pairs)
+        pairs = [(x_hbm, x_ref), (n_hbm, n_ref), (library_hbm, library_ref)]
+        pairs += [
+            (image_hbm.at[:, pl.ds(i * T, T)], stacked.at[pl.ds(i * slices, slices)]) for i in range(blocks)
+        ]
         pairs += [(entry_hbm, entry_ref), (place_hbm, place_ref), (slot_hbm, slot_ref)]
         fetches = [pltpu.make_async_copy(a, b, load_sems.at[n]) for n, (a, b) in enumerate(pairs)]
         for fetch in fetches:
             fetch.start()
-
-        spread[...] = jnp.zeros_like(spread)
-        row[...] = jnp.zeros_like(row)
-        wide[block(0), :] = jnp.zeros((slices, T), BF16)
-        wide[block(1), :] = l_ref[...]
-        wide[block(per + 2), :] = r_ref[...]
-        wide[block(per + 3), :] = jnp.zeros((slices, T), BF16)
-        line[...] = jnp.zeros_like(line)
-        line[0:1, : taps_ref.shape[1]] = taps_ref[...].astype(F32)
-        spun = pltpu.roll(jnp.broadcast_to(line[0:1, :], (T, 3 * T)), T // 2, 1, stride=1, stride_axis=0)
-        band[...] = spun.astype(BF16)
-        for fetch in fetches[:early]:
+        total[...] = jnp.zeros_like(total)
+        row_ref[...] = jnp.zeros_like(row_ref)
+        for fetch in fetches[:2]:
             fetch.wait()
-        filtered = sum(
-            lax.dot_general(
-                wide[n * slices : (n + per + 2) * slices, :],
-                band[:, n * T : (n + 1) * T],
-                NT,
-                preferred_element_type=F32,
-            )
-            for n in range(3)
-        ).astype(BF16)
-
-        def put(at, value):
-            spread[pl.ds(at, slices, stride=SECTION), :] = value.astype(F32)
-
-        for b in range(per):
-            value = filtered[(b + 1) * slices : (b + 2) * slices]
-            phase_ref[:, b * T : (b + 1) * T] = value
-            put(b, value)
-        put(per, filtered[:slices])
-        put(per + 1, filtered[(per + 1) * slices :])
-        row[0:1, :owners] = n_ref[...].astype(F32)
-        put(per + 2, jnp.broadcast_to(row[0:1, :], (slices, T)))
-        section[...] = spread[...].astype(BF16).reshape(slices, SECTION, T)
-        copies = [pltpu.make_async_copy(section, send_ref.at[:, pl.ds(slices, SECTION), :], sems.at[parts])]
+        head_ref[...] = x_ref[:, :T]
+        tail_ref[...] = x_ref[:, columns - T :]
+        row_ref[0:1, :owners] = n_ref[...]
+        for b in range(PER):
+            spread[pl.ds(b, slices, stride=PER), :] = x_ref[:, b * T : (b + 1) * T].astype(F32)
+        section[...] = spread[...].astype(BF16).reshape(slices, PER, T)
+        copies = [pltpu.make_async_copy(section, send_ref.at[:, pl.ds(slices, PER), :], sems.at[parts])]
         copies[0].start()
-
-        total[...] = jnp.zeros_like(total)
-        for fetch in fetches[early:late]:
+        for fetch in fetches[2:]:
             fetch.wait()
         for e in range(0, entries, 2):
             product[:, e * T : (e + 2) * T] = lax.dot_general(
                 stacked[...], library_ref[e : e + 2].reshape(2 * T, T), NT, preferred_element_type=F32
             )
-        for fetch in fetches[late:]:
-            fetch.wait()
 
         def add(k):
             live = k < count_ref[0, 0]
@@ -149,27 +115,26 @@
     return pl.pallas_call(
         kernel,
         out_shape=[
-            jax.ShapeDtypeStruct((slices, columns), BF16),
             pltpu.HBM((owners, rows, T), BF16),
-        ],
-        in_specs=[HBM] * 3 + [SMEM] + [HBM] * 2 + [VMEM] * 3 + [HBM] * 2,
-        out_specs=[VMEM, HBM],
+            jax.ShapeDtypeStruct((slices, T), BF16),
+            jax.ShapeDtypeStruct((slices, T), BF16),
+            jax.ShapeDtypeStruct((8, T), jnp.int32),
+        ],
+        in_specs=[HBM] * 3 + [SMEM] + [HBM] * 4,
+        out_specs=[HBM] + [VMEM] * 3,
         scratch_shapes=[
             pltpu.SMEM(entry.shape, jnp.int32),
             pltpu.SMEM(place.shape, jnp.int32),
             pltpu.SMEM(slot.shape, jnp.int32),
             pltpu.VMEM(numbers.shape, jnp.int32),
             pltpu.VMEM(library.shape, BF16),
-            pltpu.VMEM(((per + 4) * slices, T), BF16),
-            pltpu.VMEM((T, 3 * T), BF16),
-            pltpu.VMEM((slices * SECTION, T), F32),
-            pltpu.VMEM((8, T), F32),
-            pltpu.VMEM((8, 3 * T), F32),
+            pltpu.VMEM((slices, columns), BF16),
+            pltpu.VMEM((slices * PER, T), F32),
             pltpu.VMEM((blocks * slices, T), BF16),
             pltpu.VMEM((blocks * slices, entries * T), F32),
             pltpu.VMEM((owners + 1, slices, T), F32),
             pltpu.VMEM((owners, slices, T), BF16),
-            pltpu.VMEM((slices, SECTION, T), BF16),
+            pltpu.VMEM((slices, PER, T), BF16),
             pltpu.SemaphoreType.DMA((parts + 1,)),
             pltpu.SemaphoreType.DMA((loads,)),
         ],
@@ -177,19 +142,84 @@
         cost_estimate=pl.CostEstimate(
             flops=2 * capacity * slices * T * T, bytes_accessed=8 * 2**20, transcendentals=0
         ),
-        name="filter_and_forward",
-    )(*map(in_hbm, (entry, place, slot)), count, *map(in_hbm, (numbers, projections)), left, right, taps,
-      *map(in_hbm, (image, library)))
-
-
-def stripe_of(quarter, quarters, arrived_ref, offset, values, rimmed):
-    angles = arrived_ref.shape[0]
-    values[...] = arrived_ref[:, offset:, :].astype(F32)
+        name="forward_tiles",
+    )(*map(in_hbm, (entry, place, slot)), count, *map(in_hbm, (numbers, projections, image, library)))
+
+
+def phase_call(projections, left, right, taps):
+    slices, columns = projections.shape
+    per = columns // T
+
+    def kernel(x_hbm, l_ref, r_ref, taps_hbm, phase_ref, band_ref, taps_ref, line, wide, sems):
+        fetches = [
+            pltpu.make_async_copy(x_hbm, wide.at[:, pl.ds(T, columns)], sems.at[0]),
+            pltpu.make_async_copy(taps_hbm, taps_ref, sems.at[1]),
+        ]
+        for fetch in fetches:
+            fetch.start()
+        wide[:, :T] = l_ref[...]
+        wide[:, T + columns :] = r_ref[...]
+        line[...] = jnp.zeros_like(line)
+        for fetch in fetches:
+            fetch.wait()
+        line[0:1, : taps_ref.shape[0]] = taps_ref[...].astype(F32).reshape(1, -1)
+        spun = pltpu.roll(jnp.broadcast_to(line[0:1, :], (T, 3 * T)), T // 2, 1, stride=1, stride_axis=0)
+        band_ref[...] = spun.astype(BF16)
+        for b in range(per):
+            phase_ref[:, b * T : (b + 1) * T] = lax.dot_general(
+                wide[:, b * T : (b + 3) * T], band_ref[...], NT, preferred_element_type=F32
+            ).astype(BF16)
+
+    return pl.pallas_call(
+        kernel,
+        out_shape=[
+            jax.ShapeDtypeStruct((slices, columns), BF16),
+            jax.ShapeDtypeStruct((T, 3 * T), BF16),
+        ],
+        in_specs=[HBM, VMEM, VMEM, HBM],
+        out_specs=[VMEM, VMEM],
+        scratch_shapes=[
+            pltpu.VMEM(taps.shape, BF16),
+            pltpu.VMEM((8, 3 * T), F32),
+            pltpu.VMEM((slices, columns + 2 * T), BF16),
+            pltpu.SemaphoreType.DMA((2,)),
+        ],
+        compiler_params=params(),
+        cost_estimate=pl.CostEstimate(flops=2**26, bytes_accessed=2**20, transcendentals=0),
+        name="phase_filter",
+    )(in_hbm(projections), left, right, in_hbm(taps))
+
+
+def rim_call(arrived, band, rows_by_z):
+    angles = arrived.shape[0]
+    size = arrived.shape[1] - PER
+
+    def kernel(arrived_ref, _, *refs):
+        n = len(rows_by_z)
+        z_refs, (head_ref, tail_ref, stack_ref, flat) = refs[:n], refs[n:]
+        for m, ref in enumerate(z_refs):
+            stack_ref[m : m + 1, :] = ref[0:1, :]
+        flat[...] = arrived_ref[:, size:, :].astype(F32).reshape(angles * PER, T)
+        head_ref[...] = flat[pl.ds(0, angles, stride=PER), :].astype(BF16)
+        tail_ref[...] = flat[pl.ds(PER - 1, angles, stride=PER), :].astype(BF16)
+
+    return pl.pallas_call(
+        kernel,
+        out_shape=[jax.ShapeDtypeStruct((angles, T), BF16)] * 2 + [jax.ShapeDtypeStruct((8, T), jnp.int32)],
+        in_specs=[VMEM, HBM] + [VMEM] * len(rows_by_z),
+        out_specs=[VMEM] * 3,
+        scratch_shapes=[pltpu.VMEM((angles * PER, T), F32)],
+        compiler_params=params(),
+        cost_estimate=pl.CostEstimate(flops=2**17, bytes_accessed=2**18, transcendentals=0),
+        name="rim",
+    )(arrived, band, *rows_by_z)
+
+
+def stripe_of(quarter, quarters, angles, values, rimmed):
     network = middle_network(angles)
 
     def middle(g, carry):
-        rows = pl.ds(pl.multiple_of(g * 8, 8), 8)
-        v = [values[a, rows, :] for a in range(angles)]
+        v = [values[pl.ds(pl.multiple_of(a * ROOM + g * 8, 8), 8), :] for a in range(angles)]
         for a, b, low, high in network:
             x, y = v[a], v[b]
             if low:
@@ -215,30 +245,29 @@
     return cur - total / count.astype(F32)
 
 
-def back_call(carried, quarter, arrived, phase, quarters):
+def back_call(carried, arrived, phase, stacked):
     owners = arrived.shape[0]
     size, columns = phase.shape
-    rows = size + 16
+    rows = size + PER
     parts = 4
 
     def kernel(
-        c_ref, q_ref, arrived_ref, phase_ref, forward_hbm, send_ref, values, rimmed, forward, less, packed, sems
+        c_ref, arrived_ref, phase_ref, stacked_ref, forward_hbm, send_ref, stack_ref, forward, less, packed, sems
     ):
         forward[...] = jnp.zeros_like(forward)
         for d in range(owners):
             forward[:, lanes(c_ref[0, d])] += arrived_ref[d, :size, :].astype(F32)
         copies = [pltpu.make_async_copy(forward, forward_hbm, sems.at[parts])]
         copies[0].start()
-        stripe = stripe_of(q_ref[0], quarters, arrived_ref, size, values, rimmed).astype(BF16)
         less[...] = (phase_ref[...].astype(F32) - forward[...]).astype(BF16)
         step = owners // parts
         for n in range(parts):
             for d in range(n * step, (n + 1) * step):
-                packed[d, :size, :] = less[:, lanes(c_ref[0, d])]
-                packed[d, size:, :] = stripe
+                packed[d] = less[:, lanes(c_ref[0, d])]
             here = pl.ds(n * step, step)
-            copies.append(pltpu.make_async_copy(packed.at[here], send_ref.at[here], sems.at[n]))
+            copies.append(pltpu.make_async_copy(packed.at[here], send_ref.at[here, pl.ds(0, size), :], sems.at[n]))
             copies[-1].start()
+        stack_ref[...] = stacked_ref[...]
         for copy in copies:
             copy.wait()
 
@@ -247,38 +276,91 @@
         out_shape=[
             pltpu.HBM((size, columns), F32),
             pltpu.HBM((owners, rows, T), BF16),
-        ],
-        in_specs=[SMEM, SMEM, VMEM, VMEM],
-        out_specs=[HBM, HBM],
+            jax.ShapeDtypeStruct((8, T), jnp.int32),
+        ],
+        in_specs=[SMEM] + [VMEM] * 3,
+        out_specs=[HBM, HBM, VMEM],
         scratch_shapes=[
-            pltpu.VMEM((owners, SECTION, T), F32),
-            pltpu.VMEM((32, T), F32),
             pltpu.VMEM((size, columns), F32),
             pltpu.VMEM((size, columns), BF16),
-            pltpu.VMEM((owners, rows, T), BF16),
+            pltpu.VMEM((owners, size, T), BF16),
             pltpu.SemaphoreType.DMA((parts + 1,)),
         ],
         compiler_params=params(),
         cost_estimate=pl.CostEstimate(flops=2**24, bytes_accessed=8 * 2**20, transcendentals=0),
-        name="sum_and_stripe",
-    )(carried, quarter, arrived, phase)
-
-
-def counts_call(entry, place, slot, count, owner, arrived, entries, blocks):
+        name="slot_sums",
+    )(carried, arrived, phase, stacked)
+
+
+def stripe_call(quarter, arrived, left, right, band, back, quarters):
+    angles = arrived.shape[0]
+    size = arrived.shape[1] - PER
+
+    def kernel(
+        q_ref, arrived_ref, l_ref, r_ref, band_ref, _, back_ref, flat, wide, values, rimmed, repeated, sem
+    ):
+        def block(n):
+            return pl.ds(n * angles, angles)
+
+        flat[...] = arrived_ref[:, size:, :].astype(F32).reshape(angles * PER, T)
+        for b in range(PER):
+            wide[block(b + 2), :] = flat[pl.ds(b, angles, stride=PER), :].astype(BF16)
+        wide[block(0), :] = jnp.zeros((angles, T), BF16)
+        wide[block(1), :] = l_ref[...]
+        wide[block(PER + 2), :] = r_ref[...]
+        wide[block(PER + 3), :] = jnp.zeros((angles, T), BF16)
+        values[...] = jnp.zeros_like(values)
+        filtered = sum(
+            lax.dot_general(
+                wide[n * angles : (n + PER + 2) * angles, :],
+                band_ref[:, n * T : (n + 1) * T],
+                NT,
+                preferred_element_type=F32,
+            )
+            for n in range(3)
+        ).astype(BF16)
+        for at, b in enumerate([*range(1, PER + 1), 0, PER + 1]):
+            values[pl.ds(at, angles, stride=ROOM), :] = filtered[b * angles : (b + 1) * angles].astype(F32)
+        stripe = stripe_of(q_ref[0], quarters, angles, values, rimmed).astype(BF16)
+        repeated[...] = jnp.broadcast_to(stripe[None], repeated.shape)
+        copy = pltpu.make_async_copy(repeated, back_ref.at[:, pl.ds(size, PER), :], sem)
+        copy.start()
+        copy.wait()
+
+    return pl.pallas_call(
+        kernel,
+        out_shape=pltpu.HBM(back.shape, BF16),
+        in_specs=[SMEM] + [VMEM] * 4 + [HBM],
+        out_specs=HBM,
+        scratch_shapes=[
+            pltpu.VMEM((angles * PER, T), F32),
+            pltpu.VMEM(((PER + 4) * angles, T), BF16),
+            pltpu.VMEM((angles * ROOM, T), F32),
+            pltpu.VMEM((32, T), F32),
+            pltpu.VMEM((angles, PER, T), BF16),
+            pltpu.SemaphoreType.DMA,
+        ],
+        input_output_aliases={5: 0},
+        compiler_params=params(),
+        cost_estimate=pl.CostEstimate(flops=2**26, bytes_accessed=2**20, transcendentals=0),
+        name="stripe",
+    )(quarter, arrived, left, right, band, in_hbm(back))
+
+
+def counts_call(entry, place, slot, count, owner, stacks, owners, entries, blocks):
     capacity = entry.shape[1]
-    owners = arrived.shape[0]
-    size = arrived.shape[1] - SECTION
 
     def kernel(
-        entry_hbm, place_hbm, slot_hbm, count_ref, owner_ref, arrived_ref,
-        weights_ref, entry_ref, place_ref, slot_ref, loads,
+        entry_hbm, place_hbm, slot_hbm, count_ref, owner_ref, *refs
     ):
+        n = len(stacks)
+        stack_refs, (weights_ref, entry_ref, place_ref, slot_ref, loads) = refs[:n], refs[n:]
         pairs = [(entry_hbm, entry_ref), (place_hbm, place_ref), (slot_hbm, slot_ref)]
         fetches = [pltpu.make_async_copy(a, b, loads.at[n]) for n, (a, b) in enumerate(pairs)]
         for fetch in fetches:
             fetch.start()
         lane = lax.broadcasted_iota(jnp.int32, (owners, T), 1)
-        numbers = arrived_ref[:, size + 16 :, :].astype(F32)[:, 2, :]
+        numbers = jnp.concatenate([ref[...] for ref in stack_refs], axis=0).astype(F32)
         theirs = jnp.sum(jnp.where(lane == owner_ref[0], numbers, 0.0), axis=1, keepdims=True)
         carries = (theirs.astype(jnp.int32) + owners == lane).astype(F32).astype(BF16)
 
@@ -291,13 +373,16 @@
         of_bin = ones(entries * blocks, jnp.where(live, entry_ref[...] * blocks + place_ref[...], -1))
         of_slot = ones(T, slot_ref[...])
         met = lax.dot_general(of_bin, of_slot, NT, preferred_element_type=F32)
-        stripe_met = jnp.dot(met[:, :owners].astype(BF16), carries, preferred_element_type=F32)
+        k = lax.broadcasted_iota(jnp.int32, (owners, capacity), 0)
+        by_row = (owner_ref[0] ^ ((k & 7) * 8 + (k >> 3))) == slot_ref[...]
+        met_by_row = lax.dot_general(of_bin, by_row.astype(F32).astype(BF16), NT, preferred_element_type=F32)
+        stripe_met = jnp.dot(met_by_row.astype(BF16), carries, preferred_element_type=F32)
         weights_ref[...] = (met - stripe_met).astype(BF16)
 
     return pl.pallas_call(
         kernel,
         out_shape=jax.ShapeDtypeStruct((entries * blocks, T), BF16),
-        in_specs=[HBM] * 3 + [SMEM, SMEM, VMEM],
+        in_specs=[HBM] * 3 + [SMEM, SMEM] + [VMEM] * len(stacks),
         out_specs=VMEM,
         scratch_shapes=[
             pltpu.VMEM(entry.shape, jnp.int32),
@@ -308,7 +393,7 @@
         compiler_params=params(),
         cost_estimate=pl.CostEstimate(flops=2**24, bytes_accessed=2**20, transcendentals=0),
         name="tile_counts",
-    )(*map(in_hbm, (entry, place, slot)), count, owner, arrived)
+    )(*map(in_hbm, (entry, place, slot)), count, owner, *stacks)
 
 
 def adjoint_call(quarter, weights, returned, library, blocks, quarters):
@@ -434,16 +519,29 @@
     tiles = (tile_entry[0], tile_image[0], tile_slot[0], tile_count)
     carried = slot_block[0]
 
-    left = lax.ppermute(projections[:, -T:], "ray", [(i, i + 1) for i in range(quarters - 1)])
-    right = lax.ppermute(projections[:, :T], "ray", [(i + 1, i) for i in range(quarters - 1)])
-    taps = phase_kernel.reshape(1, -1)
-    phase, send = first_call(*tiles, carried, projections, left, right, taps, image, library)
-    arrived = exchanged(send, "dom")
-    forward, back = back_call(carried, quarter, arrived, phase, quarters)
+    owners = lax.axis_size("dom")
     owner = lax.axis_index("dom").astype(jnp.int32).reshape(1)
     blocks = image.shape[1] // T
-    weights = counts_call(*tiles, owner, arrived, library.shape[0], blocks)
+
+    def rims(head, tail):
+        left = lax.ppermute(tail, "ray", [(i, i + 1) for i in range(quarters - 1)])
+        right = lax.ppermute(head, "ray", [(i + 1, i) for i in range(quarters - 1)])
+        return left, right
+
+    def swapped(array, m):
+        return lax.ppermute(array, "dom", [(i, i ^ m) for i in range(owners)])
+
+    send, head, tail, row = first_call(*tiles, carried, projections, image, library)
+    arrived = exchanged(send, "dom")
+    phase, band = phase_call(projections, *rims(head, tail), phase_kernel)
+    rows_by_z = [row] + [swapped(row, m * 8) for m in range(1, 8)]
+    head, tail, stacked = rim_call(arrived, band, rows_by_z)
+    left, right = rims(head, tail)
+    forward, back, stack = back_call(carried, arrived, phase, stacked)
+    back = stripe_call(quarter, arrived, left, right, band, back, quarters)
     returned = exchanged(back, "dom")
+    stacks = [stack] + [swapped(stack, m) for m in range(1, 8)]
+    weights = counts_call(*tiles, owner, stacks, owners, library.shape[0], blocks)
     own, *sent, stripe = adjoint_call(quarter, weights, returned, library, blocks, quarters)
     others = [
         lax.ppermute(part, "ray", [(i, (i + m) % quarters) for i in range(quarters)])

time: 126 us -> 129 us (1.024)
  starting transfers between devices: 31.1 us -> 62.6 us
  waiting for transfers between devices: 75.7 us -> 46.4 us
  Pallas kernels: 15.7 us -> 18.1 us
  local copies, waits for them, and re-layouts: 1.42 us -> 0.02 us
    all_to_all x2, waiting for transfers between devices: 73.3 us -> 23.1 us  [exchanged(): return lax.all_to_all(array, axis, split_axis=0, concat_axis=0, tiled=True)]
    ppermute x2 -> x18, starting transfers between devices: 5.83 us -> 34.5 us  [the longest x14 25.6 us: swapped(): return lax.ppermute(array, 'dom', [(i, i ^ m) for i in range(owners)])]
    ppermute x2 -> x18, waiting for transfers between devices: 0.12 us -> 21.9 us  [the longest x14 19.9 us: swapped(): return lax.ppermute(array, 'dom', [(i, i ^ m) for i in range(owners)])]
    all_to_all x2, starting transfers between devices: 18.7 us -> 22.2 us  [exchanged(): return lax.all_to_all(array, axis, split_axis=0, concat_axis=0, tiled=True)]
    pallas_call x1 -> x4, Pallas kernels: 5.82 us -> 8.58 us  [the longest x1 4.27 us: first_call(): pl.pallas_call(kernel, out_shape=[pltpu.HBM((owners, rows, T), BF16), jax...]
  transfers between devices with their start and end apart: 7 -> 23, of which waited for: 5 -> 7; matrix products, arithmetic and copies ran while one was open for 1% -> 0% of each run, Pallas kernels for 2% -> 5%
where the time goes in v8:
time: 129 us
  starting transfers between devices  62.6 us (49%)
  waiting for transfers between devices  46.4 us (36%)
  Pallas kernels  18.1 us (14%)
  between operations  1.49 us (1%)
    ppermute x14, starting transfers between devices, swapped(): return lax.ppermute(array, 'dom', [(i, i ^ m) for i in range(owners)])  25.6 us
    all_to_all x2, waiting for transfers between devices, exchanged(): return lax.all_to_all(array, axis, split_axis=0, concat_axis=0, tiled=True)  23.1 us
    all_to_all x2, starting transfers between devices, exchanged(): return lax.all_to_all(array, axis, split_axis=0, concat_axis=0, tiled=True)  22.2 us
    ppermute x14, waiting for transfers between devices, swapped(): return lax.ppermute(array, 'dom', [(i, i ^ m) for i in range(owners)])  19.9 us
    ppermute x2, starting transfers between devices, rims(): left = lax.ppermute(tail, 'ray', [(i, i + 1) for i in range(quarters - 1)])  6.26 us
    ppermute x3, starting transfers between devices, shards(): lax.ppermute(part, 'ray', [(i, (i + m) % quarters) for i in range(quarter...  5.88 us
    pallas_call x1, Pallas kernels, adjoint_call(): pl.pallas_call(kernel, out_shape=[*(jax.ShapeDtypeStruct((held, size, T),...  4.58 us
    pallas_call x1, Pallas kernels, first_call(): pl.pallas_call(kernel, out_shape=[pltpu.HBM((owners, rows, T), BF16), jax...  4.27 us
  transfers between devices with their start and end apart: 23, of which 7 were waited for; matrix products, arithmetic and copies ran while one was open for 0% of the time, Pallas kernels for 5%

profile of v8, /device:TPU:8, one launch (start us, length us, event | category | flops | bytes accessed | tf_op | source)
XLA Modules:
  0.0 128.6 jit_solution(15423876408715389344)
XLA Ops:
  1.3 4.3 %forward_tiles.1 = (bf16[64,80,128]{2,1,0:T(8,128)(2,1)}, bf16[64,128]{1,0:T(8,128)(2,1)S(1)}, bf16[64,128]{1,0:T(8,128)(2,1)S(1)}, s32[8,128]{1,0:T(8,128)S(1)}) custom-call(s32[1,256]{1,0:T(1,128)} %bitcast.19, s32[1,256]{1,0:T(1,128)} %bitcast.21, s32[1,256]{1,0:T(1,128)} %bitcast.23, s32[1,1]{1,0:T(1,128)S(6)} %copy.13.count_ref, s32[1,64]{1,0:T(1,128)} %bitcast.13, ...), custom_call_target="tpu_custom_call" | custom-call | flops 536870912 | bytes 8388608 | tf_op jit(solution)/shard_map/forward_tiles/pallas_call | solution.py:115
  5.6 13.3 %all-to-all-start = ((bf16[64,80,128]{2,1,0:T(8,128)(2,1)}), bf16[64,80,128]{2,1,0:T(8,128)(2,1)S(1)}, u32[]{:S(2)}, u32[]{:S(2)}) async-start(bf16[64,80,128]{2,1,0:T(8,128)(2,1)} %get-tuple-element.22), calls=%async_computation | async-start | bytes 2621440 | tf_op jit(solution)/shard_map/all_to_all | solution.py:509
  18.9 3.1 %collective-permute-start = (bf16[64,128]{1,0:T(8,128)(2,1)S(1)}, bf16[64,128]{1,0:T(8,128)(2,1)S(1)}, u32[]{:S(2)}, u32[]{:S(2)}) collective-permute-start(bf16[64,128]{1,0:T(8,128)(2,1)S(1)} %get-tuple-element.19), channel_id=1, source_target_pairs={{0,1},{1,2},{2,3},{4,5},{5,6},{6,7},{8,9},{9,10},{10,11},{12,13},{... | collective-permute-start | bytes 49160 | tf_op jit(solution)/shard_map/ppermute | solution.py:527
  22.0 1.3 %collective-permute-start.1 = (bf16[64,128]{1,0:T(8,128)(2,1)S(1)}, bf16[64,128]{1,0:T(8,128)(2,1)S(1)}, u32[]{:S(2)}, u32[]{:S(2)}) collective-permute-start(bf16[64,128]{1,0:T(8,128)(2,1)S(1)} %get-tuple-element.20), channel_id=1, source_target_pairs={{1,0},{2,1},{3,2},{5,4},{6,5},{7,6},{9,8},{10,9},{11,10},{13,12},{... | collective-permute-start | bytes 49160 | tf_op jit(solution)/shard_map/ppermute | solution.py:528
  23.3 3.0 %collective-permute-start.8 = (s32[8,128]{1,0:T(8,128)S(1)}, s32[8,128]{1,0:T(8,128)S(1)}, u32[]{:S(2)}, u32[]{:S(2)}) collective-permute-start(s32[8,128]{1,0:T(8,128)S(1)} %get-tuple-element.24.refs_0_), channel_id=1, source_target_pairs={{0,224},{4,228},{8,232},{12,236},{16,240},{20,244},{24,248},{28,25... | collective-permute-start | bytes 12296 | tf_op jit(solution)/shard_map/ppermute | solution.py:532
  26.3 2.1 %collective-permute-start.7 = (s32[8,128]{1,0:T(8,128)S(1)}, s32[8,128]{1,0:T(8,128)S(1)}, u32[]{:S(2)}, u32[]{:S(2)}) collective-permute-start(s32[8,128]{1,0:T(8,128)S(1)} %get-tuple-element.24.refs_0_), channel_id=1, source_target_pairs={{0,192},{4,196},{8,200},{12,204},{16,208},{20,212},{24,216},{28,22... | collective-permute-start | bytes 12296 | tf_op jit(solution)/shard_map/ppermute | solution.py:532
  28.4 3.7 %collective-permute-start.6 = (s32[8,128]{1,0:T(8,128)S(1)}, s32[8,128]{1,0:T(8,128)S(1)}, u32[]{:S(2)}, u32[]{:S(2)}) collective-permute-start(s32[8,128]{1,0:T(8,128)S(1)} %get-tuple-element.24.refs_0_), channel_id=1, source_target_pairs={{0,160},{4,164},{8,168},{12,172},{16,176},{20,180},{24,184},{28,18... | collective-permute-start | bytes 12296 | tf_op jit(solution)/shard_map/ppermute | solution.py:532
  32.1 16.8 %collective-permute-done.8.refs_7_ = s32[8,128]{1,0:T(8,128)S(1)} collective-permute-done((s32[8,128]{1,0:T(8,128)S(1)}, s32[8,128]{1,0:T(8,128)S(1)}, u32[]{:S(2)}, u32[]{:S(2)}) %collective-permute-start.8) | collective-permute-done | bytes 4128 | tf_op jit(solution)/shard_map/ppermute | solution.py:532
  48.9 5.3 %collective-permute-start.5 = (s32[8,128]{1,0:T(8,128)S(1)}, s32[8,128]{1,0:T(8,128)S(1)}, u32[]{:S(2)}, u32[]{:S(2)}) collective-permute-start(s32[8,128]{1,0:T(8,128)S(1)} %get-tuple-element.24.refs_0_), channel_id=1, source_target_pairs={{0,128},{4,132},{8,136},{12,140},{16,144},{20,148},{24,152},{28,15... | collective-permute-start | bytes 12296 | tf_op jit(solution)/shard_map/ppermute | solution.py:532
  54.3 2.6 %collective-permute-start.3 = (s32[8,128]{1,0:T(8,128)S(1)}, s32[8,128]{1,0:T(8,128)S(1)}, u32[]{:S(2)}, u32[]{:S(2)}) collective-permute-start(s32[8,128]{1,0:T(8,128)S(1)} %get-tuple-element.24.refs_0_), channel_id=1, source_target_pairs={{0,64},{4,68},{8,72},{12,76},{16,80},{20,84},{24,88},{28,92},{32,9... | collective-permute-start | bytes 12296 | tf_op jit(solution)/shard_map/ppermute | solution.py:532
  56.9 1.7 %collective-permute-start.2 = (s32[8,128]{1,0:T(8,128)S(1)}, s32[8,128]{1,0:T(8,128)S(1)}, u32[]{:S(2)}, u32[]{:S(2)}) collective-permute-start(s32[8,128]{1,0:T(8,128)S(1)} %get-tuple-element.24.refs_0_), channel_id=1, source_target_pairs={{0,32},{4,36},{8,40},{12,44},{16,48},{20,52},{24,56},{28,60},{32,0... | collective-permute-start | bytes 12296 | tf_op jit(solution)/shard_map/ppermute | solution.py:532
  58.6 1.9 %phase_filter.1 = (bf16[64,2048]{1,0:T(8,128)(2,1)S(1)}, bf16[128,384]{1,0:T(8,128)(2,1)S(1)}) custom-call(bf16[64,2048]{1,0:T(8,128)(2,1)} %bitcast.16, bf16[64,128]{1,0:T(8,128)(2,1)S(1)} %collective-permute-done.l_ref, bf16[64,128]{1,0:T(8,128)(2,1)S(1)} %collective-permute-done.1.r_ref, bf16[129]{0:T(256)(128)(2,1)} %taps_hbm.1), custom_call_target="tpu_custom_call" | custom-call | flops 67108864 | bytes 1048576 | tf_op jit(solution)/shard_map/phase_filter/pallas_call | solution.py:173
  60.7 3.1 %collective-permute-start.16 = (bf16[64,128]{1,0:T(8,128)(2,1)S(1)}, bf16[64,128]{1,0:T(8,128)(2,1)S(1)}, u32[]{:S(2)}, u32[]{:S(2)}) collective-permute-start(bf16[64,128]{1,0:T(8,128)(2,1)S(1)} %get-tuple-element.27), channel_id=1, source_target_pairs={{0,1},{1,2},{2,3},{4,5},{5,6},{6,7},{8,9},{9,10},{10,11},{12,13},{... | collective-permute-start | bytes 49160 | tf_op jit(solution)/shard_map/ppermute | solution.py:527
  63.8 1.3 %collective-permute-start.17 = (bf16[64,128]{1,0:T(8,128)(2,1)S(1)}, bf16[64,128]{1,0:T(8,128)(2,1)S(1)}, u32[]{:S(2)}, u32[]{:S(2)}) collective-permute-start(bf16[64,128]{1,0:T(8,128)(2,1)S(1)} %get-tuple-element.28), channel_id=1, source_target_pairs={{1,0},{2,1},{3,2},{5,4},{6,5},{7,6},{9,8},{10,9},{11,10},{13,12},{... | collective-permute-start | bytes 49160 | tf_op jit(solution)/shard_map/ppermute | solution.py:528
  65.1 2.3 %slot_sums.1 = (f32[64,2048]{1,0:T(8,128)}, bf16[64,80,128]{2,1,0:T(8,128)(2,1)}, s32[8,128]{1,0:T(8,128)S(1)}) custom-call(s32[1,64]{1,0:T(1,128)S(1)} %bitcast.14, bf16[64,80,128]{2,1,0:T(8,128)(2,1)S(1)} %all-to-all-done.arrived_ref, bf16[64,2048]{1,0:T(8,128)(2,1)S(1)} %get-tuple-element.21.phase_ref, s32[8,128]{1,0:T(8,128)S(1)} %get-tuple-element.25.stacked_ref), custom_call_target="tpu_custom_call" | custom-call | flops 16777216 | bytes 8388608 | tf_op jit(solution)/shard_map/slot_sums/pallas_call | solution.py:274
  67.4 2.0 %collective-permute-done.17.r_ref = bf16[64,128]{1,0:T(8,128)(2,1)S(1)} collective-permute-done((bf16[64,128]{1,0:T(8,128)(2,1)S(1)}, bf16[64,128]{1,0:T(8,128)(2,1)S(1)}, u32[]{:S(2)}, u32[]{:S(2)}) %collective-permute-start.17) | collective-permute-done | bytes 16416 | tf_op jit(solution)/shard_map/ppermute | solution.py:528
  69.4 2.3 %stripe.1 = bf16[64,80,128]{2,1,0:T(8,128)(2,1)} custom-call(s32[1]{0:T(128)} %bitcast.7.q_ref, bf16[64,80,128]{2,1,0:T(8,128)(2,1)S(1)} %all-to-all-done.arrived_ref, bf16[64,128]{1,0:T(8,128)(2,1)S(1)} %collective-permute-done.16.l_ref, bf16[64,128]{1,0:T(8,128)(2,1)S(1)} %collective-permute-done.17.r_ref, ...), custom_call_target="tpu_custom_call", output_to_operand_aliasing={{}: (5, {})} | custom-call | flops 67108864 | bytes 1048576 | tf_op jit(solution)/shard_map/stripe/pallas_call | solution.py:330
  71.8 8.9 %all-to-all-start.1 = ((bf16[64,80,128]{2,1,0:T(8,128)(2,1)}), bf16[64,80,128]{2,1,0:T(8,128)(2,1)S(1)}, u32[]{:S(2)}, u32[]{:S(2)}) async-start(bf16[64,80,128]{2,1,0:T(8,128)(2,1)} %stripe.1), calls=%async_computation.1 | async-start | bytes 2621440 | tf_op jit(solution)/shard_map/all_to_all | solution.py:509
  80.7 1.3 %collective-permute-start.15 = (s32[8,128]{1,0:T(8,128)S(1)}, s32[8,128]{1,0:T(8,128)S(1)}, u32[]{:S(2)}, u32[]{:S(2)}) collective-permute-start(s32[8,128]{1,0:T(8,128)S(1)} %get-tuple-element.26.refs_0_), channel_id=1, source_target_pairs={{0,28},{4,24},{8,20},{12,16},{16,12},{20,8},{24,4},{28,0},{32,60},... | collective-permute-start | bytes 12296 | tf_op jit(solution)/shard_map/ppermute | solution.py:532
  82.0 0.6 collective-permute-start.14
  82.6 3.0 %collective-permute-start.13 = (s32[8,128]{1,0:T(8,128)S(1)}, s32[8,128]{1,0:T(8,128)S(1)}, u32[]{:S(2)}, u32[]{:S(2)}) collective-permute-start(s32[8,128]{1,0:T(8,128)S(1)} %get-tuple-element.26.refs_0_), channel_id=1, source_target_pairs={{0,20},{4,16},{8,28},{12,24},{16,4},{20,0},{24,12},{28,8},{32,52},... | collective-permute-start | bytes 12296 | tf_op jit(solution)/shard_map/ppermute | solution.py:532
  85.9 1.2 collective-permute-start.11
  87.8 2.9 %collective-permute-done.12.refs_4_ = s32[8,128]{1,0:T(8,128)S(1)} collective-permute-done((s32[8,128]{1,0:T(8,128)S(1)}, s32[8,128]{1,0:T(8,128)S(1)}, u32[]{:S(2)}, u32[]{:S(2)}) %collective-permute-start.12) | collective-permute-done | bytes 4128 | tf_op jit(solution)/shard_map/ppermute | solution.py:532
  90.9 1.1 tile_counts.1.weights_ref
  92.1 23.1 %all-to-all-done.1.returned_ref = bf16[64,80,128]{2,1,0:T(8,128)(2,1)S(1)} async-done(((bf16[64,80,128]{2,1,0:T(8,128)(2,1)}), bf16[64,80,128]{2,1,0:T(8,128)(2,1)S(1)}, u32[]{:S(2)}, u32[]{:S(2)}) %all-to-all-start.1) | async-done | bytes 1310752 | tf_op jit(solution)/shard_map/all_to_all | solution.py:509
  115.1 4.6 %adjoint_tiles.1 = (f32[4,64,128]{2,1,0:T(8,128)S(1)}, bf16[4,64,128]{2,1,0:T(8,128)(2,1)S(1)}, bf16[4,64,128]{2,1,0:T(8,128)(2,1)S(1)}, bf16[4,64,128]{2,1,0:T(8,128)(2,1)S(1)}, f32[16,64,128]{2,1,0:T(8,128)S(1)}) custom-call(s32[1]{0:T(128)} %bitcast.7.q_ref, bf16[256,128]{1,0:T(8,128)(2,1)S(1)} %tile_counts.1.weights_ref, ...), custom_call_target="tpu_custom_call" | custom-call | flops 536870912 | bytes 8388608 | tf_op jit(solution)/shard_map/adjoint_tiles/pallas_call | solution.py:436
  119.7 2.0 %collective-permute-start.18 = (bf16[4,64,128]{2,1,0:T(8,128)(2,1)S(1)}, bf16[4,64,128]{2,1,0:T(8,128)(2,1)S(1)}, u32[]{:S(2)}, u32[]{:S(2)}) collective-permute-start(bf16[4,64,128]{2,1,0:T(8,128)(2,1)S(1)} %get-tuple-element.33), channel_id=1, source_target_pairs={{0,1},{1,2},{2,3},{3,0},{4,5},{5,6},{6,7},{7,4},{8,9},{9,10},{10,1... | collective-permute-start | bytes 196616 | tf_op jit(solution)/shard_map/ppermute | solution.py:547
  121.7 1.9 %collective-permute-start.19 = (bf16[4,64,128]{2,1,0:T(8,128)(2,1)S(1)}, bf16[4,64,128]{2,1,0:T(8,128)(2,1)S(1)}, u32[]{:S(2)}, u32[]{:S(2)}) collective-permute-start(bf16[4,64,128]{2,1,0:T(8,128)(2,1)S(1)} %get-tuple-element.34), channel_id=1, source_target_pairs={{0,2},{1,3},{2,0},{3,1},{4,6},{5,7},{6,4},{7,5},{8,10},{9,11},{10,... | collective-permute-start | bytes 196616 | tf_op jit(solution)/shard_map/ppermute | solution.py:547
  123.6 2.0 %collective-permute-start.20 = (bf16[4,64,128]{2,1,0:T(8,128)(2,1)S(1)}, bf16[4,64,128]{2,1,0:T(8,128)(2,1)S(1)}, u32[]{:S(2)}, u32[]{:S(2)}) collective-permute-start(bf16[4,64,128]{2,1,0:T(8,128)(2,1)S(1)} %get-tuple-element.35), channel_id=1, source_target_pairs={{0,3},{1,0},{2,1},{3,2},{4,7},{5,4},{6,5},{7,6},{8,11},{9,8},{10,9... | collective-permute-start | bytes 196616 | tf_op jit(solution)/shard_map/ppermute | solution.py:547
  125.6 0.8 residual.1
  126.4 1.1 collective-permute-done.19.refs_1_
  127.8 0.7 image_step.1
  (29 shorter events, 1.8 us)
Async XLA Ops:
  5.6 55.0 %all-to-all-start = ((bf16[64,80,128]{2,1,0:T(8,128)(2,1)}), bf16[64,80,128]{2,1,0:T(8,128)(2,1)S(1)}, u32[]{:S(2)}, u32[]{:S(2)}) async-start(bf16[64,80,128]{2,1,0:T(8,128)(2,1)} %get-tuple-element.22), calls=%async_computation | async-start | bytes 2621440 | tf_op jit(solution)/shard_map/all_to_all | solution.py:509
  18.8 46.3 %copy-start.2 = (s32[1,1,64]{2,1,0:T(1,128)S(1)}, s32[1,1,64]{2,1,0:T(1,128)}, u32[]{:S(2)}) copy-start(s32[1,1,64]{2,1,0:T(1,128)} %param.17) | copy-start | bytes 772
  18.9 35.4 %collective-permute-start = (bf16[64,128]{1,0:T(8,128)(2,1)S(1)}, bf16[64,128]{1,0:T(8,128)(2,1)S(1)}, u32[]{:S(2)}, u32[]{:S(2)}) collective-permute-start(bf16[64,128]{1,0:T(8,128)(2,1)S(1)} %get-tuple-element.19), channel_id=1, source_target_pairs={{0,1},{1,2},{2,3},{4,5},{5,6},{6,7},{8,9},{9,10},{10,11},{12,13},{... | collective-permute-start | bytes 49160 | tf_op jit(solution)/shard_map/ppermute | solution.py:527
  22.0 34.9 %collective-permute-start.1 = (bf16[64,128]{1,0:T(8,128)(2,1)S(1)}, bf16[64,128]{1,0:T(8,128)(2,1)S(1)}, u32[]{:S(2)}, u32[]{:S(2)}) collective-permute-start(bf16[64,128]{1,0:T(8,128)(2,1)S(1)} %get-tuple-element.20), channel_id=1, source_target_pairs={{1,0},{2,1},{3,2},{5,4},{6,5},{7,6},{9,8},{10,9},{11,10},{13,12},{... | collective-permute-start | bytes 49160 | tf_op jit(solution)/shard_map/ppermute | solution.py:528
  23.3 25.6 %collective-permute-start.8 = (s32[8,128]{1,0:T(8,128)S(1)}, s32[8,128]{1,0:T(8,128)S(1)}, u32[]{:S(2)}, u32[]{:S(2)}) collective-permute-start(s32[8,128]{1,0:T(8,128)S(1)} %get-tuple-element.24.refs_0_), channel_id=1, source_target_pairs={{0,224},{4,228},{8,232},{12,236},{16,240},{20,244},{24,248},{28,25... | collective-permute-start | bytes 12296 | tf_op jit(solution)/shard_map/ppermute | solution.py:532
  26.3 27.9 %collective-permute-start.7 = (s32[8,128]{1,0:T(8,128)S(1)}, s32[8,128]{1,0:T(8,128)S(1)}, u32[]{:S(2)}, u32[]{:S(2)}) collective-permute-start(s32[8,128]{1,0:T(8,128)S(1)} %get-tuple-element.24.refs_0_), channel_id=1, source_target_pairs={{0,192},{4,196},{8,200},{12,204},{16,208},{20,212},{24,216},{28,22... | collective-permute-start | bytes 12296 | tf_op jit(solution)/shard_map/ppermute | solution.py:532
  28.4 32.1 %collective-permute-start.6 = (s32[8,128]{1,0:T(8,128)S(1)}, s32[8,128]{1,0:T(8,128)S(1)}, u32[]{:S(2)}, u32[]{:S(2)}) collective-permute-start(s32[8,128]{1,0:T(8,128)S(1)} %get-tuple-element.24.refs_0_), channel_id=1, source_target_pairs={{0,160},{4,164},{8,168},{12,172},{16,176},{20,180},{24,184},{28,18... | collective-permute-start | bytes 12296 | tf_op jit(solution)/shard_map/ppermute | solution.py:532
  48.9 11.7 %collective-permute-start.5 = (s32[8,128]{1,0:T(8,128)S(1)}, s32[8,128]{1,0:T(8,128)S(1)}, u32[]{:S(2)}, u32[]{:S(2)}) collective-permute-start(s32[8,128]{1,0:T(8,128)S(1)} %get-tuple-element.24.refs_0_), channel_id=1, source_target_pairs={{0,128},{4,132},{8,136},{12,140},{16,144},{20,148},{24,152},{28,15... | collective-permute-start | bytes 12296 | tf_op jit(solution)/shard_map/ppermute | solution.py:532
  54.2 6.3 %collective-permute-start.4 = (s32[8,128]{1,0:T(8,128)S(1)}, s32[8,128]{1,0:T(8,128)S(1)}, u32[]{:S(2)}, u32[]{:S(2)}) collective-permute-start(s32[8,128]{1,0:T(8,128)S(1)} %get-tuple-element.24.refs_0_), channel_id=1, source_target_pairs={{0,96},{4,100},{8,104},{12,108},{16,112},{20,116},{24,120},{28,124... | collective-permute-start | bytes 12296 | tf_op jit(solution)/shard_map/ppermute | solution.py:532
  54.3 6.3 %collective-permute-start.3 = (s32[8,128]{1,0:T(8,128)S(1)}, s32[8,128]{1,0:T(8,128)S(1)}, u32[]{:S(2)}, u32[]{:S(2)}) collective-permute-start(s32[8,128]{1,0:T(8,128)S(1)} %get-tuple-element.24.refs_0_), channel_id=1, source_target_pairs={{0,64},{4,68},{8,72},{12,76},{16,80},{20,84},{24,88},{28,92},{32,9... | collective-permute-start | bytes 12296 | tf_op jit(solution)/shard_map/ppermute | solution.py:532
  56.9 3.7 %collective-permute-start.2 = (s32[8,128]{1,0:T(8,128)S(1)}, s32[8,128]{1,0:T(8,128)S(1)}, u32[]{:S(2)}, u32[]{:S(2)}) collective-permute-start(s32[8,128]{1,0:T(8,128)S(1)} %get-tuple-element.24.refs_0_), channel_id=1, source_target_pairs={{0,32},{4,36},{8,40},{12,44},{16,48},{20,52},{24,56},{28,60},{32,0... | collective-permute-start | bytes 12296 | tf_op jit(solution)/shard_map/ppermute | solution.py:532
  60.7 6.7 %collective-permute-start.16 = (bf16[64,128]{1,0:T(8,128)(2,1)S(1)}, bf16[64,128]{1,0:T(8,128)(2,1)S(1)}, u32[]{:S(2)}, u32[]{:S(2)}) collective-permute-start(bf16[64,128]{1,0:T(8,128)(2,1)S(1)} %get-tuple-element.27), channel_id=1, source_target_pairs={{0,1},{1,2},{2,3},{4,5},{5,6},{6,7},{8,9},{9,10},{10,11},{12,13},{... | collective-permute-start | bytes 49160 | tf_op jit(solution)/shard_map/ppermute | solution.py:527
  63.8 5.6 %collective-permute-start.17 = (bf16[64,128]{1,0:T(8,128)(2,1)S(1)}, bf16[64,128]{1,0:T(8,128)(2,1)S(1)}, u32[]{:S(2)}, u32[]{:S(2)}) collective-permute-start(bf16[64,128]{1,0:T(8,128)(2,1)S(1)} %get-tuple-element.28), channel_id=1, source_target_pairs={{1,0},{2,1},{3,2},{5,4},{6,5},{7,6},{9,8},{10,9},{11,10},{13,12},{... | collective-permute-start | bytes 49160 | tf_op jit(solution)/shard_map/ppermute | solution.py:528
  71.8 43.4 %all-to-all-start.1 = ((bf16[64,80,128]{2,1,0:T(8,128)(2,1)}), bf16[64,80,128]{2,1,0:T(8,128)(2,1)S(1)}, u32[]{:S(2)}, u32[]{:S(2)}) async-start(bf16[64,80,128]{2,1,0:T(8,128)(2,1)} %stripe.1), calls=%async_computation.1 | async-start | bytes 2621440 | tf_op jit(solution)/shard_map/all_to_all | solution.py:509
  80.7 44.9 %copy-start = (f32[64,2048]{1,0:T(8,128)S(1)}, f32[64,2048]{1,0:T(8,128)}, u32[]{:S(2)}) copy-start(f32[64,2048]{1,0:T(8,128)} %get-tuple-element.31.forward_ref) | copy-start | bytes 1572868
  80.7 6.4 %collective-permute-start.15 = (s32[8,128]{1,0:T(8,128)S(1)}, s32[8,128]{1,0:T(8,128)S(1)}, u32[]{:S(2)}, u32[]{:S(2)}) collective-permute-start(s32[8,128]{1,0:T(8,128)S(1)} %get-tuple-element.26.refs_0_), channel_id=1, source_target_pairs={{0,28},{4,24},{8,20},{12,16},{16,12},{20,8},{24,4},{28,0},{32,60},... | collective-permute-start | bytes 12296 | tf_op jit(solution)/shard_map/ppermute | solution.py:532
  82.0 5.6 %collective-permute-start.14 = (s32[8,128]{1,0:T(8,128)S(1)}, s32[8,128]{1,0:T(8,128)S(1)}, u32[]{:S(2)}, u32[]{:S(2)}) collective-permute-start(s32[8,128]{1,0:T(8,128)S(1)} %get-tuple-element.26.refs_0_), channel_id=1, source_target_pairs={{0,24},{4,28},{8,16},{12,20},{16,8},{20,12},{24,0},{28,4},{32,56},... | collective-permute-start | bytes 12296 | tf_op jit(solution)/shard_map/ppermute | solution.py:532
  82.6 5.2 %collective-permute-start.13 = (s32[8,128]{1,0:T(8,128)S(1)}, s32[8,128]{1,0:T(8,128)S(1)}, u32[]{:S(2)}, u32[]{:S(2)}) collective-permute-start(s32[8,128]{1,0:T(8,128)S(1)} %get-tuple-element.26.refs_0_), channel_id=1, source_target_pairs={{0,20},{4,16},{8,28},{12,24},{16,4},{20,0},{24,12},{28,8},{32,52},... | collective-permute-start | bytes 12296 | tf_op jit(solution)/shard_map/ppermute | solution.py:532
  85.6 5.1 %collective-permute-start.12 = (s32[8,128]{1,0:T(8,128)S(1)}, s32[8,128]{1,0:T(8,128)S(1)}, u32[]{:S(2)}, u32[]{:S(2)}) collective-permute-start(s32[8,128]{1,0:T(8,128)S(1)} %get-tuple-element.26.refs_0_), channel_id=1, source_target_pairs={{0,16},{4,20},{8,24},{12,28},{16,0},{20,4},{24,8},{28,12},{32,48},... | collective-permute-start | bytes 12296 | tf_op jit(solution)/shard_map/ppermute | solution.py:532
  85.9 4.8 %collective-permute-start.11 = (s32[8,128]{1,0:T(8,128)S(1)}, s32[8,128]{1,0:T(8,128)S(1)}, u32[]{:S(2)}, u32[]{:S(2)}) collective-permute-start(s32[8,128]{1,0:T(8,128)S(1)} %get-tuple-element.26.refs_0_), channel_id=1, source_target_pairs={{0,12},{4,8},{8,4},{12,0},{16,28},{20,24},{24,20},{28,16},{32,44},... | collective-permute-start | bytes 12296 | tf_op jit(solution)/shard_map/ppermute | solution.py:532
  87.1 3.8 %collective-permute-start.10 = (s32[8,128]{1,0:T(8,128)S(1)}, s32[8,128]{1,0:T(8,128)S(1)}, u32[]{:S(2)}, u32[]{:S(2)}) collective-permute-start(s32[8,128]{1,0:T(8,128)S(1)} %get-tuple-element.26.refs_0_), channel_id=1, source_target_pairs={{0,8},{4,12},{8,0},{12,4},{16,24},{20,28},{24,16},{28,20},{32,40},... | collective-permute-start | bytes 12296 | tf_op jit(solution)/shard_map/ppermute | solution.py:532
  87.7 3.2 %collective-permute-start.9 = (s32[8,128]{1,0:T(8,128)S(1)}, s32[8,128]{1,0:T(8,128)S(1)}, u32[]{:S(2)}, u32[]{:S(2)}) collective-permute-start(s32[8,128]{1,0:T(8,128)S(1)} %get-tuple-element.26.refs_0_), channel_id=1, source_target_pairs={{0,4},{4,0},{8,12},{12,8},{16,20},{20,16},{24,28},{28,24},{32,36},... | collective-permute-start | bytes 12296 | tf_op jit(solution)/shard_map/ppermute | solution.py:532
  92.1 35.8 %copy-start.1 = (bf16[2048,64]{0,1:T(8,128)(2,1)S(1)}, bf16[2048,64]{0,1:T(8,128)(2,1)}, u32[]{:S(2)}) copy-start(bf16[2048,64]{0,1:T(8,128)(2,1)} %param.11) | copy-start | bytes 786436
  119.7 6.7 %collective-permute-start.18 = (bf16[4,64,128]{2,1,0:T(8,128)(2,1)S(1)}, bf16[4,64,128]{2,1,0:T(8,128)(2,1)S(1)}, u32[]{:S(2)}, u32[]{:S(2)}) collective-permute-start(bf16[4,64,128]{2,1,0:T(8,128)(2,1)S(1)} %get-tuple-element.33), channel_id=1, source_target_pairs={{0,1},{1,2},{2,3},{3,0},{4,5},{5,6},{6,7},{7,4},{8,9},{9,10},{10,1... | collective-permute-start | bytes 196616 | tf_op jit(solution)/shard_map/ppermute | solution.py:547
  121.7 5.8 %collective-permute-start.19 = (bf16[4,64,128]{2,1,0:T(8,128)(2,1)S(1)}, bf16[4,64,128]{2,1,0:T(8,128)(2,1)S(1)}, u32[]{:S(2)}, u32[]{:S(2)}) collective-permute-start(bf16[4,64,128]{2,1,0:T(8,128)(2,1)S(1)} %get-tuple-element.34), channel_id=1, source_target_pairs={{0,2},{1,3},{2,0},{3,1},{4,6},{5,7},{6,4},{7,5},{8,10},{9,11},{10,... | collective-permute-start | bytes 196616 | tf_op jit(solution)/shard_map/ppermute | solution.py:547
  123.6 4.3 %collective-permute-start.20 = (bf16[4,64,128]{2,1,0:T(8,128)(2,1)S(1)}, bf16[4,64,128]{2,1,0:T(8,128)(2,1)S(1)}, u32[]{:S(2)}, u32[]{:S(2)}) collective-permute-start(bf16[4,64,128]{2,1,0:T(8,128)(2,1)S(1)} %get-tuple-element.35), channel_id=1, source_target_pairs={{0,3},{1,0},{2,1},{3,2},{4,7},{5,4},{6,5},{7,6},{8,11},{9,8},{10,9... | collective-permute-start | bytes 196616 | tf_op jit(solution)/shard_map/ppermute | solution.py:547

commit v9 on v8

--- a/solution.py
+++ b/solution.py
@@ -10,6 +10,7 @@
 RELAX = 0.25
 PER = 16
 ROOM = 32
+EARLY = 4
 MIB = 2**20
 F32, BF16 = jnp.float32, jnp.bfloat16
 NT = (((1,), (1,)), ((), ()))
@@ -146,11 +147,15 @@
     )(*map(in_hbm, (entry, place, slot)), count, *map(in_hbm, (numbers, projections, image, library)))
 
 
-def phase_call(projections, left, right, taps):
+def phase_call(projections, left, right, taps, rows):
     slices, columns = projections.shape
     per = columns // T
 
-    def kernel(x_hbm, l_ref, r_ref, taps_hbm, phase_ref, band_ref, taps_ref, line, wide, sems):
+    def kernel(x_hbm, l_ref, r_ref, taps_hbm, *refs):
+        n = len(rows)
+        row_refs, (phase_ref, band_ref, stack_ref, taps_ref, line, wide, sems) = refs[:n], refs[n:]
+        for m, ref in enumerate(row_refs):
+            stack_ref[m : m + 1, :] = ref[0:1, :]
         fetches = [
             pltpu.make_async_copy(x_hbm, wide.at[:, pl.ds(T, columns)], sems.at[0]),
             pltpu.make_async_copy(taps_hbm, taps_ref, sems.at[1]),
@@ -175,9 +180,10 @@
         out_shape=[
             jax.ShapeDtypeStruct((slices, columns), BF16),
             jax.ShapeDtypeStruct((T, 3 * T), BF16),
-        ],
-        in_specs=[HBM, VMEM, VMEM, HBM],
-        out_specs=[VMEM, VMEM],
+            jax.ShapeDtypeStruct((8, T), jnp.int32),
+        ],
+        in_specs=[HBM, VMEM, VMEM, HBM] + [VMEM] * len(rows),
+        out_specs=[VMEM] * 3,
         scratch_shapes=[
             pltpu.VMEM(taps.shape, BF16),
             pltpu.VMEM((8, 3 * T), F32),
@@ -187,32 +193,33 @@
         compiler_params=params(),
         cost_estimate=pl.CostEstimate(flops=2**26, bytes_accessed=2**20, transcendentals=0),
         name="phase_filter",
-    )(in_hbm(projections), left, right, in_hbm(taps))
-
-
-def rim_call(arrived, band, rows_by_z):
+    )(in_hbm(projections), left, right, in_hbm(taps), *rows)
+
+
+def rim_call(arrived, band, stacks):
     angles = arrived.shape[0]
     size = arrived.shape[1] - PER
 
     def kernel(arrived_ref, _, *refs):
-        n = len(rows_by_z)
-        z_refs, (head_ref, tail_ref, stack_ref, flat) = refs[:n], refs[n:]
-        for m, ref in enumerate(z_refs):
-            stack_ref[m : m + 1, :] = ref[0:1, :]
+        n = len(stacks)
+        stack_refs, (head_ref, tail_ref, near_ref, flat) = refs[:n], refs[n:]
+        for m, ref in enumerate(stack_refs):
+            near_ref[m * 8 : (m + 1) * 8, :] = ref[...]
         flat[...] = arrived_ref[:, size:, :].astype(F32).reshape(angles * PER, T)
         head_ref[...] = flat[pl.ds(0, angles, stride=PER), :].astype(BF16)
         tail_ref[...] = flat[pl.ds(PER - 1, angles, stride=PER), :].astype(BF16)
 
     return pl.pallas_call(
         kernel,
-        out_shape=[jax.ShapeDtypeStruct((angles, T), BF16)] * 2 + [jax.ShapeDtypeStruct((8, T), jnp.int32)],
-        in_specs=[VMEM, HBM] + [VMEM] * len(rows_by_z),
+        out_shape=[jax.ShapeDtypeStruct((angles, T), BF16)] * 2
+        + [jax.ShapeDtypeStruct((8 * len(stacks), T), jnp.int32)],
+        in_specs=[VMEM, HBM] + [VMEM] * len(stacks),
         out_specs=[VMEM] * 3,
         scratch_shapes=[pltpu.VMEM((angles * PER, T), F32)],
         compiler_params=params(),
         cost_estimate=pl.CostEstimate(flops=2**17, bytes_accessed=2**18, transcendentals=0),
         name="rim",
-    )(arrived, band, *rows_by_z)
+    )(arrived, band, *stacks)
 
 
 def stripe_of(quarter, quarters, angles, values, rimmed):
@@ -374,7 +381,7 @@
         of_slot = ones(T, slot_ref[...])
         met = lax.dot_general(of_bin, of_slot, NT, preferred_element_type=F32)
         k = lax.broadcasted_iota(jnp.int32, (owners, capacity), 0)
-        by_row = (owner_ref[0] ^ ((k & 7) * 8 + (k >> 3))) == slot_ref[...]
+        by_row = (owner_ref[0] ^ k) == slot_ref[...]
         met_by_row = lax.dot_general(of_bin, by_row.astype(F32).astype(BF16), NT, preferred_element_type=F32)
         stripe_met = jnp.dot(met_by_row.astype(BF16), carries, preferred_element_type=F32)
         weights_ref[...] = (met - stripe_met).astype(BF16)
@@ -533,14 +540,15 @@
 
     send, head, tail, row = first_call(*tiles, carried, projections, image, library)
     arrived = exchanged(send, "dom")
-    phase, band = phase_call(projections, *rims(head, tail), phase_kernel)
-    rows_by_z = [row] + [swapped(row, m * 8) for m in range(1, 8)]
-    head, tail, stacked = rim_call(arrived, band, rows_by_z)
+    rows = [row] + [swapped(row, m) for m in range(1, 8)]
+    phase, band, stack = phase_call(projections, *rims(head, tail), phase_kernel, rows)
+    stacks = [stack] + [swapped(stack, m * 8) for m in range(1, EARLY)]
+    head, tail, near = rim_call(arrived, band, stacks)
     left, right = rims(head, tail)
-    forward, back, stack = back_call(carried, arrived, phase, stacked)
+    forward, back, stack = back_call(carried, arrived, phase, stack)
     back = stripe_call(quarter, arrived, left, right, band, back, quarters)
     returned = exchanged(back, "dom")
-    stacks = [stack] + [swapped(stack, m) for m in range(1, 8)]
+    stacks = [near] + [swapped(stack, m * 8) for m in range(EARLY, 8)]
     weights = counts_call(*tiles, owner, stacks, owners, library.shape[0], blocks)
     own, *sent, stripe = adjoint_call(quarter, weights, returned, library, blocks, quarters)
     others = [

time: 129 us -> 119 us (0.922)
  starting transfers between devices: 62.6 us -> 54.5 us
  waiting for transfers between devices: 46.4 us -> 43 us
  Pallas kernels: 18.1 us -> 19.4 us
    all_to_all x2, waiting for transfers between devices: 23.1 us -> 3.83 us  [exchanged(): return lax.all_to_all(array, axis, split_axis=0, concat_axis=0, tiled=True)]
    ppermute x14, waiting for transfers between devices: 19.9 us -> 35.7 us  [swapped(): return lax.ppermute(array, 'dom', [(i, i ^ m) for i in range(owners)])]
    all_to_all x2, starting transfers between devices: 22.2 us -> 17.1 us  [exchanged(): return lax.all_to_all(array, axis, split_axis=0, concat_axis=0, tiled=True)]
    ppermute x14, starting transfers between devices: 25.6 us -> 22.6 us  [swapped(): return lax.ppermute(array, 'dom', [(i, i ^ m) for i in range(owners)])]
    pallas_call x1, Pallas kernels: 4.27 us -> 5.61 us  [first_call(): pl.pallas_call(kernel, out_shape=[pltpu.HBM((owners, rows, T), BF16), jax...]
  transfers between devices with their start and end apart: 23 -> 23, of which waited for: 7 -> 11; matrix products, arithmetic and copies ran while one was open for 0% -> 0% of each run, Pallas kernels for 5% -> 5%
where the time goes in v9:
time: 119 us; the launch traced here: 118 us
  starting transfers between devices  54.5 us (46%)
  waiting for transfers between devices  43 us (36%)
  Pallas kernels  19.4 us (16%)
  between operations  1.45 us (1%)
    ppermute x14, waiting for transfers between devices, swapped(): return lax.ppermute(array, 'dom', [(i, i ^ m) for i in range(owners)])  35.7 us
    ppermute x14, starting transfers between devices, swapped(): return lax.ppermute(array, 'dom', [(i, i ^ m) for i in range(owners)])  22.6 us
    all_to_all x2, starting transfers between devices, exchanged(): return lax.all_to_all(array, axis, split_axis=0, concat_axis=0, tiled=True)  17.1 us
    ppermute x2, starting transfers between devices, rims(): left = lax.ppermute(tail, 'ray', [(i, i + 1) for i in range(quarters - 1)])  6.79 us
    pallas_call x1, Pallas kernels, first_call(): pl.pallas_call(kernel, out_shape=[pltpu.HBM((owners, rows, T), BF16), jax...  5.61 us
    ppermute x3, starting transfers between devices, shards(): lax.ppermute(part, 'ray', [(i, (i + m) % quarters) for i in range(quarter...  5.37 us
    pallas_call x1, Pallas kernels, adjoint_call(): pl.pallas_call(kernel, out_shape=[*(jax.ShapeDtypeStruct((held, size, T),...  4.59 us
    all_to_all x2, waiting for transfers between devices, exchanged(): return lax.all_to_all(array, axis, split_axis=0, concat_axis=0, tiled=True)  3.83 us
  transfers between devices with their start and end apart: 23, of which 11 were waited for; matrix products, arithmetic and copies ran while one was open for 0% of the time, Pallas kernels for 5%

profile of v9, /device:TPU:8, one launch (start us, length us, event | category | flops | bytes accessed | tf_op | source)
XLA Modules:
  0.0 118.4 jit_solution(15107696322506072203)
XLA Ops:
  1.3 5.6 %forward_tiles.1 = (bf16[64,80,128]{2,1,0:T(8,128)(2,1)}, bf16[64,128]{1,0:T(8,128)(2,1)S(1)}, bf16[64,128]{1,0:T(8,128)(2,1)S(1)}, s32[8,128]{1,0:T(8,128)S(1)}) custom-call(s32[1,256]{1,0:T(1,128)} %bitcast.19, s32[1,256]{1,0:T(1,128)} %bitcast.21, s32[1,256]{1,0:T(1,128)} %bitcast.23, s32[1,1]{1,0:T(1,128)S(6)} %copy.13.count_ref, s32[1,64]{1,0:T(1,128)} %bitcast.13, ...), custom_call_target="tpu_custom_call" | custom-call | flops 536870912 | bytes 8388608 | tf_op jit(solution)/shard_map/forward_tiles/pallas_call | solution.py:116
  6.9 11.6 %all-to-all-start = ((bf16[64,80,128]{2,1,0:T(8,128)(2,1)}), bf16[64,80,128]{2,1,0:T(8,128)(2,1)S(1)}, u32[]{:S(2)}, u32[]{:S(2)}) async-start(bf16[64,80,128]{2,1,0:T(8,128)(2,1)} %get-tuple-element.24), calls=%async_computation | async-start | bytes 2621440 | tf_op jit(solution)/shard_map/all_to_all | solution.py:516
  18.5 3.4 %collective-permute-start = (bf16[64,128]{1,0:T(8,128)(2,1)S(1)}, bf16[64,128]{1,0:T(8,128)(2,1)S(1)}, u32[]{:S(2)}, u32[]{:S(2)}) collective-permute-start(bf16[64,128]{1,0:T(8,128)(2,1)S(1)} %get-tuple-element.20), channel_id=1, source_target_pairs={{0,1},{1,2},{2,3},{4,5},{5,6},{6,7},{8,9},{9,10},{10,11},{12,13},{... | collective-permute-start | bytes 49160 | tf_op jit(solution)/shard_map/ppermute | solution.py:534
  21.9 1.3 %collective-permute-start.1 = (bf16[64,128]{1,0:T(8,128)(2,1)S(1)}, bf16[64,128]{1,0:T(8,128)(2,1)S(1)}, u32[]{:S(2)}, u32[]{:S(2)}) collective-permute-start(bf16[64,128]{1,0:T(8,128)(2,1)S(1)} %get-tuple-element.21), channel_id=1, source_target_pairs={{1,0},{2,1},{3,2},{5,4},{6,5},{7,6},{9,8},{10,9},{11,10},{13,12},{... | collective-permute-start | bytes 49160 | tf_op jit(solution)/shard_map/ppermute | solution.py:535
  23.2 1.0 collective-permute-start.8
  24.8 3.2 %collective-permute-start.6 = (s32[8,128]{1,0:T(8,128)S(1)}, s32[8,128]{1,0:T(8,128)S(1)}, u32[]{:S(2)}, u32[]{:S(2)}) collective-permute-start(s32[8,128]{1,0:T(8,128)S(1)} %get-tuple-element.22.refs_0_), channel_id=1, source_target_pairs={{0,20},{4,16},{8,28},{12,24},{16,4},{20,0},{24,12},{28,8},{32,52},... | collective-permute-start | bytes 12296 | tf_op jit(solution)/shard_map/ppermute | solution.py:539
  28.0 1.8 %collective-permute-start.5 = (s32[8,128]{1,0:T(8,128)S(1)}, s32[8,128]{1,0:T(8,128)S(1)}, u32[]{:S(2)}, u32[]{:S(2)}) collective-permute-start(s32[8,128]{1,0:T(8,128)S(1)} %get-tuple-element.22.refs_0_), channel_id=1, source_target_pairs={{0,16},{4,20},{8,24},{12,28},{16,0},{20,4},{24,8},{28,12},{32,48},... | collective-permute-start | bytes 12296 | tf_op jit(solution)/shard_map/ppermute | solution.py:539
  30.3 1.0 collective-permute-start.3
  31.3 1.8 %collective-permute-done.5.refs_4_ = s32[8,128]{1,0:T(8,128)S(1)} collective-permute-done((s32[8,128]{1,0:T(8,128)S(1)}, s32[8,128]{1,0:T(8,128)S(1)}, u32[]{:S(2)}, u32[]{:S(2)}) %collective-permute-start.5) | collective-permute-done | bytes 4128 | tf_op jit(solution)/shard_map/ppermute | solution.py:539
  34.3 1.9 %phase_filter.1 = (bf16[64,2048]{1,0:T(8,128)(2,1)S(1)}, bf16[128,384]{1,0:T(8,128)(2,1)S(1)}, s32[8,128]{1,0:T(8,128)S(1)}) custom-call(bf16[64,2048]{1,0:T(8,128)(2,1)} %bitcast.16, bf16[64,128]{1,0:T(8,128)(2,1)S(1)} %collective-permute-done.l_ref, bf16[64,128]{1,0:T(8,128)(2,1)S(1)} %collective-permute-done.1.r_ref, bf16[129]{0:T(256)(128)(2,1)} %taps_hbm.1, ...), custom_call_target="tpu_custom_call" | custom-call | flops 67108864 | bytes 1048576 | tf_op jit(solution)/shard_map/phase_filter/pallas_call | solution.py:178
  36.2 3.5 %collective-permute-start.11 = (s32[8,128]{1,0:T(8,128)S(1)}, s32[8,128]{1,0:T(8,128)S(1)}, u32[]{:S(2)}, u32[]{:S(2)}) collective-permute-start(s32[8,128]{1,0:T(8,128)S(1)} %get-tuple-element.26.refs_0_.stacked_ref), channel_id=1, source_target_pairs={{0,96},{4,100},{8,104},{12,108},{16,112},{20,116},{24,120},{28,124... | collective-permute-start | bytes 12296 | tf_op jit(solution)/shard_map/ppermute | solution.py:539
  40.7 8.5 %collective-permute-done.11.refs_3_ = s32[8,128]{1,0:T(8,128)S(1)} collective-permute-done((s32[8,128]{1,0:T(8,128)S(1)}, s32[8,128]{1,0:T(8,128)S(1)}, u32[]{:S(2)}, u32[]{:S(2)}) %collective-permute-start.11) | collective-permute-done | bytes 4128 | tf_op jit(solution)/shard_map/ppermute | solution.py:539
  49.2 3.8 %all-to-all-done.arrived_ref = bf16[64,80,128]{2,1,0:T(8,128)(2,1)S(1)} async-done(((bf16[64,80,128]{2,1,0:T(8,128)(2,1)}), bf16[64,80,128]{2,1,0:T(8,128)(2,1)S(1)}, u32[]{:S(2)}, u32[]{:S(2)}) %all-to-all-start) | async-done | bytes 1310752 | tf_op jit(solution)/shard_map/all_to_all | solution.py:516
  53.1 3.4 %collective-permute-start.16 = (bf16[64,128]{1,0:T(8,128)(2,1)S(1)}, bf16[64,128]{1,0:T(8,128)(2,1)S(1)}, u32[]{:S(2)}, u32[]{:S(2)}) collective-permute-start(bf16[64,128]{1,0:T(8,128)(2,1)S(1)} %get-tuple-element.29), channel_id=1, source_target_pairs={{0,1},{1,2},{2,3},{4,5},{5,6},{6,7},{8,9},{9,10},{10,11},{12,13},{... | collective-permute-start | bytes 49160 | tf_op jit(solution)/shard_map/ppermute | solution.py:534
  56.5 1.3 %collective-permute-start.17 = (bf16[64,128]{1,0:T(8,128)(2,1)S(1)}, bf16[64,128]{1,0:T(8,128)(2,1)S(1)}, u32[]{:S(2)}, u32[]{:S(2)}) collective-permute-start(bf16[64,128]{1,0:T(8,128)(2,1)S(1)} %get-tuple-element.30), channel_id=1, source_target_pairs={{1,0},{2,1},{3,2},{5,4},{6,5},{7,6},{9,8},{10,9},{11,10},{13,12},{... | collective-permute-start | bytes 49160 | tf_op jit(solution)/shard_map/ppermute | solution.py:535
  57.8 2.3 %slot_sums.1 = (f32[64,2048]{1,0:T(8,128)}, bf16[64,80,128]{2,1,0:T(8,128)(2,1)}, s32[8,128]{1,0:T(8,128)S(1)}) custom-call(s32[1,64]{1,0:T(1,128)S(1)} %bitcast.14, bf16[64,80,128]{2,1,0:T(8,128)(2,1)S(1)} %all-to-all-done.arrived_ref, bf16[64,2048]{1,0:T(8,128)(2,1)S(1)} %get-tuple-element.23.phase_ref, s32[8,128]{1,0:T(8,128)S(1)} %get-tuple-element.26.refs_0_.stacked_ref), custom_call_target="tpu_custom_call" | custom-call | flops 16777216 | bytes 8388608 | tf_op jit(solution)/shard_map/slot_sums/pallas_call | solution.py:281
  60.1 2.0 %collective-permute-done.17.r_ref = bf16[64,128]{1,0:T(8,128)(2,1)S(1)} collective-permute-done((bf16[64,128]{1,0:T(8,128)(2,1)S(1)}, bf16[64,128]{1,0:T(8,128)(2,1)S(1)}, u32[]{:S(2)}, u32[]{:S(2)}) %collective-permute-start.17) | collective-permute-done | bytes 16416 | tf_op jit(solution)/shard_map/ppermute | solution.py:535
  62.1 2.3 %stripe.1 = bf16[64,80,128]{2,1,0:T(8,128)(2,1)} custom-call(s32[1]{0:T(128)} %bitcast.7.q_ref, bf16[64,80,128]{2,1,0:T(8,128)(2,1)S(1)} %all-to-all-done.arrived_ref, bf16[64,128]{1,0:T(8,128)(2,1)S(1)} %collective-permute-done.16.l_ref, bf16[64,128]{1,0:T(8,128)(2,1)S(1)} %collective-permute-done.17.r_ref, ...), custom_call_target="tpu_custom_call", output_to_operand_aliasing={{}: (5, {})} | custom-call | flops 67108864 | bytes 1048576 | tf_op jit(solution)/shard_map/stripe/pallas_call | solution.py:337
  64.4 5.6 %all-to-all-start.1 = ((bf16[64,80,128]{2,1,0:T(8,128)(2,1)}), bf16[64,80,128]{2,1,0:T(8,128)(2,1)S(1)}, u32[]{:S(2)}, u32[]{:S(2)}) async-start(bf16[64,80,128]{2,1,0:T(8,128)(2,1)} %stripe.1), calls=%async_computation.1 | async-start | bytes 2621440 | tf_op jit(solution)/shard_map/all_to_all | solution.py:516
  70.0 3.2 %collective-permute-start.15 = (s32[8,128]{1,0:T(8,128)S(1)}, s32[8,128]{1,0:T(8,128)S(1)}, u32[]{:S(2)}, u32[]{:S(2)}) collective-permute-start(s32[8,128]{1,0:T(8,128)S(1)} %get-tuple-element.28), channel_id=1, source_target_pairs={{0,224},{4,228},{8,232},{12,236},{16,240},{20,244},{24,248},{28,25... | collective-permute-start | bytes 12296 | tf_op jit(solution)/shard_map/ppermute | solution.py:539
  73.2 2.1 %collective-permute-start.14 = (s32[8,128]{1,0:T(8,128)S(1)}, s32[8,128]{1,0:T(8,128)S(1)}, u32[]{:S(2)}, u32[]{:S(2)}) collective-permute-start(s32[8,128]{1,0:T(8,128)S(1)} %get-tuple-element.28), channel_id=1, source_target_pairs={{0,192},{4,196},{8,200},{12,204},{16,208},{20,212},{24,216},{28,22... | collective-permute-start | bytes 12296 | tf_op jit(solution)/shard_map/ppermute | solution.py:539
  75.3 3.7 %collective-permute-start.13 = (s32[8,128]{1,0:T(8,128)S(1)}, s32[8,128]{1,0:T(8,128)S(1)}, u32[]{:S(2)}, u32[]{:S(2)}) collective-permute-start(s32[8,128]{1,0:T(8,128)S(1)} %get-tuple-element.28), channel_id=1, source_target_pairs={{0,160},{4,164},{8,168},{12,172},{16,176},{20,180},{24,184},{28,18... | collective-permute-start | bytes 12296 | tf_op jit(solution)/shard_map/ppermute | solution.py:539
  79.0 1.0 collective-permute-start.12
  80.0 20.0 %collective-permute-done.15.refs_4_ = s32[8,128]{1,0:T(8,128)S(1)} collective-permute-done((s32[8,128]{1,0:T(8,128)S(1)}, s32[8,128]{1,0:T(8,128)S(1)}, u32[]{:S(2)}, u32[]{:S(2)}) %collective-permute-start.15) | collective-permute-done | bytes 4128 | tf_op jit(solution)/shard_map/ppermute | solution.py:539
  100.0 2.7 %collective-permute-done.14.refs_3_ = s32[8,128]{1,0:T(8,128)S(1)} collective-permute-done((s32[8,128]{1,0:T(8,128)S(1)}, s32[8,128]{1,0:T(8,128)S(1)}, u32[]{:S(2)}, u32[]{:S(2)}) %collective-permute-start.14) | collective-permute-done | bytes 4128 | tf_op jit(solution)/shard_map/ppermute | solution.py:539
  102.7 1.5 %collective-permute-done.12.refs_1_ = s32[8,128]{1,0:T(8,128)S(1)} collective-permute-done((s32[8,128]{1,0:T(8,128)S(1)}, s32[8,128]{1,0:T(8,128)S(1)}, u32[]{:S(2)}, u32[]{:S(2)}) %collective-permute-start.12) | collective-permute-done | bytes 4128 | tf_op jit(solution)/shard_map/ppermute | solution.py:539
  104.3 1.1 tile_counts.1.weights_ref
  105.4 4.6 %adjoint_tiles.1 = (f32[4,64,128]{2,1,0:T(8,128)S(1)}, bf16[4,64,128]{2,1,0:T(8,128)(2,1)S(1)}, bf16[4,64,128]{2,1,0:T(8,128)(2,1)S(1)}, bf16[4,64,128]{2,1,0:T(8,128)(2,1)S(1)}, f32[16,64,128]{2,1,0:T(8,128)S(1)}) custom-call(s32[1]{0:T(128)} %bitcast.7.q_ref, bf16[256,128]{1,0:T(8,128)(2,1)S(1)} %tile_counts.1.weights_ref, ...), custom_call_target="tpu_custom_call" | custom-call | flops 536870912 | bytes 8388608 | tf_op jit(solution)/shard_map/adjoint_tiles/pallas_call | solution.py:443
  110.0 1.5 %collective-permute-start.18 = (bf16[4,64,128]{2,1,0:T(8,128)(2,1)S(1)}, bf16[4,64,128]{2,1,0:T(8,128)(2,1)S(1)}, u32[]{:S(2)}, u32[]{:S(2)}) collective-permute-start(bf16[4,64,128]{2,1,0:T(8,128)(2,1)S(1)} %get-tuple-element.35), channel_id=1, source_target_pairs={{0,1},{1,2},{2,3},{3,0},{4,5},{5,6},{6,7},{7,4},{8,9},{9,10},{10,1... | collective-permute-start | bytes 196616 | tf_op jit(solution)/shard_map/ppermute | solution.py:555
  111.5 1.9 %collective-permute-start.19 = (bf16[4,64,128]{2,1,0:T(8,128)(2,1)S(1)}, bf16[4,64,128]{2,1,0:T(8,128)(2,1)S(1)}, u32[]{:S(2)}, u32[]{:S(2)}) collective-permute-start(bf16[4,64,128]{2,1,0:T(8,128)(2,1)S(1)} %get-tuple-element.36), channel_id=1, source_target_pairs={{0,2},{1,3},{2,0},{3,1},{4,6},{5,7},{6,4},{7,5},{8,10},{9,11},{10,... | collective-permute-start | bytes 196616 | tf_op jit(solution)/shard_map/ppermute | solution.py:555
  113.4 2.0 %collective-permute-start.20 = (bf16[4,64,128]{2,1,0:T(8,128)(2,1)S(1)}, bf16[4,64,128]{2,1,0:T(8,128)(2,1)S(1)}, u32[]{:S(2)}, u32[]{:S(2)}) collective-permute-start(bf16[4,64,128]{2,1,0:T(8,128)(2,1)S(1)} %get-tuple-element.37), channel_id=1, source_target_pairs={{0,3},{1,0},{2,1},{3,2},{4,7},{5,4},{6,5},{7,6},{8,11},{9,8},{10,9... | collective-permute-start | bytes 196616 | tf_op jit(solution)/shard_map/ppermute | solution.py:555
  116.2 1.1 collective-permute-done.19.refs_1_
  (29 shorter events, 5.2 us)
Async XLA Ops:
  6.9 46.1 %all-to-all-start = ((bf16[64,80,128]{2,1,0:T(8,128)(2,1)}), bf16[64,80,128]{2,1,0:T(8,128)(2,1)S(1)}, u32[]{:S(2)}, u32[]{:S(2)}) async-start(bf16[64,80,128]{2,1,0:T(8,128)(2,1)} %get-tuple-element.24), calls=%async_computation | async-start | bytes 2621440 | tf_op jit(solution)/shard_map/all_to_all | solution.py:516
  18.5 39.3 %copy-start.2 = (s32[1,1,64]{2,1,0:T(1,128)S(1)}, s32[1,1,64]{2,1,0:T(1,128)}, u32[]{:S(2)}) copy-start(s32[1,1,64]{2,1,0:T(1,128)} %param.17) | copy-start | bytes 772
  18.5 15.8 %collective-permute-start = (bf16[64,128]{1,0:T(8,128)(2,1)S(1)}, bf16[64,128]{1,0:T(8,128)(2,1)S(1)}, u32[]{:S(2)}, u32[]{:S(2)}) collective-permute-start(bf16[64,128]{1,0:T(8,128)(2,1)S(1)} %get-tuple-element.20), channel_id=1, source_target_pairs={{0,1},{1,2},{2,3},{4,5},{5,6},{6,7},{8,9},{9,10},{10,11},{12,13},{... | collective-permute-start | bytes 49160 | tf_op jit(solution)/shard_map/ppermute | solution.py:534
  21.9 12.4 %collective-permute-start.1 = (bf16[64,128]{1,0:T(8,128)(2,1)S(1)}, bf16[64,128]{1,0:T(8,128)(2,1)S(1)}, u32[]{:S(2)}, u32[]{:S(2)}) collective-permute-start(bf16[64,128]{1,0:T(8,128)(2,1)S(1)} %get-tuple-element.21), channel_id=1, source_target_pairs={{1,0},{2,1},{3,2},{5,4},{6,5},{7,6},{9,8},{10,9},{11,10},{13,12},{... | collective-permute-start | bytes 49160 | tf_op jit(solution)/shard_map/ppermute | solution.py:535
  23.2 4.8 %collective-permute-start.8 = (s32[8,128]{1,0:T(8,128)S(1)}, s32[8,128]{1,0:T(8,128)S(1)}, u32[]{:S(2)}, u32[]{:S(2)}) collective-permute-start(s32[8,128]{1,0:T(8,128)S(1)} %get-tuple-element.22.refs_0_), channel_id=1, source_target_pairs={{0,28},{4,24},{8,20},{12,16},{16,12},{20,8},{24,4},{28,0},{32,60},... | collective-permute-start | bytes 12296 | tf_op jit(solution)/shard_map/ppermute | solution.py:539
  24.2 5.6 %collective-permute-start.7 = (s32[8,128]{1,0:T(8,128)S(1)}, s32[8,128]{1,0:T(8,128)S(1)}, u32[]{:S(2)}, u32[]{:S(2)}) collective-permute-start(s32[8,128]{1,0:T(8,128)S(1)} %get-tuple-element.22.refs_0_), channel_id=1, source_target_pairs={{0,24},{4,28},{8,16},{12,20},{16,8},{20,12},{24,0},{28,4},{32,56},... | collective-permute-start | bytes 12296 | tf_op jit(solution)/shard_map/ppermute | solution.py:539
  24.8 5.4 %collective-permute-start.6 = (s32[8,128]{1,0:T(8,128)S(1)}, s32[8,128]{1,0:T(8,128)S(1)}, u32[]{:S(2)}, u32[]{:S(2)}) collective-permute-start(s32[8,128]{1,0:T(8,128)S(1)} %get-tuple-element.22.refs_0_), channel_id=1, source_target_pairs={{0,20},{4,16},{8,28},{12,24},{16,4},{20,0},{24,12},{28,8},{32,52},... | collective-permute-start | bytes 12296 | tf_op jit(solution)/shard_map/ppermute | solution.py:539
  28.0 5.1 %collective-permute-start.5 = (s32[8,128]{1,0:T(8,128)S(1)}, s32[8,128]{1,0:T(8,128)S(1)}, u32[]{:S(2)}, u32[]{:S(2)}) collective-permute-start(s32[8,128]{1,0:T(8,128)S(1)} %get-tuple-element.22.refs_0_), channel_id=1, source_target_pairs={{0,16},{4,20},{8,24},{12,28},{16,0},{20,4},{24,8},{28,12},{32,48},... | collective-permute-start | bytes 12296 | tf_op jit(solution)/shard_map/ppermute | solution.py:539
  29.8 3.3 %collective-permute-start.4 = (s32[8,128]{1,0:T(8,128)S(1)}, s32[8,128]{1,0:T(8,128)S(1)}, u32[]{:S(2)}, u32[]{:S(2)}) collective-permute-start(s32[8,128]{1,0:T(8,128)S(1)} %get-tuple-element.22.refs_0_), channel_id=1, source_target_pairs={{0,12},{4,8},{8,4},{12,0},{16,28},{20,24},{24,20},{28,16},{32,44},... | collective-permute-start | bytes 12296 | tf_op jit(solution)/shard_map/ppermute | solution.py:539
  30.3 3.6 %collective-permute-start.3 = (s32[8,128]{1,0:T(8,128)S(1)}, s32[8,128]{1,0:T(8,128)S(1)}, u32[]{:S(2)}, u32[]{:S(2)}) collective-permute-start(s32[8,128]{1,0:T(8,128)S(1)} %get-tuple-element.22.refs_0_), channel_id=1, source_target_pairs={{0,8},{4,12},{8,0},{12,4},{16,24},{20,28},{24,16},{28,20},{32,40},... | collective-permute-start | bytes 12296 | tf_op jit(solution)/shard_map/ppermute | solution.py:539
  33.1 1.2 collective-permute-start.2
  36.2 12.9 %collective-permute-start.11 = (s32[8,128]{1,0:T(8,128)S(1)}, s32[8,128]{1,0:T(8,128)S(1)}, u32[]{:S(2)}, u32[]{:S(2)}) collective-permute-start(s32[8,128]{1,0:T(8,128)S(1)} %get-tuple-element.26.refs_0_.stacked_ref), channel_id=1, source_target_pairs={{0,96},{4,100},{8,104},{12,108},{16,112},{20,116},{24,120},{28,124... | collective-permute-start | bytes 12296 | tf_op jit(solution)/shard_map/ppermute | solution.py:539
  39.7 9.5 %collective-permute-start.10 = (s32[8,128]{1,0:T(8,128)S(1)}, s32[8,128]{1,0:T(8,128)S(1)}, u32[]{:S(2)}, u32[]{:S(2)}) collective-permute-start(s32[8,128]{1,0:T(8,128)S(1)} %get-tuple-element.26.refs_0_.stacked_ref), channel_id=1, source_target_pairs={{0,64},{4,68},{8,72},{12,76},{16,80},{20,84},{24,88},{28,92},{32,9... | collective-permute-start | bytes 12296 | tf_op jit(solution)/shard_map/ppermute | solution.py:539
  39.7 9.5 %collective-permute-start.9 = (s32[8,128]{1,0:T(8,128)S(1)}, s32[8,128]{1,0:T(8,128)S(1)}, u32[]{:S(2)}, u32[]{:S(2)}) collective-permute-start(s32[8,128]{1,0:T(8,128)S(1)} %get-tuple-element.26.refs_0_.stacked_ref), channel_id=1, source_target_pairs={{0,32},{4,36},{8,40},{12,44},{16,48},{20,52},{24,56},{28,60},{32,0... | collective-permute-start | bytes 12296 | tf_op jit(solution)/shard_map/ppermute | solution.py:539
  53.1 7.0 %collective-permute-start.16 = (bf16[64,128]{1,0:T(8,128)(2,1)S(1)}, bf16[64,128]{1,0:T(8,128)(2,1)S(1)}, u32[]{:S(2)}, u32[]{:S(2)}) collective-permute-start(bf16[64,128]{1,0:T(8,128)(2,1)S(1)} %get-tuple-element.29), channel_id=1, source_target_pairs={{0,1},{1,2},{2,3},{4,5},{5,6},{6,7},{8,9},{9,10},{10,11},{12,13},{... | collective-permute-start | bytes 49160 | tf_op jit(solution)/shard_map/ppermute | solution.py:534
  56.5 5.6 %collective-permute-start.17 = (bf16[64,128]{1,0:T(8,128)(2,1)S(1)}, bf16[64,128]{1,0:T(8,128)(2,1)S(1)}, u32[]{:S(2)}, u32[]{:S(2)}) collective-permute-start(bf16[64,128]{1,0:T(8,128)(2,1)S(1)} %get-tuple-element.30), channel_id=1, source_target_pairs={{1,0},{2,1},{3,2},{5,4},{6,5},{7,6},{9,8},{10,9},{11,10},{13,12},{... | collective-permute-start | bytes 49160 | tf_op jit(solution)/shard_map/ppermute | solution.py:535
  64.4 41.0 %all-to-all-start.1 = ((bf16[64,80,128]{2,1,0:T(8,128)(2,1)}), bf16[64,80,128]{2,1,0:T(8,128)(2,1)S(1)}, u32[]{:S(2)}, u32[]{:S(2)}) async-start(bf16[64,80,128]{2,1,0:T(8,128)(2,1)} %stripe.1), calls=%async_computation.1 | async-start | bytes 2621440 | tf_op jit(solution)/shard_map/all_to_all | solution.py:516
  70.0 45.4 %copy-start = (f32[64,2048]{1,0:T(8,128)S(1)}, f32[64,2048]{1,0:T(8,128)}, u32[]{:S(2)}) copy-start(f32[64,2048]{1,0:T(8,128)} %get-tuple-element.33.forward_ref) | copy-start | bytes 1572868
  70.0 30.0 %collective-permute-start.15 = (s32[8,128]{1,0:T(8,128)S(1)}, s32[8,128]{1,0:T(8,128)S(1)}, u32[]{:S(2)}, u32[]{:S(2)}) collective-permute-start(s32[8,128]{1,0:T(8,128)S(1)} %get-tuple-element.28), channel_id=1, source_target_pairs={{0,224},{4,228},{8,232},{12,236},{16,240},{20,244},{24,248},{28,25... | collective-permute-start | bytes 12296 | tf_op jit(solution)/shard_map/ppermute | solution.py:539
  73.2 29.5 %collective-permute-start.14 = (s32[8,128]{1,0:T(8,128)S(1)}, s32[8,128]{1,0:T(8,128)S(1)}, u32[]{:S(2)}, u32[]{:S(2)}) collective-permute-start(s32[8,128]{1,0:T(8,128)S(1)} %get-tuple-element.28), channel_id=1, source_target_pairs={{0,192},{4,196},{8,200},{12,204},{16,208},{20,212},{24,216},{28,22... | collective-permute-start | bytes 12296 | tf_op jit(solution)/shard_map/ppermute | solution.py:539
  75.3 27.4 %collective-permute-start.13 = (s32[8,128]{1,0:T(8,128)S(1)}, s32[8,128]{1,0:T(8,128)S(1)}, u32[]{:S(2)}, u32[]{:S(2)}) collective-permute-start(s32[8,128]{1,0:T(8,128)S(1)} %get-tuple-element.28), channel_id=1, source_target_pairs={{0,160},{4,164},{8,168},{12,172},{16,176},{20,180},{24,184},{28,18... | collective-permute-start | bytes 12296 | tf_op jit(solution)/shard_map/ppermute | solution.py:539
  79.0 25.2 %collective-permute-start.12 = (s32[8,128]{1,0:T(8,128)S(1)}, s32[8,128]{1,0:T(8,128)S(1)}, u32[]{:S(2)}, u32[]{:S(2)}) collective-permute-start(s32[8,128]{1,0:T(8,128)S(1)} %get-tuple-element.28), channel_id=1, source_target_pairs={{0,128},{4,132},{8,136},{12,140},{16,144},{20,148},{24,152},{28,15... | collective-permute-start | bytes 12296 | tf_op jit(solution)/shard_map/ppermute | solution.py:539
  105.4 12.3 %copy-start.1 = (bf16[2048,64]{0,1:T(8,128)(2,1)S(1)}, bf16[2048,64]{0,1:T(8,128)(2,1)}, u32[]{:S(2)}) copy-start(bf16[2048,64]{0,1:T(8,128)(2,1)} %param.11) | copy-start | bytes 786436
  110.0 6.2 %collective-permute-start.18 = (bf16[4,64,128]{2,1,0:T(8,128)(2,1)S(1)}, bf16[4,64,128]{2,1,0:T(8,128)(2,1)S(1)}, u32[]{:S(2)}, u32[]{:S(2)}) collective-permute-start(bf16[4,64,128]{2,1,0:T(8,128)(2,1)S(1)} %get-tuple-element.35), channel_id=1, source_target_pairs={{0,1},{1,2},{2,3},{3,0},{4,5},{5,6},{6,7},{7,4},{8,9},{9,10},{10,1... | collective-permute-start | bytes 196616 | tf_op jit(solution)/shard_map/ppermute | solution.py:555
  111.5 5.8 %collective-permute-start.19 = (bf16[4,64,128]{2,1,0:T(8,128)(2,1)S(1)}, bf16[4,64,128]{2,1,0:T(8,128)(2,1)S(1)}, u32[]{:S(2)}, u32[]{:S(2)}) collective-permute-start(bf16[4,64,128]{2,1,0:T(8,128)(2,1)S(1)} %get-tuple-element.36), channel_id=1, source_target_pairs={{0,2},{1,3},{2,0},{3,1},{4,6},{5,7},{6,4},{7,5},{8,10},{9,11},{10,... | collective-permute-start | bytes 196616 | tf_op jit(solution)/shard_map/ppermute | solution.py:555
  113.4 4.3 %collective-permute-start.20 = (bf16[4,64,128]{2,1,0:T(8,128)(2,1)S(1)}, bf16[4,64,128]{2,1,0:T(8,128)(2,1)S(1)}, u32[]{:S(2)}, u32[]{:S(2)}) collective-permute-start(bf16[4,64,128]{2,1,0:T(8,128)(2,1)S(1)} %get-tuple-element.37), channel_id=1, source_target_pairs={{0,3},{1,0},{2,1},{3,2},{4,7},{5,4},{6,5},{7,6},{8,11},{9,8},{10,9... | collective-permute-start | bytes 196616 | tf_op jit(solution)/shard_map/ppermute | solution.py:555

commit v10 on v9

--- a/solution.py
+++ b/solution.py
@@ -10,7 +10,6 @@
 RELAX = 0.25
 PER = 16
 ROOM = 32
-EARLY = 4
 MIB = 2**20
 F32, BF16 = jnp.float32, jnp.bfloat16
 NT = (((1,), (1,)), ((), ()))
@@ -196,30 +195,25 @@
     )(in_hbm(projections), left, right, in_hbm(taps), *rows)
 
 
-def rim_call(arrived, band, stacks):
+def rim_call(arrived, after):
     angles = arrived.shape[0]
     size = arrived.shape[1] - PER
 
-    def kernel(arrived_ref, _, *refs):
-        n = len(stacks)
-        stack_refs, (head_ref, tail_ref, near_ref, flat) = refs[:n], refs[n:]
-        for m, ref in enumerate(stack_refs):
-            near_ref[m * 8 : (m + 1) * 8, :] = ref[...]
+    def kernel(arrived_ref, _, head_ref, tail_ref, flat):
         flat[...] = arrived_ref[:, size:, :].astype(F32).reshape(angles * PER, T)
         head_ref[...] = flat[pl.ds(0, angles, stride=PER), :].astype(BF16)
         tail_ref[...] = flat[pl.ds(PER - 1, angles, stride=PER), :].astype(BF16)
 
     return pl.pallas_call(
         kernel,
-        out_shape=[jax.ShapeDtypeStruct((angles, T), BF16)] * 2
-        + [jax.ShapeDtypeStruct((8 * len(stacks), T), jnp.int32)],
-        in_specs=[VMEM, HBM] + [VMEM] * len(stacks),
-        out_specs=[VMEM] * 3,
+        out_shape=[jax.ShapeDtypeStruct((angles, T), BF16)] * 2,
+        in_specs=[VMEM, VMEM],
+        out_specs=[VMEM] * 2,
         scratch_shapes=[pltpu.VMEM((angles * PER, T), F32)],
         compiler_params=params(),
         cost_estimate=pl.CostEstimate(flops=2**17, bytes_accessed=2**18, transcendentals=0),
         name="rim",
-    )(arrived, band, *stacks)
+    )(arrived, after)
 
 
 def stripe_of(quarter, quarters, angles, values, rimmed):
@@ -255,7 +249,6 @@
 def back_call(carried, arrived, phase, stacked):
     owners = arrived.shape[0]
     size, columns = phase.shape
-    rows = size + PER
     parts = 4
 
     def kernel(
@@ -272,7 +265,7 @@
             for d in range(n * step, (n + 1) * step):
                 packed[d] = less[:, lanes(c_ref[0, d])]
             here = pl.ds(n * step, step)
-            copies.append(pltpu.make_async_copy(packed.at[here], send_ref.at[here, pl.ds(0, size), :], sems.at[n]))
+            copies.append(pltpu.make_async_copy(packed.at[here], send_ref.at[here], sems.at[n]))
             copies[-1].start()
         stack_ref[...] = stacked_ref[...]
         for copy in copies:
@@ -282,7 +275,7 @@
         kernel,
         out_shape=[
             pltpu.HBM((size, columns), F32),
-            pltpu.HBM((owners, rows, T), BF16),
+            pltpu.HBM((owners, size, T), BF16),
             jax.ShapeDtypeStruct((8, T), jnp.int32),
         ],
         in_specs=[SMEM] + [VMEM] * 3,
@@ -299,12 +292,12 @@
     )(carried, arrived, phase, stacked)
 
 
-def stripe_call(quarter, arrived, left, right, band, back, quarters):
+def stripe_call(quarter, arrived, left, right, band, quarters):
     angles = arrived.shape[0]
     size = arrived.shape[1] - PER
 
     def kernel(
-        q_ref, arrived_ref, l_ref, r_ref, band_ref, _, back_ref, flat, wide, values, rimmed, repeated, sem
+        q_ref, arrived_ref, l_ref, r_ref, band_ref, stripe_ref, flat, wide, values, rimmed
     ):
         def block(n):
             return pl.ds(n * angles, angles)
@@ -328,48 +321,57 @@
         ).astype(BF16)
         for at, b in enumerate([*range(1, PER + 1), 0, PER + 1]):
             values[pl.ds(at, angles, stride=ROOM), :] = filtered[b * angles : (b + 1) * angles].astype(F32)
-        stripe = stripe_of(q_ref[0], quarters, angles, values, rimmed).astype(BF16)
-        repeated[...] = jnp.broadcast_to(stripe[None], repeated.shape)
-        copy = pltpu.make_async_copy(repeated, back_ref.at[:, pl.ds(size, PER), :], sem)
-        copy.start()
-        copy.wait()
-
-    return pl.pallas_call(
-        kernel,
-        out_shape=pltpu.HBM(back.shape, BF16),
-        in_specs=[SMEM] + [VMEM] * 4 + [HBM],
-        out_specs=HBM,
+        stripe_ref[...] = stripe_of(q_ref[0], quarters, angles, values, rimmed).astype(BF16)
+
+    return pl.pallas_call(
+        kernel,
+        out_shape=jax.ShapeDtypeStruct((PER, T), BF16),
+        in_specs=[SMEM] + [VMEM] * 4,
+        out_specs=VMEM,
         scratch_shapes=[
             pltpu.VMEM((angles * PER, T), F32),
             pltpu.VMEM(((PER + 4) * angles, T), BF16),
             pltpu.VMEM((angles * ROOM, T), F32),
             pltpu.VMEM((32, T), F32),
-            pltpu.VMEM((angles, PER, T), BF16),
-            pltpu.SemaphoreType.DMA,
-        ],
-        input_output_aliases={5: 0},
+        ],
         compiler_params=params(),
         cost_estimate=pl.CostEstimate(flops=2**26, bytes_accessed=2**20, transcendentals=0),
         name="stripe",
-    )(quarter, arrived, left, right, band, in_hbm(back))
-
-
-def counts_call(entry, place, slot, count, owner, stacks, owners, entries, blocks):
+    )(quarter, arrived, left, right, band)
+
+
+def bundle_call(stripes, stack):
+    count = len(stripes)
+
+    def kernel(*refs):
+        stripe_refs, (stack_ref, out_ref) = refs[:count], refs[count:]
+        for m, ref in enumerate(stripe_refs):
+            out_ref[m] = ref[...]
+        numbers = stack_ref[...].astype(F32)
+        out_ref[count] = jnp.concatenate([numbers, jnp.zeros_like(numbers)], axis=0).astype(BF16)
+
+    return pl.pallas_call(
+        kernel,
+        out_shape=jax.ShapeDtypeStruct((count + 1, PER, T), BF16),
+        in_specs=[VMEM] * (count + 1),
+        out_specs=VMEM,
+        compiler_params=params(),
+        cost_estimate=pl.CostEstimate(flops=2**15, bytes_accessed=2**16, transcendentals=0),
+        name="bundle",
+    )(*stripes, stack)
+
+
+def counts_call(entry, place, slot, count, owner, after, owners, entries, blocks):
     capacity = entry.shape[1]
 
     def kernel(
-        entry_hbm, place_hbm, slot_hbm, count_ref, owner_ref, *refs
+        entry_hbm, place_hbm, slot_hbm, count_ref, owner_ref, _,
+        met_ref, by_row_ref, entry_ref, place_ref, slot_ref, loads,
     ):
-        n = len(stacks)
-        stack_refs, (weights_ref, entry_ref, place_ref, slot_ref, loads) = refs[:n], refs[n:]
         pairs = [(entry_hbm, entry_ref), (place_hbm, place_ref), (slot_hbm, slot_ref)]
         fetches = [pltpu.make_async_copy(a, b, loads.at[n]) for n, (a, b) in enumerate(pairs)]
         for fetch in fetches:
             fetch.start()
-        lane = lax.broadcasted_iota(jnp.int32, (owners, T), 1)
-        numbers = jnp.concatenate([ref[...] for ref in stack_refs], axis=0).astype(F32)
-        theirs = jnp.sum(jnp.where(lane == owner_ref[0], numbers, 0.0), axis=1, keepdims=True)
-        carries = (theirs.astype(jnp.int32) + owners == lane).astype(F32).astype(BF16)
 
         def ones(rows, match):
             return (lax.broadcasted_iota(jnp.int32, (rows, match.shape[1]), 0) == match).astype(F32).astype(BF16)
@@ -378,19 +380,18 @@
             fetch.wait()
         live = lax.broadcasted_iota(jnp.int32, (1, capacity), 1) < count_ref[0, 0]
         of_bin = ones(entries * blocks, jnp.where(live, entry_ref[...] * blocks + place_ref[...], -1))
-        of_slot = ones(T, slot_ref[...])
-        met = lax.dot_general(of_bin, of_slot, NT, preferred_element_type=F32)
-        k = lax.broadcasted_iota(jnp.int32, (owners, capacity), 0)
-        by_row = (owner_ref[0] ^ k) == slot_ref[...]
-        met_by_row = lax.dot_general(of_bin, by_row.astype(F32).astype(BF16), NT, preferred_element_type=F32)
-        stripe_met = jnp.dot(met_by_row.astype(BF16), carries, preferred_element_type=F32)
-        weights_ref[...] = (met - stripe_met).astype(BF16)
-
-    return pl.pallas_call(
-        kernel,
-        out_shape=jax.ShapeDtypeStruct((entries * blocks, T), BF16),
-        in_specs=[HBM] * 3 + [SMEM, SMEM] + [VMEM] * len(stacks),
-        out_specs=VMEM,
+        met = lax.dot_general(of_bin, ones(T, slot_ref[...]), NT, preferred_element_type=F32)
+        met_ref[...] = met.astype(BF16)
+        k = lax.broadcasted_iota(jnp.int32, (T, capacity), 0)
+        by_row = (k < owners) & ((owner_ref[0] ^ k) == slot_ref[...])
+        by_row = lax.dot_general(of_bin, by_row.astype(F32).astype(BF16), NT, preferred_element_type=F32)
+        by_row_ref[...] = by_row.astype(BF16)
+
+    return pl.pallas_call(
+        kernel,
+        out_shape=[jax.ShapeDtypeStruct((entries * blocks, T), BF16)] * 2,
+        in_specs=[HBM] * 3 + [SMEM, SMEM, VMEM],
+        out_specs=[VMEM, VMEM],
         scratch_shapes=[
             pltpu.VMEM(entry.shape, jnp.int32),
             pltpu.VMEM(place.shape, jnp.int32),
@@ -400,27 +401,36 @@
         compiler_params=params(),
         cost_estimate=pl.CostEstimate(flops=2**24, bytes_accessed=2**20, transcendentals=0),
         name="tile_counts",
-    )(*map(in_hbm, (entry, place, slot)), count, owner, *stacks)
-
-
-def adjoint_call(quarter, weights, returned, library, blocks, quarters):
+    )(*map(in_hbm, (entry, place, slot)), count, owner, after)
+
+
+def adjoint_call(quarter, owner, met, by_row, returned, bundles, library, blocks, quarters):
     entries = library.shape[0]
     owners = returned.shape[0]
-    per = 16
-    size = returned.shape[1] - per
+    per = PER
+    size = returned.shape[1]
+    near = bundles[0].shape[0] - 1
     held = blocks // quarters
 
-    def kernel(q_ref, weights_ref, returned_ref, library_hbm, *refs):
-        outs, (stripe_ref, library_ref, stripes, terms, bins, whole, load) = refs[:quarters], refs[quarters:]
+    def kernel(q_ref, owner_ref, met_ref, by_row_ref, returned_ref, library_hbm, *refs):
+        bundle_refs, refs = refs[: len(bundles)], refs[len(bundles) :]
+        outs, refs = refs[:quarters], refs[quarters:]
+        stripe_ref, library_ref, every, stripes, terms, bins, whole, load = refs
         fetch = pltpu.make_async_copy(library_hbm, library_ref, load)
         fetch.start()
-        stripes[...] = returned_ref[:, size:, :].astype(F32).reshape(owners * per, T)
-        terms[...] = returned_ref[:, :size, :].astype(F32).reshape(owners * size, T)
-        weights = weights_ref[:, : owners + per]
+        terms[...] = returned_ref[...].astype(F32).reshape(owners * size, T)
+        for m, ref in enumerate(bundle_refs):
+            every[m * near : (m + 1) * near] = ref[:near]
+        numbers = jnp.concatenate([ref[near].astype(F32)[:near] for ref in bundle_refs], axis=0)
+        lane = lax.broadcasted_iota(jnp.int32, (owners, T), 1)
+        theirs = jnp.sum(jnp.where(lane == owner_ref[0], numbers, 0.0), axis=1, keepdims=True)
+        carries = (theirs.astype(jnp.int32) + owners == lane).astype(F32).astype(BF16)
+        stripe_met = jnp.dot(by_row_ref[:, :owners], carries, preferred_element_type=F32)
+        weights = (met_ref[...].astype(F32) - stripe_met).astype(BF16)[:, : owners + per]
 
         def both(n):
             here = terms[pl.ds(n, owners, stride=size), :].astype(BF16)
-            return jnp.concatenate([here, returned_ref[n, size:, :]], axis=0)
+            return jnp.concatenate([here, every[owner_ref[0] ^ n]], axis=0)
 
         for n in range(0, size, 2):
             made = jnp.dot(
@@ -437,6 +447,8 @@
             start = lax.rem(q_ref[0] + m, quarters) * held
             for t in range(held):
                 out_ref[t] = whole[pl.ds(start + t, size, stride=blocks), :].astype(out_ref.dtype)
+        for n in range(size):
+            stripes[n * per : (n + 1) * per, :] = every[owner_ref[0] ^ n].astype(F32)
         for b in range(per):
             stripe_ref[b] = stripes[pl.ds(b, size, stride=per), :]
 
@@ -446,10 +458,11 @@
             *(jax.ShapeDtypeStruct((held, size, T), BF16 if m else F32) for m in range(quarters)),
             jax.ShapeDtypeStruct((per, size, T), F32),
         ],
-        in_specs=[SMEM, VMEM, VMEM, HBM],
+        in_specs=[SMEM, SMEM, VMEM, VMEM, VMEM, HBM] + [VMEM] * len(bundles),
         out_specs=[VMEM] * (quarters + 1),
         scratch_shapes=[
             pltpu.VMEM(library.shape, BF16),
+            pltpu.VMEM((owners, per, T), BF16),
             pltpu.VMEM((owners * per, T), F32),
             pltpu.VMEM((owners * size, T), F32),
             pltpu.VMEM((size * blocks, entries * T), BF16),
@@ -461,7 +474,7 @@
             flops=2 * 256 * size * T * T, bytes_accessed=8 * 2**20, transcendentals=0
         ),
         name="adjoint_tiles",
-    )(quarter, weights, returned, in_hbm(library))
+    )(quarter, owner, met, by_row, returned, in_hbm(library), *bundles)
 
 
 def residual_call(phase, stripe, forward):
@@ -542,15 +555,13 @@
     arrived = exchanged(send, "dom")
     rows = [row] + [swapped(row, m) for m in range(1, 8)]
     phase, band, stack = phase_call(projections, *rims(head, tail), phase_kernel, rows)
-    stacks = [stack] + [swapped(stack, m * 8) for m in range(1, EARLY)]
-    head, tail, near = rim_call(arrived, band, stacks)
-    left, right = rims(head, tail)
     forward, back, stack = back_call(carried, arrived, phase, stack)
-    back = stripe_call(quarter, arrived, left, right, band, back, quarters)
     returned = exchanged(back, "dom")
-    stacks = [near] + [swapped(stack, m * 8) for m in range(EARLY, 8)]
-    weights = counts_call(*tiles, owner, stacks, owners, library.shape[0], blocks)
-    own, *sent, stripe = adjoint_call(quarter, weights, returned, library, blocks, quarters)
+    met, by_row = counts_call(*tiles, owner, stack, owners, library.shape[0], blocks)
+    stripe = stripe_call(quarter, arrived, *rims(*rim_call(arrived, stack)), band, quarters)
+    bundle = bundle_call([stripe] + [swapped(stripe, m) for m in range(1, 8)], stack)
+    bundles = [bundle] + [swapped(bundle, m * 8) for m in range(1, 8)]
+    own, *sent, stripe = adjoint_call(quarter, owner, met, by_row, returned, bundles, library, blocks, quarters)
     others = [
         lax.ppermute(part, "ray", [(i, (i + m) % quarters) for i in range(quarters)])
         for m, part in enumerate(sent, 1)

time: 119 us -> 117 us (0.983)
  the two profiles are of different devices: /device:TPU:8 before, /device:TPU:32 now
where the time goes in v10:
time: 117 us; the launch traced here: 116 us
  starting transfers between devices  66.4 us (57%)
  waiting for transfers between devices  29.8 us (25%)
  Pallas kernels  18.4 us (16%)
  between operations  1.46 us (1%)
    ppermute x21, starting transfers between devices, swapped(): return lax.ppermute(array, 'dom', [(i, i ^ m) for i in range(owners)])  31.7 us
    all_to_all x2, starting transfers between devices, exchanged(): return lax.all_to_all(array, axis, split_axis=0, concat_axis=0, tiled=True)  18.2 us
    all_to_all x2, waiting for transfers between devices, exchanged(): return lax.all_to_all(array, axis, split_axis=0, concat_axis=0, tiled=True)  15.1 us
    ppermute x21, waiting for transfers between devices, swapped(): return lax.ppermute(array, 'dom', [(i, i ^ m) for i in range(owners)])  11 us
    ppermute x2, starting transfers between devices, rims(): left = lax.ppermute(tail, 'ray', [(i, i + 1) for i in range(quarters - 1)])  7.5 us
    ppermute x3, starting transfers between devices, shards(): lax.ppermute(part, 'ray', [(i, (i + m) % quarters) for i in range(quarter...  6.41 us
    pallas_call x1, Pallas kernels, first_call(): pl.pallas_call(kernel, out_shape=[pltpu.HBM((owners, rows, T), BF16), jax...  5.59 us
    pallas_call x1, Pallas kernels, adjoint_call(): pl.pallas_call(kernel, out_shape=[*(jax.ShapeDtypeStruct((held, size, T),...  4.56 us
  transfers between devices with their start and end apart: 30, of which 12 were waited for; matrix products, arithmetic and copies ran while one was open for 0% of the time, Pallas kernels for 5%

profile of v10, /device:TPU:32, one launch (start us, length us, event | category | flops | bytes accessed | tf_op | source)
XLA Modules:
  0.0 116.1 jit_solution(11153074125525851364)
XLA Ops:
  1.3 5.6 %forward_tiles.1 = (bf16[64,80,128]{2,1,0:T(8,128)(2,1)}, bf16[64,128]{1,0:T(8,128)(2,1)S(1)}, bf16[64,128]{1,0:T(8,128)(2,1)S(1)}, s32[8,128]{1,0:T(8,128)S(1)}) custom-call(s32[1,256]{1,0:T(1,128)} %bitcast.21, s32[1,256]{1,0:T(1,128)} %bitcast.23, s32[1,256]{1,0:T(1,128)} %bitcast.25, s32[1,1]{1,0:T(1,128)S(6)} %copy.11.count_ref, s32[1,64]{1,0:T(1,128)} %bitcast.13, ...), custom_call_target="tpu_custom_call" | custom-call | flops 536870912 | bytes 8388608 | tf_op jit(solution)/shard_map/forward_tiles/pallas_call | solution.py:115
  6.9 11.8 %all-to-all-start = ((bf16[64,80,128]{2,1,0:T(8,128)(2,1)}), bf16[64,80,128]{2,1,0:T(8,128)(2,1)S(1)}, u32[]{:S(2)}, u32[]{:S(2)}) async-start(bf16[64,80,128]{2,1,0:T(8,128)(2,1)} %get-tuple-element.25), calls=%async_computation | async-start | bytes 2621440 | tf_op jit(solution)/shard_map/all_to_all | solution.py:529
  18.7 3.0 %collective-permute-start = (bf16[64,128]{1,0:T(8,128)(2,1)S(1)}, bf16[64,128]{1,0:T(8,128)(2,1)S(1)}, u32[]{:S(2)}, u32[]{:S(2)}) collective-permute-start(bf16[64,128]{1,0:T(8,128)(2,1)S(1)} %get-tuple-element.21), channel_id=1, source_target_pairs={{0,1},{1,2},{2,3},{4,5},{5,6},{6,7},{8,9},{9,10},{10,11},{12,13},{... | collective-permute-start | bytes 49160 | tf_op jit(solution)/shard_map/ppermute | solution.py:547
  21.6 1.3 %collective-permute-start.1 = (bf16[64,128]{1,0:T(8,128)(2,1)S(1)}, bf16[64,128]{1,0:T(8,128)(2,1)S(1)}, u32[]{:S(2)}, u32[]{:S(2)}) collective-permute-start(bf16[64,128]{1,0:T(8,128)(2,1)S(1)} %get-tuple-element.22), channel_id=1, source_target_pairs={{1,0},{2,1},{3,2},{5,4},{6,5},{7,6},{9,8},{10,9},{11,10},{13,12},{... | collective-permute-start | bytes 49160 | tf_op jit(solution)/shard_map/ppermute | solution.py:548
  23.0 1.6 %collective-permute-start.3 = (s32[8,128]{1,0:T(8,128)S(1)}, s32[8,128]{1,0:T(8,128)S(1)}, u32[]{:S(2)}, u32[]{:S(2)}) collective-permute-start(s32[8,128]{1,0:T(8,128)S(1)} %get-tuple-element.23.refs_0_), channel_id=1, source_target_pairs={{0,8},{4,12},{8,0},{12,4},{16,24},{20,28},{24,16},{28,20},{32,40},... | collective-permute-start | bytes 12296 | tf_op jit(solution)/shard_map/ppermute | solution.py:552
  24.9 3.0 %collective-permute-start.5 = (s32[8,128]{1,0:T(8,128)S(1)}, s32[8,128]{1,0:T(8,128)S(1)}, u32[]{:S(2)}, u32[]{:S(2)}) collective-permute-start(s32[8,128]{1,0:T(8,128)S(1)} %get-tuple-element.23.refs_0_), channel_id=1, source_target_pairs={{0,16},{4,20},{8,24},{12,28},{16,0},{20,4},{24,8},{28,12},{32,48},... | collective-permute-start | bytes 12296 | tf_op jit(solution)/shard_map/ppermute | solution.py:552
  28.6 2.2 %collective-permute-start.7 = (s32[8,128]{1,0:T(8,128)S(1)}, s32[8,128]{1,0:T(8,128)S(1)}, u32[]{:S(2)}, u32[]{:S(2)}) collective-permute-start(s32[8,128]{1,0:T(8,128)S(1)} %get-tuple-element.23.refs_0_), channel_id=1, source_target_pairs={{0,24},{4,28},{8,16},{12,20},{16,8},{20,12},{24,0},{28,4},{32,56},... | collective-permute-start | bytes 12296 | tf_op jit(solution)/shard_map/ppermute | solution.py:552
  30.8 1.6 %collective-permute-start.8 = (s32[8,128]{1,0:T(8,128)S(1)}, s32[8,128]{1,0:T(8,128)S(1)}, u32[]{:S(2)}, u32[]{:S(2)}) collective-permute-start(s32[8,128]{1,0:T(8,128)S(1)} %get-tuple-element.23.refs_0_), channel_id=1, source_target_pairs={{0,28},{4,24},{8,20},{12,16},{16,12},{20,8},{24,4},{28,0},{32,60},... | collective-permute-start | bytes 12296 | tf_op jit(solution)/shard_map/ppermute | solution.py:552
  33.4 1.8 %collective-permute-done.8.refs_7_ = s32[8,128]{1,0:T(8,128)S(1)} collective-permute-done((s32[8,128]{1,0:T(8,128)S(1)}, s32[8,128]{1,0:T(8,128)S(1)}, u32[]{:S(2)}, u32[]{:S(2)}) %collective-permute-start.8) | collective-permute-done | bytes 4128 | tf_op jit(solution)/shard_map/ppermute | solution.py:552
  35.2 1.9 %phase_filter.1 = (bf16[64,2048]{1,0:T(8,128)(2,1)S(1)}, bf16[128,384]{1,0:T(8,128)(2,1)S(1)}, s32[8,128]{1,0:T(8,128)S(1)}) custom-call(bf16[64,2048]{1,0:T(8,128)(2,1)} %bitcast.18, bf16[64,128]{1,0:T(8,128)(2,1)S(1)} %collective-permute-done.l_ref, bf16[64,128]{1,0:T(8,128)(2,1)S(1)} %collective-permute-done.1.r_ref, bf16[129]{0:T(256)(128)(2,1)} %taps_hbm.1, ...), custom_call_target="tpu_custom_call" | custom-call | flops 67108864 | bytes 1048576 | tf_op jit(solution)/shard_map/phase_filter/pallas_call | solution.py:177
  37.1 15.1 %all-to-all-done.arrived_ref = bf16[64,80,128]{2,1,0:T(8,128)(2,1)S(1)} async-done(((bf16[64,80,128]{2,1,0:T(8,128)(2,1)}), bf16[64,80,128]{2,1,0:T(8,128)(2,1)S(1)}, u32[]{:S(2)}, u32[]{:S(2)}) %all-to-all-start) | async-done | bytes 1310752 | tf_op jit(solution)/shard_map/all_to_all | solution.py:529
  52.2 2.2 %slot_sums.1 = (f32[64,2048]{1,0:T(8,128)}, bf16[64,64,128]{2,1,0:T(8,128)(2,1)}, s32[8,128]{1,0:T(8,128)S(1)}) custom-call(s32[1,64]{1,0:T(1,128)S(1)} %bitcast.14, bf16[64,80,128]{2,1,0:T(8,128)(2,1)S(1)} %all-to-all-done.arrived_ref, bf16[64,2048]{1,0:T(8,128)(2,1)S(1)} %get-tuple-element.24.phase_ref, s32[8,128]{1,0:T(8,128)S(1)} %get-tuple-element.26.stacked_ref), custom_call_target="tpu_custom_call" | custom-call | flops 16777216 | bytes 8388608 | tf_op jit(solution)/shard_map/slot_sums/pallas_call | solution.py:274
  54.5 6.4 %all-to-all-start.1 = ((bf16[64,64,128]{2,1,0:T(8,128)(2,1)}), bf16[64,64,128]{2,1,0:T(8,128)(2,1)S(1)}, u32[]{:S(2)}, u32[]{:S(2)}) async-start(bf16[64,64,128]{2,1,0:T(8,128)(2,1)} %get-tuple-element.30), calls=%async_computation.1 | async-start | bytes 2097152 | tf_op jit(solution)/shard_map/all_to_all | solution.py:529
  60.9 1.3 %collective-permute-start.10 = (bf16[64,128]{1,0:T(8,128)(2,1)S(1)}, bf16[64,128]{1,0:T(8,128)(2,1)S(1)}, u32[]{:S(2)}, u32[]{:S(2)}) collective-permute-start(bf16[64,128]{1,0:T(8,128)(2,1)S(1)} %get-tuple-element.32), channel_id=1, source_target_pairs={{1,0},{2,1},{3,2},{5,4},{6,5},{7,6},{9,8},{10,9},{11,10},{13,12},{... | collective-permute-start | bytes 49160 | tf_op jit(solution)/shard_map/ppermute | solution.py:548
  62.2 4.5 %collective-permute-start.9 = (bf16[64,128]{1,0:T(8,128)(2,1)S(1)}, bf16[64,128]{1,0:T(8,128)(2,1)S(1)}, u32[]{:S(2)}, u32[]{:S(2)}) collective-permute-start(bf16[64,128]{1,0:T(8,128)(2,1)S(1)} %get-tuple-element.31), channel_id=1, source_target_pairs={{0,1},{1,2},{2,3},{4,5},{5,6},{6,7},{8,9},{9,10},{10,11},{12,13},{... | collective-permute-start | bytes 49160 | tf_op jit(solution)/shard_map/ppermute | solution.py:547
  66.8 1.4 %collective-permute-done.9.l_ref = bf16[64,128]{1,0:T(8,128)(2,1)S(1)} collective-permute-done((bf16[64,128]{1,0:T(8,128)(2,1)S(1)}, bf16[64,128]{1,0:T(8,128)(2,1)S(1)}, u32[]{:S(2)}, u32[]{:S(2)}) %collective-permute-start.9) | collective-permute-done | bytes 16416 | tf_op jit(solution)/shard_map/ppermute | solution.py:547
  68.2 1.5 %stripe.1.refs_0_ = bf16[16,128]{1,0:T(8,128)(2,1)S(1)} custom-call(s32[1]{0:T(128)} %bitcast.7.q_ref, bf16[64,80,128]{2,1,0:T(8,128)(2,1)S(1)} %all-to-all-done.arrived_ref, bf16[64,128]{1,0:T(8,128)(2,1)S(1)} %collective-permute-done.9.l_ref, bf16[64,128]{1,0:T(8,128)(2,1)S(1)} %collective-permute-done.10.r_ref, ...), custom_call_target="tpu_custom_call" | custom-call | flops 67108864 | bytes 1048576 | tf_op jit(solution)/shard_map/stripe/pallas_call | solution.py:326
  69.9 1.5 %collective-permute-start.12 = (bf16[16,128]{1,0:T(8,128)(2,1)S(1)}, bf16[16,128]{1,0:T(8,128)(2,1)S(1)}, u32[]{:S(2)}, u32[]{:S(2)}) collective-permute-start(bf16[16,128]{1,0:T(8,128)(2,1)S(1)} %stripe.1.refs_0_), channel_id=1, source_target_pairs={{0,8},{4,12},{8,0},{12,4},{16,24},{20,28},{24,16},{28,20},{32,40},... | collective-permute-start | bytes 12296 | tf_op jit(solution)/shard_map/ppermute | solution.py:552
  71.7 3.0 %collective-permute-start.14 = (bf16[16,128]{1,0:T(8,128)(2,1)S(1)}, bf16[16,128]{1,0:T(8,128)(2,1)S(1)}, u32[]{:S(2)}, u32[]{:S(2)}) collective-permute-start(bf16[16,128]{1,0:T(8,128)(2,1)S(1)} %stripe.1.refs_0_), channel_id=1, source_target_pairs={{0,16},{4,20},{8,24},{12,28},{16,0},{20,4},{24,8},{28,12},{32,48},... | collective-permute-start | bytes 12296 | tf_op jit(solution)/shard_map/ppermute | solution.py:552
  74.9 2.7 %collective-permute-start.16 = (bf16[16,128]{1,0:T(8,128)(2,1)S(1)}, bf16[16,128]{1,0:T(8,128)(2,1)S(1)}, u32[]{:S(2)}, u32[]{:S(2)}) collective-permute-start(bf16[16,128]{1,0:T(8,128)(2,1)S(1)} %stripe.1.refs_0_), channel_id=1, source_target_pairs={{0,24},{4,28},{8,16},{12,20},{16,8},{20,12},{24,0},{28,4},{32,56},... | collective-permute-start | bytes 12296 | tf_op jit(solution)/shard_map/ppermute | solution.py:552
  78.0 1.5 %collective-permute-done.15.refs_5_ = bf16[16,128]{1,0:T(8,128)(2,1)S(1)} collective-permute-done((bf16[16,128]{1,0:T(8,128)(2,1)S(1)}, bf16[16,128]{1,0:T(8,128)(2,1)S(1)}, u32[]{:S(2)}, u32[]{:S(2)}) %collective-permute-start.15) | collective-permute-done | bytes 4128 | tf_op jit(solution)/shard_map/ppermute | solution.py:552
  80.1 1.8 %collective-permute-done.17.refs_7_ = bf16[16,128]{1,0:T(8,128)(2,1)S(1)} collective-permute-done((bf16[16,128]{1,0:T(8,128)(2,1)S(1)}, bf16[16,128]{1,0:T(8,128)(2,1)S(1)}, u32[]{:S(2)}, u32[]{:S(2)}) %collective-permute-start.17) | collective-permute-done | bytes 4128 | tf_op jit(solution)/shard_map/ppermute | solution.py:552
  82.6 2.3 %collective-permute-start.19 = (bf16[9,16,128]{2,1,0:T(8,128)(2,1)S(1)}, bf16[9,16,128]{2,1,0:T(8,128)(2,1)S(1)}, u32[]{:S(2)}, u32[]{:S(2)}) collective-permute-start(bf16[9,16,128]{2,1,0:T(8,128)(2,1)S(1)} %bundle.1.refs_0_), channel_id=1, source_target_pairs={{0,64},{4,68},{8,72},{12,76},{16,80},{20,84},{24,88},{28,92},{32,9... | collective-permute-start | bytes 110600 | tf_op jit(solution)/shard_map/ppermute | solution.py:552
  85.5 4.6 %collective-permute-start.21 = (bf16[9,16,128]{2,1,0:T(8,128)(2,1)S(1)}, bf16[9,16,128]{2,1,0:T(8,128)(2,1)S(1)}, u32[]{:S(2)}, u32[]{:S(2)}) collective-permute-start(bf16[9,16,128]{2,1,0:T(8,128)(2,1)S(1)} %bundle.1.refs_0_), channel_id=1, source_target_pairs={{0,128},{4,132},{8,136},{12,140},{16,144},{20,148},{24,152},{28,15... | collective-permute-start | bytes 110600 | tf_op jit(solution)/shard_map/ppermute | solution.py:552
  90.1 1.4 %collective-permute-start.22 = (bf16[9,16,128]{2,1,0:T(8,128)(2,1)S(1)}, bf16[9,16,128]{2,1,0:T(8,128)(2,1)S(1)}, u32[]{:S(2)}, u32[]{:S(2)}) collective-permute-start(bf16[9,16,128]{2,1,0:T(8,128)(2,1)S(1)} %bundle.1.refs_0_), channel_id=1, source_target_pairs={{0,160},{4,164},{8,168},{12,172},{16,176},{20,180},{24,184},{28,18... | collective-permute-start | bytes 110600 | tf_op jit(solution)/shard_map/ppermute | solution.py:552
  91.5 2.8 %collective-permute-start.23 = (bf16[9,16,128]{2,1,0:T(8,128)(2,1)S(1)}, bf16[9,16,128]{2,1,0:T(8,128)(2,1)S(1)}, u32[]{:S(2)}, u32[]{:S(2)}) collective-permute-start(bf16[9,16,128]{2,1,0:T(8,128)(2,1)S(1)} %bundle.1.refs_0_), channel_id=1, source_target_pairs={{0,192},{4,196},{8,200},{12,204},{16,208},{20,212},{24,216},{28,22... | collective-permute-start | bytes 110600 | tf_op jit(solution)/shard_map/ppermute | solution.py:552
  94.3 1.7 %collective-permute-start.24 = (bf16[9,16,128]{2,1,0:T(8,128)(2,1)S(1)}, bf16[9,16,128]{2,1,0:T(8,128)(2,1)S(1)}, u32[]{:S(2)}, u32[]{:S(2)}) collective-permute-start(bf16[9,16,128]{2,1,0:T(8,128)(2,1)S(1)} %bundle.1.refs_0_), channel_id=1, source_target_pairs={{0,224},{4,228},{8,232},{12,236},{16,240},{20,244},{24,248},{28,25... | collective-permute-start | bytes 110600 | tf_op jit(solution)/shard_map/ppermute | solution.py:552
  98.2 3.1 %collective-permute-done.24.refs_7_ = bf16[9,16,128]{2,1,0:T(8,128)(2,1)S(1)} collective-permute-done((bf16[9,16,128]{2,1,0:T(8,128)(2,1)S(1)}, bf16[9,16,128]{2,1,0:T(8,128)(2,1)S(1)}, u32[]{:S(2)}, u32[]{:S(2)}) %collective-permute-start.24) | collective-permute-done | bytes 36896 | tf_op jit(solution)/shard_map/ppermute | solution.py:552
  101.3 4.6 %adjoint_tiles.1 = (f32[4,64,128]{2,1,0:T(8,128)S(1)}, bf16[4,64,128]{2,1,0:T(8,128)(2,1)S(1)}, bf16[4,64,128]{2,1,0:T(8,128)(2,1)S(1)}, bf16[4,64,128]{2,1,0:T(8,128)(2,1)S(1)}, f32[16,64,128]{2,1,0:T(8,128)S(1)}) custom-call(s32[1]{0:T(128)} %bitcast.7.q_ref, s32[1]{0:T(128)} %bitcast.8.owner_ref, bf16[256,128]{1,0:T(8,128)(2,1)S(1)} %get-tuple-element.28.met_ref, ...), custom_call_target="tpu_custom_call" | custom-call | flops 536870912 | bytes 8388608 | tf_op jit(solution)/shard_map/adjoint_tiles/pallas_call | solution.py:455
  105.9 2.4 %collective-permute-start.25 = (bf16[4,64,128]{2,1,0:T(8,128)(2,1)S(1)}, bf16[4,64,128]{2,1,0:T(8,128)(2,1)S(1)}, u32[]{:S(2)}, u32[]{:S(2)}) collective-permute-start(bf16[4,64,128]{2,1,0:T(8,128)(2,1)S(1)} %get-tuple-element.37), channel_id=1, source_target_pairs={{0,1},{1,2},{2,3},{3,0},{4,5},{5,6},{6,7},{7,4},{8,9},{9,10},{10,1... | collective-permute-start | bytes 196616 | tf_op jit(solution)/shard_map/ppermute | solution.py:566
  108.2 2.9 %collective-permute-start.26 = (bf16[4,64,128]{2,1,0:T(8,128)(2,1)S(1)}, bf16[4,64,128]{2,1,0:T(8,128)(2,1)S(1)}, u32[]{:S(2)}, u32[]{:S(2)}) collective-permute-start(bf16[4,64,128]{2,1,0:T(8,128)(2,1)S(1)} %get-tuple-element.38), channel_id=1, source_target_pairs={{0,2},{1,3},{2,0},{3,1},{4,6},{5,7},{6,4},{7,5},{8,10},{9,11},{10,... | collective-permute-start | bytes 196616 | tf_op jit(solution)/shard_map/ppermute | solution.py:566
  114.0 1.3 %collective-permute-done.27.refs_2_ = bf16[4,64,128]{2,1,0:T(8,128)(2,1)S(1)} collective-permute-done((bf16[4,64,128]{2,1,0:T(8,128)(2,1)S(1)}, bf16[4,64,128]{2,1,0:T(8,128)(2,1)S(1)}, u32[]{:S(2)}, u32[]{:S(2)}) %collective-permute-start.27) | collective-permute-done | bytes 65568 | tf_op jit(solution)/shard_map/ppermute | solution.py:566
  (44 shorter events, 10.9 us)
Async XLA Ops:
  6.9 45.3 %copy-start.2 = (s32[1,1,64]{2,1,0:T(1,128)S(1)}, s32[1,1,64]{2,1,0:T(1,128)}, u32[]{:S(2)}) copy-start(s32[1,1,64]{2,1,0:T(1,128)} %param.17) | copy-start | bytes 772
  6.9 45.3 %all-to-all-start = ((bf16[64,80,128]{2,1,0:T(8,128)(2,1)}), bf16[64,80,128]{2,1,0:T(8,128)(2,1)S(1)}, u32[]{:S(2)}, u32[]{:S(2)}) async-start(bf16[64,80,128]{2,1,0:T(8,128)(2,1)} %get-tuple-element.25), calls=%async_computation | async-start | bytes 2621440 | tf_op jit(solution)/shard_map/all_to_all | solution.py:529
  18.7 16.5 %collective-permute-start = (bf16[64,128]{1,0:T(8,128)(2,1)S(1)}, bf16[64,128]{1,0:T(8,128)(2,1)S(1)}, u32[]{:S(2)}, u32[]{:S(2)}) collective-permute-start(bf16[64,128]{1,0:T(8,128)(2,1)S(1)} %get-tuple-element.21), channel_id=1, source_target_pairs={{0,1},{1,2},{2,3},{4,5},{5,6},{6,7},{8,9},{9,10},{10,11},{12,13},{... | collective-permute-start | bytes 49160 | tf_op jit(solution)/shard_map/ppermute | solution.py:547
  21.6 13.6 %collective-permute-start.1 = (bf16[64,128]{1,0:T(8,128)(2,1)S(1)}, bf16[64,128]{1,0:T(8,128)(2,1)S(1)}, u32[]{:S(2)}, u32[]{:S(2)}) collective-permute-start(bf16[64,128]{1,0:T(8,128)(2,1)S(1)} %get-tuple-element.22), channel_id=1, source_target_pairs={{1,0},{2,1},{3,2},{5,4},{6,5},{7,6},{9,8},{10,9},{11,10},{13,12},{... | collective-permute-start | bytes 49160 | tf_op jit(solution)/shard_map/ppermute | solution.py:548
  22.9 2.0 %collective-permute-start.2 = (s32[8,128]{1,0:T(8,128)S(1)}, s32[8,128]{1,0:T(8,128)S(1)}, u32[]{:S(2)}, u32[]{:S(2)}) collective-permute-start(s32[8,128]{1,0:T(8,128)S(1)} %get-tuple-element.23.refs_0_), channel_id=1, source_target_pairs={{0,4},{4,0},{8,12},{12,8},{16,20},{20,16},{24,28},{28,24},{32,36},... | collective-permute-start | bytes 12296 | tf_op jit(solution)/shard_map/ppermute | solution.py:552
  23.0 4.9 %collective-permute-start.3 = (s32[8,128]{1,0:T(8,128)S(1)}, s32[8,128]{1,0:T(8,128)S(1)}, u32[]{:S(2)}, u32[]{:S(2)}) collective-permute-start(s32[8,128]{1,0:T(8,128)S(1)} %get-tuple-element.23.refs_0_), channel_id=1, source_target_pairs={{0,8},{4,12},{8,0},{12,4},{16,24},{20,28},{24,16},{28,20},{32,40},... | collective-permute-start | bytes 12296 | tf_op jit(solution)/shard_map/ppermute | solution.py:552
  24.6 4.0 %collective-permute-start.4 = (s32[8,128]{1,0:T(8,128)S(1)}, s32[8,128]{1,0:T(8,128)S(1)}, u32[]{:S(2)}, u32[]{:S(2)}) collective-permute-start(s32[8,128]{1,0:T(8,128)S(1)} %get-tuple-element.23.refs_0_), channel_id=1, source_target_pairs={{0,12},{4,8},{8,4},{12,0},{16,28},{20,24},{24,20},{28,16},{32,44},... | collective-permute-start | bytes 12296 | tf_op jit(solution)/shard_map/ppermute | solution.py:552
  24.9 5.9 %collective-permute-start.5 = (s32[8,128]{1,0:T(8,128)S(1)}, s32[8,128]{1,0:T(8,128)S(1)}, u32[]{:S(2)}, u32[]{:S(2)}) collective-permute-start(s32[8,128]{1,0:T(8,128)S(1)} %get-tuple-element.23.refs_0_), channel_id=1, source_target_pairs={{0,16},{4,20},{8,24},{12,28},{16,0},{20,4},{24,8},{28,12},{32,48},... | collective-permute-start | bytes 12296 | tf_op jit(solution)/shard_map/ppermute | solution.py:552
  27.9 4.6 %collective-permute-start.6 = (s32[8,128]{1,0:T(8,128)S(1)}, s32[8,128]{1,0:T(8,128)S(1)}, u32[]{:S(2)}, u32[]{:S(2)}) collective-permute-start(s32[8,128]{1,0:T(8,128)S(1)} %get-tuple-element.23.refs_0_), channel_id=1, source_target_pairs={{0,20},{4,16},{8,28},{12,24},{16,4},{20,0},{24,12},{28,8},{32,52},... | collective-permute-start | bytes 12296 | tf_op jit(solution)/shard_map/ppermute | solution.py:552
  28.6 4.8 %collective-permute-start.7 = (s32[8,128]{1,0:T(8,128)S(1)}, s32[8,128]{1,0:T(8,128)S(1)}, u32[]{:S(2)}, u32[]{:S(2)}) collective-permute-start(s32[8,128]{1,0:T(8,128)S(1)} %get-tuple-element.23.refs_0_), channel_id=1, source_target_pairs={{0,24},{4,28},{8,16},{12,20},{16,8},{20,12},{24,0},{28,4},{32,56},... | collective-permute-start | bytes 12296 | tf_op jit(solution)/shard_map/ppermute | solution.py:552
  30.8 4.4 %collective-permute-start.8 = (s32[8,128]{1,0:T(8,128)S(1)}, s32[8,128]{1,0:T(8,128)S(1)}, u32[]{:S(2)}, u32[]{:S(2)}) collective-permute-start(s32[8,128]{1,0:T(8,128)S(1)} %get-tuple-element.23.refs_0_), channel_id=1, source_target_pairs={{0,28},{4,24},{8,20},{12,16},{16,12},{20,8},{24,4},{28,0},{32,60},... | collective-permute-start | bytes 12296 | tf_op jit(solution)/shard_map/ppermute | solution.py:552
  54.5 46.8 %all-to-all-start.1 = ((bf16[64,64,128]{2,1,0:T(8,128)(2,1)}), bf16[64,64,128]{2,1,0:T(8,128)(2,1)S(1)}, u32[]{:S(2)}, u32[]{:S(2)}) async-start(bf16[64,64,128]{2,1,0:T(8,128)(2,1)} %get-tuple-element.30), calls=%async_computation.1 | async-start | bytes 2097152 | tf_op jit(solution)/shard_map/all_to_all | solution.py:529
  60.9 5.9 %collective-permute-start.10 = (bf16[64,128]{1,0:T(8,128)(2,1)S(1)}, bf16[64,128]{1,0:T(8,128)(2,1)S(1)}, u32[]{:S(2)}, u32[]{:S(2)}) collective-permute-start(bf16[64,128]{1,0:T(8,128)(2,1)S(1)} %get-tuple-element.32), channel_id=1, source_target_pairs={{1,0},{2,1},{3,2},{5,4},{6,5},{7,6},{9,8},{10,9},{11,10},{13,12},{... | collective-permute-start | bytes 49160 | tf_op jit(solution)/shard_map/ppermute | solution.py:548
  62.2 6.0 %collective-permute-start.9 = (bf16[64,128]{1,0:T(8,128)(2,1)S(1)}, bf16[64,128]{1,0:T(8,128)(2,1)S(1)}, u32[]{:S(2)}, u32[]{:S(2)}) collective-permute-start(bf16[64,128]{1,0:T(8,128)(2,1)S(1)} %get-tuple-element.31), channel_id=1, source_target_pairs={{0,1},{1,2},{2,3},{4,5},{5,6},{6,7},{8,9},{9,10},{10,11},{12,13},{... | collective-permute-start | bytes 49160 | tf_op jit(solution)/shard_map/ppermute | solution.py:547
  69.7 42.5 %copy-start = (f32[64,2048]{1,0:T(8,128)S(1)}, f32[64,2048]{1,0:T(8,128)}, u32[]{:S(2)}) copy-start(f32[64,2048]{1,0:T(8,128)} %get-tuple-element.35.forward_ref) | copy-start | bytes 1572868
  69.8 5.2 %collective-permute-start.11 = (bf16[16,128]{1,0:T(8,128)(2,1)S(1)}, bf16[16,128]{1,0:T(8,128)(2,1)S(1)}, u32[]{:S(2)}, u32[]{:S(2)}) collective-permute-start(bf16[16,128]{1,0:T(8,128)(2,1)S(1)} %stripe.1.refs_0_), channel_id=1, source_target_pairs={{0,4},{4,0},{8,12},{12,8},{16,20},{20,16},{24,28},{28,24},{32,36},... | collective-permute-start | bytes 12296 | tf_op jit(solution)/shard_map/ppermute | solution.py:552
  69.9 7.8 %collective-permute-start.12 = (bf16[16,128]{1,0:T(8,128)(2,1)S(1)}, bf16[16,128]{1,0:T(8,128)(2,1)S(1)}, u32[]{:S(2)}, u32[]{:S(2)}) collective-permute-start(bf16[16,128]{1,0:T(8,128)(2,1)S(1)} %stripe.1.refs_0_), channel_id=1, source_target_pairs={{0,8},{4,12},{8,0},{12,4},{16,24},{20,28},{24,16},{28,20},{32,40},... | collective-permute-start | bytes 12296 | tf_op jit(solution)/shard_map/ppermute | solution.py:552
  71.4 6.6 %collective-permute-start.13 = (bf16[16,128]{1,0:T(8,128)(2,1)S(1)}, bf16[16,128]{1,0:T(8,128)(2,1)S(1)}, u32[]{:S(2)}, u32[]{:S(2)}) collective-permute-start(bf16[16,128]{1,0:T(8,128)(2,1)S(1)} %stripe.1.refs_0_), channel_id=1, source_target_pairs={{0,12},{4,8},{8,4},{12,0},{16,28},{20,24},{24,20},{28,16},{32,44},... | collective-permute-start | bytes 12296 | tf_op jit(solution)/shard_map/ppermute | solution.py:552
  71.7 6.2 %collective-permute-start.14 = (bf16[16,128]{1,0:T(8,128)(2,1)S(1)}, bf16[16,128]{1,0:T(8,128)(2,1)S(1)}, u32[]{:S(2)}, u32[]{:S(2)}) collective-permute-start(bf16[16,128]{1,0:T(8,128)(2,1)S(1)} %stripe.1.refs_0_), channel_id=1, source_target_pairs={{0,16},{4,20},{8,24},{12,28},{16,0},{20,4},{24,8},{28,12},{32,48},... | collective-permute-start | bytes 12296 | tf_op jit(solution)/shard_map/ppermute | solution.py:552
  74.7 4.8 %collective-permute-start.15 = (bf16[16,128]{1,0:T(8,128)(2,1)S(1)}, bf16[16,128]{1,0:T(8,128)(2,1)S(1)}, u32[]{:S(2)}, u32[]{:S(2)}) collective-permute-start(bf16[16,128]{1,0:T(8,128)(2,1)S(1)} %stripe.1.refs_0_), channel_id=1, source_target_pairs={{0,20},{4,16},{8,28},{12,24},{16,4},{20,0},{24,12},{28,8},{32,52},... | collective-permute-start | bytes 12296 | tf_op jit(solution)/shard_map/ppermute | solution.py:552
  74.9 5.1 %collective-permute-start.16 = (bf16[16,128]{1,0:T(8,128)(2,1)S(1)}, bf16[16,128]{1,0:T(8,128)(2,1)S(1)}, u32[]{:S(2)}, u32[]{:S(2)}) collective-permute-start(bf16[16,128]{1,0:T(8,128)(2,1)S(1)} %stripe.1.refs_0_), channel_id=1, source_target_pairs={{0,24},{4,28},{8,16},{12,20},{16,8},{20,12},{24,0},{28,4},{32,56},... | collective-permute-start | bytes 12296 | tf_op jit(solution)/shard_map/ppermute | solution.py:552
  77.6 4.3 %collective-permute-start.17 = (bf16[16,128]{1,0:T(8,128)(2,1)S(1)}, bf16[16,128]{1,0:T(8,128)(2,1)S(1)}, u32[]{:S(2)}, u32[]{:S(2)}) collective-permute-start(bf16[16,128]{1,0:T(8,128)(2,1)S(1)} %stripe.1.refs_0_), channel_id=1, source_target_pairs={{0,28},{4,24},{8,20},{12,16},{16,12},{20,8},{24,4},{28,0},{32,60},... | collective-permute-start | bytes 12296 | tf_op jit(solution)/shard_map/ppermute | solution.py:552
  81.9 9.6 %collective-permute-start.18 = (bf16[9,16,128]{2,1,0:T(8,128)(2,1)S(1)}, bf16[9,16,128]{2,1,0:T(8,128)(2,1)S(1)}, u32[]{:S(2)}, u32[]{:S(2)}) collective-permute-start(bf16[9,16,128]{2,1,0:T(8,128)(2,1)S(1)} %bundle.1.refs_0_), channel_id=1, source_target_pairs={{0,32},{4,36},{8,40},{12,44},{16,48},{20,52},{24,56},{28,60},{32,0... | collective-permute-start | bytes 110600 | tf_op jit(solution)/shard_map/ppermute | solution.py:552
  82.6 11.7 %collective-permute-start.19 = (bf16[9,16,128]{2,1,0:T(8,128)(2,1)S(1)}, bf16[9,16,128]{2,1,0:T(8,128)(2,1)S(1)}, u32[]{:S(2)}, u32[]{:S(2)}) collective-permute-start(bf16[9,16,128]{2,1,0:T(8,128)(2,1)S(1)} %bundle.1.refs_0_), channel_id=1, source_target_pairs={{0,64},{4,68},{8,72},{12,76},{16,80},{20,84},{24,88},{28,92},{32,9... | collective-permute-start | bytes 110600 | tf_op jit(solution)/shard_map/ppermute | solution.py:552
  84.9 12.1 %collective-permute-start.20 = (bf16[9,16,128]{2,1,0:T(8,128)(2,1)S(1)}, bf16[9,16,128]{2,1,0:T(8,128)(2,1)S(1)}, u32[]{:S(2)}, u32[]{:S(2)}) collective-permute-start(bf16[9,16,128]{2,1,0:T(8,128)(2,1)S(1)} %bundle.1.refs_0_), channel_id=1, source_target_pairs={{0,96},{4,100},{8,104},{12,108},{16,112},{20,116},{24,120},{28,124... | collective-permute-start | bytes 110600 | tf_op jit(solution)/shard_map/ppermute | solution.py:552
  85.5 11.5 %collective-permute-start.21 = (bf16[9,16,128]{2,1,0:T(8,128)(2,1)S(1)}, bf16[9,16,128]{2,1,0:T(8,128)(2,1)S(1)}, u32[]{:S(2)}, u32[]{:S(2)}) collective-permute-start(bf16[9,16,128]{2,1,0:T(8,128)(2,1)S(1)} %bundle.1.refs_0_), channel_id=1, source_target_pairs={{0,128},{4,132},{8,136},{12,140},{16,144},{20,148},{24,152},{28,15... | collective-permute-start | bytes 110600 | tf_op jit(solution)/shard_map/ppermute | solution.py:552
  90.1 8.1 %collective-permute-start.22 = (bf16[9,16,128]{2,1,0:T(8,128)(2,1)S(1)}, bf16[9,16,128]{2,1,0:T(8,128)(2,1)S(1)}, u32[]{:S(2)}, u32[]{:S(2)}) collective-permute-start(bf16[9,16,128]{2,1,0:T(8,128)(2,1)S(1)} %bundle.1.refs_0_), channel_id=1, source_target_pairs={{0,160},{4,164},{8,168},{12,172},{16,176},{20,180},{24,184},{28,18... | collective-permute-start | bytes 110600 | tf_op jit(solution)/shard_map/ppermute | solution.py:552
  91.5 6.7 %collective-permute-start.23 = (bf16[9,16,128]{2,1,0:T(8,128)(2,1)S(1)}, bf16[9,16,128]{2,1,0:T(8,128)(2,1)S(1)}, u32[]{:S(2)}, u32[]{:S(2)}) collective-permute-start(bf16[9,16,128]{2,1,0:T(8,128)(2,1)S(1)} %bundle.1.refs_0_), channel_id=1, source_target_pairs={{0,192},{4,196},{8,200},{12,204},{16,208},{20,212},{24,216},{28,22... | collective-permute-start | bytes 110600 | tf_op jit(solution)/shard_map/ppermute | solution.py:552
  94.3 7.0 %collective-permute-start.24 = (bf16[9,16,128]{2,1,0:T(8,128)(2,1)S(1)}, bf16[9,16,128]{2,1,0:T(8,128)(2,1)S(1)}, u32[]{:S(2)}, u32[]{:S(2)}) collective-permute-start(bf16[9,16,128]{2,1,0:T(8,128)(2,1)S(1)} %bundle.1.refs_0_), channel_id=1, source_target_pairs={{0,224},{4,228},{8,232},{12,236},{16,240},{20,244},{24,248},{28,25... | collective-permute-start | bytes 110600 | tf_op jit(solution)/shard_map/ppermute | solution.py:552
  105.9 7.2 %collective-permute-start.25 = (bf16[4,64,128]{2,1,0:T(8,128)(2,1)S(1)}, bf16[4,64,128]{2,1,0:T(8,128)(2,1)S(1)}, u32[]{:S(2)}, u32[]{:S(2)}) collective-permute-start(bf16[4,64,128]{2,1,0:T(8,128)(2,1)S(1)} %get-tuple-element.37), channel_id=1, source_target_pairs={{0,1},{1,2},{2,3},{3,0},{4,5},{5,6},{6,7},{7,4},{8,9},{9,10},{10,1... | collective-permute-start | bytes 196616 | tf_op jit(solution)/shard_map/ppermute | solution.py:566
  108.2 5.8 %collective-permute-start.26 = (bf16[4,64,128]{2,1,0:T(8,128)(2,1)S(1)}, bf16[4,64,128]{2,1,0:T(8,128)(2,1)S(1)}, u32[]{:S(2)}, u32[]{:S(2)}) collective-permute-start(bf16[4,64,128]{2,1,0:T(8,128)(2,1)S(1)} %get-tuple-element.38), channel_id=1, source_target_pairs={{0,2},{1,3},{2,0},{3,1},{4,6},{5,7},{6,4},{7,5},{8,10},{9,11},{10,... | collective-permute-start | bytes 196616 | tf_op jit(solution)/shard_map/ppermute | solution.py:566
  111.1 4.3 %collective-permute-start.27 = (bf16[4,64,128]{2,1,0:T(8,128)(2,1)S(1)}, bf16[4,64,128]{2,1,0:T(8,128)(2,1)S(1)}, u32[]{:S(2)}, u32[]{:S(2)}) collective-permute-start(bf16[4,64,128]{2,1,0:T(8,128)(2,1)S(1)} %get-tuple-element.39), channel_id=1, source_target_pairs={{0,3},{1,0},{2,1},{3,2},{4,7},{5,4},{6,5},{7,6},{8,11},{9,8},{10,9... | collective-permute-start | bytes 196616 | tf_op jit(solution)/shard_map/ppermute | solution.py:566
  (1 other events, 14.1 us)

commit v11 on v10

--- a/solution.py
+++ b/solution.py
@@ -321,11 +321,11 @@
         ).astype(BF16)
         for at, b in enumerate([*range(1, PER + 1), 0, PER + 1]):
             values[pl.ds(at, angles, stride=ROOM), :] = filtered[b * angles : (b + 1) * angles].astype(F32)
-        stripe_ref[...] = stripe_of(q_ref[0], quarters, angles, values, rimmed).astype(BF16)
-
-    return pl.pallas_call(
-        kernel,
-        out_shape=jax.ShapeDtypeStruct((PER, T), BF16),
+        stripe_ref[0] = stripe_of(q_ref[0], quarters, angles, values, rimmed).astype(BF16)
+
+    return pl.pallas_call(
+        kernel,
+        out_shape=jax.ShapeDtypeStruct((1, PER, T), BF16),
         in_specs=[SMEM] + [VMEM] * 4,
         out_specs=VMEM,
         scratch_shapes=[
@@ -340,25 +340,30 @@
     )(quarter, arrived, left, right, band)
 
 
-def bundle_call(stripes, stack):
-    count = len(stripes)
+def joined_call(arrays, stack=None):
+    lengths = [array.shape[0] for array in arrays]
+    whole = sum(lengths)
+    given = list(arrays) + ([] if stack is None else [stack])
 
     def kernel(*refs):
-        stripe_refs, (stack_ref, out_ref) = refs[:count], refs[count:]
-        for m, ref in enumerate(stripe_refs):
-            out_ref[m] = ref[...]
-        numbers = stack_ref[...].astype(F32)
-        out_ref[count] = jnp.concatenate([numbers, jnp.zeros_like(numbers)], axis=0).astype(BF16)
-
-    return pl.pallas_call(
-        kernel,
-        out_shape=jax.ShapeDtypeStruct((count + 1, PER, T), BF16),
-        in_specs=[VMEM] * (count + 1),
+        out_ref = refs[-1]
+        start = 0
+        for ref, length in zip(refs, lengths):
+            out_ref[start : start + length] = ref[...]
+            start += length
+        if stack is not None:
+            numbers = refs[-2][...].astype(F32)
+            out_ref[whole] = jnp.concatenate([numbers, jnp.zeros_like(numbers)], axis=0).astype(BF16)
+
+    return pl.pallas_call(
+        kernel,
+        out_shape=jax.ShapeDtypeStruct((whole + (stack is not None), PER, T), BF16),
+        in_specs=[VMEM] * len(given),
         out_specs=VMEM,
         compiler_params=params(),
         cost_estimate=pl.CostEstimate(flops=2**15, bytes_accessed=2**16, transcendentals=0),
-        name="bundle",
-    )(*stripes, stack)
+        name="joined",
+    )(*given)
 
 
 def counts_call(entry, place, slot, count, owner, after, owners, entries, blocks):
@@ -409,7 +414,8 @@
     owners = returned.shape[0]
     per = PER
     size = returned.shape[1]
-    near = bundles[0].shape[0] - 1
+    near = 8
+    each = bundles[0].shape[0] // (near + 1)
     held = blocks // quarters
 
     def kernel(q_ref, owner_ref, met_ref, by_row_ref, returned_ref, library_hbm, *refs):
@@ -419,9 +425,13 @@
         fetch = pltpu.make_async_copy(library_hbm, library_ref, load)
         fetch.start()
         terms[...] = returned_ref[...].astype(F32).reshape(owners * size, T)
-        for m, ref in enumerate(bundle_refs):
-            every[m * near : (m + 1) * near] = ref[:near]
-        numbers = jnp.concatenate([ref[near].astype(F32)[:near] for ref in bundle_refs], axis=0)
+        numbers = []
+        for ref in bundle_refs:
+            for t in range(0, each * (near + 1), near + 1):
+                m = len(numbers)
+                every[m * near : (m + 1) * near] = ref[t : t + near]
+                numbers.append(ref[t + near].astype(F32)[:near])
+        numbers = jnp.concatenate(numbers, axis=0)
         lane = lax.broadcasted_iota(jnp.int32, (owners, T), 1)
         theirs = jnp.sum(jnp.where(lane == owner_ref[0], numbers, 0.0), axis=1, keepdims=True)
         carries = (theirs.astype(jnp.int32) + owners == lane).astype(F32).astype(BF16)
@@ -559,8 +569,10 @@
     returned = exchanged(back, "dom")
     met, by_row = counts_call(*tiles, owner, stack, owners, library.shape[0], blocks)
     stripe = stripe_call(quarter, arrived, *rims(*rim_call(arrived, stack)), band, quarters)
-    bundle = bundle_call([stripe] + [swapped(stripe, m) for m in range(1, 8)], stack)
-    bundles = [bundle] + [swapped(bundle, m * 8) for m in range(1, 8)]
+    pair = joined_call([stripe, swapped(stripe, 1)])
+    bundle = joined_call([pair] + [swapped(pair, m) for m in (2, 4, 6)], stack)
+    twin = joined_call([bundle, swapped(bundle, 8)])
+    bundles = [twin] + [swapped(twin, m) for m in (16, 32, 48)]
     own, *sent, stripe = adjoint_call(quarter, owner, met, by_row, returned, bundles, library, blocks, quarters)
     others = [
         lax.ppermute(part, "ray", [(i, (i + m) % quarters) for i in range(quarters)])

time: 117 us -> 114 us (0.974)
  the two profiles are of different devices: /device:TPU:32 before, /device:TPU:8 now
where the time goes in v11:
time: 114 us; the launch traced here: 112 us
  starting transfers between devices  52.5 us (46%)
  waiting for transfers between devices  41 us (36%)
  Pallas kernels  17.2 us (15%)
  between operations  1.45 us (1%)
    ppermute x15, waiting for transfers between devices, swapped(): return lax.ppermute(array, 'dom', [(i, i ^ m) for i in range(owners)])  19.3 us
    ppermute x15, starting transfers between devices, swapped(): return lax.ppermute(array, 'dom', [(i, i ^ m) for i in range(owners)])  18.8 us
    all_to_all x2, starting transfers between devices, exchanged(): return lax.all_to_all(array, axis, split_axis=0, concat_axis=0, tiled=True)  18.2 us
    all_to_all x2, waiting for transfers between devices, exchanged(): return lax.all_to_all(array, axis, split_axis=0, concat_axis=0, tiled=True)  18 us
    ppermute x2, starting transfers between devices, rims(): left = lax.ppermute(tail, 'ray', [(i, i + 1) for i in range(quarters - 1)])  7.5 us
    ppermute x3, starting transfers between devices, shards(): lax.ppermute(part, 'ray', [(i, (i + m) % quarters) for i in range(quarter...  5.41 us
    pallas_call x1, Pallas kernels, adjoint_call(): pl.pallas_call(kernel, out_shape=[*(jax.ShapeDtypeStruct((held, size, T),...  4.55 us
    pallas_call x1, Pallas kernels, first_call(): pl.pallas_call(kernel, out_shape=[pltpu.HBM((owners, rows, T), BF16), jax...  4.42 us
  transfers between devices with their start and end apart: 24, of which 15 were waited for; matrix products, arithmetic and copies ran while one was open for 0% of the time, Pallas kernels for 5%

profile of v11, /device:TPU:8, one launch (start us, length us, event | category | flops | bytes accessed | tf_op | source)
XLA Modules:
  0.0 112.2 jit_solution(484512351469582288)
XLA Ops:
  1.3 4.4 %forward_tiles.1 = (bf16[64,80,128]{2,1,0:T(8,128)(2,1)}, bf16[64,128]{1,0:T(8,128)(2,1)S(1)}, bf16[64,128]{1,0:T(8,128)(2,1)S(1)}, s32[8,128]{1,0:T(8,128)S(1)}) custom-call(s32[1,256]{1,0:T(1,128)} %bitcast.21, s32[1,256]{1,0:T(1,128)} %bitcast.23, s32[1,256]{1,0:T(1,128)} %bitcast.25, s32[1,1]{1,0:T(1,128)S(6)} %copy.11.count_ref, s32[1,64]{1,0:T(1,128)} %bitcast.13, ...), custom_call_target="tpu_custom_call" | custom-call | flops 536870912 | bytes 8388608 | tf_op jit(solution)/shard_map/forward_tiles/pallas_call | solution.py:115
  5.7 12.7 %all-to-all-start = ((bf16[64,80,128]{2,1,0:T(8,128)(2,1)}), bf16[64,80,128]{2,1,0:T(8,128)(2,1)S(1)}, u32[]{:S(2)}, u32[]{:S(2)}) async-start(bf16[64,80,128]{2,1,0:T(8,128)(2,1)} %get-tuple-element.25), calls=%async_computation | async-start | bytes 2621440 | tf_op jit(solution)/shard_map/all_to_all | solution.py:539
  18.4 3.0 %collective-permute-start = (bf16[64,128]{1,0:T(8,128)(2,1)S(1)}, bf16[64,128]{1,0:T(8,128)(2,1)S(1)}, u32[]{:S(2)}, u32[]{:S(2)}) collective-permute-start(bf16[64,128]{1,0:T(8,128)(2,1)S(1)} %get-tuple-element.21), channel_id=1, source_target_pairs={{0,1},{1,2},{2,3},{4,5},{5,6},{6,7},{8,9},{9,10},{10,11},{12,13},{... | collective-permute-start | bytes 49160 | tf_op jit(solution)/shard_map/ppermute | solution.py:557
  21.4 1.3 %collective-permute-start.1 = (bf16[64,128]{1,0:T(8,128)(2,1)S(1)}, bf16[64,128]{1,0:T(8,128)(2,1)S(1)}, u32[]{:S(2)}, u32[]{:S(2)}) collective-permute-start(bf16[64,128]{1,0:T(8,128)(2,1)S(1)} %get-tuple-element.22), channel_id=1, source_target_pairs={{1,0},{2,1},{3,2},{5,4},{6,5},{7,6},{9,8},{10,9},{11,10},{13,12},{... | collective-permute-start | bytes 49160 | tf_op jit(solution)/shard_map/ppermute | solution.py:558
  23.3 1.3 %collective-permute-start.4 = (s32[8,128]{1,0:T(8,128)S(1)}, s32[8,128]{1,0:T(8,128)S(1)}, u32[]{:S(2)}, u32[]{:S(2)}) collective-permute-start(s32[8,128]{1,0:T(8,128)S(1)} %get-tuple-element.23.refs_0_), channel_id=1, source_target_pairs={{0,12},{4,8},{8,4},{12,0},{16,28},{20,24},{24,20},{28,16},{32,44},... | collective-permute-start | bytes 12296 | tf_op jit(solution)/shard_map/ppermute | solution.py:562
  24.7 2.1 %collective-permute-start.5 = (s32[8,128]{1,0:T(8,128)S(1)}, s32[8,128]{1,0:T(8,128)S(1)}, u32[]{:S(2)}, u32[]{:S(2)}) collective-permute-start(s32[8,128]{1,0:T(8,128)S(1)} %get-tuple-element.23.refs_0_), channel_id=1, source_target_pairs={{0,16},{4,20},{8,24},{12,28},{16,0},{20,4},{24,8},{28,12},{32,48},... | collective-permute-start | bytes 12296 | tf_op jit(solution)/shard_map/ppermute | solution.py:562
  26.8 1.1 %collective-permute-start.6 = (s32[8,128]{1,0:T(8,128)S(1)}, s32[8,128]{1,0:T(8,128)S(1)}, u32[]{:S(2)}, u32[]{:S(2)}) collective-permute-start(s32[8,128]{1,0:T(8,128)S(1)} %get-tuple-element.23.refs_0_), channel_id=1, source_target_pairs={{0,20},{4,16},{8,28},{12,24},{16,4},{20,0},{24,12},{28,8},{32,52},... | collective-permute-start | bytes 12296 | tf_op jit(solution)/shard_map/ppermute | solution.py:562
  27.9 1.5 %collective-permute-start.7 = (s32[8,128]{1,0:T(8,128)S(1)}, s32[8,128]{1,0:T(8,128)S(1)}, u32[]{:S(2)}, u32[]{:S(2)}) collective-permute-start(s32[8,128]{1,0:T(8,128)S(1)} %get-tuple-element.23.refs_0_), channel_id=1, source_target_pairs={{0,24},{4,28},{8,16},{12,20},{16,8},{20,12},{24,0},{28,4},{32,56},... | collective-permute-start | bytes 12296 | tf_op jit(solution)/shard_map/ppermute | solution.py:562
  31.7 1.2 %collective-permute-done.8.refs_7_ = s32[8,128]{1,0:T(8,128)S(1)} collective-permute-done((s32[8,128]{1,0:T(8,128)S(1)}, s32[8,128]{1,0:T(8,128)S(1)}, u32[]{:S(2)}, u32[]{:S(2)}) %collective-permute-start.8) | collective-permute-done | bytes 4128 | tf_op jit(solution)/shard_map/ppermute | solution.py:562
  32.9 1.9 %phase_filter.1 = (bf16[64,2048]{1,0:T(8,128)(2,1)S(1)}, bf16[128,384]{1,0:T(8,128)(2,1)S(1)}, s32[8,128]{1,0:T(8,128)S(1)}) custom-call(bf16[64,2048]{1,0:T(8,128)(2,1)} %bitcast.18, bf16[64,128]{1,0:T(8,128)(2,1)S(1)} %collective-permute-done.l_ref, bf16[64,128]{1,0:T(8,128)(2,1)S(1)} %collective-permute-done.1.r_ref, bf16[129]{0:T(256)(128)(2,1)} %taps_hbm.1, ...), custom_call_target="tpu_custom_call" | custom-call | flops 67108864 | bytes 1048576 | tf_op jit(solution)/shard_map/phase_filter/pallas_call | solution.py:177
  34.8 18.0 %all-to-all-done.arrived_ref = bf16[64,80,128]{2,1,0:T(8,128)(2,1)S(1)} async-done(((bf16[64,80,128]{2,1,0:T(8,128)(2,1)}), bf16[64,80,128]{2,1,0:T(8,128)(2,1)S(1)}, u32[]{:S(2)}, u32[]{:S(2)}) %all-to-all-start) | async-done | bytes 1310752 | tf_op jit(solution)/shard_map/all_to_all | solution.py:539
  52.9 2.2 %slot_sums.1 = (f32[64,2048]{1,0:T(8,128)}, bf16[64,64,128]{2,1,0:T(8,128)(2,1)}, s32[8,128]{1,0:T(8,128)S(1)}) custom-call(s32[1,64]{1,0:T(1,128)S(1)} %bitcast.14, bf16[64,80,128]{2,1,0:T(8,128)(2,1)S(1)} %all-to-all-done.arrived_ref, bf16[64,2048]{1,0:T(8,128)(2,1)S(1)} %get-tuple-element.24.phase_ref, s32[8,128]{1,0:T(8,128)S(1)} %get-tuple-element.26.stacked_ref), custom_call_target="tpu_custom_call" | custom-call | flops 16777216 | bytes 8388608 | tf_op jit(solution)/shard_map/slot_sums/pallas_call | solution.py:274
  55.1 5.5 %all-to-all-start.1 = ((bf16[64,64,128]{2,1,0:T(8,128)(2,1)}), bf16[64,64,128]{2,1,0:T(8,128)(2,1)S(1)}, u32[]{:S(2)}, u32[]{:S(2)}) async-start(bf16[64,64,128]{2,1,0:T(8,128)(2,1)} %get-tuple-element.30), calls=%async_computation.1 | async-start | bytes 2097152 | tf_op jit(solution)/shard_map/all_to_all | solution.py:539
  60.7 1.3 %collective-permute-start.10 = (bf16[64,128]{1,0:T(8,128)(2,1)S(1)}, bf16[64,128]{1,0:T(8,128)(2,1)S(1)}, u32[]{:S(2)}, u32[]{:S(2)}) collective-permute-start(bf16[64,128]{1,0:T(8,128)(2,1)S(1)} %get-tuple-element.32), channel_id=1, source_target_pairs={{1,0},{2,1},{3,2},{5,4},{6,5},{7,6},{9,8},{10,9},{11,10},{13,12},{... | collective-permute-start | bytes 49160 | tf_op jit(solution)/shard_map/ppermute | solution.py:558
  62.0 4.5 %collective-permute-start.9 = (bf16[64,128]{1,0:T(8,128)(2,1)S(1)}, bf16[64,128]{1,0:T(8,128)(2,1)S(1)}, u32[]{:S(2)}, u32[]{:S(2)}) collective-permute-start(bf16[64,128]{1,0:T(8,128)(2,1)S(1)} %get-tuple-element.31), channel_id=1, source_target_pairs={{0,1},{1,2},{2,3},{4,5},{5,6},{6,7},{8,9},{9,10},{10,11},{12,13},{... | collective-permute-start | bytes 49160 | tf_op jit(solution)/shard_map/ppermute | solution.py:557
  66.5 1.4 %collective-permute-done.9.l_ref = bf16[64,128]{1,0:T(8,128)(2,1)S(1)} collective-permute-done((bf16[64,128]{1,0:T(8,128)(2,1)S(1)}, bf16[64,128]{1,0:T(8,128)(2,1)S(1)}, u32[]{:S(2)}, u32[]{:S(2)}) %collective-permute-start.9) | collective-permute-done | bytes 16416 | tf_op jit(solution)/shard_map/ppermute | solution.py:557
  68.0 1.5 %stripe.1.refs_0_ = bf16[1,16,128]{2,1,0:T(8,128)(2,1)S(1)} custom-call(s32[1]{0:T(128)} %bitcast.7.q_ref, bf16[64,80,128]{2,1,0:T(8,128)(2,1)S(1)} %all-to-all-done.arrived_ref, bf16[64,128]{1,0:T(8,128)(2,1)S(1)} %collective-permute-done.9.l_ref, bf16[64,128]{1,0:T(8,128)(2,1)S(1)} %collective-permute-done.10.r_ref, ...), custom_call_target="tpu_custom_call" | custom-call | flops 67108864 | bytes 1048576 | tf_op jit(solution)/shard_map/stripe/pallas_call | solution.py:326
  69.6 1.2 %collective-permute-done.11.refs_1_ = bf16[1,16,128]{2,1,0:T(8,128)(2,1)S(1)} collective-permute-done((bf16[1,16,128]{2,1,0:T(8,128)(2,1)S(1)}, bf16[1,16,128]{2,1,0:T(8,128)(2,1)S(1)}, u32[]{:S(2)}, u32[]{:S(2)}) %collective-permute-start.11) | collective-permute-done | bytes 4128 | tf_op jit(solution)/shard_map/ppermute | solution.py:562
  71.2 2.5 %collective-permute-start.13 = (bf16[2,16,128]{2,1,0:T(8,128)(2,1)S(1)}, bf16[2,16,128]{2,1,0:T(8,128)(2,1)S(1)}, u32[]{:S(2)}, u32[]{:S(2)}) collective-permute-start(bf16[2,16,128]{2,1,0:T(8,128)(2,1)S(1)} %joined.3.refs_0_), channel_id=1, source_target_pairs={{0,16},{4,20},{8,24},{12,28},{16,0},{20,4},{24,8},{28,12},{32,48},... | collective-permute-start | bytes 24584 | tf_op jit(solution)/shard_map/ppermute | solution.py:562
  74.4 2.0 %collective-permute-done.13.refs_2_ = bf16[2,16,128]{2,1,0:T(8,128)(2,1)S(1)} collective-permute-done((bf16[2,16,128]{2,1,0:T(8,128)(2,1)S(1)}, bf16[2,16,128]{2,1,0:T(8,128)(2,1)S(1)}, u32[]{:S(2)}, u32[]{:S(2)}) %collective-permute-start.13) | collective-permute-done | bytes 8224 | tf_op jit(solution)/shard_map/ppermute | solution.py:562
  77.4 1.5 %collective-permute-start.15 = (bf16[9,16,128]{2,1,0:T(8,128)(2,1)S(1)}, bf16[9,16,128]{2,1,0:T(8,128)(2,1)S(1)}, u32[]{:S(2)}, u32[]{:S(2)}) collective-permute-start(bf16[9,16,128]{2,1,0:T(8,128)(2,1)S(1)} %joined.4.refs_0_), channel_id=1, source_target_pairs={{0,32},{4,36},{8,40},{12,44},{16,48},{20,52},{24,56},{28,60},{32,0... | collective-permute-start | bytes 110600 | tf_op jit(solution)/shard_map/ppermute | solution.py:562
  78.9 7.3 %collective-permute-done.15.refs_1_ = bf16[9,16,128]{2,1,0:T(8,128)(2,1)S(1)} collective-permute-done((bf16[9,16,128]{2,1,0:T(8,128)(2,1)S(1)}, bf16[9,16,128]{2,1,0:T(8,128)(2,1)S(1)}, u32[]{:S(2)}, u32[]{:S(2)}) %collective-permute-start.15) | collective-permute-done | bytes 36896 | tf_op jit(solution)/shard_map/ppermute | solution.py:562
  86.2 1.4 %collective-permute-start.16 = (bf16[18,16,128]{2,1,0:T(8,128)(2,1)S(1)}, bf16[18,16,128]{2,1,0:T(8,128)(2,1)S(1)}, u32[]{:S(2)}, u32[]{:S(2)}) collective-permute-start(bf16[18,16,128]{2,1,0:T(8,128)(2,1)S(1)} %joined.5.refs_0_), channel_id=1, source_target_pairs={{0,64},{4,68},{8,72},{12,76},{16,80},{20,84},{24,88},{28,92},{32,9... | collective-permute-start | bytes 221192 | tf_op jit(solution)/shard_map/ppermute | solution.py:562
  87.6 3.6 %collective-permute-start.17 = (bf16[18,16,128]{2,1,0:T(8,128)(2,1)S(1)}, bf16[18,16,128]{2,1,0:T(8,128)(2,1)S(1)}, u32[]{:S(2)}, u32[]{:S(2)}) collective-permute-start(bf16[18,16,128]{2,1,0:T(8,128)(2,1)S(1)} %joined.5.refs_0_), channel_id=1, source_target_pairs={{0,128},{4,132},{8,136},{12,140},{16,144},{20,148},{24,152},{28,15... | collective-permute-start | bytes 221192 | tf_op jit(solution)/shard_map/ppermute | solution.py:562
  91.1 1.5 %collective-permute-start.18 = (bf16[18,16,128]{2,1,0:T(8,128)(2,1)S(1)}, bf16[18,16,128]{2,1,0:T(8,128)(2,1)S(1)}, u32[]{:S(2)}, u32[]{:S(2)}) collective-permute-start(bf16[18,16,128]{2,1,0:T(8,128)(2,1)S(1)} %joined.5.refs_0_), channel_id=1, source_target_pairs={{0,192},{4,196},{8,200},{12,204},{16,208},{20,212},{24,216},{28,22... | collective-permute-start | bytes 221192 | tf_op jit(solution)/shard_map/ppermute | solution.py:562
  93.7 2.3 %collective-permute-done.17.refs_2_ = bf16[18,16,128]{2,1,0:T(8,128)(2,1)S(1)} collective-permute-done((bf16[18,16,128]{2,1,0:T(8,128)(2,1)S(1)}, bf16[18,16,128]{2,1,0:T(8,128)(2,1)S(1)}, u32[]{:S(2)}, u32[]{:S(2)}) %collective-permute-start.17) | collective-permute-done | bytes 73760 | tf_op jit(solution)/shard_map/ppermute | solution.py:562
  95.9 2.5 %collective-permute-done.18.refs_3_ = bf16[18,16,128]{2,1,0:T(8,128)(2,1)S(1)} collective-permute-done((bf16[18,16,128]{2,1,0:T(8,128)(2,1)S(1)}, bf16[18,16,128]{2,1,0:T(8,128)(2,1)S(1)}, u32[]{:S(2)}, u32[]{:S(2)}) %collective-permute-start.18) | collective-permute-done | bytes 73760 | tf_op jit(solution)/shard_map/ppermute | solution.py:562
  98.4 4.6 %adjoint_tiles.1 = (f32[4,64,128]{2,1,0:T(8,128)S(1)}, bf16[4,64,128]{2,1,0:T(8,128)(2,1)S(1)}, bf16[4,64,128]{2,1,0:T(8,128)(2,1)S(1)}, bf16[4,64,128]{2,1,0:T(8,128)(2,1)S(1)}, f32[16,64,128]{2,1,0:T(8,128)S(1)}) custom-call(s32[1]{0:T(128)} %bitcast.7.q_ref, s32[1]{0:T(128)} %bitcast.8.owner_ref, bf16[256,128]{1,0:T(8,128)(2,1)S(1)} %get-tuple-element.28.met_ref, ...), custom_call_target="tpu_custom_call" | custom-call | flops 536870912 | bytes 8388608 | tf_op jit(solution)/shard_map/adjoint_tiles/pallas_call | solution.py:465
  103.0 1.1 collective-permute-start.19
  104.1 3.1 %collective-permute-start.20 = (bf16[4,64,128]{2,1,0:T(8,128)(2,1)S(1)}, bf16[4,64,128]{2,1,0:T(8,128)(2,1)S(1)}, u32[]{:S(2)}, u32[]{:S(2)}) collective-permute-start(bf16[4,64,128]{2,1,0:T(8,128)(2,1)S(1)} %get-tuple-element.38), channel_id=1, source_target_pairs={{0,2},{1,3},{2,0},{3,1},{4,6},{5,7},{6,4},{7,5},{8,10},{9,11},{10,... | collective-permute-start | bytes 196616 | tf_op jit(solution)/shard_map/ppermute | solution.py:578
  107.2 1.2 %collective-permute-start.21 = (bf16[4,64,128]{2,1,0:T(8,128)(2,1)S(1)}, bf16[4,64,128]{2,1,0:T(8,128)(2,1)S(1)}, u32[]{:S(2)}, u32[]{:S(2)}) collective-permute-start(bf16[4,64,128]{2,1,0:T(8,128)(2,1)S(1)} %get-tuple-element.39), channel_id=1, source_target_pairs={{0,3},{1,0},{2,1},{3,2},{4,7},{5,4},{6,5},{7,6},{8,11},{9,8},{10,9... | collective-permute-start | bytes 196616 | tf_op jit(solution)/shard_map/ppermute | solution.py:578
  110.2 1.3 %collective-permute-done.21.refs_2_ = bf16[4,64,128]{2,1,0:T(8,128)(2,1)S(1)} collective-permute-done((bf16[4,64,128]{2,1,0:T(8,128)(2,1)S(1)}, bf16[4,64,128]{2,1,0:T(8,128)(2,1)S(1)}, u32[]{:S(2)}, u32[]{:S(2)}) %collective-permute-start.21) | collective-permute-done | bytes 65568 | tf_op jit(solution)/shard_map/ppermute | solution.py:578
  (34 shorter events, 8.8 us)
Async XLA Ops:
  5.7 47.2 %copy-start.2 = (s32[1,1,64]{2,1,0:T(1,128)S(1)}, s32[1,1,64]{2,1,0:T(1,128)}, u32[]{:S(2)}) copy-start(s32[1,1,64]{2,1,0:T(1,128)} %param.17) | copy-start | bytes 772
  5.7 47.1 %all-to-all-start = ((bf16[64,80,128]{2,1,0:T(8,128)(2,1)}), bf16[64,80,128]{2,1,0:T(8,128)(2,1)S(1)}, u32[]{:S(2)}, u32[]{:S(2)}) async-start(bf16[64,80,128]{2,1,0:T(8,128)(2,1)} %get-tuple-element.25), calls=%async_computation | async-start | bytes 2621440 | tf_op jit(solution)/shard_map/all_to_all | solution.py:539
  18.4 14.5 %collective-permute-start = (bf16[64,128]{1,0:T(8,128)(2,1)S(1)}, bf16[64,128]{1,0:T(8,128)(2,1)S(1)}, u32[]{:S(2)}, u32[]{:S(2)}) collective-permute-start(bf16[64,128]{1,0:T(8,128)(2,1)S(1)} %get-tuple-element.21), channel_id=1, source_target_pairs={{0,1},{1,2},{2,3},{4,5},{5,6},{6,7},{8,9},{9,10},{10,11},{12,13},{... | collective-permute-start | bytes 49160 | tf_op jit(solution)/shard_map/ppermute | solution.py:557
  21.4 11.5 %collective-permute-start.1 = (bf16[64,128]{1,0:T(8,128)(2,1)S(1)}, bf16[64,128]{1,0:T(8,128)(2,1)S(1)}, u32[]{:S(2)}, u32[]{:S(2)}) collective-permute-start(bf16[64,128]{1,0:T(8,128)(2,1)S(1)} %get-tuple-element.22), channel_id=1, source_target_pairs={{1,0},{2,1},{3,2},{5,4},{6,5},{7,6},{9,8},{10,9},{11,10},{13,12},{... | collective-permute-start | bytes 49160 | tf_op jit(solution)/shard_map/ppermute | solution.py:558
  22.7 2.0 %collective-permute-start.2 = (s32[8,128]{1,0:T(8,128)S(1)}, s32[8,128]{1,0:T(8,128)S(1)}, u32[]{:S(2)}, u32[]{:S(2)}) collective-permute-start(s32[8,128]{1,0:T(8,128)S(1)} %get-tuple-element.23.refs_0_), channel_id=1, source_target_pairs={{0,4},{4,0},{8,12},{12,8},{16,20},{20,16},{24,28},{28,24},{32,36},... | collective-permute-start | bytes 12296 | tf_op jit(solution)/shard_map/ppermute | solution.py:562
  22.8 4.0 %collective-permute-start.3 = (s32[8,128]{1,0:T(8,128)S(1)}, s32[8,128]{1,0:T(8,128)S(1)}, u32[]{:S(2)}, u32[]{:S(2)}) collective-permute-start(s32[8,128]{1,0:T(8,128)S(1)} %get-tuple-element.23.refs_0_), channel_id=1, source_target_pairs={{0,8},{4,12},{8,0},{12,4},{16,24},{20,28},{24,16},{28,20},{32,40},... | collective-permute-start | bytes 12296 | tf_op jit(solution)/shard_map/ppermute | solution.py:562
  23.3 4.6 %collective-permute-start.4 = (s32[8,128]{1,0:T(8,128)S(1)}, s32[8,128]{1,0:T(8,128)S(1)}, u32[]{:S(2)}, u32[]{:S(2)}) collective-permute-start(s32[8,128]{1,0:T(8,128)S(1)} %get-tuple-element.23.refs_0_), channel_id=1, source_target_pairs={{0,12},{4,8},{8,4},{12,0},{16,28},{20,24},{24,20},{28,16},{32,44},... | collective-permute-start | bytes 12296 | tf_op jit(solution)/shard_map/ppermute | solution.py:562
  24.7 5.2 %collective-permute-start.5 = (s32[8,128]{1,0:T(8,128)S(1)}, s32[8,128]{1,0:T(8,128)S(1)}, u32[]{:S(2)}, u32[]{:S(2)}) collective-permute-start(s32[8,128]{1,0:T(8,128)S(1)} %get-tuple-element.23.refs_0_), channel_id=1, source_target_pairs={{0,16},{4,20},{8,24},{12,28},{16,0},{20,4},{24,8},{28,12},{32,48},... | collective-permute-start | bytes 12296 | tf_op jit(solution)/shard_map/ppermute | solution.py:562
  26.8 4.6 %collective-permute-start.6 = (s32[8,128]{1,0:T(8,128)S(1)}, s32[8,128]{1,0:T(8,128)S(1)}, u32[]{:S(2)}, u32[]{:S(2)}) collective-permute-start(s32[8,128]{1,0:T(8,128)S(1)} %get-tuple-element.23.refs_0_), channel_id=1, source_target_pairs={{0,20},{4,16},{8,28},{12,24},{16,4},{20,0},{24,12},{28,8},{32,52},... | collective-permute-start | bytes 12296 | tf_op jit(solution)/shard_map/ppermute | solution.py:562
  27.9 3.8 %collective-permute-start.7 = (s32[8,128]{1,0:T(8,128)S(1)}, s32[8,128]{1,0:T(8,128)S(1)}, u32[]{:S(2)}, u32[]{:S(2)}) collective-permute-start(s32[8,128]{1,0:T(8,128)S(1)} %get-tuple-element.23.refs_0_), channel_id=1, source_target_pairs={{0,24},{4,28},{8,16},{12,20},{16,8},{20,12},{24,0},{28,4},{32,56},... | collective-permute-start | bytes 12296 | tf_op jit(solution)/shard_map/ppermute | solution.py:562
  29.8 3.1 %collective-permute-start.8 = (s32[8,128]{1,0:T(8,128)S(1)}, s32[8,128]{1,0:T(8,128)S(1)}, u32[]{:S(2)}, u32[]{:S(2)}) collective-permute-start(s32[8,128]{1,0:T(8,128)S(1)} %get-tuple-element.23.refs_0_), channel_id=1, source_target_pairs={{0,28},{4,24},{8,20},{12,16},{16,12},{20,8},{24,4},{28,0},{32,60},... | collective-permute-start | bytes 12296 | tf_op jit(solution)/shard_map/ppermute | solution.py:562
  55.1 43.4 %all-to-all-start.1 = ((bf16[64,64,128]{2,1,0:T(8,128)(2,1)}), bf16[64,64,128]{2,1,0:T(8,128)(2,1)S(1)}, u32[]{:S(2)}, u32[]{:S(2)}) async-start(bf16[64,64,128]{2,1,0:T(8,128)(2,1)} %get-tuple-element.30), calls=%async_computation.1 | async-start | bytes 2097152 | tf_op jit(solution)/shard_map/all_to_all | solution.py:539
  60.7 5.9 %collective-permute-start.10 = (bf16[64,128]{1,0:T(8,128)(2,1)S(1)}, bf16[64,128]{1,0:T(8,128)(2,1)S(1)}, u32[]{:S(2)}, u32[]{:S(2)}) collective-permute-start(bf16[64,128]{1,0:T(8,128)(2,1)S(1)} %get-tuple-element.32), channel_id=1, source_target_pairs={{1,0},{2,1},{3,2},{5,4},{6,5},{7,6},{9,8},{10,9},{11,10},{13,12},{... | collective-permute-start | bytes 49160 | tf_op jit(solution)/shard_map/ppermute | solution.py:558
  62.0 6.0 %collective-permute-start.9 = (bf16[64,128]{1,0:T(8,128)(2,1)S(1)}, bf16[64,128]{1,0:T(8,128)(2,1)S(1)}, u32[]{:S(2)}, u32[]{:S(2)}) collective-permute-start(bf16[64,128]{1,0:T(8,128)(2,1)S(1)} %get-tuple-element.31), channel_id=1, source_target_pairs={{0,1},{1,2},{2,3},{4,5},{5,6},{6,7},{8,9},{9,10},{10,11},{12,13},{... | collective-permute-start | bytes 49160 | tf_op jit(solution)/shard_map/ppermute | solution.py:557
  69.5 38.9 %copy-start = (f32[64,2048]{1,0:T(8,128)S(1)}, f32[64,2048]{1,0:T(8,128)}, u32[]{:S(2)}) copy-start(f32[64,2048]{1,0:T(8,128)} %get-tuple-element.35.forward_ref) | copy-start | bytes 1572868
  69.5 1.3 %collective-permute-start.11 = (bf16[1,16,128]{2,1,0:T(8,128)(2,1)S(1)}, bf16[1,16,128]{2,1,0:T(8,128)(2,1)S(1)}, u32[]{:S(2)}, u32[]{:S(2)}) collective-permute-start(bf16[1,16,128]{2,1,0:T(8,128)(2,1)S(1)} %stripe.1.refs_0_), channel_id=1, source_target_pairs={{0,4},{4,0},{8,12},{12,8},{16,20},{20,16},{24,28},{28,24},{32,36},... | collective-permute-start | bytes 12296 | tf_op jit(solution)/shard_map/ppermute | solution.py:562
  70.8 3.7 %collective-permute-start.12 = (bf16[2,16,128]{2,1,0:T(8,128)(2,1)S(1)}, bf16[2,16,128]{2,1,0:T(8,128)(2,1)S(1)}, u32[]{:S(2)}, u32[]{:S(2)}) collective-permute-start(bf16[2,16,128]{2,1,0:T(8,128)(2,1)S(1)} %joined.3.refs_0_), channel_id=1, source_target_pairs={{0,8},{4,12},{8,0},{12,4},{16,24},{20,28},{24,16},{28,20},{32,40},... | collective-permute-start | bytes 24584 | tf_op jit(solution)/shard_map/ppermute | solution.py:562
  71.2 5.2 %collective-permute-start.13 = (bf16[2,16,128]{2,1,0:T(8,128)(2,1)S(1)}, bf16[2,16,128]{2,1,0:T(8,128)(2,1)S(1)}, u32[]{:S(2)}, u32[]{:S(2)}) collective-permute-start(bf16[2,16,128]{2,1,0:T(8,128)(2,1)S(1)} %joined.3.refs_0_), channel_id=1, source_target_pairs={{0,16},{4,20},{8,24},{12,28},{16,0},{20,4},{24,8},{28,12},{32,48},... | collective-permute-start | bytes 24584 | tf_op jit(solution)/shard_map/ppermute | solution.py:562
  73.7 3.7 %collective-permute-start.14 = (bf16[2,16,128]{2,1,0:T(8,128)(2,1)S(1)}, bf16[2,16,128]{2,1,0:T(8,128)(2,1)S(1)}, u32[]{:S(2)}, u32[]{:S(2)}) collective-permute-start(bf16[2,16,128]{2,1,0:T(8,128)(2,1)S(1)} %joined.3.refs_0_), channel_id=1, source_target_pairs={{0,24},{4,28},{8,16},{12,20},{16,8},{20,12},{24,0},{28,4},{32,56},... | collective-permute-start | bytes 24584 | tf_op jit(solution)/shard_map/ppermute | solution.py:562
  77.4 8.8 %collective-permute-start.15 = (bf16[9,16,128]{2,1,0:T(8,128)(2,1)S(1)}, bf16[9,16,128]{2,1,0:T(8,128)(2,1)S(1)}, u32[]{:S(2)}, u32[]{:S(2)}) collective-permute-start(bf16[9,16,128]{2,1,0:T(8,128)(2,1)S(1)} %joined.4.refs_0_), channel_id=1, source_target_pairs={{0,32},{4,36},{8,40},{12,44},{16,48},{20,52},{24,56},{28,60},{32,0... | collective-permute-start | bytes 110600 | tf_op jit(solution)/shard_map/ppermute | solution.py:562
  86.2 7.5 %collective-permute-start.16 = (bf16[18,16,128]{2,1,0:T(8,128)(2,1)S(1)}, bf16[18,16,128]{2,1,0:T(8,128)(2,1)S(1)}, u32[]{:S(2)}, u32[]{:S(2)}) collective-permute-start(bf16[18,16,128]{2,1,0:T(8,128)(2,1)S(1)} %joined.5.refs_0_), channel_id=1, source_target_pairs={{0,64},{4,68},{8,72},{12,76},{16,80},{20,84},{24,88},{28,92},{32,9... | collective-permute-start | bytes 221192 | tf_op jit(solution)/shard_map/ppermute | solution.py:562
  87.6 8.4 %collective-permute-start.17 = (bf16[18,16,128]{2,1,0:T(8,128)(2,1)S(1)}, bf16[18,16,128]{2,1,0:T(8,128)(2,1)S(1)}, u32[]{:S(2)}, u32[]{:S(2)}) collective-permute-start(bf16[18,16,128]{2,1,0:T(8,128)(2,1)S(1)} %joined.5.refs_0_), channel_id=1, source_target_pairs={{0,128},{4,132},{8,136},{12,140},{16,144},{20,148},{24,152},{28,15... | collective-permute-start | bytes 221192 | tf_op jit(solution)/shard_map/ppermute | solution.py:562
  91.1 7.3 %collective-permute-start.18 = (bf16[18,16,128]{2,1,0:T(8,128)(2,1)S(1)}, bf16[18,16,128]{2,1,0:T(8,128)(2,1)S(1)}, u32[]{:S(2)}, u32[]{:S(2)}) collective-permute-start(bf16[18,16,128]{2,1,0:T(8,128)(2,1)S(1)} %joined.5.refs_0_), channel_id=1, source_target_pairs={{0,192},{4,196},{8,200},{12,204},{16,208},{20,212},{24,216},{28,22... | collective-permute-start | bytes 221192 | tf_op jit(solution)/shard_map/ppermute | solution.py:562
  98.4 13.1 %copy-start.1 = (bf16[2048,64]{0,1:T(8,128)(2,1)S(1)}, bf16[2048,64]{0,1:T(8,128)(2,1)}, u32[]{:S(2)}) copy-start(bf16[2048,64]{0,1:T(8,128)(2,1)} %param.11) | copy-start | bytes 786436
  103.0 6.2 %collective-permute-start.19 = (bf16[4,64,128]{2,1,0:T(8,128)(2,1)S(1)}, bf16[4,64,128]{2,1,0:T(8,128)(2,1)S(1)}, u32[]{:S(2)}, u32[]{:S(2)}) collective-permute-start(bf16[4,64,128]{2,1,0:T(8,128)(2,1)S(1)} %get-tuple-element.37), channel_id=1, source_target_pairs={{0,1},{1,2},{2,3},{3,0},{4,5},{5,6},{6,7},{7,4},{8,9},{9,10},{10,1... | collective-permute-start | bytes 196616 | tf_op jit(solution)/shard_map/ppermute | solution.py:578
  104.1 6.1 %collective-permute-start.20 = (bf16[4,64,128]{2,1,0:T(8,128)(2,1)S(1)}, bf16[4,64,128]{2,1,0:T(8,128)(2,1)S(1)}, u32[]{:S(2)}, u32[]{:S(2)}) collective-permute-start(bf16[4,64,128]{2,1,0:T(8,128)(2,1)S(1)} %get-tuple-element.38), channel_id=1, source_target_pairs={{0,2},{1,3},{2,0},{3,1},{4,6},{5,7},{6,4},{7,5},{8,10},{9,11},{10,... | collective-permute-start | bytes 196616 | tf_op jit(solution)/shard_map/ppermute | solution.py:578
  107.2 4.3 %collective-permute-start.21 = (bf16[4,64,128]{2,1,0:T(8,128)(2,1)S(1)}, bf16[4,64,128]{2,1,0:T(8,128)(2,1)S(1)}, u32[]{:S(2)}, u32[]{:S(2)}) collective-permute-start(bf16[4,64,128]{2,1,0:T(8,128)(2,1)S(1)} %get-tuple-element.39), channel_id=1, source_target_pairs={{0,3},{1,0},{2,1},{3,2},{4,7},{5,4},{6,5},{7,6},{8,11},{9,8},{10,9... | collective-permute-start | bytes 196616 | tf_op jit(solution)/shard_map/ppermute | solution.py:578

commit v12 on v11

--- a/solution.py
+++ b/solution.py
@@ -570,7 +570,8 @@
     met, by_row = counts_call(*tiles, owner, stack, owners, library.shape[0], blocks)
     stripe = stripe_call(quarter, arrived, *rims(*rim_call(arrived, stack)), band, quarters)
     pair = joined_call([stripe, swapped(stripe, 1)])
-    bundle = joined_call([pair] + [swapped(pair, m) for m in (2, 4, 6)], stack)
+    quad = joined_call([pair, swapped(pair, 2)])
+    bundle = joined_call([quad, swapped(quad, 4)], stack)
     twin = joined_call([bundle, swapped(bundle, 8)])
     bundles = [twin] + [swapped(twin, m) for m in (16, 32, 48)]
     own, *sent, stripe = adjoint_call(quarter, owner, met, by_row, returned, bundles, library, blocks, quarters)

time: 114 us -> 114 us (level)
  starting transfers between devices: 52.5 us -> 50.3 us
  waiting for transfers between devices: 41 us -> 42.7 us
  Pallas kernels: 17.2 us -> 18.4 us
    ppermute x15 -> x14, waiting for transfers between devices: 19.3 us -> 20.7 us  [swapped(): return lax.ppermute(array, 'dom', [(i, i ^ m) for i in range(owners)])]
    ppermute x15 -> x14, starting transfers between devices: 18.8 us -> 17.6 us  [swapped(): return lax.ppermute(array, 'dom', [(i, i ^ m) for i in range(owners)])]
    pallas_call x1, Pallas kernels: 4.42 us -> 5.6 us  [first_call(): pl.pallas_call(kernel, out_shape=[pltpu.HBM((owners, rows, T), BF16), jax...]
  transfers between devices with their start and end apart: 24 -> 23, of which waited for: 15 -> 14; matrix products, arithmetic and copies ran while one was open for 0% -> 0% of each run, Pallas kernels for 5% -> 5%
where the time goes in v12:
time: 114 us; the launch traced here: 113 us
  starting transfers between devices  50.3 us (44%)
  waiting for transfers between devices  42.7 us (37%)
  Pallas kernels  18.4 us (16%)
  between operations  1.45 us (1%)
    ppermute x14, waiting for transfers between devices, swapped(): return lax.ppermute(array, 'dom', [(i, i ^ m) for i in range(owners)])  20.7 us
    all_to_all x2, waiting for transfers between devices, exchanged(): return lax.all_to_all(array, axis, split_axis=0, concat_axis=0, tiled=True)  18.1 us
    ppermute x14, starting transfers between devices, swapped(): return lax.ppermute(array, 'dom', [(i, i ^ m) for i in range(owners)])  17.6 us
    all_to_all x2, starting transfers between devices, exchanged(): return lax.all_to_all(array, axis, split_axis=0, concat_axis=0, tiled=True)  17.5 us
    ppermute x2, starting transfers between devices, rims(): left = lax.ppermute(tail, 'ray', [(i, i + 1) for i in range(quarters - 1)])  7.24 us
    pallas_call x1, Pallas kernels, first_call(): pl.pallas_call(kernel, out_shape=[pltpu.HBM((owners, rows, T), BF16), jax...  5.6 us
    ppermute x3, starting transfers between devices, shards(): lax.ppermute(part, 'ray', [(i, (i + m) % quarters) for i in range(quarter...  5.47 us
    pallas_call x1, Pallas kernels, adjoint_call(): pl.pallas_call(kernel, out_shape=[*(jax.ShapeDtypeStruct((held, size, T),...  4.55 us
  transfers between devices with their start and end apart: 23, of which 14 were waited for; matrix products, arithmetic and copies ran while one was open for 0% of the time, Pallas kernels for 5%

profile of v12, /device:TPU:8, one launch (start us, length us, event | category | flops | bytes accessed | tf_op | source)
XLA Modules:
  0.0 112.9 jit_solution(17364057506572535822)
XLA Ops:
  1.3 5.6 %forward_tiles.1 = (bf16[64,80,128]{2,1,0:T(8,128)(2,1)}, bf16[64,128]{1,0:T(8,128)(2,1)S(1)}, bf16[64,128]{1,0:T(8,128)(2,1)S(1)}, s32[8,128]{1,0:T(8,128)S(1)}) custom-call(s32[1,256]{1,0:T(1,128)} %bitcast.21, s32[1,256]{1,0:T(1,128)} %bitcast.23, s32[1,256]{1,0:T(1,128)} %bitcast.25, s32[1,1]{1,0:T(1,128)S(6)} %copy.11.count_ref, s32[1,64]{1,0:T(1,128)} %bitcast.13, ...), custom_call_target="tpu_custom_call" | custom-call | flops 536870912 | bytes 8388608 | tf_op jit(solution)/shard_map/forward_tiles/pallas_call | solution.py:115
  6.9 11.9 %all-to-all-start = ((bf16[64,80,128]{2,1,0:T(8,128)(2,1)}), bf16[64,80,128]{2,1,0:T(8,128)(2,1)S(1)}, u32[]{:S(2)}, u32[]{:S(2)}) async-start(bf16[64,80,128]{2,1,0:T(8,128)(2,1)} %get-tuple-element.25), calls=%async_computation | async-start | bytes 2621440 | tf_op jit(solution)/shard_map/all_to_all | solution.py:539
  18.8 2.7 %collective-permute-start = (bf16[64,128]{1,0:T(8,128)(2,1)S(1)}, bf16[64,128]{1,0:T(8,128)(2,1)S(1)}, u32[]{:S(2)}, u32[]{:S(2)}) collective-permute-start(bf16[64,128]{1,0:T(8,128)(2,1)S(1)} %get-tuple-element.21), channel_id=1, source_target_pairs={{0,1},{1,2},{2,3},{4,5},{5,6},{6,7},{8,9},{9,10},{10,11},{12,13},{... | collective-permute-start | bytes 49160 | tf_op jit(solution)/shard_map/ppermute | solution.py:557
  21.5 1.3 %collective-permute-start.1 = (bf16[64,128]{1,0:T(8,128)(2,1)S(1)}, bf16[64,128]{1,0:T(8,128)(2,1)S(1)}, u32[]{:S(2)}, u32[]{:S(2)}) collective-permute-start(bf16[64,128]{1,0:T(8,128)(2,1)S(1)} %get-tuple-element.22), channel_id=1, source_target_pairs={{1,0},{2,1},{3,2},{5,4},{6,5},{7,6},{9,8},{10,9},{11,10},{13,12},{... | collective-permute-start | bytes 49160 | tf_op jit(solution)/shard_map/ppermute | solution.py:558
  23.5 1.3 %collective-permute-start.4 = (s32[8,128]{1,0:T(8,128)S(1)}, s32[8,128]{1,0:T(8,128)S(1)}, u32[]{:S(2)}, u32[]{:S(2)}) collective-permute-start(s32[8,128]{1,0:T(8,128)S(1)} %get-tuple-element.23.refs_0_), channel_id=1, source_target_pairs={{0,12},{4,8},{8,4},{12,0},{16,28},{20,24},{24,20},{28,16},{32,44},... | collective-permute-start | bytes 12296 | tf_op jit(solution)/shard_map/ppermute | solution.py:562
  24.8 2.1 %collective-permute-start.5 = (s32[8,128]{1,0:T(8,128)S(1)}, s32[8,128]{1,0:T(8,128)S(1)}, u32[]{:S(2)}, u32[]{:S(2)}) collective-permute-start(s32[8,128]{1,0:T(8,128)S(1)} %get-tuple-element.23.refs_0_), channel_id=1, source_target_pairs={{0,16},{4,20},{8,24},{12,28},{16,0},{20,4},{24,8},{28,12},{32,48},... | collective-permute-start | bytes 12296 | tf_op jit(solution)/shard_map/ppermute | solution.py:562
  26.9 1.1 %collective-permute-start.6 = (s32[8,128]{1,0:T(8,128)S(1)}, s32[8,128]{1,0:T(8,128)S(1)}, u32[]{:S(2)}, u32[]{:S(2)}) collective-permute-start(s32[8,128]{1,0:T(8,128)S(1)} %get-tuple-element.23.refs_0_), channel_id=1, source_target_pairs={{0,20},{4,16},{8,28},{12,24},{16,4},{20,0},{24,12},{28,8},{32,52},... | collective-permute-start | bytes 12296 | tf_op jit(solution)/shard_map/ppermute | solution.py:562
  28.0 1.5 %collective-permute-start.7 = (s32[8,128]{1,0:T(8,128)S(1)}, s32[8,128]{1,0:T(8,128)S(1)}, u32[]{:S(2)}, u32[]{:S(2)}) collective-permute-start(s32[8,128]{1,0:T(8,128)S(1)} %get-tuple-element.23.refs_0_), channel_id=1, source_target_pairs={{0,24},{4,28},{8,16},{12,20},{16,8},{20,12},{24,0},{28,4},{32,56},... | collective-permute-start | bytes 12296 | tf_op jit(solution)/shard_map/ppermute | solution.py:562
  31.8 1.4 %collective-permute-done.8.refs_7_ = s32[8,128]{1,0:T(8,128)S(1)} collective-permute-done((s32[8,128]{1,0:T(8,128)S(1)}, s32[8,128]{1,0:T(8,128)S(1)}, u32[]{:S(2)}, u32[]{:S(2)}) %collective-permute-start.8) | collective-permute-done | bytes 4128 | tf_op jit(solution)/shard_map/ppermute | solution.py:562
  33.2 1.9 %phase_filter.1 = (bf16[64,2048]{1,0:T(8,128)(2,1)S(1)}, bf16[128,384]{1,0:T(8,128)(2,1)S(1)}, s32[8,128]{1,0:T(8,128)S(1)}) custom-call(bf16[64,2048]{1,0:T(8,128)(2,1)} %bitcast.18, bf16[64,128]{1,0:T(8,128)(2,1)S(1)} %collective-permute-done.l_ref, bf16[64,128]{1,0:T(8,128)(2,1)S(1)} %collective-permute-done.1.r_ref, bf16[129]{0:T(256)(128)(2,1)} %taps_hbm.1, ...), custom_call_target="tpu_custom_call" | custom-call | flops 67108864 | bytes 1048576 | tf_op jit(solution)/shard_map/phase_filter/pallas_call | solution.py:177
  35.1 18.1 %all-to-all-done.arrived_ref = bf16[64,80,128]{2,1,0:T(8,128)(2,1)S(1)} async-done(((bf16[64,80,128]{2,1,0:T(8,128)(2,1)}), bf16[64,80,128]{2,1,0:T(8,128)(2,1)S(1)}, u32[]{:S(2)}, u32[]{:S(2)}) %all-to-all-start) | async-done | bytes 1310752 | tf_op jit(solution)/shard_map/all_to_all | solution.py:539
  53.3 2.2 %slot_sums.1 = (f32[64,2048]{1,0:T(8,128)}, bf16[64,64,128]{2,1,0:T(8,128)(2,1)}, s32[8,128]{1,0:T(8,128)S(1)}) custom-call(s32[1,64]{1,0:T(1,128)S(1)} %bitcast.14, bf16[64,80,128]{2,1,0:T(8,128)(2,1)S(1)} %all-to-all-done.arrived_ref, bf16[64,2048]{1,0:T(8,128)(2,1)S(1)} %get-tuple-element.24.phase_ref, s32[8,128]{1,0:T(8,128)S(1)} %get-tuple-element.26.stacked_ref), custom_call_target="tpu_custom_call" | custom-call | flops 16777216 | bytes 8388608 | tf_op jit(solution)/shard_map/slot_sums/pallas_call | solution.py:274
  55.5 5.5 %all-to-all-start.1 = ((bf16[64,64,128]{2,1,0:T(8,128)(2,1)}), bf16[64,64,128]{2,1,0:T(8,128)(2,1)S(1)}, u32[]{:S(2)}, u32[]{:S(2)}) async-start(bf16[64,64,128]{2,1,0:T(8,128)(2,1)} %get-tuple-element.30), calls=%async_computation.1 | async-start | bytes 2097152 | tf_op jit(solution)/shard_map/all_to_all | solution.py:539
  61.1 1.3 %collective-permute-start.10 = (bf16[64,128]{1,0:T(8,128)(2,1)S(1)}, bf16[64,128]{1,0:T(8,128)(2,1)S(1)}, u32[]{:S(2)}, u32[]{:S(2)}) collective-permute-start(bf16[64,128]{1,0:T(8,128)(2,1)S(1)} %get-tuple-element.32), channel_id=1, source_target_pairs={{1,0},{2,1},{3,2},{5,4},{6,5},{7,6},{9,8},{10,9},{11,10},{13,12},{... | collective-permute-start | bytes 49160 | tf_op jit(solution)/shard_map/ppermute | solution.py:558
  62.4 4.5 %collective-permute-start.9 = (bf16[64,128]{1,0:T(8,128)(2,1)S(1)}, bf16[64,128]{1,0:T(8,128)(2,1)S(1)}, u32[]{:S(2)}, u32[]{:S(2)}) collective-permute-start(bf16[64,128]{1,0:T(8,128)(2,1)S(1)} %get-tuple-element.31), channel_id=1, source_target_pairs={{0,1},{1,2},{2,3},{4,5},{5,6},{6,7},{8,9},{9,10},{10,11},{12,13},{... | collective-permute-start | bytes 49160 | tf_op jit(solution)/shard_map/ppermute | solution.py:557
  66.9 1.4 %collective-permute-done.9.l_ref = bf16[64,128]{1,0:T(8,128)(2,1)S(1)} collective-permute-done((bf16[64,128]{1,0:T(8,128)(2,1)S(1)}, bf16[64,128]{1,0:T(8,128)(2,1)S(1)}, u32[]{:S(2)}, u32[]{:S(2)}) %collective-permute-start.9) | collective-permute-done | bytes 16416 | tf_op jit(solution)/shard_map/ppermute | solution.py:557
  68.4 1.5 %stripe.1.refs_0_ = bf16[1,16,128]{2,1,0:T(8,128)(2,1)S(1)} custom-call(s32[1]{0:T(128)} %bitcast.7.q_ref, bf16[64,80,128]{2,1,0:T(8,128)(2,1)S(1)} %all-to-all-done.arrived_ref, bf16[64,128]{1,0:T(8,128)(2,1)S(1)} %collective-permute-done.9.l_ref, bf16[64,128]{1,0:T(8,128)(2,1)S(1)} %collective-permute-done.10.r_ref, ...), custom_call_target="tpu_custom_call" | custom-call | flops 67108864 | bytes 1048576 | tf_op jit(solution)/shard_map/stripe/pallas_call | solution.py:326
  70.0 1.2 %collective-permute-done.11.refs_1_ = bf16[1,16,128]{2,1,0:T(8,128)(2,1)S(1)} collective-permute-done((bf16[1,16,128]{2,1,0:T(8,128)(2,1)S(1)}, bf16[1,16,128]{2,1,0:T(8,128)(2,1)S(1)}, u32[]{:S(2)}, u32[]{:S(2)}) %collective-permute-start.11) | collective-permute-done | bytes 4128 | tf_op jit(solution)/shard_map/ppermute | solution.py:562
  71.6 3.2 %collective-permute-done.12.refs_1_ = bf16[2,16,128]{2,1,0:T(8,128)(2,1)S(1)} collective-permute-done((bf16[2,16,128]{2,1,0:T(8,128)(2,1)S(1)}, bf16[2,16,128]{2,1,0:T(8,128)(2,1)S(1)}, u32[]{:S(2)}, u32[]{:S(2)}) %collective-permute-start.12) | collective-permute-done | bytes 8224 | tf_op jit(solution)/shard_map/ppermute | solution.py:562
  74.8 2.1 %collective-permute-start.13 = (bf16[4,16,128]{2,1,0:T(8,128)(2,1)S(1)}, bf16[4,16,128]{2,1,0:T(8,128)(2,1)S(1)}, u32[]{:S(2)}, u32[]{:S(2)}) collective-permute-start(bf16[4,16,128]{2,1,0:T(8,128)(2,1)S(1)} %joined.5.refs_0_), channel_id=1, source_target_pairs={{0,16},{4,20},{8,24},{12,28},{16,0},{20,4},{24,8},{28,12},{32,48},... | collective-permute-start | bytes 49160 | tf_op jit(solution)/shard_map/ppermute | solution.py:562
  76.9 3.7 %collective-permute-done.13.refs_1_ = bf16[4,16,128]{2,1,0:T(8,128)(2,1)S(1)} collective-permute-done((bf16[4,16,128]{2,1,0:T(8,128)(2,1)S(1)}, bf16[4,16,128]{2,1,0:T(8,128)(2,1)S(1)}, u32[]{:S(2)}, u32[]{:S(2)}) %collective-permute-start.13) | collective-permute-done | bytes 16416 | tf_op jit(solution)/shard_map/ppermute | solution.py:562
  80.6 1.4 %collective-permute-start.14 = (bf16[9,16,128]{2,1,0:T(8,128)(2,1)S(1)}, bf16[9,16,128]{2,1,0:T(8,128)(2,1)S(1)}, u32[]{:S(2)}, u32[]{:S(2)}) collective-permute-start(bf16[9,16,128]{2,1,0:T(8,128)(2,1)S(1)} %joined.6.refs_0_), channel_id=1, source_target_pairs={{0,32},{4,36},{8,40},{12,44},{16,48},{20,52},{24,56},{28,60},{32,0... | collective-permute-start | bytes 110600 | tf_op jit(solution)/shard_map/ppermute | solution.py:562
  82.0 4.6 %collective-permute-done.14.refs_1_ = bf16[9,16,128]{2,1,0:T(8,128)(2,1)S(1)} collective-permute-done((bf16[9,16,128]{2,1,0:T(8,128)(2,1)S(1)}, bf16[9,16,128]{2,1,0:T(8,128)(2,1)S(1)}, u32[]{:S(2)}, u32[]{:S(2)}) %collective-permute-start.14) | collective-permute-done | bytes 36896 | tf_op jit(solution)/shard_map/ppermute | solution.py:562
  86.6 1.4 %collective-permute-start.15 = (bf16[18,16,128]{2,1,0:T(8,128)(2,1)S(1)}, bf16[18,16,128]{2,1,0:T(8,128)(2,1)S(1)}, u32[]{:S(2)}, u32[]{:S(2)}) collective-permute-start(bf16[18,16,128]{2,1,0:T(8,128)(2,1)S(1)} %joined.7.refs_0_), channel_id=1, source_target_pairs={{0,64},{4,68},{8,72},{12,76},{16,80},{20,84},{24,88},{28,92},{32,9... | collective-permute-start | bytes 221192 | tf_op jit(solution)/shard_map/ppermute | solution.py:562
  88.0 3.6 %collective-permute-start.16 = (bf16[18,16,128]{2,1,0:T(8,128)(2,1)S(1)}, bf16[18,16,128]{2,1,0:T(8,128)(2,1)S(1)}, u32[]{:S(2)}, u32[]{:S(2)}) collective-permute-start(bf16[18,16,128]{2,1,0:T(8,128)(2,1)S(1)} %joined.7.refs_0_), channel_id=1, source_target_pairs={{0,128},{4,132},{8,136},{12,140},{16,144},{20,148},{24,152},{28,15... | collective-permute-start | bytes 221192 | tf_op jit(solution)/shard_map/ppermute | solution.py:562
  91.5 1.5 %collective-permute-start.17 = (bf16[18,16,128]{2,1,0:T(8,128)(2,1)S(1)}, bf16[18,16,128]{2,1,0:T(8,128)(2,1)S(1)}, u32[]{:S(2)}, u32[]{:S(2)}) collective-permute-start(bf16[18,16,128]{2,1,0:T(8,128)(2,1)S(1)} %joined.7.refs_0_), channel_id=1, source_target_pairs={{0,192},{4,196},{8,200},{12,204},{16,208},{20,212},{24,216},{28,22... | collective-permute-start | bytes 221192 | tf_op jit(solution)/shard_map/ppermute | solution.py:562
  94.1 2.3 %collective-permute-done.16.refs_2_ = bf16[18,16,128]{2,1,0:T(8,128)(2,1)S(1)} collective-permute-done((bf16[18,16,128]{2,1,0:T(8,128)(2,1)S(1)}, bf16[18,16,128]{2,1,0:T(8,128)(2,1)S(1)}, u32[]{:S(2)}, u32[]{:S(2)}) %collective-permute-start.16) | collective-permute-done | bytes 73760 | tf_op jit(solution)/shard_map/ppermute | solution.py:562
  96.3 2.5 %collective-permute-done.17.refs_3_ = bf16[18,16,128]{2,1,0:T(8,128)(2,1)S(1)} collective-permute-done((bf16[18,16,128]{2,1,0:T(8,128)(2,1)S(1)}, bf16[18,16,128]{2,1,0:T(8,128)(2,1)S(1)}, u32[]{:S(2)}, u32[]{:S(2)}) %collective-permute-start.17) | collective-permute-done | bytes 73760 | tf_op jit(solution)/shard_map/ppermute | solution.py:562
  98.8 4.6 %adjoint_tiles.1 = (f32[4,64,128]{2,1,0:T(8,128)S(1)}, bf16[4,64,128]{2,1,0:T(8,128)(2,1)S(1)}, bf16[4,64,128]{2,1,0:T(8,128)(2,1)S(1)}, bf16[4,64,128]{2,1,0:T(8,128)(2,1)S(1)}, f32[16,64,128]{2,1,0:T(8,128)S(1)}) custom-call(s32[1]{0:T(128)} %bitcast.7.q_ref, s32[1]{0:T(128)} %bitcast.8.owner_ref, bf16[256,128]{1,0:T(8,128)(2,1)S(1)} %get-tuple-element.28.met_ref, ...), custom_call_target="tpu_custom_call" | custom-call | flops 536870912 | bytes 8388608 | tf_op jit(solution)/shard_map/adjoint_tiles/pallas_call | solution.py:465
  104.4 3.5 %collective-permute-start.19 = (bf16[4,64,128]{2,1,0:T(8,128)(2,1)S(1)}, bf16[4,64,128]{2,1,0:T(8,128)(2,1)S(1)}, u32[]{:S(2)}, u32[]{:S(2)}) collective-permute-start(bf16[4,64,128]{2,1,0:T(8,128)(2,1)S(1)} %get-tuple-element.38), channel_id=1, source_target_pairs={{0,2},{1,3},{2,0},{3,1},{4,6},{5,7},{6,4},{7,5},{8,10},{9,11},{10,... | collective-permute-start | bytes 196616 | tf_op jit(solution)/shard_map/ppermute | solution.py:579
  109.7 1.2 %collective-permute-done.19.refs_1_ = bf16[4,64,128]{2,1,0:T(8,128)(2,1)S(1)} collective-permute-done((bf16[4,64,128]{2,1,0:T(8,128)(2,1)S(1)}, bf16[4,64,128]{2,1,0:T(8,128)(2,1)S(1)}, u32[]{:S(2)}, u32[]{:S(2)}) %collective-permute-start.19) | collective-permute-done | bytes 65568 | tf_op jit(solution)/shard_map/ppermute | solution.py:579
  110.8 1.3 %collective-permute-done.20.refs_2_ = bf16[4,64,128]{2,1,0:T(8,128)(2,1)S(1)} collective-permute-done((bf16[4,64,128]{2,1,0:T(8,128)(2,1)S(1)}, bf16[4,64,128]{2,1,0:T(8,128)(2,1)S(1)}, u32[]{:S(2)}, u32[]{:S(2)}) %collective-permute-start.20) | collective-permute-done | bytes 65568 | tf_op jit(solution)/shard_map/ppermute | solution.py:579
  (33 shorter events, 8.0 us)
Async XLA Ops:
  6.9 46.4 %copy-start.2 = (s32[1,1,64]{2,1,0:T(1,128)S(1)}, s32[1,1,64]{2,1,0:T(1,128)}, u32[]{:S(2)}) copy-start(s32[1,1,64]{2,1,0:T(1,128)} %param.17) | copy-start | bytes 772
  6.9 46.4 %all-to-all-start = ((bf16[64,80,128]{2,1,0:T(8,128)(2,1)}), bf16[64,80,128]{2,1,0:T(8,128)(2,1)S(1)}, u32[]{:S(2)}, u32[]{:S(2)}) async-start(bf16[64,80,128]{2,1,0:T(8,128)(2,1)} %get-tuple-element.25), calls=%async_computation | async-start | bytes 2621440 | tf_op jit(solution)/shard_map/all_to_all | solution.py:539
  18.8 14.4 %collective-permute-start = (bf16[64,128]{1,0:T(8,128)(2,1)S(1)}, bf16[64,128]{1,0:T(8,128)(2,1)S(1)}, u32[]{:S(2)}, u32[]{:S(2)}) collective-permute-start(bf16[64,128]{1,0:T(8,128)(2,1)S(1)} %get-tuple-element.21), channel_id=1, source_target_pairs={{0,1},{1,2},{2,3},{4,5},{5,6},{6,7},{8,9},{9,10},{10,11},{12,13},{... | collective-permute-start | bytes 49160 | tf_op jit(solution)/shard_map/ppermute | solution.py:557
  21.5 11.7 %collective-permute-start.1 = (bf16[64,128]{1,0:T(8,128)(2,1)S(1)}, bf16[64,128]{1,0:T(8,128)(2,1)S(1)}, u32[]{:S(2)}, u32[]{:S(2)}) collective-permute-start(bf16[64,128]{1,0:T(8,128)(2,1)S(1)} %get-tuple-element.22), channel_id=1, source_target_pairs={{1,0},{2,1},{3,2},{5,4},{6,5},{7,6},{9,8},{10,9},{11,10},{13,12},{... | collective-permute-start | bytes 49160 | tf_op jit(solution)/shard_map/ppermute | solution.py:558
  22.8 2.0 %collective-permute-start.2 = (s32[8,128]{1,0:T(8,128)S(1)}, s32[8,128]{1,0:T(8,128)S(1)}, u32[]{:S(2)}, u32[]{:S(2)}) collective-permute-start(s32[8,128]{1,0:T(8,128)S(1)} %get-tuple-element.23.refs_0_), channel_id=1, source_target_pairs={{0,4},{4,0},{8,12},{12,8},{16,20},{20,16},{24,28},{28,24},{32,36},... | collective-permute-start | bytes 12296 | tf_op jit(solution)/shard_map/ppermute | solution.py:562
  22.9 4.0 %collective-permute-start.3 = (s32[8,128]{1,0:T(8,128)S(1)}, s32[8,128]{1,0:T(8,128)S(1)}, u32[]{:S(2)}, u32[]{:S(2)}) collective-permute-start(s32[8,128]{1,0:T(8,128)S(1)} %get-tuple-element.23.refs_0_), channel_id=1, source_target_pairs={{0,8},{4,12},{8,0},{12,4},{16,24},{20,28},{24,16},{28,20},{32,40},... | collective-permute-start | bytes 12296 | tf_op jit(solution)/shard_map/ppermute | solution.py:562
  23.5 4.6 %collective-permute-start.4 = (s32[8,128]{1,0:T(8,128)S(1)}, s32[8,128]{1,0:T(8,128)S(1)}, u32[]{:S(2)}, u32[]{:S(2)}) collective-permute-start(s32[8,128]{1,0:T(8,128)S(1)} %get-tuple-element.23.refs_0_), channel_id=1, source_target_pairs={{0,12},{4,8},{8,4},{12,0},{16,28},{20,24},{24,20},{28,16},{32,44},... | collective-permute-start | bytes 12296 | tf_op jit(solution)/shard_map/ppermute | solution.py:562
  24.8 5.4 %collective-permute-start.5 = (s32[8,128]{1,0:T(8,128)S(1)}, s32[8,128]{1,0:T(8,128)S(1)}, u32[]{:S(2)}, u32[]{:S(2)}) collective-permute-start(s32[8,128]{1,0:T(8,128)S(1)} %get-tuple-element.23.refs_0_), channel_id=1, source_target_pairs={{0,16},{4,20},{8,24},{12,28},{16,0},{20,4},{24,8},{28,12},{32,48},... | collective-permute-start | bytes 12296 | tf_op jit(solution)/shard_map/ppermute | solution.py:562
  26.9 4.6 %collective-permute-start.6 = (s32[8,128]{1,0:T(8,128)S(1)}, s32[8,128]{1,0:T(8,128)S(1)}, u32[]{:S(2)}, u32[]{:S(2)}) collective-permute-start(s32[8,128]{1,0:T(8,128)S(1)} %get-tuple-element.23.refs_0_), channel_id=1, source_target_pairs={{0,20},{4,16},{8,28},{12,24},{16,4},{20,0},{24,12},{28,8},{32,52},... | collective-permute-start | bytes 12296 | tf_op jit(solution)/shard_map/ppermute | solution.py:562
  28.0 3.7 %collective-permute-start.7 = (s32[8,128]{1,0:T(8,128)S(1)}, s32[8,128]{1,0:T(8,128)S(1)}, u32[]{:S(2)}, u32[]{:S(2)}) collective-permute-start(s32[8,128]{1,0:T(8,128)S(1)} %get-tuple-element.23.refs_0_), channel_id=1, source_target_pairs={{0,24},{4,28},{8,16},{12,20},{16,8},{20,12},{24,0},{28,4},{32,56},... | collective-permute-start | bytes 12296 | tf_op jit(solution)/shard_map/ppermute | solution.py:562
  30.2 3.0 %collective-permute-start.8 = (s32[8,128]{1,0:T(8,128)S(1)}, s32[8,128]{1,0:T(8,128)S(1)}, u32[]{:S(2)}, u32[]{:S(2)}) collective-permute-start(s32[8,128]{1,0:T(8,128)S(1)} %get-tuple-element.23.refs_0_), channel_id=1, source_target_pairs={{0,28},{4,24},{8,20},{12,16},{16,12},{20,8},{24,4},{28,0},{32,60},... | collective-permute-start | bytes 12296 | tf_op jit(solution)/shard_map/ppermute | solution.py:562
  55.5 43.4 %all-to-all-start.1 = ((bf16[64,64,128]{2,1,0:T(8,128)(2,1)}), bf16[64,64,128]{2,1,0:T(8,128)(2,1)S(1)}, u32[]{:S(2)}, u32[]{:S(2)}) async-start(bf16[64,64,128]{2,1,0:T(8,128)(2,1)} %get-tuple-element.30), calls=%async_computation.1 | async-start | bytes 2097152 | tf_op jit(solution)/shard_map/all_to_all | solution.py:539
  61.1 5.9 %collective-permute-start.10 = (bf16[64,128]{1,0:T(8,128)(2,1)S(1)}, bf16[64,128]{1,0:T(8,128)(2,1)S(1)}, u32[]{:S(2)}, u32[]{:S(2)}) collective-permute-start(bf16[64,128]{1,0:T(8,128)(2,1)S(1)} %get-tuple-element.32), channel_id=1, source_target_pairs={{1,0},{2,1},{3,2},{5,4},{6,5},{7,6},{9,8},{10,9},{11,10},{13,12},{... | collective-permute-start | bytes 49160 | tf_op jit(solution)/shard_map/ppermute | solution.py:558
  62.4 6.0 %collective-permute-start.9 = (bf16[64,128]{1,0:T(8,128)(2,1)S(1)}, bf16[64,128]{1,0:T(8,128)(2,1)S(1)}, u32[]{:S(2)}, u32[]{:S(2)}) collective-permute-start(bf16[64,128]{1,0:T(8,128)(2,1)S(1)} %get-tuple-element.31), channel_id=1, source_target_pairs={{0,1},{1,2},{2,3},{4,5},{5,6},{6,7},{8,9},{9,10},{10,11},{12,13},{... | collective-permute-start | bytes 49160 | tf_op jit(solution)/shard_map/ppermute | solution.py:557
  69.9 39.0 %copy-start = (f32[64,2048]{1,0:T(8,128)S(1)}, f32[64,2048]{1,0:T(8,128)}, u32[]{:S(2)}) copy-start(f32[64,2048]{1,0:T(8,128)} %get-tuple-element.35.forward_ref) | copy-start | bytes 1572868
  69.9 1.3 %collective-permute-start.11 = (bf16[1,16,128]{2,1,0:T(8,128)(2,1)S(1)}, bf16[1,16,128]{2,1,0:T(8,128)(2,1)S(1)}, u32[]{:S(2)}, u32[]{:S(2)}) collective-permute-start(bf16[1,16,128]{2,1,0:T(8,128)(2,1)S(1)} %stripe.1.refs_0_), channel_id=1, source_target_pairs={{0,4},{4,0},{8,12},{12,8},{16,20},{20,16},{24,28},{28,24},{32,36},... | collective-permute-start | bytes 12296 | tf_op jit(solution)/shard_map/ppermute | solution.py:562
  71.2 3.7 %collective-permute-start.12 = (bf16[2,16,128]{2,1,0:T(8,128)(2,1)S(1)}, bf16[2,16,128]{2,1,0:T(8,128)(2,1)S(1)}, u32[]{:S(2)}, u32[]{:S(2)}) collective-permute-start(bf16[2,16,128]{2,1,0:T(8,128)(2,1)S(1)} %joined.4.refs_0_), channel_id=1, source_target_pairs={{0,8},{4,12},{8,0},{12,4},{16,24},{20,28},{24,16},{28,20},{32,40},... | collective-permute-start | bytes 24584 | tf_op jit(solution)/shard_map/ppermute | solution.py:562
  74.8 5.8 %collective-permute-start.13 = (bf16[4,16,128]{2,1,0:T(8,128)(2,1)S(1)}, bf16[4,16,128]{2,1,0:T(8,128)(2,1)S(1)}, u32[]{:S(2)}, u32[]{:S(2)}) collective-permute-start(bf16[4,16,128]{2,1,0:T(8,128)(2,1)S(1)} %joined.5.refs_0_), channel_id=1, source_target_pairs={{0,16},{4,20},{8,24},{12,28},{16,0},{20,4},{24,8},{28,12},{32,48},... | collective-permute-start | bytes 49160 | tf_op jit(solution)/shard_map/ppermute | solution.py:562
  80.6 6.0 %collective-permute-start.14 = (bf16[9,16,128]{2,1,0:T(8,128)(2,1)S(1)}, bf16[9,16,128]{2,1,0:T(8,128)(2,1)S(1)}, u32[]{:S(2)}, u32[]{:S(2)}) collective-permute-start(bf16[9,16,128]{2,1,0:T(8,128)(2,1)S(1)} %joined.6.refs_0_), channel_id=1, source_target_pairs={{0,32},{4,36},{8,40},{12,44},{16,48},{20,52},{24,56},{28,60},{32,0... | collective-permute-start | bytes 110600 | tf_op jit(solution)/shard_map/ppermute | solution.py:562
  86.6 7.5 %collective-permute-start.15 = (bf16[18,16,128]{2,1,0:T(8,128)(2,1)S(1)}, bf16[18,16,128]{2,1,0:T(8,128)(2,1)S(1)}, u32[]{:S(2)}, u32[]{:S(2)}) collective-permute-start(bf16[18,16,128]{2,1,0:T(8,128)(2,1)S(1)} %joined.7.refs_0_), channel_id=1, source_target_pairs={{0,64},{4,68},{8,72},{12,76},{16,80},{20,84},{24,88},{28,92},{32,9... | collective-permute-start | bytes 221192 | tf_op jit(solution)/shard_map/ppermute | solution.py:562
  88.0 8.4 %collective-permute-start.16 = (bf16[18,16,128]{2,1,0:T(8,128)(2,1)S(1)}, bf16[18,16,128]{2,1,0:T(8,128)(2,1)S(1)}, u32[]{:S(2)}, u32[]{:S(2)}) collective-permute-start(bf16[18,16,128]{2,1,0:T(8,128)(2,1)S(1)} %joined.7.refs_0_), channel_id=1, source_target_pairs={{0,128},{4,132},{8,136},{12,140},{16,144},{20,148},{24,152},{28,15... | collective-permute-start | bytes 221192 | tf_op jit(solution)/shard_map/ppermute | solution.py:562
  91.5 7.3 %collective-permute-start.17 = (bf16[18,16,128]{2,1,0:T(8,128)(2,1)S(1)}, bf16[18,16,128]{2,1,0:T(8,128)(2,1)S(1)}, u32[]{:S(2)}, u32[]{:S(2)}) collective-permute-start(bf16[18,16,128]{2,1,0:T(8,128)(2,1)S(1)} %joined.7.refs_0_), channel_id=1, source_target_pairs={{0,192},{4,196},{8,200},{12,204},{16,208},{20,212},{24,216},{28,22... | collective-permute-start | bytes 221192 | tf_op jit(solution)/shard_map/ppermute | solution.py:562
  98.8 13.3 %copy-start.1 = (bf16[2048,64]{0,1:T(8,128)(2,1)S(1)}, bf16[2048,64]{0,1:T(8,128)(2,1)}, u32[]{:S(2)}) copy-start(bf16[2048,64]{0,1:T(8,128)(2,1)} %param.11) | copy-start | bytes 786436
  103.4 6.3 %collective-permute-start.18 = (bf16[4,64,128]{2,1,0:T(8,128)(2,1)S(1)}, bf16[4,64,128]{2,1,0:T(8,128)(2,1)S(1)}, u32[]{:S(2)}, u32[]{:S(2)}) collective-permute-start(bf16[4,64,128]{2,1,0:T(8,128)(2,1)S(1)} %get-tuple-element.37), channel_id=1, source_target_pairs={{0,1},{1,2},{2,3},{3,0},{4,5},{5,6},{6,7},{7,4},{8,9},{9,10},{10,1... | collective-permute-start | bytes 196616 | tf_op jit(solution)/shard_map/ppermute | solution.py:579
  104.4 6.5 %collective-permute-start.19 = (bf16[4,64,128]{2,1,0:T(8,128)(2,1)S(1)}, bf16[4,64,128]{2,1,0:T(8,128)(2,1)S(1)}, u32[]{:S(2)}, u32[]{:S(2)}) collective-permute-start(bf16[4,64,128]{2,1,0:T(8,128)(2,1)S(1)} %get-tuple-element.38), channel_id=1, source_target_pairs={{0,2},{1,3},{2,0},{3,1},{4,6},{5,7},{6,4},{7,5},{8,10},{9,11},{10,... | collective-permute-start | bytes 196616 | tf_op jit(solution)/shard_map/ppermute | solution.py:579
  107.9 4.3 %collective-permute-start.20 = (bf16[4,64,128]{2,1,0:T(8,128)(2,1)S(1)}, bf16[4,64,128]{2,1,0:T(8,128)(2,1)S(1)}, u32[]{:S(2)}, u32[]{:S(2)}) collective-permute-start(bf16[4,64,128]{2,1,0:T(8,128)(2,1)S(1)} %get-tuple-element.39), channel_id=1, source_target_pairs={{0,3},{1,0},{2,1},{3,2},{4,7},{5,4},{6,5},{7,6},{8,11},{9,8},{10,9... | collective-permute-start | bytes 196616 | tf_op jit(solution)/shard_map/ppermute | solution.py:579

commit v13 on v11

--- a/solution.py
+++ b/solution.py
@@ -426,8 +426,8 @@
         fetch.start()
         terms[...] = returned_ref[...].astype(F32).reshape(owners * size, T)
         numbers = []
-        for ref in bundle_refs:
-            for t in range(0, each * (near + 1), near + 1):
+        for t in range(0, each * (near + 1), near + 1):
+            for ref in bundle_refs:
                 m = len(numbers)
                 every[m * near : (m + 1) * near] = ref[t : t + near]
                 numbers.append(ref[t + near].astype(F32)[:near])
@@ -571,8 +571,8 @@
     stripe = stripe_call(quarter, arrived, *rims(*rim_call(arrived, stack)), band, quarters)
     pair = joined_call([stripe, swapped(stripe, 1)])
     bundle = joined_call([pair] + [swapped(pair, m) for m in (2, 4, 6)], stack)
-    twin = joined_call([bundle, swapped(bundle, 8)])
-    bundles = [twin] + [swapped(twin, m) for m in (16, 32, 48)]
+    twin = joined_call([bundle, swapped(bundle, 32)])
+    bundles = [twin] + [swapped(twin, m) for m in (8, 16, 24)]
     own, *sent, stripe = adjoint_call(quarter, owner, met, by_row, returned, bundles, library, blocks, quarters)
     others = [
         lax.ppermute(part, "ray", [(i, (i + m) % quarters) for i in range(quarters)])

time: 114 us -> 115 us (level)
  starting transfers between devices: 52.5 us -> 57.3 us
  waiting for transfers between devices: 41 us -> 37.9 us
    ppermute x15, starting transfers between devices: 18.8 us -> 21 us  [swapped(): return lax.ppermute(array, 'dom', [(i, i ^ m) for i in range(owners)])]
    ppermute x3, starting transfers between devices: 5.41 us -> 6.66 us  [shards(): lax.ppermute(part, 'ray', [(i, (i + m) % quarters) for i in range(quarter...]
    ppermute x2, starting transfers between devices: 7.5 us -> 8.67 us  [rims(): left = lax.ppermute(tail, 'ray', [(i, i + 1) for i in range(quarters - 1)])]
  transfers between devices with their start and end apart: 24 -> 24, of which waited for: 15 -> 14; matrix products, arithmetic and copies ran while one was open for 0% -> 0% of each run, Pallas kernels for 5% -> 5%
where the time goes in v13:
time: 115 us; the launch traced here: 114 us
  starting transfers between devices  57.3 us (50%)
  waiting for transfers between devices  37.9 us (33%)
  Pallas kernels  17 us (15%)
  between operations  1.45 us (1%)
    ppermute x15, starting transfers between devices, swapped(): return lax.ppermute(array, 'dom', [(i, i ^ m) for i in range(owners)])  21 us
    all_to_all x2, starting transfers between devices, exchanged(): return lax.all_to_all(array, axis, split_axis=0, concat_axis=0, tiled=True)  18.4 us
    ppermute x15, waiting for transfers between devices, swapped(): return lax.ppermute(array, 'dom', [(i, i ^ m) for i in range(owners)])  18.3 us
    all_to_all x2, waiting for transfers between devices, exchanged(): return lax.all_to_all(array, axis, split_axis=0, concat_axis=0, tiled=True)  16.9 us
    ppermute x2, starting transfers between devices, rims(): left = lax.ppermute(tail, 'ray', [(i, i + 1) for i in range(quarters - 1)])  8.67 us
    ppermute x3, starting transfers between devices, shards(): lax.ppermute(part, 'ray', [(i, (i + m) % quarters) for i in range(quarter...  6.66 us
    pallas_call x1, Pallas kernels, adjoint_call(): pl.pallas_call(kernel, out_shape=[*(jax.ShapeDtypeStruct((held, size, T),...  4.55 us
    pallas_call x1, Pallas kernels, first_call(): pl.pallas_call(kernel, out_shape=[pltpu.HBM((owners, rows, T), BF16), jax...  4.24 us
  transfers between devices with their start and end apart: 24, of which 14 were waited for; matrix products, arithmetic and copies ran while one was open for 0% of the time, Pallas kernels for 5%

profile of v13, /device:TPU:8, one launch (start us, length us, event | category | flops | bytes accessed | tf_op | source)
XLA Modules:
  0.0 113.7 jit_solution(4507802933216174446)
XLA Ops:
  1.3 4.2 %forward_tiles.1 = (bf16[64,80,128]{2,1,0:T(8,128)(2,1)}, bf16[64,128]{1,0:T(8,128)(2,1)S(1)}, bf16[64,128]{1,0:T(8,128)(2,1)S(1)}, s32[8,128]{1,0:T(8,128)S(1)}) custom-call(s32[1,256]{1,0:T(1,128)} %bitcast.21, s32[1,256]{1,0:T(1,128)} %bitcast.23, s32[1,256]{1,0:T(1,128)} %bitcast.25, s32[1,1]{1,0:T(1,128)S(6)} %copy.11.count_ref, s32[1,64]{1,0:T(1,128)} %bitcast.13, ...), custom_call_target="tpu_custom_call" | custom-call | flops 536870912 | bytes 8388608 | tf_op jit(solution)/shard_map/forward_tiles/pallas_call | solution.py:115
  5.5 12.8 %all-to-all-start = ((bf16[64,80,128]{2,1,0:T(8,128)(2,1)}), bf16[64,80,128]{2,1,0:T(8,128)(2,1)S(1)}, u32[]{:S(2)}, u32[]{:S(2)}) async-start(bf16[64,80,128]{2,1,0:T(8,128)(2,1)} %get-tuple-element.25), calls=%async_computation | async-start | bytes 2621440 | tf_op jit(solution)/shard_map/all_to_all | solution.py:539
  18.4 4.0 %collective-permute-start = (bf16[64,128]{1,0:T(8,128)(2,1)S(1)}, bf16[64,128]{1,0:T(8,128)(2,1)S(1)}, u32[]{:S(2)}, u32[]{:S(2)}) collective-permute-start(bf16[64,128]{1,0:T(8,128)(2,1)S(1)} %get-tuple-element.21), channel_id=1, source_target_pairs={{0,1},{1,2},{2,3},{4,5},{5,6},{6,7},{8,9},{9,10},{10,11},{12,13},{... | collective-permute-start | bytes 49160 | tf_op jit(solution)/shard_map/ppermute | solution.py:557
  22.4 1.3 %collective-permute-start.1 = (bf16[64,128]{1,0:T(8,128)(2,1)S(1)}, bf16[64,128]{1,0:T(8,128)(2,1)S(1)}, u32[]{:S(2)}, u32[]{:S(2)}) collective-permute-start(bf16[64,128]{1,0:T(8,128)(2,1)S(1)} %get-tuple-element.22), channel_id=1, source_target_pairs={{1,0},{2,1},{3,2},{5,4},{6,5},{7,6},{9,8},{10,9},{11,10},{13,12},{... | collective-permute-start | bytes 49160 | tf_op jit(solution)/shard_map/ppermute | solution.py:558
  24.3 1.3 %collective-permute-start.4 = (s32[8,128]{1,0:T(8,128)S(1)}, s32[8,128]{1,0:T(8,128)S(1)}, u32[]{:S(2)}, u32[]{:S(2)}) collective-permute-start(s32[8,128]{1,0:T(8,128)S(1)} %get-tuple-element.23.refs_0_), channel_id=1, source_target_pairs={{0,12},{4,8},{8,4},{12,0},{16,28},{20,24},{24,20},{28,16},{32,44},... | collective-permute-start | bytes 12296 | tf_op jit(solution)/shard_map/ppermute | solution.py:562
  25.7 2.1 %collective-permute-start.5 = (s32[8,128]{1,0:T(8,128)S(1)}, s32[8,128]{1,0:T(8,128)S(1)}, u32[]{:S(2)}, u32[]{:S(2)}) collective-permute-start(s32[8,128]{1,0:T(8,128)S(1)} %get-tuple-element.23.refs_0_), channel_id=1, source_target_pairs={{0,16},{4,20},{8,24},{12,28},{16,0},{20,4},{24,8},{28,12},{32,48},... | collective-permute-start | bytes 12296 | tf_op jit(solution)/shard_map/ppermute | solution.py:562
  27.8 1.1 collective-permute-start.6
  28.9 1.5 %collective-permute-start.7 = (s32[8,128]{1,0:T(8,128)S(1)}, s32[8,128]{1,0:T(8,128)S(1)}, u32[]{:S(2)}, u32[]{:S(2)}) collective-permute-start(s32[8,128]{1,0:T(8,128)S(1)} %get-tuple-element.23.refs_0_), channel_id=1, source_target_pairs={{0,24},{4,28},{8,16},{12,20},{16,8},{20,12},{24,0},{28,4},{32,56},... | collective-permute-start | bytes 12296 | tf_op jit(solution)/shard_map/ppermute | solution.py:562
  30.8 1.0 collective-permute-start.8
  32.5 1.4 %collective-permute-done.8.refs_7_ = s32[8,128]{1,0:T(8,128)S(1)} collective-permute-done((s32[8,128]{1,0:T(8,128)S(1)}, s32[8,128]{1,0:T(8,128)S(1)}, u32[]{:S(2)}, u32[]{:S(2)}) %collective-permute-start.8) | collective-permute-done | bytes 4128 | tf_op jit(solution)/shard_map/ppermute | solution.py:562
  33.9 1.9 %phase_filter.1 = (bf16[64,2048]{1,0:T(8,128)(2,1)S(1)}, bf16[128,384]{1,0:T(8,128)(2,1)S(1)}, s32[8,128]{1,0:T(8,128)S(1)}) custom-call(bf16[64,2048]{1,0:T(8,128)(2,1)} %bitcast.18, bf16[64,128]{1,0:T(8,128)(2,1)S(1)} %collective-permute-done.l_ref, bf16[64,128]{1,0:T(8,128)(2,1)S(1)} %collective-permute-done.1.r_ref, bf16[129]{0:T(256)(128)(2,1)} %taps_hbm.1, ...), custom_call_target="tpu_custom_call" | custom-call | flops 67108864 | bytes 1048576 | tf_op jit(solution)/shard_map/phase_filter/pallas_call | solution.py:177
  35.9 16.9 %all-to-all-done.arrived_ref = bf16[64,80,128]{2,1,0:T(8,128)(2,1)S(1)} async-done(((bf16[64,80,128]{2,1,0:T(8,128)(2,1)}), bf16[64,80,128]{2,1,0:T(8,128)(2,1)S(1)}, u32[]{:S(2)}, u32[]{:S(2)}) %all-to-all-start) | async-done | bytes 1310752 | tf_op jit(solution)/shard_map/all_to_all | solution.py:539
  52.8 2.2 %slot_sums.1 = (f32[64,2048]{1,0:T(8,128)}, bf16[64,64,128]{2,1,0:T(8,128)(2,1)}, s32[8,128]{1,0:T(8,128)S(1)}) custom-call(s32[1,64]{1,0:T(1,128)S(1)} %bitcast.14, bf16[64,80,128]{2,1,0:T(8,128)(2,1)S(1)} %all-to-all-done.arrived_ref, bf16[64,2048]{1,0:T(8,128)(2,1)S(1)} %get-tuple-element.24.phase_ref, s32[8,128]{1,0:T(8,128)S(1)} %get-tuple-element.26.stacked_ref), custom_call_target="tpu_custom_call" | custom-call | flops 16777216 | bytes 8388608 | tf_op jit(solution)/shard_map/slot_sums/pallas_call | solution.py:274
  55.0 5.5 %all-to-all-start.1 = ((bf16[64,64,128]{2,1,0:T(8,128)(2,1)}), bf16[64,64,128]{2,1,0:T(8,128)(2,1)S(1)}, u32[]{:S(2)}, u32[]{:S(2)}) async-start(bf16[64,64,128]{2,1,0:T(8,128)(2,1)} %get-tuple-element.30), calls=%async_computation.1 | async-start | bytes 2097152 | tf_op jit(solution)/shard_map/all_to_all | solution.py:539
  60.6 1.3 %collective-permute-start.10 = (bf16[64,128]{1,0:T(8,128)(2,1)S(1)}, bf16[64,128]{1,0:T(8,128)(2,1)S(1)}, u32[]{:S(2)}, u32[]{:S(2)}) collective-permute-start(bf16[64,128]{1,0:T(8,128)(2,1)S(1)} %get-tuple-element.32), channel_id=1, source_target_pairs={{1,0},{2,1},{3,2},{5,4},{6,5},{7,6},{9,8},{10,9},{11,10},{13,12},{... | collective-permute-start | bytes 49160 | tf_op jit(solution)/shard_map/ppermute | solution.py:558
  61.9 4.6 %collective-permute-start.9 = (bf16[64,128]{1,0:T(8,128)(2,1)S(1)}, bf16[64,128]{1,0:T(8,128)(2,1)S(1)}, u32[]{:S(2)}, u32[]{:S(2)}) collective-permute-start(bf16[64,128]{1,0:T(8,128)(2,1)S(1)} %get-tuple-element.31), channel_id=1, source_target_pairs={{0,1},{1,2},{2,3},{4,5},{5,6},{6,7},{8,9},{9,10},{10,11},{12,13},{... | collective-permute-start | bytes 49160 | tf_op jit(solution)/shard_map/ppermute | solution.py:557
  66.6 1.4 %collective-permute-done.9.l_ref = bf16[64,128]{1,0:T(8,128)(2,1)S(1)} collective-permute-done((bf16[64,128]{1,0:T(8,128)(2,1)S(1)}, bf16[64,128]{1,0:T(8,128)(2,1)S(1)}, u32[]{:S(2)}, u32[]{:S(2)}) %collective-permute-start.9) | collective-permute-done | bytes 16416 | tf_op jit(solution)/shard_map/ppermute | solution.py:557
  68.0 1.5 %stripe.1.refs_0_ = bf16[1,16,128]{2,1,0:T(8,128)(2,1)S(1)} custom-call(s32[1]{0:T(128)} %bitcast.7.q_ref, bf16[64,80,128]{2,1,0:T(8,128)(2,1)S(1)} %all-to-all-done.arrived_ref, bf16[64,128]{1,0:T(8,128)(2,1)S(1)} %collective-permute-done.9.l_ref, bf16[64,128]{1,0:T(8,128)(2,1)S(1)} %collective-permute-done.10.r_ref, ...), custom_call_target="tpu_custom_call" | custom-call | flops 67108864 | bytes 1048576 | tf_op jit(solution)/shard_map/stripe/pallas_call | solution.py:326
  69.7 1.2 %collective-permute-done.11.refs_1_ = bf16[1,16,128]{2,1,0:T(8,128)(2,1)S(1)} collective-permute-done((bf16[1,16,128]{2,1,0:T(8,128)(2,1)S(1)}, bf16[1,16,128]{2,1,0:T(8,128)(2,1)S(1)}, u32[]{:S(2)}, u32[]{:S(2)}) %collective-permute-start.11) | collective-permute-done | bytes 4128 | tf_op jit(solution)/shard_map/ppermute | solution.py:562
  71.3 2.5 %collective-permute-start.13 = (bf16[2,16,128]{2,1,0:T(8,128)(2,1)S(1)}, bf16[2,16,128]{2,1,0:T(8,128)(2,1)S(1)}, u32[]{:S(2)}, u32[]{:S(2)}) collective-permute-start(bf16[2,16,128]{2,1,0:T(8,128)(2,1)S(1)} %joined.3.refs_0_), channel_id=1, source_target_pairs={{0,16},{4,20},{8,24},{12,28},{16,0},{20,4},{24,8},{28,12},{32,48},... | collective-permute-start | bytes 24584 | tf_op jit(solution)/shard_map/ppermute | solution.py:562
  74.5 2.0 %collective-permute-done.13.refs_2_ = bf16[2,16,128]{2,1,0:T(8,128)(2,1)S(1)} collective-permute-done((bf16[2,16,128]{2,1,0:T(8,128)(2,1)S(1)}, bf16[2,16,128]{2,1,0:T(8,128)(2,1)S(1)}, u32[]{:S(2)}, u32[]{:S(2)}) %collective-permute-start.13) | collective-permute-done | bytes 8224 | tf_op jit(solution)/shard_map/ppermute | solution.py:562
  76.5 1.1 collective-permute-done.14.refs_3_
  77.5 5.4 %collective-permute-start.15 = (bf16[9,16,128]{2,1,0:T(8,128)(2,1)S(1)}, bf16[9,16,128]{2,1,0:T(8,128)(2,1)S(1)}, u32[]{:S(2)}, u32[]{:S(2)}) collective-permute-start(bf16[9,16,128]{2,1,0:T(8,128)(2,1)S(1)} %joined.4.refs_0_), channel_id=1, source_target_pairs={{0,128},{4,132},{8,136},{12,140},{16,144},{20,148},{24,152},{28,15... | collective-permute-start | bytes 110600 | tf_op jit(solution)/shard_map/ppermute | solution.py:562
  83.0 8.0 %collective-permute-done.15.refs_1_ = bf16[9,16,128]{2,1,0:T(8,128)(2,1)S(1)} collective-permute-done((bf16[9,16,128]{2,1,0:T(8,128)(2,1)S(1)}, bf16[9,16,128]{2,1,0:T(8,128)(2,1)S(1)}, u32[]{:S(2)}, u32[]{:S(2)}) %collective-permute-start.15) | collective-permute-done | bytes 36896 | tf_op jit(solution)/shard_map/ppermute | solution.py:562
  91.6 3.8 %collective-permute-start.18 = (bf16[18,16,128]{2,1,0:T(8,128)(2,1)S(1)}, bf16[18,16,128]{2,1,0:T(8,128)(2,1)S(1)}, u32[]{:S(2)}, u32[]{:S(2)}) collective-permute-start(bf16[18,16,128]{2,1,0:T(8,128)(2,1)S(1)} %joined.5.refs_0_), channel_id=1, source_target_pairs={{0,96},{4,100},{8,104},{12,108},{16,112},{20,116},{24,120},{28,124... | collective-permute-start | bytes 221192 | tf_op jit(solution)/shard_map/ppermute | solution.py:562
  95.3 1.0 tile_counts.1
  96.3 3.3 %collective-permute-done.17.refs_2_ = bf16[18,16,128]{2,1,0:T(8,128)(2,1)S(1)} collective-permute-done((bf16[18,16,128]{2,1,0:T(8,128)(2,1)S(1)}, bf16[18,16,128]{2,1,0:T(8,128)(2,1)S(1)}, u32[]{:S(2)}, u32[]{:S(2)}) %collective-permute-start.17) | collective-permute-done | bytes 73760 | tf_op jit(solution)/shard_map/ppermute | solution.py:562
  99.6 4.6 %adjoint_tiles.1 = (f32[4,64,128]{2,1,0:T(8,128)S(1)}, bf16[4,64,128]{2,1,0:T(8,128)(2,1)S(1)}, bf16[4,64,128]{2,1,0:T(8,128)(2,1)S(1)}, bf16[4,64,128]{2,1,0:T(8,128)(2,1)S(1)}, f32[16,64,128]{2,1,0:T(8,128)S(1)}) custom-call(s32[1]{0:T(128)} %bitcast.7.q_ref, s32[1]{0:T(128)} %bitcast.8.owner_ref, bf16[256,128]{1,0:T(8,128)(2,1)S(1)} %get-tuple-element.28.met_ref, ...), custom_call_target="tpu_custom_call" | custom-call | flops 536870912 | bytes 8388608 | tf_op jit(solution)/shard_map/adjoint_tiles/pallas_call | solution.py:465
  104.2 2.4 %collective-permute-start.19 = (bf16[4,64,128]{2,1,0:T(8,128)(2,1)S(1)}, bf16[4,64,128]{2,1,0:T(8,128)(2,1)S(1)}, u32[]{:S(2)}, u32[]{:S(2)}) collective-permute-start(bf16[4,64,128]{2,1,0:T(8,128)(2,1)S(1)} %get-tuple-element.37), channel_id=1, source_target_pairs={{0,1},{1,2},{2,3},{3,0},{4,5},{5,6},{6,7},{7,4},{8,9},{9,10},{10,1... | collective-permute-start | bytes 196616 | tf_op jit(solution)/shard_map/ppermute | solution.py:578
  106.6 2.1 %collective-permute-start.20 = (bf16[4,64,128]{2,1,0:T(8,128)(2,1)S(1)}, bf16[4,64,128]{2,1,0:T(8,128)(2,1)S(1)}, u32[]{:S(2)}, u32[]{:S(2)}) collective-permute-start(bf16[4,64,128]{2,1,0:T(8,128)(2,1)S(1)} %get-tuple-element.38), channel_id=1, source_target_pairs={{0,2},{1,3},{2,0},{3,1},{4,6},{5,7},{6,4},{7,5},{8,10},{9,11},{10,... | collective-permute-start | bytes 196616 | tf_op jit(solution)/shard_map/ppermute | solution.py:578
  108.7 2.1 %collective-permute-start.21 = (bf16[4,64,128]{2,1,0:T(8,128)(2,1)S(1)}, bf16[4,64,128]{2,1,0:T(8,128)(2,1)S(1)}, u32[]{:S(2)}, u32[]{:S(2)}) collective-permute-start(bf16[4,64,128]{2,1,0:T(8,128)(2,1)S(1)} %get-tuple-element.39), channel_id=1, source_target_pairs={{0,3},{1,0},{2,1},{3,2},{4,7},{5,4},{6,5},{7,6},{8,11},{9,8},{10,9... | collective-permute-start | bytes 196616 | tf_op jit(solution)/shard_map/ppermute | solution.py:578
  110.9 0.8 residual.1
  (34 shorter events, 5.8 us)
Async XLA Ops:
  5.5 47.3 %copy-start.2 = (s32[1,1,64]{2,1,0:T(1,128)S(1)}, s32[1,1,64]{2,1,0:T(1,128)}, u32[]{:S(2)}) copy-start(s32[1,1,64]{2,1,0:T(1,128)} %param.17) | copy-start | bytes 772
  5.5 47.2 %all-to-all-start = ((bf16[64,80,128]{2,1,0:T(8,128)(2,1)}), bf16[64,80,128]{2,1,0:T(8,128)(2,1)S(1)}, u32[]{:S(2)}, u32[]{:S(2)}) async-start(bf16[64,80,128]{2,1,0:T(8,128)(2,1)} %get-tuple-element.25), calls=%async_computation | async-start | bytes 2621440 | tf_op jit(solution)/shard_map/all_to_all | solution.py:539
  18.4 15.6 %collective-permute-start = (bf16[64,128]{1,0:T(8,128)(2,1)S(1)}, bf16[64,128]{1,0:T(8,128)(2,1)S(1)}, u32[]{:S(2)}, u32[]{:S(2)}) collective-permute-start(bf16[64,128]{1,0:T(8,128)(2,1)S(1)} %get-tuple-element.21), channel_id=1, source_target_pairs={{0,1},{1,2},{2,3},{4,5},{5,6},{6,7},{8,9},{9,10},{10,11},{12,13},{... | collective-permute-start | bytes 49160 | tf_op jit(solution)/shard_map/ppermute | solution.py:557
  22.4 11.5 %collective-permute-start.1 = (bf16[64,128]{1,0:T(8,128)(2,1)S(1)}, bf16[64,128]{1,0:T(8,128)(2,1)S(1)}, u32[]{:S(2)}, u32[]{:S(2)}) collective-permute-start(bf16[64,128]{1,0:T(8,128)(2,1)S(1)} %get-tuple-element.22), channel_id=1, source_target_pairs={{1,0},{2,1},{3,2},{5,4},{6,5},{7,6},{9,8},{10,9},{11,10},{13,12},{... | collective-permute-start | bytes 49160 | tf_op jit(solution)/shard_map/ppermute | solution.py:558
  23.7 2.0 %collective-permute-start.2 = (s32[8,128]{1,0:T(8,128)S(1)}, s32[8,128]{1,0:T(8,128)S(1)}, u32[]{:S(2)}, u32[]{:S(2)}) collective-permute-start(s32[8,128]{1,0:T(8,128)S(1)} %get-tuple-element.23.refs_0_), channel_id=1, source_target_pairs={{0,4},{4,0},{8,12},{12,8},{16,20},{20,16},{24,28},{28,24},{32,36},... | collective-permute-start | bytes 12296 | tf_op jit(solution)/shard_map/ppermute | solution.py:562
  23.8 4.0 %collective-permute-start.3 = (s32[8,128]{1,0:T(8,128)S(1)}, s32[8,128]{1,0:T(8,128)S(1)}, u32[]{:S(2)}, u32[]{:S(2)}) collective-permute-start(s32[8,128]{1,0:T(8,128)S(1)} %get-tuple-element.23.refs_0_), channel_id=1, source_target_pairs={{0,8},{4,12},{8,0},{12,4},{16,24},{20,28},{24,16},{28,20},{32,40},... | collective-permute-start | bytes 12296 | tf_op jit(solution)/shard_map/ppermute | solution.py:562
  24.3 4.6 %collective-permute-start.4 = (s32[8,128]{1,0:T(8,128)S(1)}, s32[8,128]{1,0:T(8,128)S(1)}, u32[]{:S(2)}, u32[]{:S(2)}) collective-permute-start(s32[8,128]{1,0:T(8,128)S(1)} %get-tuple-element.23.refs_0_), channel_id=1, source_target_pairs={{0,12},{4,8},{8,4},{12,0},{16,28},{20,24},{24,20},{28,16},{32,44},... | collective-permute-start | bytes 12296 | tf_op jit(solution)/shard_map/ppermute | solution.py:562
  25.7 5.1 %collective-permute-start.5 = (s32[8,128]{1,0:T(8,128)S(1)}, s32[8,128]{1,0:T(8,128)S(1)}, u32[]{:S(2)}, u32[]{:S(2)}) collective-permute-start(s32[8,128]{1,0:T(8,128)S(1)} %get-tuple-element.23.refs_0_), channel_id=1, source_target_pairs={{0,16},{4,20},{8,24},{12,28},{16,0},{20,4},{24,8},{28,12},{32,48},... | collective-permute-start | bytes 12296 | tf_op jit(solution)/shard_map/ppermute | solution.py:562
  27.8 4.6 %collective-permute-start.6 = (s32[8,128]{1,0:T(8,128)S(1)}, s32[8,128]{1,0:T(8,128)S(1)}, u32[]{:S(2)}, u32[]{:S(2)}) collective-permute-start(s32[8,128]{1,0:T(8,128)S(1)} %get-tuple-element.23.refs_0_), channel_id=1, source_target_pairs={{0,20},{4,16},{8,28},{12,24},{16,4},{20,0},{24,12},{28,8},{32,52},... | collective-permute-start | bytes 12296 | tf_op jit(solution)/shard_map/ppermute | solution.py:562
  28.9 3.6 %collective-permute-start.7 = (s32[8,128]{1,0:T(8,128)S(1)}, s32[8,128]{1,0:T(8,128)S(1)}, u32[]{:S(2)}, u32[]{:S(2)}) collective-permute-start(s32[8,128]{1,0:T(8,128)S(1)} %get-tuple-element.23.refs_0_), channel_id=1, source_target_pairs={{0,24},{4,28},{8,16},{12,20},{16,8},{20,12},{24,0},{28,4},{32,56},... | collective-permute-start | bytes 12296 | tf_op jit(solution)/shard_map/ppermute | solution.py:562
  30.8 3.1 %collective-permute-start.8 = (s32[8,128]{1,0:T(8,128)S(1)}, s32[8,128]{1,0:T(8,128)S(1)}, u32[]{:S(2)}, u32[]{:S(2)}) collective-permute-start(s32[8,128]{1,0:T(8,128)S(1)} %get-tuple-element.23.refs_0_), channel_id=1, source_target_pairs={{0,28},{4,24},{8,20},{12,16},{16,12},{20,8},{24,4},{28,0},{32,60},... | collective-permute-start | bytes 12296 | tf_op jit(solution)/shard_map/ppermute | solution.py:562
  55.0 44.6 %all-to-all-start.1 = ((bf16[64,64,128]{2,1,0:T(8,128)(2,1)}), bf16[64,64,128]{2,1,0:T(8,128)(2,1)S(1)}, u32[]{:S(2)}, u32[]{:S(2)}) async-start(bf16[64,64,128]{2,1,0:T(8,128)(2,1)} %get-tuple-element.30), calls=%async_computation.1 | async-start | bytes 2097152 | tf_op jit(solution)/shard_map/all_to_all | solution.py:539
  60.6 6.0 %collective-permute-start.10 = (bf16[64,128]{1,0:T(8,128)(2,1)S(1)}, bf16[64,128]{1,0:T(8,128)(2,1)S(1)}, u32[]{:S(2)}, u32[]{:S(2)}) collective-permute-start(bf16[64,128]{1,0:T(8,128)(2,1)S(1)} %get-tuple-element.32), channel_id=1, source_target_pairs={{1,0},{2,1},{3,2},{5,4},{6,5},{7,6},{9,8},{10,9},{11,10},{13,12},{... | collective-permute-start | bytes 49160 | tf_op jit(solution)/shard_map/ppermute | solution.py:558
  61.9 6.1 %collective-permute-start.9 = (bf16[64,128]{1,0:T(8,128)(2,1)S(1)}, bf16[64,128]{1,0:T(8,128)(2,1)S(1)}, u32[]{:S(2)}, u32[]{:S(2)}) collective-permute-start(bf16[64,128]{1,0:T(8,128)(2,1)S(1)} %get-tuple-element.31), channel_id=1, source_target_pairs={{0,1},{1,2},{2,3},{4,5},{5,6},{6,7},{8,9},{9,10},{10,11},{12,13},{... | collective-permute-start | bytes 49160 | tf_op jit(solution)/shard_map/ppermute | solution.py:557
  69.5 41.3 %copy-start = (f32[64,2048]{1,0:T(8,128)S(1)}, f32[64,2048]{1,0:T(8,128)}, u32[]{:S(2)}) copy-start(f32[64,2048]{1,0:T(8,128)} %get-tuple-element.35.forward_ref) | copy-start | bytes 1572868
  69.6 1.3 %collective-permute-start.11 = (bf16[1,16,128]{2,1,0:T(8,128)(2,1)S(1)}, bf16[1,16,128]{2,1,0:T(8,128)(2,1)S(1)}, u32[]{:S(2)}, u32[]{:S(2)}) collective-permute-start(bf16[1,16,128]{2,1,0:T(8,128)(2,1)S(1)} %stripe.1.refs_0_), channel_id=1, source_target_pairs={{0,4},{4,0},{8,12},{12,8},{16,20},{20,16},{24,28},{28,24},{32,36},... | collective-permute-start | bytes 12296 | tf_op jit(solution)/shard_map/ppermute | solution.py:562
  70.8 3.7 %collective-permute-start.12 = (bf16[2,16,128]{2,1,0:T(8,128)(2,1)S(1)}, bf16[2,16,128]{2,1,0:T(8,128)(2,1)S(1)}, u32[]{:S(2)}, u32[]{:S(2)}) collective-permute-start(bf16[2,16,128]{2,1,0:T(8,128)(2,1)S(1)} %joined.3.refs_0_), channel_id=1, source_target_pairs={{0,8},{4,12},{8,0},{12,4},{16,24},{20,28},{24,16},{28,20},{32,40},... | collective-permute-start | bytes 24584 | tf_op jit(solution)/shard_map/ppermute | solution.py:562
  71.3 5.2 %collective-permute-start.13 = (bf16[2,16,128]{2,1,0:T(8,128)(2,1)S(1)}, bf16[2,16,128]{2,1,0:T(8,128)(2,1)S(1)}, u32[]{:S(2)}, u32[]{:S(2)}) collective-permute-start(bf16[2,16,128]{2,1,0:T(8,128)(2,1)S(1)} %joined.3.refs_0_), channel_id=1, source_target_pairs={{0,16},{4,20},{8,24},{12,28},{16,0},{20,4},{24,8},{28,12},{32,48},... | collective-permute-start | bytes 24584 | tf_op jit(solution)/shard_map/ppermute | solution.py:562
  73.7 3.8 %collective-permute-start.14 = (bf16[2,16,128]{2,1,0:T(8,128)(2,1)S(1)}, bf16[2,16,128]{2,1,0:T(8,128)(2,1)S(1)}, u32[]{:S(2)}, u32[]{:S(2)}) collective-permute-start(bf16[2,16,128]{2,1,0:T(8,128)(2,1)S(1)} %joined.3.refs_0_), channel_id=1, source_target_pairs={{0,24},{4,28},{8,16},{12,20},{16,8},{20,12},{24,0},{28,4},{32,56},... | collective-permute-start | bytes 24584 | tf_op jit(solution)/shard_map/ppermute | solution.py:562
  77.5 13.4 %collective-permute-start.15 = (bf16[9,16,128]{2,1,0:T(8,128)(2,1)S(1)}, bf16[9,16,128]{2,1,0:T(8,128)(2,1)S(1)}, u32[]{:S(2)}, u32[]{:S(2)}) collective-permute-start(bf16[9,16,128]{2,1,0:T(8,128)(2,1)S(1)} %joined.4.refs_0_), channel_id=1, source_target_pairs={{0,128},{4,132},{8,136},{12,140},{16,144},{20,148},{24,152},{28,15... | collective-permute-start | bytes 110600 | tf_op jit(solution)/shard_map/ppermute | solution.py:562
  90.9 5.4 %collective-permute-start.16 = (bf16[18,16,128]{2,1,0:T(8,128)(2,1)S(1)}, bf16[18,16,128]{2,1,0:T(8,128)(2,1)S(1)}, u32[]{:S(2)}, u32[]{:S(2)}) collective-permute-start(bf16[18,16,128]{2,1,0:T(8,128)(2,1)S(1)} %joined.5.refs_0_), channel_id=1, source_target_pairs={{0,32},{4,36},{8,40},{12,44},{16,48},{20,52},{24,56},{28,60},{32,0... | collective-permute-start | bytes 221192 | tf_op jit(solution)/shard_map/ppermute | solution.py:562
  91.5 8.1 %collective-permute-start.17 = (bf16[18,16,128]{2,1,0:T(8,128)(2,1)S(1)}, bf16[18,16,128]{2,1,0:T(8,128)(2,1)S(1)}, u32[]{:S(2)}, u32[]{:S(2)}) collective-permute-start(bf16[18,16,128]{2,1,0:T(8,128)(2,1)S(1)} %joined.5.refs_0_), channel_id=1, source_target_pairs={{0,64},{4,68},{8,72},{12,76},{16,80},{20,84},{24,88},{28,92},{32,9... | collective-permute-start | bytes 221192 | tf_op jit(solution)/shard_map/ppermute | solution.py:562
  91.6 8.1 %collective-permute-start.18 = (bf16[18,16,128]{2,1,0:T(8,128)(2,1)S(1)}, bf16[18,16,128]{2,1,0:T(8,128)(2,1)S(1)}, u32[]{:S(2)}, u32[]{:S(2)}) collective-permute-start(bf16[18,16,128]{2,1,0:T(8,128)(2,1)S(1)} %joined.5.refs_0_), channel_id=1, source_target_pairs={{0,96},{4,100},{8,104},{12,108},{16,112},{20,116},{24,120},{28,124... | collective-permute-start | bytes 221192 | tf_op jit(solution)/shard_map/ppermute | solution.py:562
  99.6 13.3 %copy-start.1 = (bf16[2048,64]{0,1:T(8,128)(2,1)S(1)}, bf16[2048,64]{0,1:T(8,128)(2,1)}, u32[]{:S(2)}) copy-start(bf16[2048,64]{0,1:T(8,128)(2,1)} %param.11) | copy-start | bytes 786436
  104.2 7.5 %collective-permute-start.19 = (bf16[4,64,128]{2,1,0:T(8,128)(2,1)S(1)}, bf16[4,64,128]{2,1,0:T(8,128)(2,1)S(1)}, u32[]{:S(2)}, u32[]{:S(2)}) collective-permute-start(bf16[4,64,128]{2,1,0:T(8,128)(2,1)S(1)} %get-tuple-element.37), channel_id=1, source_target_pairs={{0,1},{1,2},{2,3},{3,0},{4,5},{5,6},{6,7},{7,4},{8,9},{9,10},{10,1... | collective-permute-start | bytes 196616 | tf_op jit(solution)/shard_map/ppermute | solution.py:578
  106.6 5.8 %collective-permute-start.20 = (bf16[4,64,128]{2,1,0:T(8,128)(2,1)S(1)}, bf16[4,64,128]{2,1,0:T(8,128)(2,1)S(1)}, u32[]{:S(2)}, u32[]{:S(2)}) collective-permute-start(bf16[4,64,128]{2,1,0:T(8,128)(2,1)S(1)} %get-tuple-element.38), channel_id=1, source_target_pairs={{0,2},{1,3},{2,0},{3,1},{4,6},{5,7},{6,4},{7,5},{8,10},{9,11},{10,... | collective-permute-start | bytes 196616 | tf_op jit(solution)/shard_map/ppermute | solution.py:578
  108.7 4.3 %collective-permute-start.21 = (bf16[4,64,128]{2,1,0:T(8,128)(2,1)S(1)}, bf16[4,64,128]{2,1,0:T(8,128)(2,1)S(1)}, u32[]{:S(2)}, u32[]{:S(2)}) collective-permute-start(bf16[4,64,128]{2,1,0:T(8,128)(2,1)S(1)} %get-tuple-element.39), channel_id=1, source_target_pairs={{0,3},{1,0},{2,1},{3,2},{4,7},{5,4},{6,5},{7,6},{8,11},{9,8},{10,9... | collective-permute-start | bytes 196616 | tf_op jit(solution)/shard_map/ppermute | solution.py:578
